TPU v7x, 32 devices: a whole 2x2x4 slice. The times are simulated.
32 devices in a mesh: slab: 8 (over z, x), chan: 4 (over y, core).
Axes of the slice: x: 2, y: 2, z: 4, core: 2. Of those that a mesh axis runs over, the one named last changes fastest.
Arguments:
- stream_speed_field: bfloat16 [3, 8, 8, 8, 16384], P(None, None, None, None, ('slab', 'chan')), may hold values from -6 to 6
- liquid_to_solid_element: int32 [16384], P(('slab', 'chan')), may hold values from 0 to 16383, as said below
- previous_panel_warmth: float32 [8, 8, 8, 8, 2048], P(None, None, None, 'chan', 'slab'), may hold values from -6 to 6
- pointwise_energy_source: float32 [8, 8, 8, 8, 2048], P(None, None, None, 'chan', 'slab'), may hold values from -6 to 6
- coked_element_flags: int32 [8, 2048], P('chan', 'slab'), may hold values from 0 to 1, as said below
- coking_thickness_plies: int32 [8, 2048], P('chan', 'slab'), may hold values from 1 to 8
Outputs:
- stepped_stream_speed: bfloat16 [3, 8, 8, 8, 16384], P(None, None, None, None, ('slab', 'chan'))
- solved_panel_warmth: float32 [8, 8, 8, 8, 2048], P(None, None, None, 'chan', 'slab')
Inputs may be any that keep to these rules, and one draw needn't show every extreme that they name: `liquid_to_solid_element`: A permutation of the element numbers. Element n belongs to thermal device n // 512 (devices numbered slab first, then chan) at local position n % 512. The fluid device f holds 256 elements of thermal device f and at most 128 of each of the thermal devices f + 1, f - 1 and f + 4 (modulo the number of devices), none of any other; these three counts are the same for every f, and one of them is 128. `coked_element_flags`: at most 192 flagged elements among one thermal device's elements, and exactly 192 on some device.
All inputs are finite; a program needn't handle non-finite values.
Results may differ from a plain program's by a relative error of at most 0.005.
Values may be sent and summed in bfloat16 or wider, within the bound.
No kernel may reach another device: no remote copies, remote signals or barrier semaphores. Data moves between devices by JAX's collectives and lax.ppermute only.
A program may use at most 128 MiB of HBM per device.

v0:
```python
import jax
import jax.numpy as jnp
import numpy as np
from jax import lax
from jax.sharding import PartitionSpec as P

ITERS = 5


highest = lax.Precision.HIGHEST
coolant_throughput = 0.05
time_step = 0.01
viscosity = 0.02
cross_gain = 0.4
layer_damp = 0.25
forward_forms = ("ir,rst...->ist...", "js,rst...->rjt...", "kt,rst...->rsk...")
backward_forms = ("ir,ist...->rst...", "js,rjt...->rst...", "kt,rsk...->rst...")
fluid_forms = ("ir,crste->ciste", "js,crste->crjte", "kt,crste->crske")


def from_behind(block, axis, distance):
    devices = range(lax.axis_size(axis))
    route = [((i - distance) % len(devices), i) for i in devices]
    return lax.ppermute(block, axis, route)


def with_halo(x, sides, width):
    for axis, dim in sides:
        devices, length = (lax.axis_size(axis), x.shape[dim])
        up = [(i, (i + 1) % devices) for i in range(devices - 1)]
        down = [(j, i) for i, j in up]
        last = lax.slice_in_dim(x, length - width, length, axis=dim)
        initial = lax.slice_in_dim(x, 0, width, axis=dim)
        before = lax.ppermute(last, axis, up)
        after = lax.ppermute(initial, axis, down)
        x = jnp.concatenate([before, x, after], axis=dim)
    return x


def gll_tables():
    points = np.array(
        [
            -1.0,
            -0.8717401485096066,
            -0.5917001814331423,
            -0.2092992179024789,
            0.2092992179024789,
            0.5917001814331423,
            0.8717401485096066,
            1.0,
        ]
    )
    weights = np.array(
        [
            1.0 / 28.0,
            0.2107042271435061,
            0.3411226924835044,
            0.4124587946587038,
            0.4124587946587038,
            0.3411226924835044,
            0.2107042271435061,
            1.0 / 28.0,
        ]
    )
    lower_poly = np.ones(8)
    upper_poly = points.copy()
    for degree in range(1, 7):
        next_poly = ((2 * degree + 1) * points * upper_poly - degree * lower_poly) / (degree + 1)
        lower_poly = upper_poly
        upper_poly = next_poly
    gaps_matrix = points[:, None] - points[None, :] + np.eye(8)
    derivative = upper_poly[:, None] / (upper_poly[None, :] * gaps_matrix)
    derivative = derivative * (1.0 - np.eye(8))
    derivative[0, 0] = -14.0
    derivative[7, 7] = 14.0
    return (jnp.asarray(derivative, jnp.float32), jnp.asarray(weights, jnp.float32))


def forward(matrix, field, conjugate_update_vector):
    return jnp.einsum(forward_forms[conjugate_update_vector], matrix, field, precision=highest)


def backward(matrix, field, conjugate_update_vector):
    return jnp.einsum(backward_forms[conjugate_update_vector], matrix, field, precision=highest)


def fluid_update(velocity_block, matrix):
    velocity_now = velocity_block.astype(jnp.float32)
    gradients = [
        jnp.einsum(fluid_forms[conjugate_update_vector], matrix, velocity_now, precision=highest)
        for conjugate_update_vector in range(3)
    ]
    convect = (
        velocity_now[0:1] * gradients[0]
        + velocity_now[1:2] * gradients[1]
        + velocity_now[2:3] * gradients[2]
    )
    laplace = jnp.einsum(fluid_forms[0], matrix, gradients[0], precision=highest)
    laplace = laplace + jnp.einsum(fluid_forms[1], matrix, gradients[1], precision=highest)
    laplace = laplace + jnp.einsum(fluid_forms[2], matrix, gradients[2], precision=highest)
    updated = velocity_now + time_step * (viscosity * laplace - convect)
    return updated.astype(jnp.bfloat16)


def conductivity_of(stepped_stream_speed):
    faster = stepped_stream_speed.astype(jnp.float32)
    return (
        1.0 + 0.5 * (faster[0] * faster[0] + faster[1] * faster[1] + faster[2] * faster[2])
    ).astype(jnp.bfloat16)


def move_blocks(payload, liquid_to_solid_element):
    row_count, element_count = payload.shape
    kept_count = element_count // 2
    capacity = element_count // 4
    chan_count = lax.axis_size("chan")
    device_total = lax.axis_size("slab") * chan_count
    my_device = lax.axis_index("slab") * chan_count + lax.axis_index("chan")
    target_dev = liquid_to_solid_element // element_count
    target_slot = liquid_to_solid_element % element_count
    distance = (target_dev - my_device) % device_total
    offset_group = jnp.where(
        distance == 1,
        1,
        jnp.where(distance == device_total - 1, 2, jnp.where(distance == chan_count, 3, 0)),
    ).astype(jnp.int32)
    onehot = (offset_group[:, None] == jnp.arange(4, dtype=jnp.int32)[None, :]).astype(jnp.int32)
    running = jnp.cumsum(onehot, axis=0) - 1
    slot_rank = jnp.sum(onehot * running, axis=1)
    starts = jnp.array([0, kept_count, kept_count + capacity, kept_count + 2 * capacity], jnp.int32)
    position = jnp.sum(onehot * starts[None, :], axis=1) + slot_rank
    code_high = (target_slot // 32).astype(jnp.bfloat16)
    code_low = (target_slot % 32).astype(jnp.bfloat16)
    tagged = jnp.concatenate([payload, code_high[None, :], code_low[None, :]], 0)
    buffer_width = kept_count + 3 * capacity
    blank = jnp.concatenate(
        [
            jnp.zeros((row_count, buffer_width), jnp.bfloat16),
            jnp.full((1, buffer_width), element_count // 32, jnp.bfloat16),
            jnp.full((1, buffer_width), element_count % 32, jnp.bfloat16),
        ],
        0,
    )
    packed = blank.at[:, position].set(tagged)
    collected = [packed[:, :kept_count]]
    outgoing_list = [
        packed[:, kept_count + number * capacity : kept_count + (number + 1) * capacity]
        for number in range(3)
    ]
    for number, offset_step in enumerate((1, -1, chan_count)):
        collected.append(from_behind(outgoing_list[number], ("slab", "chan"), offset_step))
    combined = jnp.concatenate(collected, 1)
    slot_index = combined[row_count].astype(jnp.int32) * 32 + combined[row_count + 1].astype(
        jnp.int32
    )
    return (
        jnp.zeros((row_count, element_count), jnp.bfloat16)
        .at[:, slot_index]
        .set(combined[:row_count], mode="drop")
    )


def gather_nodes(field):
    end_faces = jnp.stack([field[0, :, :, :, 0], field[7, :, :, :, -1]])
    with_rims = with_halo(end_faces, (("slab", 0),), 1)
    shared = field[7, :, :, :, :-1] + field[0, :, :, :, 1:]
    field = field.at[7, :, :, :, :-1].set(shared).at[0, :, :, :, 1:].set(shared)
    field = field.at[0, :, :, :, 0].add(with_rims[0]).at[7, :, :, :, -1].add(with_rims[3])
    side_faces = jnp.stack([field[:, 0, :, 0, :], field[:, 7, :, -1, :]])
    side_rims = with_halo(side_faces, (("chan", 0),), 1)
    shared = field[:, 7, :, :-1, :] + field[:, 0, :, 1:, :]
    field = field.at[:, 7, :, :-1, :].set(shared).at[:, 0, :, 1:, :].set(shared)
    field = field.at[:, 0, :, 0, :].add(side_rims[0]).at[:, 7, :, -1, :].add(side_rims[3])
    return field


def multiplicity(count_l, count_a, first_l, first_a, total_l, total_a):
    node_index = jnp.arange(8, dtype=jnp.int32)
    axial_pos = first_a + jnp.arange(count_a, dtype=jnp.int32)
    lateral_pos = first_l + jnp.arange(count_l, dtype=jnp.int32)
    along_axial = (
        1
        + ((node_index[:, None] == 0) & (axial_pos[None, :] > 0)).astype(jnp.int32)
        + ((node_index[:, None] == 7) & (axial_pos[None, :] < total_a - 1)).astype(jnp.int32)
    )
    along_lateral = (
        1
        + ((node_index[:, None] == 0) & (lateral_pos[None, :] > 0)).astype(jnp.int32)
        + ((node_index[:, None] == 7) & (lateral_pos[None, :] < total_l - 1)).astype(jnp.int32)
    )
    return (along_axial[:, None, None, None, :] * along_lateral[None, :, None, :, None]).astype(
        jnp.float32
    )


def on_device(
    stream_speed_field,
    liquid_to_solid_element,
    previous_panel_warmth,
    pointwise_energy_source,
    coked_element_flags,
    coking_thickness_plies,
):
    matrix, node_gll = gll_tables()
    integration_factor = (
        node_gll[:, None, None] * node_gll[None, :, None] * node_gll[None, None, :]
    )[:, :, :, None, None]
    count_l, count_a = coked_element_flags.shape
    element_count = count_l * count_a
    stepped_stream_speed = fluid_update(stream_speed_field, matrix)
    moved = move_blocks(
        conductivity_of(stepped_stream_speed).reshape(512, element_count), liquid_to_solid_element
    )
    moved = moved.reshape(8, 8, 8, count_l, count_a)
    layer_float = coking_thickness_plies.astype(jnp.float32)
    flag_float = coked_element_flags.astype(jnp.float32)
    damping = jnp.where(
        coked_element_flags == 1, 1.0 / (1.0 + layer_damp * layer_float), jnp.ones_like(layer_float)
    )
    weighted_kappa = integration_factor * (moved.astype(jnp.float32) * damping)
    cross_el = cross_gain * flag_float * layer_float / (layer_float + 1.0)
    first_a = lax.axis_index("slab") * count_a
    first_l = lax.axis_index("chan") * count_l
    inv_mult = 1.0 / multiplicity(
        count_l,
        count_a,
        first_l,
        first_a,
        count_l * lax.axis_size("chan"),
        count_a * lax.axis_size("slab"),
    )

    def local_apply(field):
        gradients = [
            forward(matrix, field, conjugate_update_vector) for conjugate_update_vector in range(3)
        ]
        summed = coolant_throughput * integration_factor * field
        summed = summed + backward(matrix, weighted_kappa * gradients[0], 0)
        summed = summed + backward(matrix, weighted_kappa * gradients[1], 1)
        summed = summed + backward(matrix, weighted_kappa * gradients[2], 2)
        mixed = backward(matrix, weighted_kappa * gradients[1], 0) + backward(
            matrix, weighted_kappa * gradients[0], 1
        )
        return summed + cross_el * mixed

    def apply_operator(field):
        return gather_nodes(local_apply(field))

    def paired_sums(residual_now, applied_now):
        return lax.psum(
            (
                jnp.sum(residual_now * residual_now * inv_mult),
                jnp.sum(residual_now * applied_now * inv_mult),
            ),
            ("slab", "chan"),
        )

    source_vector = gather_nodes(
        integration_factor * (coolant_throughput * previous_panel_warmth + pointwise_energy_source)
    )
    solved_panel_warmth = jnp.zeros_like(source_vector)
    residual = source_vector
    applied = apply_operator(residual)
    norm_now, product = paired_sums(residual, applied)
    conjugate_alpha_factor = norm_now / product
    conjugate_update_vector = residual
    applied_dir = applied
    for number in range(ITERS):
        solved_panel_warmth = solved_panel_warmth + conjugate_alpha_factor * conjugate_update_vector
        residual = residual - conjugate_alpha_factor * applied_dir
        if number + 1 < ITERS:
            applied = apply_operator(residual)
            norm_next, product = paired_sums(residual, applied)
            scale_ratio = norm_next / norm_now
            conjugate_alpha_factor = norm_next / (
                product - scale_ratio * norm_next / conjugate_alpha_factor
            )
            conjugate_update_vector = residual + scale_ratio * conjugate_update_vector
            applied_dir = applied + scale_ratio * applied_dir
            norm_now = norm_next
    return (stepped_stream_speed, solved_panel_warmth)


def solution(mesh):
    in_specs = (
        P(None, None, None, None, ("slab", "chan")),
        P(("slab", "chan")),
        P(None, None, None, "chan", "slab"),
        P(None, None, None, "chan", "slab"),
        P("chan", "slab"),
        P("chan", "slab"),
    )
    out_specs = (P(None, None, None, None, ("slab", "chan")), P(None, None, None, "chan", "slab"))
    return jax.shard_map(
        on_device, mesh=mesh, in_specs=in_specs, out_specs=out_specs, check_vma=False
    )
```

profile of v0, /device:TPU:0, one launch (start us, length us, event | category | flops | bytes accessed | tf_op | source)
XLA Modules:
  0.0 833.2 jit_solution(10916110338567704373)
XLA Ops:
  2.2 3.5 fusion.108
  6.7 5.4 collective-permute-start
  17.8 3.6 fusion.17
  23.2 4.7 fusion.5
  27.9 5.1 fusion.8
  34.9 21.1 %fusion.150 = (f32[3,8,8,8,512]{4,1,3,2,0:T(8,128)S(1)}, bf16[3,8,8,8,512]{4,1,3,2,0:T(8,128)(2,1)}) fusion(f32[8,3,8,8,512]{4,0,3,2,1:T(8,128)} %copy-done.9, f32[8,8,8,512]{3,0,2,1:T(8,128)} %get-tuple-element.611, f32[8,3,8,8,512]{4,0,3,2,1:T(8,128)} %copy-done.10, f32[8,8,8,512]{3,0,2,1:T(8,128)} %get-tuple-element.612, ...), kind=kOutput, calls=%fused_computation.322 | convolution fusion | flops 86507520 | bytes 25166080 | tf_op jit(solution)/shard_map/ir,crste->ciste/dot_general | solution.py:98
  69.0 5.0 scatter.94
  80.4 23.5 %scatter.95 = f32[8,8,8,2,256]{4,0,3,2,1:T(8,128)S(1)} dynamic-update-slice(f32[8,8,8,2,256]{4,0,3,2,1:T(8,128)S(1)} %scatter.94, f32[1,8,8,2,255]{4,0,3,2,1:T(1,128)S(1)} %copy.422, s32[]{:T(128)S(1)} %bitcast.292, s32[]{:T(128)} %constant.1164.clone.1, s32[]{:T(128)} %constant.1164.clone.1, s32[]{:T(128)} %constant.1164.clone.1, s32[]{:T(128)} %bitcast.15) | dynamic-update-slice | bytes 261124 | tf_op jit(solution)/shard_map/scatter | solution.py:167
  107.4 10.8 %scatter-add.81 = f32[8,8,8,2,256]{4,0,3,2,1:T(8,128)S(1)} dynamic-update-slice(f32[8,8,8,2,256]{4,0,3,2,1:T(8,128)S(1)} %scatter-add.80, f32[1,8,8,2,1]{4,0,3,2,1:T(1,128)S(1)} %slice_add_fusion.33, s32[]{:T(128)} %constant.1163.clone.1, s32[]{:T(128)} %constant.1164.clone.1, s32[]{:T(128)} %constant.1164.clone.1, s32[]{:T(128)} %constant.1164.clone.1, s32[]{:T(128)} %constant.1168.clone.1) | dynamic-update-slice | bytes 1028 | tf_op jit(solution)/shard_map/scatter-add | solution.py:168
  128.1 7.4 scatter_custom_fusion.1
  152.7 4.3 collective-permute-start.7
  157.0 7.0 scatter.104
  164.0 3.1 broadcast_select_fusion.4
  167.1 24.1 %scatter.105 = f32[8,8,8,2,256]{4,0,2,3,1:T(8,128)} dynamic-update-slice(f32[8,8,8,2,256]{4,0,2,3,1:T(8,128)} %scatter.104, f32[1,8,8,2,255]{4,0,2,3,1:T(1,128)S(1)} %broadcast_select_fusion.4, s32[]{:T(128)S(1)} %bitcast.295, s32[]{:T(128)} %constant.1164.clone.1, s32[]{:T(128)} %constant.1164.clone.1, s32[]{:T(128)} %constant.1164.clone.1, s32[]{:T(128)} %bitcast.15) | dynamic-update-slice | bytes 261124 | tf_op jit(solution)/shard_map/scatter | solution.py:167
  194.6 3.6 scatter-add.86
  199.7 12.3 %scatter-add.89 = f32[8,8,8,2,256]{4,0,2,3,1:T(8,128)} dynamic-update-slice(f32[8,8,8,2,256]{4,0,2,3,1:T(8,128)} %scatter-add.86, f32[1,8,8,2,1]{4,0,2,3,1:T(1,128)S(1)} %slice_add_fusion.28, s32[]{:T(128)} %constant.1163.clone.1, s32[]{:T(128)} %constant.1164.clone.1, s32[]{:T(128)} %constant.1164.clone.1, s32[]{:T(128)} %constant.1164.clone.1, s32[]{:T(128)} %constant.1168.clone.1) | dynamic-update-slice | bytes 1028 | tf_op jit(solution)/shard_map/scatter-add | solution.py:168
  214.1 4.9 collective-permute-start.9
  225.5 42.6 %all-reduce.4 = (f32[]{:T(128)}, f32[]{:T(128)}) all-reduce(f32[]{:T(128)} %get-tuple-element.595, f32[]{:T(128)} %get-tuple-element.594), channel_id=1, replica_groups=mesh['slab'=8,'chan'=4] {'slab','chan'}, use_global_device_ids=true, to_apply=%region_3.4 | all-reduce | flops 2 | bytes 16 | tf_op jit(solution)/shard_map/psum | solution.py:250
  290.2 4.8 collective-permute-start.11
  295.0 7.0 scatter.110
  301.9 3.8 broadcast_select_fusion.3
  305.7 24.1 %scatter.111 = f32[8,8,8,2,256]{4,0,2,3,1:T(8,128)} dynamic-update-slice(f32[8,8,8,2,256]{4,0,2,3,1:T(8,128)} %scatter.110, f32[1,8,8,2,255]{4,0,2,3,1:T(1,128)S(1)} %broadcast_select_fusion.3, s32[]{:T(128)S(1)} %bitcast.298, s32[]{:T(128)} %constant.1164.clone.1, s32[]{:T(128)} %constant.1164.clone.1, s32[]{:T(128)} %constant.1164.clone.1, s32[]{:T(128)} %bitcast.15) | dynamic-update-slice | bytes 261124 | tf_op jit(solution)/shard_map/scatter | solution.py:167
  333.8 3.6 scatter-add.94
  338.9 12.3 %scatter-add.95 = f32[8,8,8,2,256]{4,0,2,3,1:T(8,128)} dynamic-update-slice(f32[8,8,8,2,256]{4,0,2,3,1:T(8,128)} %scatter-add.94, f32[1,8,8,2,1]{4,0,2,3,1:T(1,128)S(1)} %slice_add_fusion.23, s32[]{:T(128)} %constant.1163.clone.1, s32[]{:T(128)} %constant.1164.clone.1, s32[]{:T(128)} %constant.1164.clone.1, s32[]{:T(128)} %constant.1164.clone.1, s32[]{:T(128)} %constant.1168.clone.1) | dynamic-update-slice | bytes 1028 | tf_op jit(solution)/shard_map/scatter-add | solution.py:168
  362.8 42.8 %all-reduce.3 = (f32[]{:T(128)}, f32[]{:T(128)}) all-reduce(f32[]{:T(128)} %get-tuple-element.593, f32[]{:T(128)} %get-tuple-element.592), channel_id=1, replica_groups=mesh['slab'=8,'chan'=4] {'slab','chan'}, use_global_device_ids=true, to_apply=%region_13.14 | all-reduce | flops 2 | bytes 16 | tf_op jit(solution)/shard_map/psum | solution.py:250
  431.0 4.8 collective-permute-start.15
  435.7 7.0 scatter.116
  442.7 3.8 broadcast_select_fusion.2
  446.5 24.1 %scatter.119 = f32[8,8,8,2,256]{4,0,2,3,1:T(8,128)} dynamic-update-slice(f32[8,8,8,2,256]{4,0,2,3,1:T(8,128)} %scatter.116, f32[1,8,8,2,255]{4,0,2,3,1:T(1,128)S(1)} %broadcast_select_fusion.2, s32[]{:T(128)S(1)} %bitcast.301, s32[]{:T(128)} %constant.1164.clone.1, s32[]{:T(128)} %constant.1164.clone.1, s32[]{:T(128)} %constant.1164.clone.1, s32[]{:T(128)} %bitcast.15) | dynamic-update-slice | bytes 261124 | tf_op jit(solution)/shard_map/scatter | solution.py:167
  474.6 3.7 scatter-add.100
  479.7 12.3 %scatter-add.101 = f32[8,8,8,2,256]{4,0,2,3,1:T(8,128)} dynamic-update-slice(f32[8,8,8,2,256]{4,0,2,3,1:T(8,128)} %scatter-add.100, f32[1,8,8,2,1]{4,0,2,3,1:T(1,128)S(1)} %slice_add_fusion.18, s32[]{:T(128)} %constant.1163.clone.1, s32[]{:T(128)} %constant.1164.clone.1, s32[]{:T(128)} %constant.1164.clone.1, s32[]{:T(128)} %constant.1164.clone.1, s32[]{:T(128)} %constant.1168.clone.1) | dynamic-update-slice | bytes 1028 | tf_op jit(solution)/shard_map/scatter-add | solution.py:168
  499.1 4.1 collective-permute-done.18
  504.2 42.1 %all-reduce.2 = (f32[]{:T(128)}, f32[]{:T(128)}) all-reduce(f32[]{:T(128)} %get-tuple-element.591, f32[]{:T(128)} %get-tuple-element.590), channel_id=1, replica_groups=mesh['slab'=8,'chan'=4] {'slab','chan'}, use_global_device_ids=true, to_apply=%region_17.18 | all-reduce | flops 2 | bytes 16 | tf_op jit(solution)/shard_map/psum | solution.py:250
  550.2 3.6 multiply_subtract_fusion.1
  572.9 4.8 collective-permute-start.19
  577.7 7.0 scatter.124
  584.6 3.8 broadcast_select_fusion.1
  588.4 24.1 %scatter.125 = f32[8,8,8,2,256]{4,0,2,3,1:T(8,128)} dynamic-update-slice(f32[8,8,8,2,256]{4,0,2,3,1:T(8,128)} %scatter.124, f32[1,8,8,2,255]{4,0,2,3,1:T(1,128)S(1)} %broadcast_select_fusion.1, s32[]{:T(128)S(1)} %bitcast.304, s32[]{:T(128)} %constant.1164.clone.1, s32[]{:T(128)} %constant.1164.clone.1, s32[]{:T(128)} %constant.1164.clone.1, s32[]{:T(128)} %bitcast.15) | dynamic-update-slice | bytes 261124 | tf_op jit(solution)/shard_map/scatter | solution.py:167
  616.5 3.7 scatter-add.106
  621.6 12.3 %scatter-add.109 = f32[8,8,8,2,256]{4,0,2,3,1:T(8,128)} dynamic-update-slice(f32[8,8,8,2,256]{4,0,2,3,1:T(8,128)} %scatter-add.106, f32[1,8,8,2,1]{4,0,2,3,1:T(1,128)S(1)} %slice_add_fusion.13, s32[]{:T(128)} %constant.1163.clone.1, s32[]{:T(128)} %constant.1164.clone.1, s32[]{:T(128)} %constant.1164.clone.1, s32[]{:T(128)} %constant.1164.clone.1, s32[]{:T(128)} %constant.1168.clone.1) | dynamic-update-slice | bytes 1028 | tf_op jit(solution)/shard_map/scatter-add | solution.py:168
  645.1 42.7 %all-reduce.1 = (f32[]{:T(128)}, f32[]{:T(128)}) all-reduce(f32[]{:T(128)} %get-tuple-element.589, f32[]{:T(128)} %get-tuple-element.588), channel_id=1, replica_groups=mesh['slab'=8,'chan'=4] {'slab','chan'}, use_global_device_ids=true, to_apply=%region_21.22 | all-reduce | flops 2 | bytes 16 | tf_op jit(solution)/shard_map/psum | solution.py:250
  712.4 4.2 collective-permute-start.23
  716.5 7.0 scatter.156
  726.7 24.1 %scatter.157 = f32[8,8,8,2,256]{4,0,2,3,1:T(8,128)} dynamic-update-slice(f32[8,8,8,2,256]{4,0,2,3,1:T(8,128)} %scatter.156, f32[1,8,8,2,255]{4,0,2,3,1:T(1,128)S(1)} %broadcast_select_fusion, s32[]{:T(128)S(1)} %bitcast.307, s32[]{:T(128)} %constant.1164.clone.1, s32[]{:T(128)} %constant.1164.clone.1, s32[]{:T(128)} %constant.1164.clone.1, s32[]{:T(128)} %bitcast.15) | dynamic-update-slice | bytes 261124 | tf_op jit(solution)/shard_map/scatter | solution.py:167
  753.6 3.7 scatter-add.114
  758.7 12.3 %scatter-add.115 = f32[8,8,8,2,256]{4,0,2,3,1:T(8,128)} dynamic-update-slice(f32[8,8,8,2,256]{4,0,2,3,1:T(8,128)} %scatter-add.114, f32[1,8,8,2,1]{4,0,2,3,1:T(1,128)S(1)} %slice_add_fusion.8, s32[]{:T(128)} %constant.1163.clone.1, s32[]{:T(128)} %constant.1164.clone.1, s32[]{:T(128)} %constant.1164.clone.1, s32[]{:T(128)} %constant.1164.clone.1, s32[]{:T(128)} %constant.1168.clone.1) | dynamic-update-slice | bytes 1028 | tf_op jit(solution)/shard_map/scatter-add | solution.py:168
  778.1 4.0 collective-permute-done.26
  783.2 41.8 %all-reduce = (f32[]{:T(128)}, f32[]{:T(128)}) all-reduce(f32[]{:T(128)} %get-tuple-element.587, f32[]{:T(128)} %get-tuple-element.586), channel_id=1, replica_groups=mesh['slab'=8,'chan'=4] {'slab','chan'}, use_global_device_ids=true, to_apply=%region_25.26 | all-reduce | flops 2 | bytes 16 | tf_op jit(solution)/shard_map/psum | solution.py:250
  (307 shorter events, 222.6 us)
Async XLA Ops:
  0.6 13.2 %copy-start.7 = (bf16[3,8,8,8,512]{4,3,2,1,0:T(8,128)(2,1)S(1)}, bf16[3,8,8,8,512]{4,3,2,1,0:T(8,128)(2,1)}, u32[]{:S(2)}) copy-start(bf16[3,8,8,8,512]{4,3,2,1,0:T(8,128)(2,1)} %param.105) | copy-start | bytes 4718596
  5.7 9.1 %copy-start.17 = (f32[8,8,1,1,1]{1,0,4,3,2:T(8,128)S(1)}, f32[8,8,1,1,1]{1,0,4,3,2:T(8,128)}, u32[]{:S(2)}) copy-start(f32[8,8,1,1,1]{1,0,4,3,2:T(8,128)} %constant.1201) | copy-start | bytes 772
  6.7 97.1 %collective-permute-start = (f32[1,8,8,2]{2,1,3,0:T(8,128)}, f32[1,8,8,2]{2,1,3,0:T(8,128)}, u32[]{:S(2)}, u32[]{:S(2)}) collective-permute-start(f32[1,8,8,2]{2,1,3,0:T(8,128)} %bitcast.16), channel_id=1, source_target_pairs={{0,4},{4,8},{8,12},{12,16},{16,20},{20,24},{24,28},{1,5},{5,9},{9,... | collective-permute-start | bytes 1544 | tf_op jit(solution)/shard_map/ppermute | solution.py:34
  12.3 94.7 %collective-permute-start.1 = (f32[1,8,8,2]{2,1,3,0:T(8,128)S(1)}, f32[1,8,8,2]{2,1,3,0:T(8,128)S(1)}, u32[]{:S(2)}, u32[]{:S(2)}) collective-permute-start(f32[1,8,8,2]{2,1,3,0:T(8,128)S(1)} %bitcast.310), channel_id=1, source_target_pairs={{4,0},{8,4},{12,8},{16,12},{20,16},{24,20},{28,24},{5,1},{9,5},{13... | collective-permute-start | bytes 1544 | tf_op jit(solution)/shard_map/ppermute | solution.py:35
  16.2 7.0 copy-start.9
  17.8 10.1 %copy-start.10 = (f32[8,3,8,8,512]{4,0,3,2,1:T(8,128)}, f32[8,3,8,8,512]{4,0,3,2,1:T(8,128)S(1)}, u32[]{:S(2)}) copy-start(f32[8,3,8,8,512]{4,0,3,2,1:T(8,128)S(1)} %fusion.15) | copy-start | bytes 9437188
  27.9 5.1 copy-start.26
  27.9 6.8 copy-start.29
  57.1 16.9 %copy-start.31 = (s32[5]{0:T(128)S(1)}, s32[5]{0:T(128)}, u32[]{:S(2)}) copy-start(s32[5]{0:T(128)} %constant.1166.clone.1) | copy-start | bytes 64
  57.1 17.6 %copy-start.27 = (s32[2,256]{1,0:T(2,128)S(1)}, s32[2,256]{1,0:T(2,128)}, u32[]{:S(2)}) copy-start(s32[2,256]{1,0:T(2,128)} %param.109) | copy-start | bytes 6148
  57.1 17.5 %copy-start.28 = (s32[2,256]{1,0:T(2,128)S(1)}, s32[2,256]{1,0:T(2,128)}, u32[]{:S(2)}) copy-start(s32[2,256]{1,0:T(2,128)} %param.110) | copy-start | bytes 6148
  57.1 19.4 %copy-start.30 = (s32[5]{0:T(128)S(1)}, s32[5]{0:T(128)}, u32[]{:S(2)}) copy-start(s32[5]{0:T(128)} %constant.1169.clone.1) | copy-start | bytes 64
  61.0 66.8 %collective-permute-start.6 = (bf16[514,128]{0,1:T(8,128)(2,1)}, bf16[514,128]{0,1:T(8,128)(2,1)S(1)}, u32[]{:S(2)}, u32[]{:S(2)}) collective-permute-start(bf16[514,128]{0,1:T(8,128)(2,1)} %get-tuple-element.655), channel_id=1, source_target_pairs={{28,0},{29,1},{30,2},{31,3},{0,4},{1,5},{2,6},{3,7},{4,8},{5,9},{6... | collective-permute-start | bytes 394760 | tf_op jit(solution)/shard_map/ppermute | solution.py:24
  63.7 64.2 %collective-permute-start.5 = (bf16[514,128]{0,1:T(8,128)(2,1)}, bf16[514,128]{0,1:T(8,128)(2,1)S(1)}, u32[]{:S(2)}, u32[]{:S(2)}) collective-permute-start(bf16[514,128]{0,1:T(8,128)(2,1)} %get-tuple-element.656), channel_id=1, source_target_pairs={{1,0},{2,1},{3,2},{4,3},{5,4},{6,5},{7,6},{8,7},{9,8},{10,9},{11,1... | collective-permute-start | bytes 394760 | tf_op jit(solution)/shard_map/ppermute | solution.py:24
  66.0 61.9 %collective-permute-start.4 = (bf16[514,128]{0,1:T(8,128)(2,1)}, bf16[514,128]{0,1:T(8,128)(2,1)S(1)}, u32[]{:S(2)}, u32[]{:S(2)}) collective-permute-start(bf16[514,128]{0,1:T(8,128)(2,1)} %get-tuple-element.654), channel_id=1, source_target_pairs={{31,0},{0,1},{1,2},{2,3},{3,4},{4,5},{5,6},{6,7},{7,8},{8,9},{9,10... | collective-permute-start | bytes 394760 | tf_op jit(solution)/shard_map/ppermute | solution.py:24
  74.7 71.2 %copy-start.21 = (f32[2,256]{1,0:T(2,128)}, f32[2,256]{1,0:T(2,128)S(1)}, u32[]{:S(2)}) copy-start(f32[2,256]{1,0:T(2,128)S(1)} %get-tuple-element.659) | copy-start | bytes 6148
  118.4 4.2 collective-permute-start.2
  119.7 3.1 collective-permute-start.3
  141.5 3.3 copy-start.20
  152.7 40.0 %collective-permute-start.7 = (f32[1,8,8,2]{2,1,3,0:T(8,128)}, f32[1,8,8,2]{2,1,3,0:T(8,128)}, u32[]{:S(2)}, u32[]{:S(2)}) collective-permute-start(f32[1,8,8,2]{2,1,3,0:T(8,128)} %bitcast.314), channel_id=1, source_target_pairs={{0,4},{4,8},{8,12},{12,16},{16,20},{20,24},{24,28},{1,5},{5,9},{9,... | collective-permute-start | bytes 1544 | tf_op jit(solution)/shard_map/ppermute | solution.py:34
  191.3 6.9 collective-permute-start.8
  214.1 8.5 %collective-permute-start.9 = (f32[1,8,8,256]{3,1,2,0:T(8,128)S(1)}, f32[1,8,8,256]{3,1,2,0:T(8,128)S(1)}, u32[]{:S(2)}, u32[]{:S(2)}) collective-permute-start(f32[1,8,8,256]{3,1,2,0:T(8,128)S(1)} %get-tuple-element.644), channel_id=1, source_target_pairs={{0,1},{1,2},{2,3},{4,5},{5,6},{6,7},{8,9},{9,10},{10,11},{12,13},{... | collective-permute-start | bytes 196616 | tf_op jit(solution)/shard_map/ppermute | solution.py:34
  221.3 3.1 collective-permute-start.10
  224.4 43.7 %copy-start.8 = (f32[8,8,8,2,256]{4,0,2,3,1:T(8,128)}, f32[8,8,8,2,256]{4,0,2,3,1:T(8,128)S(1)}, u32[]{:S(2)}) copy-start(f32[8,8,8,2,256]{4,0,2,3,1:T(8,128)S(1)} %fusion.122) | copy-start | bytes 3145732
  279.8 3.7 copy-start.22
  290.2 41.6 %collective-permute-start.11 = (f32[1,8,8,2]{2,1,3,0:T(8,128)}, f32[1,8,8,2]{2,1,3,0:T(8,128)}, u32[]{:S(2)}, u32[]{:S(2)}) collective-permute-start(f32[1,8,8,2]{2,1,3,0:T(8,128)} %bitcast.315), channel_id=1, source_target_pairs={{0,4},{4,8},{8,12},{12,16},{16,20},{20,24},{24,28},{1,5},{5,9},{9,... | collective-permute-start | bytes 1544 | tf_op jit(solution)/shard_map/ppermute | solution.py:34
  330.5 6.9 collective-permute-start.12
  353.3 4.9 collective-permute-start.13
  356.9 3.9 collective-permute-start.14
  411.7 11.4 %copy-start = (f32[8,8,8,2,256]{4,0,2,3,1:T(8,128)}, f32[8,8,8,2,256]{4,0,2,3,1:T(8,128)S(1)}, u32[]{:S(2)}) copy-start(f32[8,8,8,2,256]{4,0,2,3,1:T(8,128)S(1)} %multiply_subtract_fusion.2) | copy-start | bytes 3145732
  431.0 41.6 %collective-permute-start.15 = (f32[1,8,8,2]{2,1,3,0:T(8,128)}, f32[1,8,8,2]{2,1,3,0:T(8,128)}, u32[]{:S(2)}, u32[]{:S(2)}) collective-permute-start(f32[1,8,8,2]{2,1,3,0:T(8,128)} %bitcast.316), channel_id=1, source_target_pairs={{0,4},{4,8},{8,12},{12,16},{16,20},{20,24},{24,28},{1,5},{5,9},{9,... | collective-permute-start | bytes 1544 | tf_op jit(solution)/shard_map/ppermute | solution.py:34
  471.3 6.9 collective-permute-start.16
  491.9 11.3 %copy-start.1 = (f32[8,8,8,2,256]{4,0,2,3,1:T(8,128)S(1)}, f32[8,8,8,2,256]{4,0,2,3,1:T(8,128)}, u32[]{:S(2)}) copy-start(f32[8,8,8,2,256]{4,0,2,3,1:T(8,128)} %copy-done) | copy-start | bytes 3145732
  494.2 4.9 collective-permute-start.17
  497.8 5.4 collective-permute-start.18
  553.7 11.5 %copy-start.3 = (f32[8,8,8,2,256]{4,0,2,3,1:T(8,128)}, f32[8,8,8,2,256]{4,0,2,3,1:T(8,128)S(1)}, u32[]{:S(2)}) copy-start(f32[8,8,8,2,256]{4,0,2,3,1:T(8,128)S(1)} %get-tuple-element.608) | copy-start | bytes 3145732
  572.9 41.6 %collective-permute-start.19 = (f32[1,8,8,2]{2,1,3,0:T(8,128)}, f32[1,8,8,2]{2,1,3,0:T(8,128)}, u32[]{:S(2)}, u32[]{:S(2)}) collective-permute-start(f32[1,8,8,2]{2,1,3,0:T(8,128)} %bitcast.317), channel_id=1, source_target_pairs={{0,4},{4,8},{8,12},{12,16},{16,20},{20,24},{24,28},{1,5},{5,9},{9,... | collective-permute-start | bytes 1544 | tf_op jit(solution)/shard_map/ppermute | solution.py:34
  613.2 6.9 collective-permute-start.20
  633.9 10.3 %copy-start.4 = (f32[8,8,8,2,256]{4,0,2,3,1:T(8,128)S(1)}, f32[8,8,8,2,256]{4,0,2,3,1:T(8,128)}, u32[]{:S(2)}) copy-start(f32[8,8,8,2,256]{4,0,2,3,1:T(8,128)} %copy-done.3) | copy-start | bytes 3145732
  636.1 4.9 collective-permute-start.21
  639.7 4.4 collective-permute-start.22
  693.8 11.4 %copy-start.5 = (f32[8,8,8,2,256]{4,0,2,3,1:T(8,128)}, f32[8,8,8,2,256]{4,0,2,3,1:T(8,128)S(1)}, u32[]{:S(2)}) copy-start(f32[8,8,8,2,256]{4,0,2,3,1:T(8,128)S(1)} %multiply_subtract_fusion) | copy-start | bytes 3145732
  712.4 39.8 %collective-permute-start.23 = (f32[1,8,8,2]{2,1,3,0:T(8,128)S(1)}, f32[1,8,8,2]{2,1,3,0:T(8,128)S(1)}, u32[]{:S(2)}, u32[]{:S(2)}) collective-permute-start(f32[1,8,8,2]{2,1,3,0:T(8,128)S(1)} %bitcast.312), channel_id=1, source_target_pairs={{0,4},{4,8},{8,12},{12,16},{16,20},{20,24},{24,28},{1,5},{5,9},{9,... | collective-permute-start | bytes 1544 | tf_op jit(solution)/shard_map/ppermute | solution.py:34
  750.9 6.3 collective-permute-start.24
  752.4 76.4 %copy-start.2 = (f32[8,8,8,2,256]{4,0,2,3,1:T(8,128)S(1)}, f32[8,8,8,2,256]{4,0,2,3,1:T(8,128)}, u32[]{:S(2)}) copy-start(f32[8,8,8,2,256]{4,0,2,3,1:T(8,128)} %copy-done) | copy-start | bytes 3145732
  770.9 11.2 %copy-start.6 = (f32[8,8,8,2,256]{4,0,2,3,1:T(8,128)S(1)}, f32[8,8,8,2,256]{4,0,2,3,1:T(8,128)}, u32[]{:S(2)}) copy-start(f32[8,8,8,2,256]{4,0,2,3,1:T(8,128)} %copy-done.5) | copy-start | bytes 3145732
  773.2 4.9 collective-permute-start.25
  776.8 5.4 collective-permute-start.26
  (11 other events, 20.5 us)
where the time goes:
time: 840 us; the launch traced here: 833 us
  local copies, waits for them, and re-layouts  325 us (39%)
  blocking collectives  212 us (25%)
  matrix products  107 us (13%)
  other arithmetic  93.5 us (11%)
  starting transfers between devices  60.4 us (7%)
  between operations  19.9 us (2%)
  waiting for transfers between devices  15.8 us (2%)
    psum x5, blocking collectives, paired_sums(): lax.psum((jnp.sum(residual_now * residual_now * inv_mult), jnp.sum(residu...  212 us
    scatter x12, local copies, waits for them, and re-layouts, gather_nodes(): field = field.at[7, :, :, :, :-1].set(shared).at[0, :, :, :, 1:].set(shared)  184 us
    scatter-add x13, local copies, waits for them, and re-layouts, gather_nodes(): field.at[0, :, :, :, 0].add(with_rims[0]).at[7, :, :, :, -1]  92.8 us
    dot_general x25, matrix products, backward(): jnp.einsum(backward_forms[conjugate_update_vector], matrix, field, precis...  44.9 us
    ppermute x12, starting transfers between devices, with_halo(): before = lax.ppermute(last, axis, up)  39.5 us
    dot_general x15, matrix products, forward(): jnp.einsum(forward_forms[conjugate_update_vector], matrix, field, precisi...  24.4 us
    another operation x10, other arithmetic  22 us
    dot_general x1, matrix products, fluid_update(): jnp.einsum(fluid_forms[0], matrix, gradients[0], precision=highest)  21.1 us
  transfers between devices with their start and end apart: 27, of which 6 were waited for; matrix products, arithmetic and copies ran while one was open for 38% of the time, Pallas kernels for 0%

commit v1 on v0

v1 whole, which is shorter than its diff:
```python
import functools

import jax
import jax.numpy as jnp
import numpy as np
from jax import lax
from jax.experimental import pallas as pl
from jax.experimental.pallas import tpu as pltpu
from jax.sharding import PartitionSpec as P

ITERS = 5
LANES = 128
RIM = 8
KRYLOV_SCALE = 1.0 / 256.0

highest = lax.Precision.HIGHEST
f32 = jnp.float32
bf16 = jnp.bfloat16
coolant_throughput = 0.05
time_step = 0.01
viscosity = 0.02
cross_gain = 0.4
layer_damp = 0.25

NT = (((1,), (1,)), ((), ()))
TN = (((0,), (0,)), ((), ()))


def gll_tables():
    points = np.array(
        [
            -1.0,
            -0.8717401485096066,
            -0.5917001814331423,
            -0.2092992179024789,
            0.2092992179024789,
            0.5917001814331423,
            0.8717401485096066,
            1.0,
        ]
    )
    weights = np.array(
        [
            1.0 / 28.0,
            0.2107042271435061,
            0.3411226924835044,
            0.4124587946587038,
            0.4124587946587038,
            0.3411226924835044,
            0.2107042271435061,
            1.0 / 28.0,
        ]
    )
    lower_poly = np.ones(8)
    upper_poly = points.copy()
    for degree in range(1, 7):
        next_poly = ((2 * degree + 1) * points * upper_poly - degree * lower_poly) / (degree + 1)
        lower_poly = upper_poly
        upper_poly = next_poly
    gaps_matrix = points[:, None] - points[None, :] + np.eye(8)
    derivative = upper_poly[:, None] / (upper_poly[None, :] * gaps_matrix)
    derivative = derivative * (1.0 - np.eye(8))
    derivative[0, 0] = -14.0
    derivative[7, 7] = 14.0
    return derivative, weights


DERIV, GLL_W = gll_tables()
DERIV = DERIV.astype(np.float32).astype(np.float64)
GLL_W = GLL_W.astype(np.float32).astype(np.float64)


def split_hi_lo(matrix):
    high = np.asarray(matrix, np.float32).astype(jnp.bfloat16)
    low = (np.asarray(matrix, np.float64) - high.astype(np.float64)).astype(np.float32)
    return high, low.astype(jnp.bfloat16)


def line_matrices():
    out = []
    for matrix in (DERIV, DERIV.T):
        high, low = split_hi_lo(np.kron(np.eye(32), matrix))
        out.append(np.concatenate([high, low, high], 1))
    return out


def fluid_matrices():
    eye8 = np.eye(8)
    square = DERIV @ DERIV
    first = np.kron(DERIV, np.eye(64))
    laplace = (
        np.kron(square, np.eye(64))
        + np.kron(np.kron(eye8, square), eye8)
        + np.kron(np.eye(64), square)
    )
    second = np.kron(np.kron(np.eye(4), DERIV), eye8)
    third = np.kron(np.eye(32), DERIV)
    return [np.concatenate(split_hi_lo(m), 1) for m in (first, laplace, second, third)]


def along(matrix, line):
    even = [line[j] + line[7 - j] for j in range(4)]
    odd = [line[j] - line[7 - j] for j in range(4)]
    result = [None] * 8
    for i in range(4):
        p = sum(float(0.5 * (matrix[i, j] + matrix[i, 7 - j])) * even[j] for j in range(4))
        q = sum(float(0.5 * (matrix[i, j] - matrix[i, 7 - j])) * odd[j] for j in range(4))
        result[i] = p + q
        result[7 - i] = q - p
    return result


def lane_index(rows=8):
    return lax.broadcasted_iota(jnp.int32, (rows, LANES), 1)


def vmem(shape, dtype=f32):
    return pltpu.VMEM(shape, dtype)


def call(kernel, out_shape, *args, smem=0, scratch=(), cost=None, limit=48, **kw):
    specs = [pl.BlockSpec(memory_space=pltpu.SMEM)] * smem
    specs += [pl.BlockSpec(memory_space=pltpu.VMEM)] * (len(args) - smem)
    outs = [pl.BlockSpec(memory_space=pltpu.VMEM) for _ in out_shape]
    return pl.pallas_call(
        kernel,
        in_specs=specs,
        out_specs=outs,
        out_shape=out_shape,
        scratch_shapes=scratch,
        cost_estimate=cost,
        compiler_params=pltpu.CompilerParams(vmem_limit_bytes=limit * 1024 * 1024),
        **kw,
    )(*args)


def weight_rows(wt):
    return [[float(GLL_W[r] * GLL_W[s]) * wt for s in range(8)] for r in range(8)]


def sel_matrix(l, first_lane):
    row = lax.broadcasted_iota(jnp.int32, (2 * RIM, LANES), 0)
    lane = lax.broadcasted_iota(jnp.int32, (2 * RIM, LANES), 1)
    return ((row - l * RIM + first_lane == lane) & (row >= l * RIM) & (row < (l + 1) * RIM)).astype(f32)


def place_matrix(first_lane):
    row = lax.broadcasted_iota(jnp.int32, (2 * RIM, LANES), 0)
    lane = lax.broadcasted_iota(jnp.int32, (2 * RIM, LANES), 1)
    target = jnp.where(row < RIM, row + first_lane, row - RIM + first_lane + LANES // 2)
    return (target == lane).astype(f32)


def send_rims(tile_rows, na):
    behind = sum(
        lax.dot_general(sel_matrix(l, 0), tile_rows(l * na), NT, precision=highest, preferred_element_type=f32)
        for l in range(2)
    )
    ahead = sum(
        lax.dot_general(
            sel_matrix(l, LANES - RIM), tile_rows(l * na + na - 1), NT, precision=highest, preferred_element_type=f32
        )
        for l in range(2)
    )
    return behind, ahead


def place_rims(from_ahead, from_behind):
    a = lax.dot_general(from_ahead, place_matrix(0), TN, precision=highest, preferred_element_type=f32)
    b = lax.dot_general(
        from_behind, place_matrix(LANES // 2 - RIM), TN, precision=highest, preferred_element_type=f32
    )
    return a + b


def source_kernel(na, p_ref, q_ref, dc_ref, wt_ref, z_ref, behind_ref, ahead_ref):
    rows = weight_rows(wt_ref[...])
    step = 2 * na
    for r in range(8):
        for s in range(8):
            base = (r * 8 + s) * 8 * step
            for l in range(2):
                for at in range(na):
                    pick = pl.ds(base + at * 2 + l, 8, stride=step)
                    z_ref[l * na + at, r, s] = rows[r][s] * (coolant_throughput * p_ref[pick, :] + q_ref[pick, :])

    def tile_rows(j):
        cols = pl.ds(j * LANES, LANES)
        extra = [
            jnp.broadcast_to(dc_ref[0:1, cols], (8, LANES)),
            jnp.broadcast_to(dc_ref[1:2, cols], (8, LANES)),
            jnp.zeros((LANES - 16, LANES), f32),
        ]
        return jnp.concatenate([z_ref[j].reshape(512, LANES)] + extra, 0)

    behind, ahead = send_rims(tile_rows, na)
    behind_ref[...] = behind
    ahead_ref[...] = ahead


def assemble(na, y, lo_ref, hi_ref):
    ghost = 2 * na
    lane = lane_index()
    first = lane == 0
    last = lane == LANES - 1
    half = LANES // 2
    roll = pltpu.roll
    for s in range(8):
        far = [y[j, 7, s] for j in range(ghost + 1)]
        near = [y[j, 0, s] for j in range(ghost + 1)]
        right = [roll(f, 1, 1) for f in far]
        left = [roll(f, LANES - 1, 1) for f in near]
        far_half = [roll(far[na * 2 - 1], half + 1, 1), roll(far[ghost], half + 1, 1)]
        near_half = [roll(near[0], half - 1, 1), roll(near[ghost], half - 1, 1)]
        for l in range(2):
            for at in range(na):
                j = l * na + at
                if at > 0:
                    carry = right[j - 1]
                else:
                    carry = far_half[1] if l == 0 else right[ghost]
                y[j, 0, s] = near[j] + jnp.where(first, carry, right[j])
                if at < na - 1:
                    carry = left[j + 1]
                else:
                    carry = left[ghost] if l == 0 else near_half[1]
                y[j, 7, s] = far[j] + jnp.where(last, carry, left[j])
        from_left = jnp.where(first, right[na - 1], jnp.where(lane == half, far_half[0], right[ghost]))
        y[ghost, 0, s] = near[ghost] + from_left
        from_right = jnp.where(last, left[na], jnp.where(lane == half - 1, near_half[0], left[ghost]))
        y[ghost, 7, s] = far[ghost] + from_right
    low = lane < half
    for r in range(8):
        for at in range(na):
            shared = y[at, r, 7] + y[na + at, r, 0]
            y[at, r, 7] = shared
            y[na + at, r, 0] = shared
            lo_ref[at, r] = y[at, r, 0]
            hi_ref[at, r] = y[na + at, r, 7]
        upper = y[ghost, r, 7]
        lower = y[ghost, r, 0]
        new_upper = upper + jnp.where(low, roll(lower, half, 1), 0.0)
        new_lower = lower + jnp.where(low, 0.0, roll(upper, half, 1))
        y[ghost, r, 7] = new_upper
        y[ghost, r, 0] = new_lower
        lo_ref[na, r] = jnp.where(low, new_lower, 0.0)
        hi_ref[na, r] = jnp.where(low, roll(new_upper, half, 1), 0.0)


def faces_out(parity, lo, hi, a_ref, b_ref):
    even = parity == 0
    a_ref[...] = jnp.where(even, hi[...], lo[...])
    b_ref[...] = jnp.where(even, lo[...], hi[...])


def add_faces(na, parity, v, a_ref, b_ref):
    even = parity == 0
    ghost = 2 * na
    for r in range(8):
        for at in range(na + 1):
            a, b = a_ref[at, r], b_ref[at, r]
            upper = jnp.where(even, a, b)
            lower = jnp.where(even, b, a)
            if at < na:
                v[at, r, 0] = v[at, r, 0] + lower
                v[na + at, r, 7] = v[na + at, r, 7] + upper
            else:
                v[ghost, r, 0] = v[ghost, r, 0] + lower
                v[ghost, r, 7] = v[ghost, r, 7] + pltpu.roll(upper, LANES // 2, 1)


def source_assembly_kernel(
    na, par_ref, z_ref, from_ahead, from_behind, dc_ref, y_ref, cr_ref, a_ref, b_ref, lo, hi
):
    ghost = 2 * na
    y_ref[0:ghost] = z_ref[...]
    tile = place_rims(from_ahead[...], from_behind[...])
    y_ref[ghost] = tile[:512].reshape(8, 8, 8, LANES)
    for j in range(ghost):
        cr_ref[j] = jnp.broadcast_to(dc_ref[1:2, j * LANES : (j + 1) * LANES], (8, LANES))
    cr_ref[ghost] = tile[520:528]
    assemble(na, y_ref, lo, hi)
    faces_out(par_ref[0], lo, hi, a_ref, b_ref)


def fluid_kernel(
    chan, total, me_ref, u_ref, l2s_ref, k1_ref, kl_ref, k2_ref, k3_ref, out_ref, own_ref, s1_ref, s2_ref, s3_ref, c_ref
):
    i = pl.program_id(0)
    width = u_ref.shape[-1]
    u = u_ref[...].astype(f32)
    ub = [u[c].reshape(512, width).astype(bf16) for c in range(3)]
    uf = [x.astype(f32) for x in ub]

    def whole(k_ref, x):
        return jnp.dot(k_ref[...], jnp.concatenate([x, x], 0), preferred_element_type=f32)

    def halves(k_ref, x):
        parts = []
        for h in range(2):
            part = x[h * 256 : (h + 1) * 256]
            parts.append(jnp.dot(k_ref[...], jnp.concatenate([part, part], 0), preferred_element_type=f32))
        return jnp.concatenate(parts, 0)

    speed = None
    for c in range(3):
        convect = uf[0] * whole(k1_ref, ub[c]) + uf[1] * halves(k2_ref, ub[c]) + uf[2] * halves(k3_ref, ub[c])
        new = (uf[c] + time_step * (viscosity * whole(kl_ref, ub[c]) - convect)).astype(bf16)
        out_ref[c] = new.reshape(8, 8, 8, width)
        new = new.astype(f32)
        speed = new * new if speed is None else speed + new * new
    c_ref[i, 0:512] = (1.0 + 0.5 * speed).astype(bf16)

    @pl.when(i == pl.num_programs(0) - 1)
    def _():
        elements = l2s_ref.shape[-1]
        cond = jnp.concatenate([c_ref[k, 0:512] for k in range(c_ref.shape[0])], 1)
        l2s = l2s_ref[...]
        if elements & (elements - 1) == 0:
            owner = lax.shift_right_logical(l2s, elements.bit_length() - 1)
            slot = l2s & (elements - 1)
        else:
            owner = l2s // elements
            slot = l2s - owner * elements
        ahead = owner - me_ref[0]
        ahead = jnp.where(ahead < 0, ahead + total, ahead)
        group = jnp.where(ahead == 1, 1, jnp.where(ahead == total - 1, 2, jnp.where(ahead == chan, 3, 0)))
        place = lax.broadcasted_iota(jnp.int32, (elements, elements), 0)
        keep = ((place == slot) & (group == 0)).astype(f32).astype(bf16)
        own_ref[...] = lax.dot_general(cond, keep, NT, preferred_element_type=f32).astype(bf16)
        kinds = lax.broadcasted_iota(jnp.int32, (16, elements), 0)
        marks = (kinds == group).astype(f32).astype(bf16)
        before = lax.broadcasted_iota(jnp.int32, (elements, elements), 0) < lax.broadcasted_iota(
            jnp.int32, (elements, elements), 1
        )
        rank = jnp.dot(marks, before.astype(f32).astype(bf16), preferred_element_type=f32).astype(jnp.int32)
        high = lax.shift_right_logical(slot, 5)
        codes = jnp.concatenate(
            [jnp.broadcast_to(high, (8, elements)), jnp.broadcast_to(slot - high * 32, (8, elements))], 0
        )
        tagged = jnp.concatenate([cond, codes.astype(f32).astype(bf16)], 0)
        room = s1_ref.shape[-1]
        position = lax.broadcasted_iota(jnp.int32, (room, elements), 0)
        for g, ref in ((1, s1_ref), (2, s2_ref), (3, s3_ref)):
            take = ((position == rank[g : g + 1]) & (group == g)).astype(f32).astype(bf16)
            ref[...] = lax.dot_general(tagged, take, NT, preferred_element_type=f32).astype(bf16)


def unpack_kernel(na, own_ref, r1_ref, r2_ref, r3_ref, dc_ref, wt_ref, wk_ref, behind_ref, ahead_ref):
    rows = weight_rows(wt_ref[...] * KRYLOV_SCALE)
    got = jnp.concatenate([r[0:512] for r in (r1_ref, r2_ref, r3_ref)], 1)
    tags = [r[512:528].astype(f32) for r in (r1_ref, r2_ref, r3_ref)]
    slots = [(t[0:1] * 32.0 + t[8:9]).astype(jnp.int32) for t in tags]
    slot = jnp.concatenate(slots, 1)
    for j in range(2 * na):
        place = lax.broadcasted_iota(jnp.int32, (LANES, slot.shape[1]), 0) + j * LANES
        put = (place == slot).astype(f32).astype(bf16)
        cols = slice(j * LANES, (j + 1) * LANES)
        moved = own_ref[:, cols].astype(f32) + lax.dot_general(got, put, NT, preferred_element_type=f32)
        kappa = (moved * dc_ref[0:1, cols]).reshape(8, 8, 8, LANES)
        for r in range(8):
            for s in range(8):
                wk_ref[j, r, s] = rows[r][s] * kappa[r, s]
    behind, ahead = send_rims(lambda j: wk_ref[j].reshape(512, LANES), na)
    behind_ref[...] = behind
    ahead_ref[...] = ahead


def lines_t(k_ref, x):
    x = x.reshape(2, 256, LANES)
    x = jnp.concatenate([x[0], x[1]], 1)
    high = x.astype(bf16)
    low = (x - high.astype(f32)).astype(bf16)
    y = jnp.dot(k_ref[...], jnp.concatenate([high, high, low], 0), preferred_element_type=f32)
    return y[:, :LANES].reshape(4, 8, 8, LANES), y[:, LANES:].reshape(4, 8, 8, LANES)


def squares(v, j, other, iw_ref):
    sums = {}
    for r in range(8):
        for s in range(8):
            key = (0 if r == 0 else 2 if r == 7 else 1, 0 if s == 0 else 2 if s == 7 else 1)
            x = v[j, r, s]
            pair = (x * x,) if other is None else (x * x, x * other[j, r, s])
            old = sums.get((key, r))
            sums[(key, r)] = pair if old is None else tuple(a + b for a, b in zip(old, pair))
    total = None
    for (key, _), pair in sums.items():
        weight = iw_ref[j, key[0] * 3 + key[1]]
        pair = tuple(weight * a for a in pair)
        total = pair if total is None else tuple(a + b for a, b in zip(total, pair))
    return total


def gradient_r(v, j, g):
    for s in range(8):
        for r, value in enumerate(along(DERIV, [v[j, r, s] for r in range(8)])):
            g[r, s] = value


def apply_tile(v, j, wk, jk, c, wt, kf_ref, kb_ref, y, g):
    gradient_r(v, j, g)
    base = weight_rows(wt * (coolant_throughput * KRYLOV_SCALE))
    for r in range(8):
        second = along(DERIV, [v[j, r, s] for s in range(8)])
        flux = []
        for s in range(8):
            first = g[r, s]
            k = wk[jk, r, s]
            flux.append(k * (second[s] + c * first))
            g[r, s] = k * (first + c * second[s])
        for s, value in enumerate(along(DERIV.T, flux)):
            y[j, r, s] = value + base[r][s] * v[j, r, s]
    for s in range(8):
        for r, value in enumerate(along(DERIV.T, [g[r, s] for r in range(8)])):
            y[j, r, s] = y[j, r, s] + value
    front, back = lines_t(kf_ref, v[j])
    third = jnp.concatenate([wk[jk, 0:4] * front, wk[jk, 4:8] * back], 0)
    front, back = lines_t(kb_ref, third)
    y[j, 0:4] = y[j, 0:4] + front
    y[j, 4:8] = y[j, 4:8] + back


def step_kernel(na, first, *refs):
    refs = list(refs)
    par_ref, y_in, a_in, b_in, wk_ref = refs[:5]
    del refs[:5]
    if first:
        from_ahead, from_behind = refs[:2]
        del refs[:2]
        prev = None
    else:
        wkg_ref, prev = refs[:2]
        del refs[:2]
    cr_ref, wt_ref, iw_ref, kf_ref, kb_ref, v, y, a_out, b_out, dots = refs[:10]
    del refs[:10]
    if first:
        wkg_ref = refs.pop(0)
    g, lo, hi = refs
    ghost = 2 * na
    parity = par_ref[0]
    if first:
        wkg_ref[0] = place_rims(from_ahead[...], from_behind[...]).reshape(8, 8, 8, LANES)
    v[...] = y_in[...]
    add_faces(na, parity, v, a_in, b_in)
    wt = wt_ref[...]
    dots[...] = jnp.zeros_like(dots)

    def own(j, carry):
        for k, value in enumerate(squares(v, j, prev, iw_ref)):
            dots[k] += value
        apply_tile(v, j, wk_ref, j, cr_ref[j], wt, kf_ref, kb_ref, y, g)
        return carry

    lax.fori_loop(0, ghost, own, 0)
    apply_tile(v, ghost, wkg_ref, 0, cr_ref[ghost], wt, kf_ref, kb_ref, y, g)
    assemble(na, y, lo, hi)
    faces_out(parity, lo, hi, a_out, b_out)


def last_kernel(na, par_ref, y_in, a_in, b_in, wk_ref, prev, cr_ref, wt_ref, iw_ref, kf_ref, d0, d1, d2, d3, v, all_dots, dots, g):
    ghost = 2 * na
    v[...] = y_in[...]
    add_faces(na, par_ref[0], v, a_in, b_in)
    wt = wt_ref[...]
    dots[...] = jnp.zeros_like(dots)

    def own(j, carry):
        for k, value in enumerate(squares(v, j, prev, iw_ref)):
            dots[k] += value
        gradient_r(v, j, g)
        c = 2.0 * cr_ref[j]
        base = weight_rows(wt * (coolant_throughput * KRYLOV_SCALE))
        front, back = lines_t(kf_ref, v[j])
        total = None
        for r in range(8):
            second = along(DERIV, [v[j, r, s] for s in range(8)])
            line = None
            for s in range(8):
                one, two = g[r, s], second[s]
                three = front[r, s] if r < 4 else back[r - 4, s]
                x = v[j, r, s]
                term = base[r][s] * x * x + wk_ref[j, r, s] * (one * (one + c * two) + two * two + three * three)
                line = term if line is None else line + term
            total = line if total is None else total + line
        dots[2] += total
        return carry

    lax.fori_loop(0, ghost, own, 0)
    lane = lane_index(1)
    rows = [d0[0], d1[1], d1[0], d2[1], d2[0], d3[1], d3[0], dots[1], dots[0], dots[2]]
    out = jnp.zeros((1, LANES), f32)
    for k, row in enumerate(rows):
        out = jnp.where(lane == k, jnp.sum(jnp.sum(row, 0, keepdims=True), 1, keepdims=True), out)
    all_dots[...] = jnp.broadcast_to(out[None], all_dots.shape)


def combine_kernel(na, m_ref, v0, v1, v2, v3, v4, out_ref):
    sums = jnp.sum(m_ref[:, 0, :], 0, keepdims=True)
    lane = lane_index(1)
    m = [jnp.sum(jnp.where(lane == k, sums, 0.0), 1, keepdims=True) for k in range(2 * ITERS)]
    n = ITERS
    low = [[None] * n for _ in range(n)]
    diag = [None] * n
    for j in range(n):
        acc = [m[i + j + 1] for i in range(n)]
        for k in range(j):
            scaled = low[j][k] * diag[k]
            for i in range(j, n):
                acc[i] = acc[i] - low[i][k] * scaled
        diag[j] = acc[j]
        for i in range(j + 1, n):
            low[i][j] = acc[i] / acc[j]
    z = []
    for i in range(n):
        value = m[i]
        for k in range(i):
            value = value - low[i][k] * z[k]
        z.append(value)
    c = [z[i] / diag[i] for i in range(n)]
    for i in reversed(range(n)):
        for k in range(i + 1, n):
            c[i] = c[i] - low[k][i] * c[k]
    c = [jnp.broadcast_to(x * KRYLOV_SCALE, (8, LANES)) for x in c]
    step = 2 * na
    vs = (v0, v1, v2, v3, v4)
    for r in range(8):
        for s in range(8):
            base = (r * 8 + s) * 8 * step
            for l in range(2):
                for at in range(na):
                    x = None
                    for coef, v in zip(c, vs):
                        term = coef * v[l * na + at, r, s]
                        x = term if x is None else x + term
                    out_ref[pl.ds(base + at * 2 + l, 8, stride=step), :] = x


def shift(x, axis, by):
    n = lax.axis_size(axis)
    return lax.ppermute(x, axis, [(i, i + by) for i in range(n) if 0 <= i + by < n])


def swap(x, axis, start):
    n = lax.axis_size(axis)
    pairs = [(i, i + 1) for i in range(start, n - 1, 2)]
    return lax.ppermute(x, axis, pairs + [(j, i) for i, j in pairs])


def around(x, by):
    n = lax.axis_size("slab") * lax.axis_size("chan")
    return lax.ppermute(x, ("slab", "chan"), [(i, (i + by) % n) for i in range(n)])


def product_weights(count_l, count_a):
    slab, chan = lax.axis_index("slab"), lax.axis_index("chan")
    axial = slab * count_a + jnp.arange(count_a)
    lateral = chan * count_l + jnp.arange(count_l)
    last_a = lax.axis_size("slab") * count_a - 1
    last_l = lax.axis_size("chan") * count_l - 1
    half = lambda cond: jnp.where(cond, 0.5, 1.0).astype(f32)
    along_a = jnp.stack([half(axial > 0), jnp.ones(count_a, f32), half(axial < last_a)])
    along_l = jnp.stack([half(lateral > 0), jnp.ones(count_l, f32), half(lateral < last_l)])
    weights = along_a[:, None, None, :] * along_l[None, :, :, None]
    weights = weights.reshape(9, -1, LANES).transpose(1, 0, 2)
    return jnp.broadcast_to(weights[:, :, None, :], weights.shape[:2] + (8, LANES))


def on_device(
    stream_speed_field,
    liquid_to_solid_element,
    previous_panel_warmth,
    pointwise_energy_source,
    coked_element_flags,
    coking_thickness_plies,
):
    count_l, count_a = coked_element_flags.shape
    assert count_l == 2 and count_a % LANES == 0
    elements = count_l * count_a
    na = count_a // LANES
    tiles = count_l * na
    chan = lax.axis_size("chan")
    total = lax.axis_size("slab") * chan
    me = (lax.axis_index("slab") * chan + lax.axis_index("chan")).astype(jnp.int32).reshape(1)
    parity = (lax.axis_index("chan") % 2).astype(jnp.int32).reshape(1)

    wt = jnp.asarray(np.broadcast_to(GLL_W[:, None], (8, LANES)), f32)
    kf, kb = (jnp.asarray(k) for k in line_matrices())
    k1, kl, k2, k3 = (jnp.asarray(k) for k in fluid_matrices())

    layers = coking_thickness_plies.astype(f32)
    flags = coked_element_flags.astype(f32)
    damping = jnp.where(coked_element_flags == 1, 1.0 / (1.0 + layer_damp * layers), jnp.ones_like(layers))
    cross = cross_gain * flags * layers / (layers + 1.0)
    dc = jnp.stack([damping.reshape(elements), cross.reshape(elements)])
    iw = product_weights(count_l, count_a)

    def as_rows(x):
        x = x.reshape(8, 8, 8, count_l, na, LANES).transpose(0, 1, 2, 4, 3, 5)
        return x.reshape(512 * tiles, LANES)

    field = (tiles, 8, 8, 8, LANES)
    whole = (tiles + 1, 8, 8, 8, LANES)
    face = (na + 1, 8, 8, LANES)
    shape = lambda s, d=f32: jax.ShapeDtypeStruct(s, d)
    z, behind, ahead = call(
        functools.partial(source_kernel, na),
        [shape(field), shape((2 * RIM, 640)), shape((2 * RIM, 640))],
        as_rows(previous_panel_warmth),
        as_rows(pointwise_energy_source),
        dc,
        wt,
    )
    from_ahead = shift(behind, "slab", -1)
    from_behind = shift(ahead, "slab", 1)

    split = 4
    width = elements // split
    room = elements // 4
    out = pl.pallas_call(
        functools.partial(fluid_kernel, chan, total),
        grid=(split,),
        in_specs=[
            pl.BlockSpec(memory_space=pltpu.SMEM),
            pl.BlockSpec((3, 8, 8, 8, width), lambda i: (0, 0, 0, 0, i)),
        ]
        + [pl.BlockSpec(memory_space=pltpu.VMEM)] * 5,
        out_specs=[pl.BlockSpec((3, 8, 8, 8, width), lambda i: (0, 0, 0, 0, i))]
        + [pl.BlockSpec(memory_space=pltpu.VMEM)] * 4,
        out_shape=[shape(stream_speed_field.shape, bf16), shape((512, elements), bf16)]
        + [shape((528, room), bf16)] * 3,
        scratch_shapes=[pltpu.VMEM((split, 512, width), bf16)],
        compiler_params=pltpu.CompilerParams(vmem_limit_bytes=48 * 1024 * 1024),
    )(me, stream_speed_field, liquid_to_solid_element.reshape(1, elements), k1, kl, k2, k3)
    stepped, own, *outgoing = out

    scratch_faces = [pltpu.VMEM(face, f32)] * 2
    y, cr, a, b = call(
        functools.partial(source_assembly_kernel, na),
        [shape(whole), shape((tiles + 1, 8, LANES)), shape(face), shape(face)],
        parity,
        z,
        from_ahead,
        from_behind,
        dc,
        smem=1,
        scratch=scratch_faces,
    )
    received = [around(x, by) for x, by in zip(outgoing, (1, -1, chan))]
    a, b = swap(a, "chan", 0), swap(b, "chan", 1)

    wk, behind, ahead = call(
        functools.partial(unpack_kernel, na),
        [shape(field), shape((2 * RIM, 512)), shape((2 * RIM, 512))],
        own,
        *received,
        dc,
        wt,
    )
    wk_ahead = shift(behind, "slab", -1)
    wk_behind = shift(ahead, "slab", 1)

    basis, products = [], []
    wkg = None
    for number in range(ITERS - 1):
        first = number == 0
        extra = (wk_ahead, wk_behind) if first else (wkg, basis[-1])
        outs = [shape(whole), shape(whole), shape(face), shape(face), shape((2, 8, LANES))]
        if first:
            outs.append(shape((1, 8, 8, 8, LANES)))
        got = call(
            functools.partial(step_kernel, na, first),
            outs,
            parity,
            y,
            a,
            b,
            wk,
            *extra,
            cr,
            wt,
            iw,
            kf,
            kb,
            smem=1,
            scratch=[pltpu.VMEM((8, 8, 8, LANES), f32)] + scratch_faces,
        )
        if first:
            wkg = got[5]
        v, y, a, b, dots = got[:5]
        basis.append(v)
        products.append(dots)
        a, b = swap(a, "chan", 0), swap(b, "chan", 1)
    v, sums = call(
        functools.partial(last_kernel, na),
        [shape(whole), shape((total, 1, LANES))],
        parity,
        y,
        a,
        b,
        wk,
        basis[-1],
        cr,
        wt,
        iw,
        kf,
        *products,
        smem=1,
        scratch=[pltpu.VMEM((3, 8, LANES), f32), pltpu.VMEM((8, 8, 8, LANES), f32)],
    )
    basis.append(v)
    sums = lax.all_to_all(sums, ("slab", "chan"), 0, 0)
    (x,) = call(functools.partial(combine_kernel, na), [shape((512 * tiles, LANES))], sums, *basis)
    x = x.reshape(8, 8, 8, na, count_l, LANES).transpose(0, 1, 2, 4, 3, 5)
    return stepped, x.reshape(8, 8, 8, count_l, count_a)


def solution(mesh):
    in_specs = (
        P(None, None, None, None, ("slab", "chan")),
        P(("slab", "chan")),
        P(None, None, None, "chan", "slab"),
        P(None, None, None, "chan", "slab"),
        P("chan", "slab"),
        P("chan", "slab"),
    )
    out_specs = (P(None, None, None, None, ("slab", "chan")), P(None, None, None, "chan", "slab"))
    return jax.shard_map(
        on_device, mesh=mesh, in_specs=in_specs, out_specs=out_specs, check_vma=False
    )
```

time: 840 us -> 128 us (0.15)
  local copies, waits for them, and re-layouts: 325 us -> 15.5 us
  blocking collectives: 212 us -> 16.3 us
  matrix products: 107 us -> 0 us
  other arithmetic: 93.5 us -> 1.03 us
  Pallas kernels: 0 us -> 49.6 us
  starting transfers between devices: 60.4 us -> 36.8 us
  between operations: 19.9 us -> 0.94 us
  waiting for transfers between devices: 15.8 us -> 7.33 us
    psum x5 -> x0, blocking collectives: 212 us -> none  [paired_sums(): lax.psum((jnp.sum(residual_now * residual_now * inv_mult), jnp.sum(residu...]
    scatter x14 -> x0, local copies, waits for them, and re-layouts: 187 us -> none  [the longest x12 184 us: gather_nodes(): field = field.at[7, :, :, :, :-1].set(shared).at[0, :, :, :, 1:].set(shared)]
    dot_general x46 -> x0, matrix products: 107 us -> none  [the longest x25 44.9 us: backward(): jnp.einsum(backward_forms[conjugate_update_vector], matrix, field, precis...]
    scatter-add x13 -> x0, local copies, waits for them, and re-layouts: 92.8 us -> none  [gather_nodes(): field.at[0, :, :, :, 0].add(with_rims[0]).at[7, :, :, :, -1]]
    pallas_call x0 -> x10, Pallas kernels: none -> 49.6 us  [the longest x9 36.6 us: call(): pl.pallas_call(kernel, in_specs=specs, out_specs=outs, out_shape=out_shap...]
    ppermute x27 -> x17, starting transfers between devices: 60.4 us -> 36.8 us  [the longest x10 18.6 us: swap(): return lax.ppermute(x, axis, pairs + [(j, i) for i, j in pairs])]
    another operation x11 -> x3, other arithmetic: 22 us -> 0.1 us  [the longest x1 0.08 us: product_weights(): jnp.stack([half(lateral > 0), jnp.ones(count_l, f32), half(lateral < last...]
    add x28 -> x0, other arithmetic: 21 us -> none  [the longest x12 12.2 us: gather_nodes(): field.at[0, :, :, :, 0].add(with_rims[0]).at[7, :, :, :, -1]]
  transfers between devices with their start and end apart: 27 -> 17, of which waited for: 6 -> 6; matrix products, arithmetic and copies ran while one was open for 38% -> 0% of each run, Pallas kernels for 0% -> 12%
where the time goes in v1:
time: 128 us
  Pallas kernels  49.6 us (39%)
  starting transfers between devices  36.8 us (29%)
  blocking collectives  16.3 us (13%)
  local copies, waits for them, and re-layouts  15.5 us (12%)
  waiting for transfers between devices  7.33 us (6%)
    pallas_call x9, Pallas kernels, call(): pl.pallas_call(kernel, in_specs=specs, out_specs=outs, out_shape=out_shap...  36.6 us
    ppermute x10, starting transfers between devices, swap(): return lax.ppermute(x, axis, pairs + [(j, i) for i, j in pairs])  18.6 us
    all_to_all x1, blocking collectives, on_device(): sums = lax.all_to_all(sums, ('slab', 'chan'), 0, 0)  16.3 us
    unnamed x48, local copies, waits for them, and re-layouts  15.3 us
    pallas_call x1, Pallas kernels, on_device(): pl.pallas_call(functools.partial(fluid_kernel, chan, total), grid=(split,...  13 us
    ppermute x4, starting transfers between devices, shift(): lax.ppermute(x, axis, [(i, i + by) for i in range(n) if 0 <= i + by < n])  12.6 us
    ppermute x3, starting transfers between devices, around(): lax.ppermute(x, ('slab', 'chan'), [(i, (i + by) % n) for i in range(n)])  5.6 us
    ppermute x3, waiting for transfers between devices, around(): lax.ppermute(x, ('slab', 'chan'), [(i, (i + by) % n) for i in range(n)])  4.54 us
  transfers between devices with their start and end apart: 17, of which 6 were waited for; matrix products, arithmetic and copies ran while one was open for 0% of the time, Pallas kernels for 12%

profile of v1, /device:TPU:0, one launch (start us, length us, event | category | flops | bytes accessed | tf_op | source)
XLA Modules:
  0.0 127.5 jit_solution(6710091452822146501)
XLA Ops:
  0.6 0.8 fusion.1
  1.5 1.2 copy-done.14
  2.7 1.2 copy-done.15
  4.0 0.7 copy-done.20
  4.7 1.6 %shard_map.141 = (f32[4,8,8,8,128]{4,3,2,1,0:T(8,128)S(1)}, f32[16,640]{1,0:T(8,128)}, f32[16,640]{1,0:T(8,128)S(1)}) custom-call(f32[2048,128]{1,0:T(8,128)S(1)} %bitcast.30, f32[2048,128]{1,0:T(8,128)S(1)} %bitcast.31, f32[2,512]{1,0:T(2,128)S(1)} %pad_maximum_fusion.dc_ref, f32[8,128]{1,0:T(8,128)S(1)} %copy-done.20), custom_call_target="tpu_custom_call" | custom-call | tf_op jit(solution)/shard_map/pallas_call | solution.py:125
  6.2 1.3 %collective-permute-start = (f32[16,640]{1,0:T(8,128)}, f32[16,640]{1,0:T(8,128)S(1)}, u32[]{:S(2)}, u32[]{:S(2)}) collective-permute-start(f32[16,640]{1,0:T(8,128)} %get-tuple-element.42), channel_id=1, source_target_pairs={{4,0},{8,4},{12,8},{16,12},{20,16},{24,20},{28,24},{5,1},{9,5},{13... | collective-permute-start | bytes 122888 | tf_op jit(solution)/shard_map/ppermute | solution.py:541
  7.5 5.5 %collective-permute-start.1 = (f32[16,640]{1,0:T(8,128)S(1)}, f32[16,640]{1,0:T(8,128)S(1)}, u32[]{:S(2)}, u32[]{:S(2)}) collective-permute-start(f32[16,640]{1,0:T(8,128)S(1)} %get-tuple-element.43), channel_id=1, source_target_pairs={{0,4},{4,8},{8,12},{12,16},{16,20},{20,24},{24,28},{1,5},{5,9},{9,... | collective-permute-start | bytes 122888 | tf_op jit(solution)/shard_map/ppermute | solution.py:541
  13.0 1.2 copy-done.16
  14.3 1.2 copy-done.17
  15.5 0.9 copy-done.19
  16.4 13.0 %shard_map.140 = (bf16[3,8,8,8,512]{4,3,2,1,0:T(8,128)(2,1)}, bf16[512,512]{1,0:T(8,128)(2,1)S(1)}, bf16[528,128]{1,0:T(8,128)(2,1)}, bf16[528,128]{1,0:T(8,128)(2,1)}, bf16[528,128]{1,0:T(8,128)(2,1)}) custom-call(s32[1]{0:T(128)} %bitcast.me_ref, bf16[3,8,8,8,512]{4,3,2,1,0:T(8,128)(2,1)S(1)} %copy-done.8, s32[1,512]{1,0:T(1,128)S(1)} %bitcast.32, ...), custom_call_target="tpu_custom_call" | custom-call | tf_op jit(solution)/shard_map/pallas_call | solution.py:620
  29.5 5.3 %collective-permute-start.5 = (bf16[528,128]{1,0:T(8,128)(2,1)}, bf16[528,128]{1,0:T(8,128)(2,1)S(1)}, u32[]{:S(2)}, u32[]{:S(2)}) collective-permute-start(bf16[528,128]{1,0:T(8,128)(2,1)} %get-tuple-element.49), channel_id=1, source_target_pairs={{0,31},{1,0},{2,1},{3,2},{4,3},{5,4},{6,5},{7,6},{8,7},{9,8},{10,9... | collective-permute-start | bytes 405512 | tf_op jit(solution)/shard_map/ppermute | solution.py:552
  34.9 0.2 collective-permute-start.6
  35.2 0.1 mul.55
  35.3 0.1 copy.20
  35.5 1.0 shard_map.142
  36.5 1.1 copy-done.9
  37.6 0.7 collective-permute-start.3
  38.3 4.5 %collective-permute-done.6.r3_ref = bf16[528,128]{1,0:T(8,128)(2,1)S(1)} collective-permute-done((bf16[528,128]{1,0:T(8,128)(2,1)}, bf16[528,128]{1,0:T(8,128)(2,1)S(1)}, u32[]{:S(2)}, u32[]{:S(2)}) %collective-permute-start.6) | collective-permute-done | bytes 135200 | tf_op jit(solution)/shard_map/ppermute | solution.py:552
  42.8 1.5 %shard_map.143 = (f32[4,8,8,8,128]{4,3,2,1,0:T(8,128)S(1)}, f32[16,512]{1,0:T(8,128)S(1)}, f32[16,512]{1,0:T(8,128)S(1)}) custom-call(bf16[512,512]{1,0:T(8,128)(2,1)S(1)} %get-tuple-element.47.own_ref, bf16[528,128]{1,0:T(8,128)(2,1)S(1)} %collective-permute-done.4.r1_ref, bf16[528,128]{1,0:T(8,128)(2,1)S(1)} %collective-permute-done.5.r2_ref, ...), custom_call_target="tpu_custom_call" | custom-call | tf_op jit(solution)/shard_map/pallas_call | solution.py:125
  44.2 1.3 %collective-permute-start.7 = (f32[16,512]{1,0:T(8,128)S(1)}, f32[16,512]{1,0:T(8,128)S(1)}, u32[]{:S(2)}, u32[]{:S(2)}) collective-permute-start(f32[16,512]{1,0:T(8,128)S(1)} %get-tuple-element.52), channel_id=1, source_target_pairs={{4,0},{8,4},{12,8},{16,12},{20,16},{24,20},{28,24},{5,1},{9,5},{13... | collective-permute-start | bytes 98312 | tf_op jit(solution)/shard_map/ppermute | solution.py:541
  45.6 4.5 %collective-permute-start.8 = (f32[16,512]{1,0:T(8,128)S(1)}, f32[16,512]{1,0:T(8,128)S(1)}, u32[]{:S(2)}, u32[]{:S(2)}) collective-permute-start(f32[16,512]{1,0:T(8,128)S(1)} %get-tuple-element.53), channel_id=1, source_target_pairs={{0,4},{4,8},{8,12},{12,16},{16,20},{20,24},{24,28},{1,5},{5,9},{9,... | collective-permute-start | bytes 98312 | tf_op jit(solution)/shard_map/ppermute | solution.py:541
  50.2 1.5 %collective-permute-done.8.refs_6_ = f32[16,512]{1,0:T(8,128)S(1)} collective-permute-done((f32[16,512]{1,0:T(8,128)S(1)}, f32[16,512]{1,0:T(8,128)S(1)}, u32[]{:S(2)}, u32[]{:S(2)}) %collective-permute-start.8) | collective-permute-done | bytes 32800 | tf_op jit(solution)/shard_map/ppermute | solution.py:541
  51.7 6.9 %shard_map.144 = (f32[5,8,8,8,128]{4,3,2,1,0:T(8,128)S(1)}, f32[5,8,8,8,128]{4,3,2,1,0:T(8,128)S(1)}, f32[3,8,8,128]{3,2,1,0:T(8,128)S(1)}, f32[3,8,8,128]{3,2,1...) custom-call(s32[1]{0:T(128)} %bitcast.2.par_ref.refs_0_, f32[5,8,8,8,128]{4,3,2,1,0:T(8,128)} %copy-done.9, ...), custom_call_target="tpu_custom_call" | custom-call | tf_op jit(solution)/shard_map/pallas_call | solution.py:125
  58.7 1.1 copy-done.2
  59.8 1.0 copy-done.10
  60.8 0.7 collective-permute-start.10
  61.5 0.6 collective-permute-done.9.refs_2_
  62.1 6.9 %shard_map.145 = (f32[5,8,8,8,128]{4,3,2,1,0:T(8,128)S(1)}, f32[5,8,8,8,128]{4,3,2,1,0:T(8,128)S(1)}, f32[3,8,8,128]{3,2,1,0:T(8,128)S(1)}, f32[3,8,8,128]{3,2,1,0:T(8,128)S(1)}, f32[2,8,128]{2,1,0:T(8,128)S(1)}) custom-call(s32[1]{0:T(128)} %bitcast.2.par_ref.refs_0_, f32[5,8,8,8,128]{4,3,2,1,0:T(8,128)} %copy-done.10, ...), custom_call_target="tpu_custom_call" | custom-call | tf_op jit(solution)/shard_map/pallas_call | solution.py:125
  69.0 1.1 copy-done.4
  70.1 1.1 copy-done.12
  71.1 5.1 %collective-permute-start.11 = (f32[3,8,8,128]{3,2,1,0:T(8,128)S(1)}, f32[3,8,8,128]{3,2,1,0:T(8,128)S(1)}, u32[]{:S(2)}, u32[]{:S(2)}) collective-permute-start(f32[3,8,8,128]{3,2,1,0:T(8,128)S(1)} %get-tuple-element.61), channel_id=1, source_target_pairs={{0,1},{2,3},{1,0},{3,2},{4,5},{6,7},{5,4},{7,6},{8,9},{10,11},{9,8... | collective-permute-start | bytes 294920 | tf_op jit(solution)/shard_map/ppermute | solution.py:547
  76.2 0.8 collective-permute-start.12
  77.1 0.1 collective-permute-done.11.refs_2_
  77.2 6.9 %shard_map.146 = (f32[5,8,8,8,128]{4,3,2,1,0:T(8,128)S(1)}, f32[5,8,8,8,128]{4,3,2,1,0:T(8,128)S(1)}, f32[3,8,8,128]{3,2,1,0:T(8,128)S(1)}, f32[3,8,8,128]{3,2,1,0:T(8,128)S(1)}, f32[2,8,128]{2,1,0:T(8,128)S(1)}) custom-call(s32[1]{0:T(128)} %bitcast.2.par_ref.refs_0_, f32[5,8,8,8,128]{4,3,2,1,0:T(8,128)} %copy-done.12, ...), custom_call_target="tpu_custom_call" | custom-call | tf_op jit(solution)/shard_map/pallas_call | solution.py:125
  84.1 1.1 copy-done.6
  85.1 1.1 copy-done.11
  86.3 5.0 %collective-permute-start.13 = (f32[3,8,8,128]{3,2,1,0:T(8,128)S(1)}, f32[3,8,8,128]{3,2,1,0:T(8,128)S(1)}, u32[]{:S(2)}, u32[]{:S(2)}) collective-permute-start(f32[3,8,8,128]{3,2,1,0:T(8,128)S(1)} %get-tuple-element.65), channel_id=1, source_target_pairs={{0,1},{2,3},{1,0},{3,2},{4,5},{6,7},{5,4},{7,6},{8,9},{10,11},{9,8... | collective-permute-start | bytes 294920 | tf_op jit(solution)/shard_map/ppermute | solution.py:547
  91.2 0.7 collective-permute-start.14
  91.9 0.3 collective-permute-done.13.refs_2_
  92.2 6.9 %shard_map.147 = (f32[5,8,8,8,128]{4,3,2,1,0:T(8,128)S(1)}, f32[5,8,8,8,128]{4,3,2,1,0:T(8,128)S(1)}, f32[3,8,8,128]{3,2,1,0:T(8,128)S(1)}, f32[3,8,8,128]{3,2,1,0:T(8,128)S(1)}, f32[2,8,128]{2,1,0:T(8,128)S(1)}) custom-call(s32[1]{0:T(128)} %bitcast.2.par_ref.refs_0_, f32[5,8,8,8,128]{4,3,2,1,0:T(8,128)} %copy-done.11, ...), custom_call_target="tpu_custom_call" | custom-call | tf_op jit(solution)/shard_map/pallas_call | solution.py:125
  99.1 5.0 %collective-permute-start.15 = (f32[3,8,8,128]{3,2,1,0:T(8,128)S(1)}, f32[3,8,8,128]{3,2,1,0:T(8,128)S(1)}, u32[]{:S(2)}, u32[]{:S(2)}) collective-permute-start(f32[3,8,8,128]{3,2,1,0:T(8,128)S(1)} %get-tuple-element.69), channel_id=1, source_target_pairs={{0,1},{2,3},{1,0},{3,2},{4,5},{6,7},{5,4},{7,6},{8,9},{10,11},{9,8... | collective-permute-start | bytes 294920 | tf_op jit(solution)/shard_map/ppermute | solution.py:547
  104.1 0.7 collective-permute-start.16
  104.7 0.3 collective-permute-done.15.a_in
  105.0 2.1 %shard_map.148 = (f32[5,8,8,8,128]{4,3,2,1,0:T(8,128)S(1)}, f32[32,1,128]{2,1,0:T(1,128)S(1)}) custom-call(s32[1]{0:T(128)} %bitcast.2.par_ref.refs_0_, f32[5,8,8,8,128]{4,3,2,1,0:T(8,128)S(1)} %get-tuple-element.68.y_in, f32[3,8,8,128]{3,2,1,0:T(8,128)S(1)} %collective-permute-done.15.a_in, f32[3,8,8,128]{3,2,1,0:T(8,128)S(1)} %collective-permute-done.16.b_in, ...), custom_call_target="tpu_custom_call" | custom-call | tf_op jit(solution)/shard_map/pallas_call | solution.py:125
  107.1 1.1 copy-done.13
  108.3 16.3 %all_to_all.5.m_ref = f32[32,1,128]{2,1,0:T(1,128)S(1)} all-to-all(f32[32,1,128]{2,1,0:T(1,128)S(1)} %get-tuple-element.76), channel_id=1, replica_groups=mesh['slab'=8,'chan'=4] {'slab','chan'}, dimensions={0} | all-to-all | bytes 32768 | tf_op jit(solution)/shard_map/all_to_all | solution.py:712
  124.6 2.9 %shard_map.149 = f32[2048,128]{1,0:T(8,128)} custom-call(f32[32,1,128]{2,1,0:T(1,128)S(1)} %all_to_all.5.m_ref, f32[5,8,8,8,128]{4,3,2,1,0:T(8,128)S(1)} %copy-done.3, f32[5,8,8,8,128]{4,3,2,1,0:T(8,128)S(1)} %copy-done.5, f32[5,8,8,8,128]{4,3,2,1,0:T(8,128)S(1)} %copy-done.7, f32[5,8,8,8,128]{4,3,2,1,0:T(8,128)S(1)} %get-tuple-element.71.prev.v3, ...), custom_call_target="tpu_custom_call" | custom-call | tf_op jit(solution)/shard_map/pallas_call | solution.py:125
  (61 shorter events, 0.4 us)
Async XLA Ops:
  0.6 12.4 %copy-start.8 = (bf16[3,8,8,8,512]{4,3,2,1,0:T(8,128)(2,1)S(1)}, bf16[3,8,8,8,512]{4,3,2,1,0:T(8,128)(2,1)}, u32[]{:S(2)}) copy-start(bf16[3,8,8,8,512]{4,3,2,1,0:T(8,128)(2,1)} %u_ref.1) | copy-start | bytes 4718596
  1.5 1.2 copy-start.14
  2.7 1.2 copy-start.15
  4.0 0.7 copy-start.20
  4.7 8.3 %copy-start.18 = (bf16[256,512]{1,0:T(8,128)(2,1)S(1)}, bf16[256,512]{1,0:T(8,128)(2,1)}, u32[]{:S(2)}) copy-start(bf16[256,512]{1,0:T(8,128)(2,1)} %constant.64.clone.k3_ref) | copy-start | bytes 786436
  4.7 8.4 %copy-start.22 = (s32[512]{0:T(512)S(1)}, s32[512]{0:T(512)}, u32[]{:S(2)}) copy-start(s32[512]{0:T(512)} %param.14) | copy-start | bytes 6148
  6.2 29.2 %collective-permute-start = (f32[16,640]{1,0:T(8,128)}, f32[16,640]{1,0:T(8,128)S(1)}, u32[]{:S(2)}, u32[]{:S(2)}) collective-permute-start(f32[16,640]{1,0:T(8,128)} %get-tuple-element.42), channel_id=1, source_target_pairs={{4,0},{8,4},{12,8},{16,12},{20,16},{24,20},{28,24},{5,1},{9,5},{13... | collective-permute-start | bytes 122888 | tf_op jit(solution)/shard_map/ppermute | solution.py:541
  7.5 28.0 %collective-permute-start.1 = (f32[16,640]{1,0:T(8,128)S(1)}, f32[16,640]{1,0:T(8,128)S(1)}, u32[]{:S(2)}, u32[]{:S(2)}) collective-permute-start(f32[16,640]{1,0:T(8,128)S(1)} %get-tuple-element.43), channel_id=1, source_target_pairs={{0,4},{4,8},{8,12},{12,16},{16,20},{20,24},{24,28},{1,5},{5,9},{9,... | collective-permute-start | bytes 122888 | tf_op jit(solution)/shard_map/ppermute | solution.py:541
  13.0 1.2 copy-start.16
  14.3 1.2 copy-start.17
  15.5 0.9 copy-start.19
  16.4 26.4 %copy-start.21 = (f32[8,128]{1,0:T(8,128)S(1)}, f32[8,128]{1,0:T(8,128)}, u32[]{:S(2)}) copy-start(f32[8,128]{1,0:T(8,128)} %constant.58.clone.wt_ref.refs_8_) | copy-start | bytes 12292
  29.5 22.2 %copy-start = (bf16[256,768]{1,0:T(8,128)(2,1)S(1)}, bf16[256,768]{1,0:T(8,128)(2,1)}, u32[]{:S(2)}) copy-start(bf16[256,768]{1,0:T(8,128)(2,1)} %constant.59.clone.refs_10_.kf_ref) | copy-start | bytes 1179652
  29.5 22.2 %copy-start.1 = (bf16[256,768]{1,0:T(8,128)(2,1)S(1)}, bf16[256,768]{1,0:T(8,128)(2,1)}, u32[]{:S(2)}) copy-start(bf16[256,768]{1,0:T(8,128)(2,1)} %constant.60.clone.refs_11_) | copy-start | bytes 1179652
  29.5 8.8 %collective-permute-start.4 = (bf16[528,128]{1,0:T(8,128)(2,1)}, bf16[528,128]{1,0:T(8,128)(2,1)S(1)}, u32[]{:S(2)}, u32[]{:S(2)}) collective-permute-start(bf16[528,128]{1,0:T(8,128)(2,1)} %get-tuple-element.48), channel_id=1, source_target_pairs={{0,1},{1,2},{2,3},{3,4},{4,5},{5,6},{6,7},{7,8},{8,9},{9,10},{10,1... | collective-permute-start | bytes 405512 | tf_op jit(solution)/shard_map/ppermute | solution.py:552
  29.5 8.7 %collective-permute-start.5 = (bf16[528,128]{1,0:T(8,128)(2,1)}, bf16[528,128]{1,0:T(8,128)(2,1)S(1)}, u32[]{:S(2)}, u32[]{:S(2)}) collective-permute-start(bf16[528,128]{1,0:T(8,128)(2,1)} %get-tuple-element.49), channel_id=1, source_target_pairs={{0,31},{1,0},{2,1},{3,2},{4,3},{5,4},{6,5},{7,6},{8,7},{9,8},{10,9... | collective-permute-start | bytes 405512 | tf_op jit(solution)/shard_map/ppermute | solution.py:552
  34.9 7.9 %collective-permute-start.6 = (bf16[528,128]{1,0:T(8,128)(2,1)}, bf16[528,128]{1,0:T(8,128)(2,1)S(1)}, u32[]{:S(2)}, u32[]{:S(2)}) collective-permute-start(bf16[528,128]{1,0:T(8,128)(2,1)} %get-tuple-element.50), channel_id=1, source_target_pairs={{0,4},{1,5},{2,6},{3,7},{4,8},{5,9},{6,10},{7,11},{8,12},{9,13},{1... | collective-permute-start | bytes 405512 | tf_op jit(solution)/shard_map/ppermute | solution.py:552
  36.5 1.1 copy-start.9
  37.6 12.6 %collective-permute-start.2 = (f32[3,8,8,128]{3,2,1,0:T(8,128)S(1)}, f32[3,8,8,128]{3,2,1,0:T(8,128)S(1)}, u32[]{:S(2)}, u32[]{:S(2)}) collective-permute-start(f32[3,8,8,128]{3,2,1,0:T(8,128)S(1)} %get-tuple-element.45), channel_id=1, source_target_pairs={{0,1},{2,3},{1,0},{3,2},{4,5},{6,7},{5,4},{7,6},{8,9},{10,11},{9,8... | collective-permute-start | bytes 294920 | tf_op jit(solution)/shard_map/ppermute | solution.py:547
  37.6 12.7 %collective-permute-start.3 = (f32[3,8,8,128]{3,2,1,0:T(8,128)S(1)}, f32[3,8,8,128]{3,2,1,0:T(8,128)S(1)}, u32[]{:S(2)}, u32[]{:S(2)}) collective-permute-start(f32[3,8,8,128]{3,2,1,0:T(8,128)S(1)} %get-tuple-element.46), channel_id=1, source_target_pairs={{1,2},{2,1},{5,6},{6,5},{9,10},{10,9},{13,14},{14,13},{17,18},{18,... | collective-permute-start | bytes 294920 | tf_op jit(solution)/shard_map/ppermute | solution.py:547
  44.2 6.0 %collective-permute-start.7 = (f32[16,512]{1,0:T(8,128)S(1)}, f32[16,512]{1,0:T(8,128)S(1)}, u32[]{:S(2)}, u32[]{:S(2)}) collective-permute-start(f32[16,512]{1,0:T(8,128)S(1)} %get-tuple-element.52), channel_id=1, source_target_pairs={{4,0},{8,4},{12,8},{16,12},{20,16},{24,20},{28,24},{5,1},{9,5},{13... | collective-permute-start | bytes 98312 | tf_op jit(solution)/shard_map/ppermute | solution.py:541
  45.6 6.1 %collective-permute-start.8 = (f32[16,512]{1,0:T(8,128)S(1)}, f32[16,512]{1,0:T(8,128)S(1)}, u32[]{:S(2)}, u32[]{:S(2)}) collective-permute-start(f32[16,512]{1,0:T(8,128)S(1)} %get-tuple-element.53), channel_id=1, source_target_pairs={{0,4},{4,8},{8,12},{12,16},{16,20},{20,24},{24,28},{1,5},{5,9},{9,... | collective-permute-start | bytes 98312 | tf_op jit(solution)/shard_map/ppermute | solution.py:541
  58.7 1.1 copy-start.2
  59.8 1.1 copy-start.10
  60.8 1.3 %collective-permute-start.9 = (f32[3,8,8,128]{3,2,1,0:T(8,128)S(1)}, f32[3,8,8,128]{3,2,1,0:T(8,128)S(1)}, u32[]{:S(2)}, u32[]{:S(2)}) collective-permute-start(f32[3,8,8,128]{3,2,1,0:T(8,128)S(1)} %get-tuple-element.56), channel_id=1, source_target_pairs={{0,1},{2,3},{1,0},{3,2},{4,5},{6,7},{5,4},{7,6},{8,9},{10,11},{9,8... | collective-permute-start | bytes 294920 | tf_op jit(solution)/shard_map/ppermute | solution.py:547
  60.8 1.3 %collective-permute-start.10 = (f32[3,8,8,128]{3,2,1,0:T(8,128)S(1)}, f32[3,8,8,128]{3,2,1,0:T(8,128)S(1)}, u32[]{:S(2)}, u32[]{:S(2)}) collective-permute-start(f32[3,8,8,128]{3,2,1,0:T(8,128)S(1)} %get-tuple-element.57), channel_id=1, source_target_pairs={{1,2},{2,1},{5,6},{6,5},{9,10},{10,9},{13,14},{14,13},{17,18},{18,... | collective-permute-start | bytes 294920 | tf_op jit(solution)/shard_map/ppermute | solution.py:547
  69.0 1.1 copy-start.4
  70.1 1.1 copy-start.12
  71.1 6.1 %collective-permute-start.11 = (f32[3,8,8,128]{3,2,1,0:T(8,128)S(1)}, f32[3,8,8,128]{3,2,1,0:T(8,128)S(1)}, u32[]{:S(2)}, u32[]{:S(2)}) collective-permute-start(f32[3,8,8,128]{3,2,1,0:T(8,128)S(1)} %get-tuple-element.61), channel_id=1, source_target_pairs={{0,1},{2,3},{1,0},{3,2},{4,5},{6,7},{5,4},{7,6},{8,9},{10,11},{9,8... | collective-permute-start | bytes 294920 | tf_op jit(solution)/shard_map/ppermute | solution.py:547
  76.2 0.9 collective-permute-start.12
  84.1 1.1 copy-start.6
  85.1 1.1 copy-start.11
  86.3 5.9 %collective-permute-start.13 = (f32[3,8,8,128]{3,2,1,0:T(8,128)S(1)}, f32[3,8,8,128]{3,2,1,0:T(8,128)S(1)}, u32[]{:S(2)}, u32[]{:S(2)}) collective-permute-start(f32[3,8,8,128]{3,2,1,0:T(8,128)S(1)} %get-tuple-element.65), channel_id=1, source_target_pairs={{0,1},{2,3},{1,0},{3,2},{4,5},{6,7},{5,4},{7,6},{8,9},{10,11},{9,8... | collective-permute-start | bytes 294920 | tf_op jit(solution)/shard_map/ppermute | solution.py:547
  91.2 0.9 collective-permute-start.14
  99.1 6.0 %collective-permute-start.15 = (f32[3,8,8,128]{3,2,1,0:T(8,128)S(1)}, f32[3,8,8,128]{3,2,1,0:T(8,128)S(1)}, u32[]{:S(2)}, u32[]{:S(2)}) collective-permute-start(f32[3,8,8,128]{3,2,1,0:T(8,128)S(1)} %get-tuple-element.69), channel_id=1, source_target_pairs={{0,1},{2,3},{1,0},{3,2},{4,5},{6,7},{5,4},{7,6},{8,9},{10,11},{9,8... | collective-permute-start | bytes 294920 | tf_op jit(solution)/shard_map/ppermute | solution.py:547
  104.1 0.9 collective-permute-start.16
  105.0 19.5 %copy-start.3 = (f32[5,8,8,8,128]{4,3,2,1,0:T(8,128)S(1)}, f32[5,8,8,8,128]{4,3,2,1,0:T(8,128)}, u32[]{:S(2)}) copy-start(f32[5,8,8,8,128]{4,3,2,1,0:T(8,128)} %copy-done.2) | copy-start | bytes 3932164
  105.0 19.5 %copy-start.5 = (f32[5,8,8,8,128]{4,3,2,1,0:T(8,128)S(1)}, f32[5,8,8,8,128]{4,3,2,1,0:T(8,128)}, u32[]{:S(2)}) copy-start(f32[5,8,8,8,128]{4,3,2,1,0:T(8,128)} %copy-done.4) | copy-start | bytes 3932164
  105.0 19.5 %copy-start.7 = (f32[5,8,8,8,128]{4,3,2,1,0:T(8,128)S(1)}, f32[5,8,8,8,128]{4,3,2,1,0:T(8,128)}, u32[]{:S(2)}) copy-start(f32[5,8,8,8,128]{4,3,2,1,0:T(8,128)} %copy-done.6) | copy-start | bytes 3932164
  107.1 1.1 copy-start.13

commit v2 on v1

--- a/solution.py
+++ b/solution.py
@@ -79,35 +79,38 @@
 def line_matrices():
     out = []
     for matrix in (DERIV, DERIV.T):
-        high, low = split_hi_lo(np.kron(np.eye(32), matrix))
-        out.append(np.concatenate([high, low, high], 1))
+        high, low = split_hi_lo(np.kron(np.eye(16), matrix))
+        upper = np.concatenate([high, high], 1)
+        out.append(np.concatenate([upper, np.concatenate([low, np.zeros_like(low)], 1)], 0))
     return out
 
 
-def fluid_matrices():
+def fluid_matrix():
     eye8 = np.eye(8)
     square = DERIV @ DERIV
-    first = np.kron(DERIV, np.eye(64))
-    laplace = (
-        np.kron(square, np.eye(64))
-        + np.kron(np.kron(eye8, square), eye8)
-        + np.kron(np.eye(64), square)
-    )
-    second = np.kron(np.kron(np.eye(4), DERIV), eye8)
-    third = np.kron(np.eye(32), DERIV)
-    return [np.concatenate(split_hi_lo(m), 1) for m in (first, laplace, second, third)]
-
-
-def along(matrix, line):
-    even = [line[j] + line[7 - j] for j in range(4)]
-    odd = [line[j] - line[7 - j] for j in range(4)]
+    second = np.kron(DERIV, eye8)
+    third = np.kron(eye8, DERIV)
+    curve = np.kron(square, eye8) + np.kron(eye8, square)
+    return np.concatenate([np.concatenate(split_hi_lo(np.kron(np.eye(2), m)), 1) for m in (second, third, curve)], 0)
+
+
+def halves_of(line):
+    return [line[j] + line[7 - j] for j in range(4)], [line[j] - line[7 - j] for j in range(4)]
+
+
+def combined(matrix, parts, sign):
+    even, odd = parts
     result = [None] * 8
     for i in range(4):
         p = sum(float(0.5 * (matrix[i, j] + matrix[i, 7 - j])) * even[j] for j in range(4))
         q = sum(float(0.5 * (matrix[i, j] - matrix[i, 7 - j])) * odd[j] for j in range(4))
         result[i] = p + q
-        result[7 - i] = q - p
+        result[7 - i] = q - p if sign < 0 else p - q
     return result
+
+
+def along(matrix, line):
+    return combined(matrix, halves_of(line), -1)
 
 
 def lane_index(rows=8):
@@ -118,7 +121,7 @@
     return pltpu.VMEM(shape, dtype)
 
 
-def call(kernel, out_shape, *args, smem=0, scratch=(), cost=None, limit=48, **kw):
+def call(kernel, out_shape, *args, smem=0, scratch=(), limit=48, **kw):
     specs = [pl.BlockSpec(memory_space=pltpu.SMEM)] * smem
     specs += [pl.BlockSpec(memory_space=pltpu.VMEM)] * (len(args) - smem)
     outs = [pl.BlockSpec(memory_space=pltpu.VMEM) for _ in out_shape]
@@ -128,7 +131,6 @@
         out_specs=outs,
         out_shape=out_shape,
         scratch_shapes=scratch,
-        cost_estimate=cost,
         compiler_params=pltpu.CompilerParams(vmem_limit_bytes=limit * 1024 * 1024),
         **kw,
     )(*args)
@@ -173,7 +175,7 @@
     return a + b
 
 
-def source_kernel(na, p_ref, q_ref, dc_ref, wt_ref, z_ref, behind_ref, ahead_ref):
+def source_kernel(na, par_ref, p_ref, q_ref, wt_ref, z_ref, a_ref, b_ref):
     rows = weight_rows(wt_ref[...])
     step = 2 * na
     for r in range(8):
@@ -183,22 +185,44 @@
                 for at in range(na):
                     pick = pl.ds(base + at * 2 + l, 8, stride=step)
                     z_ref[l * na + at, r, s] = rows[r][s] * (coolant_throughput * p_ref[pick, :] + q_ref[pick, :])
+    for r in range(8):
+        for at in range(na):
+            shared = z_ref[at, r, 7] + z_ref[na + at, r, 0]
+            z_ref[at, r, 7] = shared
+            z_ref[na + at, r, 0] = shared
+            send_faces(par_ref, (at, r), z_ref[at, r, 0], z_ref[na + at, r, 7], a_ref, b_ref)
+
+
+def rim_kernel(na, par_ref, z_in, a_ref, b_ref, dc_ref, z_ref, behind_ref, ahead_ref):
+    z_ref[...] = z_in[...]
+    for r in range(8):
+        for at in range(na):
+            lower, upper = got_faces(par_ref, (at, r), a_ref, b_ref)
+            z_ref[at, r, 0] = z_ref[at, r, 0] + lower
+            z_ref[na + at, r, 7] = z_ref[na + at, r, 7] + upper
 
     def tile_rows(j):
-        cols = pl.ds(j * LANES, LANES)
-        extra = [
-            jnp.broadcast_to(dc_ref[0:1, cols], (8, LANES)),
-            jnp.broadcast_to(dc_ref[1:2, cols], (8, LANES)),
-            jnp.zeros((LANES - 16, LANES), f32),
-        ]
-        return jnp.concatenate([z_ref[j].reshape(512, LANES)] + extra, 0)
-
-    behind, ahead = send_rims(tile_rows, na)
-    behind_ref[...] = behind
-    ahead_ref[...] = ahead
-
-
-def assemble(na, y, lo_ref, hi_ref):
+        cross = jnp.broadcast_to(dc_ref[1:2, j * LANES : (j + 1) * LANES], (LANES, LANES))
+        return jnp.concatenate([z_ref[j].reshape(512, LANES), cross], 0)
+
+    behind_ref[...], ahead_ref[...] = send_rims(tile_rows, na)
+
+
+def send_faces(par_ref, at, lower, upper, a_ref, b_ref):
+    even = par_ref[0] == 0
+    lower = jnp.where(par_ref[1] > 0, lower, 0.0)
+    upper = jnp.where(par_ref[2] > 0, upper, 0.0)
+    a_ref[at] = jnp.where(even, upper, lower)
+    b_ref[at] = jnp.where(even, lower, upper)
+
+
+def got_faces(par_ref, at, a_ref, b_ref):
+    even = par_ref[0] == 0
+    a, b = a_ref[at], b_ref[at]
+    return jnp.where(even, b, a), jnp.where(even, a, b)
+
+
+def assemble_axial(na, y):
     ghost = 2 * na
     lane = lane_index()
     first = lane == 0
@@ -229,38 +253,34 @@
         y[ghost, 0, s] = near[ghost] + from_left
         from_right = jnp.where(last, left[na], jnp.where(lane == half - 1, near_half[0], left[ghost]))
         y[ghost, 7, s] = far[ghost] + from_right
-    low = lane < half
+
+
+def assemble_lateral(na, par_ref, y, a_ref, b_ref):
+    ghost = 2 * na
+    half = LANES // 2
+    low = lane_index() < half
     for r in range(8):
         for at in range(na):
             shared = y[at, r, 7] + y[na + at, r, 0]
             y[at, r, 7] = shared
             y[na + at, r, 0] = shared
-            lo_ref[at, r] = y[at, r, 0]
-            hi_ref[at, r] = y[na + at, r, 7]
+            send_faces(par_ref, (at, r), y[at, r, 0], y[na + at, r, 7], a_ref, b_ref)
         upper = y[ghost, r, 7]
         lower = y[ghost, r, 0]
-        new_upper = upper + jnp.where(low, roll(lower, half, 1), 0.0)
-        new_lower = lower + jnp.where(low, 0.0, roll(upper, half, 1))
+        new_upper = upper + jnp.where(low, pltpu.roll(lower, half, 1), 0.0)
+        new_lower = lower + jnp.where(low, 0.0, pltpu.roll(upper, half, 1))
         y[ghost, r, 7] = new_upper
         y[ghost, r, 0] = new_lower
-        lo_ref[na, r] = jnp.where(low, new_lower, 0.0)
-        hi_ref[na, r] = jnp.where(low, roll(new_upper, half, 1), 0.0)
-
-
-def faces_out(parity, lo, hi, a_ref, b_ref):
-    even = parity == 0
-    a_ref[...] = jnp.where(even, hi[...], lo[...])
-    b_ref[...] = jnp.where(even, lo[...], hi[...])
-
-
-def add_faces(na, parity, v, a_ref, b_ref):
-    even = parity == 0
+        to_lower = jnp.where(low, new_lower, 0.0)
+        to_upper = jnp.where(low, pltpu.roll(new_upper, half, 1), 0.0)
+        send_faces(par_ref, (na, r), to_lower, to_upper, a_ref, b_ref)
+
+
+def add_faces(na, par_ref, v, a_ref, b_ref):
     ghost = 2 * na
     for r in range(8):
         for at in range(na + 1):
-            a, b = a_ref[at, r], b_ref[at, r]
-            upper = jnp.where(even, a, b)
-            lower = jnp.where(even, b, a)
+            lower, upper = got_faces(par_ref, (at, r), a_ref, b_ref)
             if at < na:
                 v[at, r, 0] = v[at, r, 0] + lower
                 v[na + at, r, 7] = v[na + at, r, 7] + upper
@@ -269,52 +289,45 @@
                 v[ghost, r, 7] = v[ghost, r, 7] + pltpu.roll(upper, LANES // 2, 1)
 
 
-def source_assembly_kernel(
-    na, par_ref, z_ref, from_ahead, from_behind, dc_ref, y_ref, cr_ref, a_ref, b_ref, lo, hi
-):
-    ghost = 2 * na
-    y_ref[0:ghost] = z_ref[...]
-    tile = place_rims(from_ahead[...], from_behind[...])
-    y_ref[ghost] = tile[:512].reshape(8, 8, 8, LANES)
-    for j in range(ghost):
-        cr_ref[j] = jnp.broadcast_to(dc_ref[1:2, j * LANES : (j + 1) * LANES], (8, LANES))
-    cr_ref[ghost] = tile[520:528]
-    assemble(na, y_ref, lo, hi)
-    faces_out(par_ref[0], lo, hi, a_ref, b_ref)
-
-
 def fluid_kernel(
-    chan, total, me_ref, u_ref, l2s_ref, k1_ref, kl_ref, k2_ref, k3_ref, out_ref, own_ref, s1_ref, s2_ref, s3_ref, c_ref
+    chan, total, me_ref, u_ref, l2s_ref, k_ref, out_ref, own_ref, s1_ref, s2_ref, s3_ref, c_ref, t_ref
 ):
     i = pl.program_id(0)
-    width = u_ref.shape[-1]
-    u = u_ref[...].astype(f32)
-    ub = [u[c].reshape(512, width).astype(bf16) for c in range(3)]
-    uf = [x.astype(f32) for x in ub]
-
-    def whole(k_ref, x):
-        return jnp.dot(k_ref[...], jnp.concatenate([x, x], 0), preferred_element_type=f32)
-
-    def halves(k_ref, x):
-        parts = []
-        for h in range(2):
-            part = x[h * 256 : (h + 1) * 256]
-            parts.append(jnp.dot(k_ref[...], jnp.concatenate([part, part], 0), preferred_element_type=f32))
-        return jnp.concatenate(parts, 0)
-
-    speed = None
+    k = k_ref[...]
+    square = DERIV @ DERIV
     for c in range(3):
-        convect = uf[0] * whole(k1_ref, ub[c]) + uf[1] * halves(k2_ref, ub[c]) + uf[2] * halves(k3_ref, ub[c])
-        new = (uf[c] + time_step * (viscosity * whole(kl_ref, ub[c]) - convect)).astype(bf16)
-        out_ref[c] = new.reshape(8, 8, 8, width)
-        new = new.astype(f32)
-        speed = new * new if speed is None else speed + new * new
-    c_ref[i, 0:512] = (1.0 + 0.5 * speed).astype(bf16)
+        for s in range(8):
+            parts = halves_of([u_ref[c, r, s].astype(f32) for r in range(8)])
+            slope = combined(DERIV, parts, -1)
+            curve = combined(square, parts, 1)
+            for r in range(8):
+                t_ref[c, r, s] = viscosity * curve[r] - u_ref[0, r, s].astype(f32) * slope[r]
+    for p in range(2):
+        speed = [None] * 4
+        for c in range(3):
+            x = u_ref[c, 4 * p : 4 * p + 4].astype(f32).reshape(2, 128, LANES)
+            x = jnp.concatenate([x[0], x[1]], 1).astype(bf16)
+            y = jnp.dot(k, jnp.concatenate([x, x], 0), preferred_element_type=f32)
+            for h in range(2):
+                part = y[:, h * LANES : (h + 1) * LANES].reshape(3, 2, 8, 8, LANES)
+                for q in range(2):
+                    r = 4 * p + 2 * h + q
+                    second, third, curve = part[0, q], part[1, q], part[2, q]
+                    u2, u3 = u_ref[1, r].astype(f32), u_ref[2, r].astype(f32)
+                    rate = t_ref[c, r] + viscosity * curve - u2 * second - u3 * third
+                    new = (u_ref[c, r].astype(f32) + time_step * rate).astype(bf16)
+                    out_ref[c, r] = new
+                    new = new.astype(f32)
+                    old = speed[2 * h + q]
+                    speed[2 * h + q] = new * new if old is None else old + new * new
+        for n, value in enumerate(speed):
+            r = 4 * p + n
+            c_ref[i, r * 64 : (r + 1) * 64] = (1.0 + 0.5 * value).astype(bf16).reshape(64, LANES)
 
     @pl.when(i == pl.num_programs(0) - 1)
     def _():
         elements = l2s_ref.shape[-1]
-        cond = jnp.concatenate([c_ref[k, 0:512] for k in range(c_ref.shape[0])], 1)
+        cond = jnp.concatenate([c_ref[n] for n in range(c_ref.shape[0])], 1)
         l2s = l2s_ref[...]
         if elements & (elements - 1) == 0:
             owner = lax.shift_right_logical(l2s, elements.bit_length() - 1)
@@ -346,7 +359,9 @@
             ref[...] = lax.dot_general(tagged, take, NT, preferred_element_type=f32).astype(bf16)
 
 
-def unpack_kernel(na, own_ref, r1_ref, r2_ref, r3_ref, dc_ref, wt_ref, wk_ref, behind_ref, ahead_ref):
+def unpack_kernel(
+    na, par_ref, own_ref, r1_ref, r2_ref, r3_ref, dc_ref, wt_ref, zb_ref, za_ref, wk_ref, behind_ref, ahead_ref
+):
     rows = weight_rows(wt_ref[...] * KRYLOV_SCALE)
     got = jnp.concatenate([r[0:512] for r in (r1_ref, r2_ref, r3_ref)], 1)
     tags = [r[512:528].astype(f32) for r in (r1_ref, r2_ref, r3_ref)]
@@ -362,17 +377,22 @@
             for s in range(8):
                 wk_ref[j, r, s] = rows[r][s] * kappa[r, s]
     behind, ahead = send_rims(lambda j: wk_ref[j].reshape(512, LANES), na)
-    behind_ref[...] = behind
-    ahead_ref[...] = ahead
+    for ref, z_rim, rim, inside in ((behind_ref, zb_ref, behind, par_ref[3]), (ahead_ref, za_ref, ahead, par_ref[4])):
+        ref[:, 0:640] = jnp.where(inside > 0, z_rim[...], 0.0)
+        ref[:, 640:1152] = jnp.where(inside > 0, rim, 0.0)
 
 
 def lines_t(k_ref, x):
-    x = x.reshape(2, 256, LANES)
-    x = jnp.concatenate([x[0], x[1]], 1)
-    high = x.astype(bf16)
-    low = (x - high.astype(f32)).astype(bf16)
-    y = jnp.dot(k_ref[...], jnp.concatenate([high, high, low], 0), preferred_element_type=f32)
-    return y[:, :LANES].reshape(4, 8, 8, LANES), y[:, LANES:].reshape(4, 8, 8, LANES)
+    x = x.reshape(4, 128, LANES)
+    out = []
+    for p in range(2):
+        pair = jnp.concatenate([x[2 * p], x[2 * p + 1]], 1)
+        high = pair.astype(bf16)
+        low = (pair - high.astype(f32)).astype(bf16)
+        y = jnp.dot(k_ref[...], jnp.concatenate([high, low], 0), preferred_element_type=f32)
+        y = y[:128] + y[128:]
+        out += [y[:, :LANES].reshape(2, 8, 8, LANES), y[:, LANES:].reshape(2, 8, 8, LANES)]
+    return out
 
 
 def squares(v, j, other, iw_ref):
@@ -398,97 +418,103 @@
             g[r, s] = value
 
 
-def apply_tile(v, j, wk, jk, c, wt, kf_ref, kb_ref, y, g):
+def apply_tile(v, j, wk, c, base, kf_ref, kb_ref, y, g, f):
+    for p, part in enumerate(lines_t(kf_ref, v[j])):
+        for q in range(2):
+            f[2 * p + q] = wk(2 * p + q) * part[q]
     gradient_r(v, j, g)
-    base = weight_rows(wt * (coolant_throughput * KRYLOV_SCALE))
-    for r in range(8):
-        second = along(DERIV, [v[j, r, s] for s in range(8)])
+    for r in range(8):
+        line = [v[j, r, s] for s in range(8)]
+        second = along(DERIV, line)
+        k = wk(r)
         flux = []
         for s in range(8):
             first = g[r, s]
-            k = wk[jk, r, s]
-            flux.append(k * (second[s] + c * first))
-            g[r, s] = k * (first + c * second[s])
+            flux.append(k[s] * (second[s] + c * first))
+            g[r, s] = k[s] * (first + c * second[s])
         for s, value in enumerate(along(DERIV.T, flux)):
-            y[j, r, s] = value + base[r][s] * v[j, r, s]
+            y[j, r, s] = value + (base[r] * float(GLL_W[s])) * line[s]
+    parts = lines_t(kb_ref, f[...])
     for s in range(8):
         for r, value in enumerate(along(DERIV.T, [g[r, s] for r in range(8)])):
             y[j, r, s] = y[j, r, s] + value
-    front, back = lines_t(kf_ref, v[j])
-    third = jnp.concatenate([wk[jk, 0:4] * front, wk[jk, 4:8] * back], 0)
-    front, back = lines_t(kb_ref, third)
-    y[j, 0:4] = y[j, 0:4] + front
-    y[j, 4:8] = y[j, 4:8] + back
+    for p, part in enumerate(parts):
+        y[j, 2 * p : 2 * p + 2] = y[j, 2 * p : 2 * p + 2] + part
+
+
+def mass_rows(wt, base):
+    for r in range(8):
+        base[r] = wt * float(GLL_W[r] * coolant_throughput * KRYLOV_SCALE)
 
 
 def step_kernel(na, first, *refs):
     refs = list(refs)
-    par_ref, y_in, a_in, b_in, wk_ref = refs[:5]
-    del refs[:5]
+    take = lambda n: [refs.pop(0) for _ in range(n)]
+    ghost = 2 * na
     if first:
-        from_ahead, from_behind = refs[:2]
-        del refs[:2]
+        par_ref, z_in, wk_ref, from_ahead, from_behind, dc_ref = take(6)
         prev = None
     else:
-        wkg_ref, prev = refs[:2]
-        del refs[:2]
-    cr_ref, wt_ref, iw_ref, kf_ref, kb_ref, v, y, a_out, b_out, dots = refs[:10]
-    del refs[:10]
+        par_ref, y_in, a_in, b_in, wk_ref, wkg_ref, cr_ref, prev = take(8)
+    wt_ref, iw_ref, kf_ref, kb_ref, v, y, a_out, b_out, dots = take(9)
     if first:
-        wkg_ref = refs.pop(0)
-    g, lo, hi = refs
-    ghost = 2 * na
-    parity = par_ref[0]
+        wkg_ref, cr_ref = take(2)
+    g, f, base = refs
     if first:
-        wkg_ref[0] = place_rims(from_ahead[...], from_behind[...]).reshape(8, 8, 8, LANES)
-    v[...] = y_in[...]
-    add_faces(na, parity, v, a_in, b_in)
-    wt = wt_ref[...]
-    dots[...] = jnp.zeros_like(dots)
-
-    def own(j, carry):
-        for k, value in enumerate(squares(v, j, prev, iw_ref)):
-            dots[k] += value
-        apply_tile(v, j, wk_ref, j, cr_ref[j], wt, kf_ref, kb_ref, y, g)
-        return carry
-
-    lax.fori_loop(0, ghost, own, 0)
-    apply_tile(v, ghost, wkg_ref, 0, cr_ref[ghost], wt, kf_ref, kb_ref, y, g)
-    assemble(na, y, lo, hi)
-    faces_out(parity, lo, hi, a_out, b_out)
-
-
-def last_kernel(na, par_ref, y_in, a_in, b_in, wk_ref, prev, cr_ref, wt_ref, iw_ref, kf_ref, d0, d1, d2, d3, v, all_dots, dots, g):
+        v[0:ghost] = z_in[...]
+        rims = place_rims(from_ahead[...], from_behind[...])
+        v[ghost] = rims[0:512].reshape(8, 8, 8, LANES)
+        wkg_ref[...] = rims[640:1152].reshape(8, 8, 8, LANES)
+        for j in range(ghost):
+            cr_ref[j] = jnp.broadcast_to(dc_ref[1:2, j * LANES : (j + 1) * LANES], (8, LANES))
+        cr_ref[ghost] = rims[512:520]
+        assemble_axial(na, v)
+    else:
+        v[...] = y_in[...]
+        add_faces(na, par_ref, v, a_in, b_in)
+    mass_rows(wt_ref[...], base)
+    totals = None
+    for j in range(ghost + 1):
+        if j < ghost:
+            sums = squares(v, j, prev, iw_ref)
+            totals = sums if totals is None else [a + b for a, b in zip(totals, sums)]
+            wk = lambda r: wk_ref[j, r]
+        else:
+            wk = lambda r: wkg_ref[r]
+        apply_tile(v, j, wk, cr_ref[j], base, kf_ref, kb_ref, y, g.at[j % 2], f.at[j % 2])
+    for k, value in enumerate(totals):
+        dots[k] = value
+    assemble_axial(na, y)
+    assemble_lateral(na, par_ref, y, a_out, b_out)
+
+
+def last_kernel(na, par_ref, y_in, a_in, b_in, wk_ref, cr_ref, prev, wt_ref, iw_ref, kf_ref, d0, d1, d2, d3, v, all_dots, g, base):
     ghost = 2 * na
     v[...] = y_in[...]
-    add_faces(na, par_ref[0], v, a_in, b_in)
-    wt = wt_ref[...]
-    dots[...] = jnp.zeros_like(dots)
-
-    def own(j, carry):
-        for k, value in enumerate(squares(v, j, prev, iw_ref)):
-            dots[k] += value
-        gradient_r(v, j, g)
+    add_faces(na, par_ref, v, a_in, b_in)
+    mass_rows(wt_ref[...], base)
+    totals = None
+    for j in range(ghost):
+        gj = g.at[j % 2]
+        third = lines_t(kf_ref, v[j])
+        sums = list(squares(v, j, prev, iw_ref))
+        gradient_r(v, j, gj)
         c = 2.0 * cr_ref[j]
-        base = weight_rows(wt * (coolant_throughput * KRYLOV_SCALE))
-        front, back = lines_t(kf_ref, v[j])
         total = None
         for r in range(8):
-            second = along(DERIV, [v[j, r, s] for s in range(8)])
-            line = None
+            line = [v[j, r, s] for s in range(8)]
+            second = along(DERIV, line)
+            row = None
             for s in range(8):
-                one, two = g[r, s], second[s]
-                three = front[r, s] if r < 4 else back[r - 4, s]
-                x = v[j, r, s]
-                term = base[r][s] * x * x + wk_ref[j, r, s] * (one * (one + c * two) + two * two + three * three)
-                line = term if line is None else line + term
-            total = line if total is None else total + line
-        dots[2] += total
-        return carry
-
-    lax.fori_loop(0, ghost, own, 0)
+                one, two, three = gj[r, s], second[s], third[r // 2][r % 2, s]
+                term = (base[r] * float(GLL_W[s])) * (line[s] * line[s])
+                term = term + wk_ref[j, r, s] * (one * (one + c * two) + two * two + three * three)
+                row = term if row is None else row + term
+            total = row if total is None else total + row
+        sums.append(total)
+        totals = sums if totals is None else [a + b for a, b in zip(totals, sums)]
     lane = lane_index(1)
-    rows = [d0[0], d1[1], d1[0], d2[1], d2[0], d3[1], d3[0], dots[1], dots[0], dots[2]]
+    rows = [d0[0], d1[1], d1[0], d2[1], d2[0], d3[1], d3[0], totals[1], totals[0], totals[2]]
     out = jnp.zeros((1, LANES), f32)
     for k, row in enumerate(rows):
         out = jnp.where(lane == k, jnp.sum(jnp.sum(row, 0, keepdims=True), 1, keepdims=True), out)
@@ -536,14 +562,14 @@
                     out_ref[pl.ds(base + at * 2 + l, 8, stride=step), :] = x
 
 
-def shift(x, axis, by):
+def ring(x, axis, by):
     n = lax.axis_size(axis)
-    return lax.ppermute(x, axis, [(i, i + by) for i in range(n) if 0 <= i + by < n])
+    return lax.ppermute(x, axis, [(i, (i + by) % n) for i in range(n)])
 
 
 def swap(x, axis, start):
     n = lax.axis_size(axis)
-    pairs = [(i, i + 1) for i in range(start, n - 1, 2)]
+    pairs = [((start + i) % n, (start + i + 1) % n) for i in range(0, n, 2)]
     return lax.ppermute(x, axis, pairs + [(j, i) for i, j in pairs])
 
 
@@ -581,12 +607,20 @@
     tiles = count_l * na
     chan = lax.axis_size("chan")
     total = lax.axis_size("slab") * chan
-    me = (lax.axis_index("slab") * chan + lax.axis_index("chan")).astype(jnp.int32).reshape(1)
-    parity = (lax.axis_index("chan") % 2).astype(jnp.int32).reshape(1)
+    slab_at, chan_at = lax.axis_index("slab"), lax.axis_index("chan")
+    me = (slab_at * chan + chan_at).astype(jnp.int32).reshape(1)
+    position = [
+        chan_at % 2,
+        chan_at > 0,
+        chan_at < chan - 1,
+        slab_at > 0,
+        slab_at < lax.axis_size("slab") - 1,
+    ]
+    position = jnp.stack([jnp.asarray(x, jnp.int32) for x in position])
 
     wt = jnp.asarray(np.broadcast_to(GLL_W[:, None], (8, LANES)), f32)
     kf, kb = (jnp.asarray(k) for k in line_matrices())
-    k1, kl, k2, k3 = (jnp.asarray(k) for k in fluid_matrices())
+    kfluid = jnp.asarray(fluid_matrix())
 
     layers = coking_thickness_plies.astype(f32)
     flags = coked_element_flags.astype(f32)
@@ -603,19 +637,9 @@
     whole = (tiles + 1, 8, 8, 8, LANES)
     face = (na + 1, 8, 8, LANES)
     shape = lambda s, d=f32: jax.ShapeDtypeStruct(s, d)
-    z, behind, ahead = call(
-        functools.partial(source_kernel, na),
-        [shape(field), shape((2 * RIM, 640)), shape((2 * RIM, 640))],
-        as_rows(previous_panel_warmth),
-        as_rows(pointwise_energy_source),
-        dc,
-        wt,
-    )
-    from_ahead = shift(behind, "slab", -1)
-    from_behind = shift(ahead, "slab", 1)
-
-    split = 4
-    width = elements // split
+    kept = vmem
+    split = elements // LANES
+    width = LANES
     room = elements // 4
     out = pl.pallas_call(
         functools.partial(fluid_kernel, chan, total),
@@ -624,89 +648,96 @@
             pl.BlockSpec(memory_space=pltpu.SMEM),
             pl.BlockSpec((3, 8, 8, 8, width), lambda i: (0, 0, 0, 0, i)),
         ]
-        + [pl.BlockSpec(memory_space=pltpu.VMEM)] * 5,
+        + [pl.BlockSpec(memory_space=pltpu.VMEM)] * 2,
         out_specs=[pl.BlockSpec((3, 8, 8, 8, width), lambda i: (0, 0, 0, 0, i))]
         + [pl.BlockSpec(memory_space=pltpu.VMEM)] * 4,
         out_shape=[shape(stream_speed_field.shape, bf16), shape((512, elements), bf16)]
         + [shape((528, room), bf16)] * 3,
-        scratch_shapes=[pltpu.VMEM((split, 512, width), bf16)],
+        scratch_shapes=[pltpu.VMEM((split, 512, width), bf16), pltpu.VMEM((3, 8, 8, 8, width), f32)],
         compiler_params=pltpu.CompilerParams(vmem_limit_bytes=48 * 1024 * 1024),
-    )(me, stream_speed_field, liquid_to_solid_element.reshape(1, elements), k1, kl, k2, k3)
+    )(me, stream_speed_field, liquid_to_solid_element.reshape(1, elements), kfluid)
     stepped, own, *outgoing = out
-
-    scratch_faces = [pltpu.VMEM(face, f32)] * 2
-    y, cr, a, b = call(
-        functools.partial(source_assembly_kernel, na),
-        [shape(whole), shape((tiles + 1, 8, LANES)), shape(face), shape(face)],
-        parity,
+    received = [around(x, by) for x, by in zip(outgoing, (1, -1, chan))]
+
+    warmth, source, own = lax.optimization_barrier((previous_panel_warmth, pointwise_energy_source, own))
+    z, a, b = call(
+        functools.partial(source_kernel, na),
+        [kept(field), shape((na, 8, 8, LANES)), shape((na, 8, 8, LANES))],
+        position,
+        as_rows(warmth),
+        as_rows(source),
+        wt,
+        smem=1,
+    )
+    a, b = swap(a, "chan", 0), swap(b, "chan", 1)
+    z, z_behind, z_ahead = call(
+        functools.partial(rim_kernel, na),
+        [kept(field), kept((2 * RIM, 640)), kept((2 * RIM, 640))],
+        position,
         z,
-        from_ahead,
-        from_behind,
+        a,
+        b,
         dc,
         smem=1,
-        scratch=scratch_faces,
-    )
-    received = [around(x, by) for x, by in zip(outgoing, (1, -1, chan))]
-    a, b = swap(a, "chan", 0), swap(b, "chan", 1)
-
+    )
     wk, behind, ahead = call(
         functools.partial(unpack_kernel, na),
-        [shape(field), shape((2 * RIM, 512)), shape((2 * RIM, 512))],
+        [kept(field), shape((2 * RIM, 1152)), shape((2 * RIM, 1152))],
+        position,
         own,
         *received,
         dc,
         wt,
-    )
-    wk_ahead = shift(behind, "slab", -1)
-    wk_behind = shift(ahead, "slab", 1)
+        z_behind,
+        z_ahead,
+        smem=1,
+    )
+    from_ahead = ring(behind, "slab", -1)
+    from_behind = ring(ahead, "slab", 1)
 
     basis, products = [], []
-    wkg = None
     for number in range(ITERS - 1):
         first = number == 0
-        extra = (wk_ahead, wk_behind) if first else (wkg, basis[-1])
-        outs = [shape(whole), shape(whole), shape(face), shape(face), shape((2, 8, LANES))]
+        outs = [kept(whole), kept(whole), shape(face), shape(face), kept((2, 8, LANES))]
         if first:
-            outs.append(shape((1, 8, 8, 8, LANES)))
+            args = (z, wk, from_ahead, from_behind, dc)
+            outs += [kept((8, 8, 8, LANES)), kept((tiles + 1, 8, LANES))]
+        else:
+            args = (y, a, b, wk, wkg, cr, basis[-1])
         got = call(
             functools.partial(step_kernel, na, first),
             outs,
-            parity,
-            y,
-            a,
-            b,
-            wk,
-            *extra,
-            cr,
+            position,
+            *args,
             wt,
             iw,
             kf,
             kb,
             smem=1,
-            scratch=[pltpu.VMEM((8, 8, 8, LANES), f32)] + scratch_faces,
+            scratch=[pltpu.VMEM((2, 8, 8, 8, LANES), f32)] * 2 + [pltpu.VMEM((8, 8, LANES), f32)],
         )
         if first:
-            wkg = got[5]
+            wkg, cr = got[5:]
         v, y, a, b, dots = got[:5]
         basis.append(v)
         products.append(dots)
         a, b = swap(a, "chan", 0), swap(b, "chan", 1)
     v, sums = call(
         functools.partial(last_kernel, na),
-        [shape(whole), shape((total, 1, LANES))],
-        parity,
+        [kept(whole), shape((total, 1, LANES))],
+        position,
         y,
         a,
         b,
         wk,
+        cr,
         basis[-1],
-        cr,
         wt,
         iw,
         kf,
         *products,
         smem=1,
-        scratch=[pltpu.VMEM((3, 8, LANES), f32), pltpu.VMEM((8, 8, 8, LANES), f32)],
+        scratch=[pltpu.VMEM((2, 8, 8, 8, LANES), f32), pltpu.VMEM((8, 8, LANES), f32)],
     )
     basis.append(v)
     sums = lax.all_to_all(sums, ("slab", "chan"), 0, 0)

time: 128 us -> 97.7 us (0.76)
  starting transfers between devices: 36.8 us -> 15.1 us
  waiting for transfers between devices: 7.33 us -> 26 us
  Pallas kernels: 49.6 us -> 37.4 us
  blocking collectives: 16.3 us -> 8.83 us
  local copies, waits for them, and re-layouts: 15.5 us -> 8.93 us
    ppermute x10, waiting for transfers between devices: 1.32 us -> 19 us  [swap(): return lax.ppermute(x, axis, pairs + [(j, i) for i, j in pairs])]
    ppermute x10, starting transfers between devices: 18.6 us -> 3.92 us  [swap(): return lax.ppermute(x, axis, pairs + [(j, i) for i, j in pairs])]
    ppermute x4 -> x2, starting transfers between devices: 12.6 us -> 4.75 us  [ring(): return lax.ppermute(x, axis, [(i, (i + by) % n) for i in range(n)])]
    all_to_all x1, blocking collectives: 16.3 us -> 8.83 us  [on_device(): sums = lax.all_to_all(sums, ('slab', 'chan'), 0, 0)]
    unnamed x48 -> x36, local copies, waits for them, and re-layouts: 15.3 us -> 8.61 us
    pallas_call x1, Pallas kernels: 13 us -> 6.87 us  [on_device(): pl.pallas_call(functools.partial(fluid_kernel, chan, total), grid=(split,...]
    pallas_call x9, Pallas kernels: 36.6 us -> 30.5 us  [call(): pl.pallas_call(kernel, in_specs=specs, out_specs=outs, out_shape=out_shap...]
    ppermute x4 -> x2, waiting for transfers between devices: 1.47 us -> 6.97 us  [ring(): return lax.ppermute(x, axis, [(i, (i + by) % n) for i in range(n)])]
  transfers between devices with their start and end apart: 17 -> 15, of which waited for: 6 -> 12; matrix products, arithmetic and copies ran while one was open for 0% -> 1% of each run, Pallas kernels for 12% -> 3%
where the time goes in v2:
time: 97.7 us; the launch traced here: 97.3 us
  Pallas kernels  37.4 us (38%)
  waiting for transfers between devices  26 us (27%)
  starting transfers between devices  15.1 us (15%)
  local copies, waits for them, and re-layouts  8.93 us (9%)
  blocking collectives  8.83 us (9%)
    pallas_call x9, Pallas kernels, call(): pl.pallas_call(kernel, in_specs=specs, out_specs=outs, out_shape=out_shap...  30.5 us
    ppermute x10, waiting for transfers between devices, swap(): return lax.ppermute(x, axis, pairs + [(j, i) for i, j in pairs])  19 us
    all_to_all x1, blocking collectives, on_device(): sums = lax.all_to_all(sums, ('slab', 'chan'), 0, 0)  8.83 us
    unnamed x36, local copies, waits for them, and re-layouts  8.61 us
    ppermute x2, waiting for transfers between devices, ring(): return lax.ppermute(x, axis, [(i, (i + by) % n) for i in range(n)])  6.97 us
    pallas_call x1, Pallas kernels, on_device(): pl.pallas_call(functools.partial(fluid_kernel, chan, total), grid=(split,...  6.87 us
    ppermute x3, starting transfers between devices, around(): lax.ppermute(x, ('slab', 'chan'), [(i, (i + by) % n) for i in range(n)])  6.43 us
    ppermute x2, starting transfers between devices, ring(): return lax.ppermute(x, axis, [(i, (i + by) % n) for i in range(n)])  4.75 us
  transfers between devices with their start and end apart: 15, of which 12 were waited for; matrix products, arithmetic and copies ran while one was open for 1% of the time, Pallas kernels for 3%

profile of v2, /device:TPU:0, one launch (start us, length us, event | category | flops | bytes accessed | tf_op | source)
XLA Modules:
  0.0 97.3 jit_solution(8107048967466178935)
XLA Ops:
  0.6 0.0 copy-start.12
  0.7 1.4 %copy-done.8 = bf16[3,8,8,8,512]{4,3,2,1,0:T(8,128)(2,1)S(1)} copy-done((bf16[3,8,8,8,512]{4,3,2,1,0:T(8,128)(2,1)S(1)}, bf16[3,8,8,8,512]{4,3,2,1,0:T(8,128)(2,1)}, u32[]{:S(2)}) %copy-start.8) | copy-done | bytes 1572888
  2.1 0.9 copy-done.13
  3.0 0.7 copy-done.14
  3.7 6.9 %shard_map.113 = (bf16[3,8,8,8,512]{4,3,2,1,0:T(8,128)(2,1)}, bf16[512,512]{1,0:T(8,128)(2,1)S(1)}, bf16[528,128]{1,0:T(8,128)(2,1)S(1)}, bf16[528,128]{1,0:T(8,128)(2,1)S(1)}, bf16[528,128]{1,0:T(8,128)(2,1)S(1)}) custom-call(s32[1]{0:T(128)} %bitcast.me_ref, bf16[3,8,8,8,512]{4,3,2,1,0:T(8,128)(2,1)S(1)} %copy-done.8, s32[1,512]{1,0:T(1,128)S(1)} %bitcast.36, ...), custom_call_target="tpu_custom_call" | custom-call | tf_op jit(solution)/shard_map/pallas_call | solution.py:644
  10.6 0.5 collective-permute-start.2
  11.0 6.0 %collective-permute-start.3 = (bf16[528,128]{1,0:T(8,128)(2,1)S(1)}, bf16[528,128]{1,0:T(8,128)(2,1)S(1)}, u32[]{:S(2)}, u32[]{:S(2)}) collective-permute-start(bf16[528,128]{1,0:T(8,128)(2,1)S(1)} %get-tuple-element.53), channel_id=1, source_target_pairs={{0,31},{1,0},{2,1},{3,2},{4,3},{5,4},{6,5},{7,6},{8,7},{9,8},{10,9... | collective-permute-start | bytes 405512 | tf_op jit(solution)/shard_map/ppermute | solution.py:578
  17.0 0.1 stack.52.par_ref.refs_0_
  17.1 1.2 %copy-done.11 = f32[8,8,8,2,256]{4,3,2,1,0:T(2,128)S(1)} copy-done((f32[8,8,8,2,256]{4,3,2,1,0:T(2,128)S(1)}, f32[8,8,8,2,256]{4,3,2,1,0:T(2,128)}, u32[]{:S(2)}) %copy-start.11) | copy-done | bytes 1048600
  18.3 1.4 %shard_map.114 = (f32[4,8,8,8,128]{4,3,2,1,0:T(8,128)S(1)}, f32[2,8,8,128]{3,2,1,0:T(8,128)}, f32[2,8,8,128]{3,2,1,0:T(8,128)S(1)}) custom-call(s32[5]{0:T(128)S(1)} %stack.52.par_ref.refs_0_, f32[2048,128]{1,0:T(8,128)S(1)} %bitcast.34, f32[2048,128]{1,0:T(8,128)S(1)} %bitcast.35, f32[8,128]{1,0:T(8,128)S(1)} %copy-done.12), custom_call_target="tpu_custom_call" | custom-call | tf_op jit(solution)/shard_map/pallas_call | solution.py:128
  19.8 0.1 pad_maximum_fusion.2
  19.9 0.1 mul.55
  20.0 0.1 copy.17
  20.1 1.0 %collective-permute-done.a_ref = f32[2,8,8,128]{3,2,1,0:T(8,128)S(1)} collective-permute-done((f32[2,8,8,128]{3,2,1,0:T(8,128)}, f32[2,8,8,128]{3,2,1,0:T(8,128)S(1)}, u32[]{:S(2)}, u32[]{:S(2)}) %collective-permute-start) | collective-permute-done | bytes 65568 | tf_op jit(solution)/shard_map/ppermute | solution.py:573
  21.1 2.3 %collective-permute-done.1.b_ref = f32[2,8,8,128]{3,2,1,0:T(8,128)S(1)} collective-permute-done((f32[2,8,8,128]{3,2,1,0:T(8,128)S(1)}, f32[2,8,8,128]{3,2,1,0:T(8,128)S(1)}, u32[]{:S(2)}, u32[]{:S(2)}) %collective-permute-start.1) | collective-permute-done | bytes 65568 | tf_op jit(solution)/shard_map/ppermute | solution.py:573
  23.4 1.9 %shard_map.115 = (f32[4,8,8,8,128]{4,3,2,1,0:T(8,128)S(1)}, f32[16,640]{1,0:T(8,128)S(1)}, f32[16,640]{1,0:T(8,128)S(1)}) custom-call(s32[5]{0:T(128)S(1)} %stack.52.par_ref.refs_0_, f32[4,8,8,8,128]{4,3,2,1,0:T(8,128)S(1)} %get-tuple-element.47.z_in, f32[2,8,8,128]{3,2,1,0:T(8,128)S(1)} %collective-permute-done.a_ref, ...), custom_call_target="tpu_custom_call" | custom-call | tf_op jit(solution)/shard_map/pallas_call | solution.py:128
  25.3 0.0 collective-permute-done.3.r2_ref
  25.3 2.0 %shard_map.116 = (f32[4,8,8,8,128]{4,3,2,1,0:T(8,128)S(1)}, f32[16,1152]{1,0:T(8,128)S(1)}, f32[16,1152]{1,0:T(8,128)S(1)}) custom-call(s32[5]{0:T(128)S(1)} %stack.52.par_ref.refs_0_, bf16[512,512]{1,0:T(8,128)(2,1)S(1)} %get-tuple-element.51.own_ref, bf16[528,128]{1,0:T(8,128)(2,1)S(1)} %collective-permute-done.2.r1_ref, ...), custom_call_target="tpu_custom_call" | custom-call | tf_op jit(solution)/shard_map/pallas_call | solution.py:128
  27.3 4.8 %collective-permute-start.5 = (f32[16,1152]{1,0:T(8,128)S(1)}, f32[16,1152]{1,0:T(8,128)S(1)}, u32[]{:S(2)}, u32[]{:S(2)}) collective-permute-start(f32[16,1152]{1,0:T(8,128)S(1)} %get-tuple-element.58), channel_id=1, source_target_pairs={{0,28},{4,0},{8,4},{12,8},{16,12},{20,16},{24,20},{28,24},{1,29},{... | collective-permute-start | bytes 221192 | tf_op jit(solution)/shard_map/ppermute | solution.py:567
  32.1 0.1 multiply_bitcast_fusion
  32.2 2.1 %collective-permute-done.5.refs_3_ = f32[16,1152]{1,0:T(8,128)S(1)} collective-permute-done((f32[16,1152]{1,0:T(8,128)S(1)}, f32[16,1152]{1,0:T(8,128)S(1)}, u32[]{:S(2)}, u32[]{:S(2)}) %collective-permute-start.5) | collective-permute-done | bytes 73760 | tf_op jit(solution)/shard_map/ppermute | solution.py:567
  34.2 4.9 %collective-permute-done.6.refs_4_ = f32[16,1152]{1,0:T(8,128)S(1)} collective-permute-done((f32[16,1152]{1,0:T(8,128)S(1)}, f32[16,1152]{1,0:T(8,128)S(1)}, u32[]{:S(2)}, u32[]{:S(2)}) %collective-permute-start.6) | collective-permute-done | bytes 73760 | tf_op jit(solution)/shard_map/ppermute | solution.py:567
  39.2 5.5 %shard_map.117 = (f32[5,8,8,8,128]{4,3,2,1,0:T(8,128)S(1)}, f32[5,8,8,8,128]{4,3,2,1,0:T(8,128)S(1)}, f32[3,8,8,128]{3,2,1,0:T(8,128)S(1)}, f32[3,8,8,128]{3,2,1...) custom-call(s32[5]{0:T(128)S(1)} %stack.52.par_ref.refs_0_, ...), custom_call_target="tpu_custom_call" | custom-call | tf_op jit(solution)/shard_map/pallas_call | solution.py:128
  44.6 1.1 %copy-done = f32[5,8,8,8,128]{4,3,2,1,0:T(8,128)} copy-done((f32[5,8,8,8,128]{4,3,2,1,0:T(8,128)}, f32[5,8,8,8,128]{4,3,2,1,0:T(8,128)S(1)}, u32[]{:S(2)}) %copy-start) | copy-done | bytes 1310744
  45.7 1.0 collective-permute-start.8
  46.7 0.3 collective-permute-done.7.refs_2_
  47.0 3.1 %collective-permute-done.8.refs_3_ = f32[3,8,8,128]{3,2,1,0:T(8,128)S(1)} collective-permute-done((f32[3,8,8,128]{3,2,1,0:T(8,128)S(1)}, f32[3,8,8,128]{3,2,1,0:T(8,128)S(1)}, u32[]{:S(2)}, u32[]{:S(2)}) %collective-permute-start.8) | collective-permute-done | bytes 98336 | tf_op jit(solution)/shard_map/ppermute | solution.py:573
  50.2 4.8 %shard_map.118 = (f32[5,8,8,8,128]{4,3,2,1,0:T(8,128)S(1)}, f32[5,8,8,8,128]{4,3,2,1,0:T(8,128)S(1)}, f32[3,8,8,128]{3,2,1,0:T(8,128)S(1)}, f32[3,8,8,128]{3,2,1,0:T(8,128)S(1)}, f32[2,8,128]{2,1,0:T(8,128)S(1)}) custom-call(s32[5]{0:T(128)S(1)} %stack.52.par_ref.refs_0_, f32[5,8,8,8,128]{4,3,2,1,0:T(8,128)S(1)} %get-tuple-element.60.refs_1_, ...), custom_call_target="tpu_custom_call" | custom-call | tf_op jit(solution)/shard_map/pallas_call | solution.py:128
  55.0 1.1 %copy-done.2 = f32[5,8,8,8,128]{4,3,2,1,0:T(8,128)} copy-done((f32[5,8,8,8,128]{4,3,2,1,0:T(8,128)}, f32[5,8,8,8,128]{4,3,2,1,0:T(8,128)S(1)}, u32[]{:S(2)}) %copy-start.2) | copy-done | bytes 1310744
  56.0 0.5 collective-permute-start.9
  56.5 0.5 collective-permute-start.10
  57.0 0.5 collective-permute-done.9.refs_2_
  57.5 3.9 %collective-permute-done.10.refs_3_ = f32[3,8,8,128]{3,2,1,0:T(8,128)S(1)} collective-permute-done((f32[3,8,8,128]{3,2,1,0:T(8,128)S(1)}, f32[3,8,8,128]{3,2,1,0:T(8,128)S(1)}, u32[]{:S(2)}, u32[]{:S(2)}) %collective-permute-start.10) | collective-permute-done | bytes 98336 | tf_op jit(solution)/shard_map/ppermute | solution.py:573
  61.4 4.8 %shard_map.119 = (f32[5,8,8,8,128]{4,3,2,1,0:T(8,128)S(1)}, f32[5,8,8,8,128]{4,3,2,1,0:T(8,128)S(1)}, f32[3,8,8,128]{3,2,1,0:T(8,128)S(1)}, f32[3,8,8,128]{3,2,1,0:T(8,128)S(1)}, f32[2,8,128]{2,1,0:T(8,128)S(1)}) custom-call(s32[5]{0:T(128)S(1)} %stack.52.par_ref.refs_0_, f32[5,8,8,8,128]{4,3,2,1,0:T(8,128)S(1)} %get-tuple-element.66.refs_1_, ...), custom_call_target="tpu_custom_call" | custom-call | tf_op jit(solution)/shard_map/pallas_call | solution.py:128
  66.2 1.1 %copy-done.4 = f32[5,8,8,8,128]{4,3,2,1,0:T(8,128)} copy-done((f32[5,8,8,8,128]{4,3,2,1,0:T(8,128)}, f32[5,8,8,8,128]{4,3,2,1,0:T(8,128)S(1)}, u32[]{:S(2)}) %copy-start.4) | copy-done | bytes 1310744
  67.2 0.1 collective-permute-start.11
  67.4 0.9 collective-permute-start.12
  68.2 0.3 collective-permute-done.11.refs_2_
  68.5 3.4 %collective-permute-done.12.refs_3_ = f32[3,8,8,128]{3,2,1,0:T(8,128)S(1)} collective-permute-done((f32[3,8,8,128]{3,2,1,0:T(8,128)S(1)}, f32[3,8,8,128]{3,2,1,0:T(8,128)S(1)}, u32[]{:S(2)}, u32[]{:S(2)}) %collective-permute-start.12) | collective-permute-done | bytes 98336 | tf_op jit(solution)/shard_map/ppermute | solution.py:573
  71.9 5.0 %shard_map.120 = (f32[5,8,8,8,128]{4,3,2,1,0:T(8,128)S(1)}, f32[5,8,8,8,128]{4,3,2,1,0:T(8,128)S(1)}, f32[3,8,8,128]{3,2,1,0:T(8,128)S(1)}, f32[3,8,8,128]{3,2,1,0:T(8,128)S(1)}, f32[2,8,128]{2,1,0:T(8,128)S(1)}) custom-call(s32[5]{0:T(128)S(1)} %stack.52.par_ref.refs_0_, f32[5,8,8,8,128]{4,3,2,1,0:T(8,128)S(1)} %get-tuple-element.70.refs_1_, ...), custom_call_target="tpu_custom_call" | custom-call | tf_op jit(solution)/shard_map/pallas_call | solution.py:128
  76.9 0.4 collective-permute-start.13
  77.3 0.6 collective-permute-start.14
  77.9 0.4 collective-permute-done.13.a_in
  78.3 3.8 %collective-permute-done.14.b_in = f32[3,8,8,128]{3,2,1,0:T(8,128)S(1)} collective-permute-done((f32[3,8,8,128]{3,2,1,0:T(8,128)S(1)}, f32[3,8,8,128]{3,2,1,0:T(8,128)S(1)}, u32[]{:S(2)}, u32[]{:S(2)}) %collective-permute-start.14) | collective-permute-done | bytes 98336 | tf_op jit(solution)/shard_map/ppermute | solution.py:573
  82.1 2.3 %shard_map.121 = (f32[5,8,8,8,128]{4,3,2,1,0:T(8,128)S(1)}, f32[32,1,128]{2,1,0:T(1,128)S(1)}) custom-call(s32[5]{0:T(128)S(1)} %stack.52.par_ref.refs_0_, f32[5,8,8,8,128]{4,3,2,1,0:T(8,128)S(1)} %get-tuple-element.74.y_in, f32[3,8,8,128]{3,2,1,0:T(8,128)S(1)} %collective-permute-done.13.a_in, f32[3,8,8,128]{3,2,1,0:T(8,128)S(1)} %collective-permute-done.14.b_in, ...), custom_call_target="tpu_custom_call" | custom-call | tf_op jit(solution)/shard_map/pallas_call | solution.py:128
  84.4 1.1 %copy-done.9 = f32[5,8,8,8,128]{4,3,2,1,0:T(8,128)} copy-done((f32[5,8,8,8,128]{4,3,2,1,0:T(8,128)}, f32[5,8,8,8,128]{4,3,2,1,0:T(8,128)S(1)}, u32[]{:S(2)}) %copy-start.9) | copy-done | bytes 1310744
  85.5 8.8 %all_to_all.5.m_ref = f32[32,1,128]{2,1,0:T(1,128)S(1)} all-to-all(f32[32,1,128]{2,1,0:T(1,128)S(1)} %get-tuple-element.82), channel_id=1, replica_groups=mesh['slab'=8,'chan'=4] {'slab','chan'}, dimensions={0} | all-to-all | bytes 32768 | tf_op jit(solution)/shard_map/all_to_all | solution.py:743
  94.4 2.9 %shard_map.122 = f32[2048,128]{1,0:T(8,128)} custom-call(f32[32,1,128]{2,1,0:T(1,128)S(1)} %all_to_all.5.m_ref, f32[5,8,8,8,128]{4,3,2,1,0:T(8,128)S(1)} %copy-done.1, f32[5,8,8,8,128]{4,3,2,1,0:T(8,128)S(1)} %copy-done.3, f32[5,8,8,8,128]{4,3,2,1,0:T(8,128)S(1)} %copy-done.5, f32[5,8,8,8,128]{4,3,2,1,0:T(8,128)S(1)} %get-tuple-element.77.prev.v3, ...), custom_call_target="tpu_custom_call" | custom-call | tf_op jit(solution)/shard_map/pallas_call | solution.py:128
  (46 shorter events, 0.2 us)
Async XLA Ops:
  0.6 16.4 %copy-start.12 = (f32[8,128]{1,0:T(8,128)S(1)}, f32[8,128]{1,0:T(8,128)}, u32[]{:S(2)}) copy-start(f32[8,128]{1,0:T(8,128)} %constant.56.clone.wt_ref.refs_6_.refs_8_) | copy-start | bytes 12292
  0.7 1.4 %copy-start.8 = (bf16[3,8,8,8,512]{4,3,2,1,0:T(8,128)(2,1)S(1)}, bf16[3,8,8,8,512]{4,3,2,1,0:T(8,128)(2,1)}, u32[]{:S(2)}) copy-start(bf16[3,8,8,8,512]{4,3,2,1,0:T(8,128)(2,1)} %u_ref.1) | copy-start | bytes 4718596
  2.1 0.9 copy-start.13
  3.0 0.7 copy-start.14
  3.7 13.4 %copy-start.10 = (f32[8,8,8,2,256]{4,3,2,1,0:T(2,128)S(1)}, f32[8,8,8,2,256]{4,3,2,1,0:T(2,128)}, u32[]{:S(2)}) copy-start(f32[8,8,8,2,256]{4,3,2,1,0:T(2,128)} %param.12) | copy-start | bytes 3145732
  10.5 9.1 %copy-start.15 = (s32[2,256]{1,0:T(2,128)S(1)}, s32[2,256]{1,0:T(2,128)}, u32[]{:S(2)}) copy-start(s32[2,256]{1,0:T(2,128)} %param.15) | copy-start | bytes 6148
  10.6 9.2 %copy-start.16 = (s32[2,256]{1,0:T(2,128)S(1)}, s32[2,256]{1,0:T(2,128)}, u32[]{:S(2)}) copy-start(s32[2,256]{1,0:T(2,128)} %param.14) | copy-start | bytes 6148
  10.6 14.7 %collective-permute-start.2 = (bf16[528,128]{1,0:T(8,128)(2,1)S(1)}, bf16[528,128]{1,0:T(8,128)(2,1)S(1)}, u32[]{:S(2)}, u32[]{:S(2)}) collective-permute-start(bf16[528,128]{1,0:T(8,128)(2,1)S(1)} %get-tuple-element.52), channel_id=1, source_target_pairs={{0,1},{1,2},{2,3},{3,4},{4,5},{5,6},{6,7},{7,8},{8,9},{9,10},{10,1... | collective-permute-start | bytes 405512 | tf_op jit(solution)/shard_map/ppermute | solution.py:578
  11.0 14.3 %collective-permute-start.3 = (bf16[528,128]{1,0:T(8,128)(2,1)S(1)}, bf16[528,128]{1,0:T(8,128)(2,1)S(1)}, u32[]{:S(2)}, u32[]{:S(2)}) collective-permute-start(bf16[528,128]{1,0:T(8,128)(2,1)S(1)} %get-tuple-element.53), channel_id=1, source_target_pairs={{0,31},{1,0},{2,1},{3,2},{4,3},{5,4},{6,5},{7,6},{8,7},{9,8},{10,9... | collective-permute-start | bytes 405512 | tf_op jit(solution)/shard_map/ppermute | solution.py:578
  17.0 8.3 %collective-permute-start.4 = (bf16[528,128]{1,0:T(8,128)(2,1)S(1)}, bf16[528,128]{1,0:T(8,128)(2,1)S(1)}, u32[]{:S(2)}, u32[]{:S(2)}) collective-permute-start(bf16[528,128]{1,0:T(8,128)(2,1)S(1)} %get-tuple-element.54), channel_id=1, source_target_pairs={{0,4},{1,5},{2,6},{3,7},{4,8},{5,9},{6,10},{7,11},{8,12},{9,13},{1... | collective-permute-start | bytes 405512 | tf_op jit(solution)/shard_map/ppermute | solution.py:578
  17.1 1.2 %copy-start.11 = (f32[8,8,8,2,256]{4,3,2,1,0:T(2,128)S(1)}, f32[8,8,8,2,256]{4,3,2,1,0:T(2,128)}, u32[]{:S(2)}) copy-start(f32[8,8,8,2,256]{4,3,2,1,0:T(2,128)} %param.13) | copy-start | bytes 3145732
  19.7 1.5 %collective-permute-start = (f32[2,8,8,128]{3,2,1,0:T(8,128)}, f32[2,8,8,128]{3,2,1,0:T(8,128)S(1)}, u32[]{:S(2)}, u32[]{:S(2)}) collective-permute-start(f32[2,8,8,128]{3,2,1,0:T(8,128)} %get-tuple-element.48), channel_id=1, source_target_pairs={{0,1},{2,3},{1,0},{3,2},{4,5},{6,7},{5,4},{7,6},{8,9},{10,11},{9,8... | collective-permute-start | bytes 196616 | tf_op jit(solution)/shard_map/ppermute | solution.py:573
  19.7 3.7 %collective-permute-start.1 = (f32[2,8,8,128]{3,2,1,0:T(8,128)S(1)}, f32[2,8,8,128]{3,2,1,0:T(8,128)S(1)}, u32[]{:S(2)}, u32[]{:S(2)}) collective-permute-start(f32[2,8,8,128]{3,2,1,0:T(8,128)S(1)} %get-tuple-element.49), channel_id=1, source_target_pairs={{1,2},{3,0},{2,1},{0,3},{5,6},{7,4},{6,5},{4,7},{9,10},{11,8},{10,... | collective-permute-start | bytes 196616 | tf_op jit(solution)/shard_map/ppermute | solution.py:573
  19.8 19.4 %copy-start.6 = (bf16[256,256]{1,0:T(8,128)(2,1)S(1)}, bf16[256,256]{1,0:T(8,128)(2,1)}, u32[]{:S(2)}) copy-start(bf16[256,256]{1,0:T(8,128)(2,1)} %constant.57.clone.refs_8_.refs_10_.kf_ref) | copy-start | bytes 393220
  19.8 19.4 %copy-start.7 = (bf16[256,256]{1,0:T(8,128)(2,1)S(1)}, bf16[256,256]{1,0:T(8,128)(2,1)}, u32[]{:S(2)}) copy-start(bf16[256,256]{1,0:T(8,128)(2,1)} %constant.58.clone.refs_9_.refs_11_) | copy-start | bytes 393220
  27.3 6.9 %collective-permute-start.5 = (f32[16,1152]{1,0:T(8,128)S(1)}, f32[16,1152]{1,0:T(8,128)S(1)}, u32[]{:S(2)}, u32[]{:S(2)}) collective-permute-start(f32[16,1152]{1,0:T(8,128)S(1)} %get-tuple-element.58), channel_id=1, source_target_pairs={{0,28},{4,0},{8,4},{12,8},{16,12},{20,16},{24,20},{28,24},{1,29},{... | collective-permute-start | bytes 221192 | tf_op jit(solution)/shard_map/ppermute | solution.py:567
  32.1 7.1 %collective-permute-start.6 = (f32[16,1152]{1,0:T(8,128)S(1)}, f32[16,1152]{1,0:T(8,128)S(1)}, u32[]{:S(2)}, u32[]{:S(2)}) collective-permute-start(f32[16,1152]{1,0:T(8,128)S(1)} %get-tuple-element.59), channel_id=1, source_target_pairs={{0,4},{4,8},{8,12},{12,16},{16,20},{20,24},{24,28},{28,0},{1,5},{5... | collective-permute-start | bytes 221192 | tf_op jit(solution)/shard_map/ppermute | solution.py:567
  44.6 1.1 %copy-start = (f32[5,8,8,8,128]{4,3,2,1,0:T(8,128)}, f32[5,8,8,8,128]{4,3,2,1,0:T(8,128)S(1)}, u32[]{:S(2)}) copy-start(f32[5,8,8,8,128]{4,3,2,1,0:T(8,128)S(1)} %get-tuple-element.65.refs_7_.v0) | copy-start | bytes 3932164
  45.7 1.3 %collective-permute-start.7 = (f32[3,8,8,128]{3,2,1,0:T(8,128)S(1)}, f32[3,8,8,128]{3,2,1,0:T(8,128)S(1)}, u32[]{:S(2)}, u32[]{:S(2)}) collective-permute-start(f32[3,8,8,128]{3,2,1,0:T(8,128)S(1)} %get-tuple-element.61), channel_id=1, source_target_pairs={{0,1},{2,3},{1,0},{3,2},{4,5},{6,7},{5,4},{7,6},{8,9},{10,11},{9,8... | collective-permute-start | bytes 294920 | tf_op jit(solution)/shard_map/ppermute | solution.py:573
  45.7 4.4 %collective-permute-start.8 = (f32[3,8,8,128]{3,2,1,0:T(8,128)S(1)}, f32[3,8,8,128]{3,2,1,0:T(8,128)S(1)}, u32[]{:S(2)}, u32[]{:S(2)}) collective-permute-start(f32[3,8,8,128]{3,2,1,0:T(8,128)S(1)} %get-tuple-element.62), channel_id=1, source_target_pairs={{1,2},{3,0},{2,1},{0,3},{5,6},{7,4},{6,5},{4,7},{9,10},{11,8},{10,... | collective-permute-start | bytes 294920 | tf_op jit(solution)/shard_map/ppermute | solution.py:573
  55.0 1.1 %copy-start.2 = (f32[5,8,8,8,128]{4,3,2,1,0:T(8,128)}, f32[5,8,8,8,128]{4,3,2,1,0:T(8,128)S(1)}, u32[]{:S(2)}) copy-start(f32[5,8,8,8,128]{4,3,2,1,0:T(8,128)S(1)} %get-tuple-element.69.refs_7_.v1) | copy-start | bytes 3932164
  56.0 1.4 %collective-permute-start.9 = (f32[3,8,8,128]{3,2,1,0:T(8,128)S(1)}, f32[3,8,8,128]{3,2,1,0:T(8,128)S(1)}, u32[]{:S(2)}, u32[]{:S(2)}) collective-permute-start(f32[3,8,8,128]{3,2,1,0:T(8,128)S(1)} %get-tuple-element.67), channel_id=1, source_target_pairs={{0,1},{2,3},{1,0},{3,2},{4,5},{6,7},{5,4},{7,6},{8,9},{10,11},{9,8... | collective-permute-start | bytes 294920 | tf_op jit(solution)/shard_map/ppermute | solution.py:573
  56.5 4.9 %collective-permute-start.10 = (f32[3,8,8,128]{3,2,1,0:T(8,128)S(1)}, f32[3,8,8,128]{3,2,1,0:T(8,128)S(1)}, u32[]{:S(2)}, u32[]{:S(2)}) collective-permute-start(f32[3,8,8,128]{3,2,1,0:T(8,128)S(1)} %get-tuple-element.68), channel_id=1, source_target_pairs={{1,2},{3,0},{2,1},{0,3},{5,6},{7,4},{6,5},{4,7},{9,10},{11,8},{10,... | collective-permute-start | bytes 294920 | tf_op jit(solution)/shard_map/ppermute | solution.py:573
  66.2 1.1 %copy-start.4 = (f32[5,8,8,8,128]{4,3,2,1,0:T(8,128)}, f32[5,8,8,8,128]{4,3,2,1,0:T(8,128)S(1)}, u32[]{:S(2)}) copy-start(f32[5,8,8,8,128]{4,3,2,1,0:T(8,128)S(1)} %get-tuple-element.73.refs_7_.v2) | copy-start | bytes 3932164
  67.2 1.3 %collective-permute-start.11 = (f32[3,8,8,128]{3,2,1,0:T(8,128)S(1)}, f32[3,8,8,128]{3,2,1,0:T(8,128)S(1)}, u32[]{:S(2)}, u32[]{:S(2)}) collective-permute-start(f32[3,8,8,128]{3,2,1,0:T(8,128)S(1)} %get-tuple-element.71), channel_id=1, source_target_pairs={{0,1},{2,3},{1,0},{3,2},{4,5},{6,7},{5,4},{7,6},{8,9},{10,11},{9,8... | collective-permute-start | bytes 294920 | tf_op jit(solution)/shard_map/ppermute | solution.py:573
  67.4 4.5 %collective-permute-start.12 = (f32[3,8,8,128]{3,2,1,0:T(8,128)S(1)}, f32[3,8,8,128]{3,2,1,0:T(8,128)S(1)}, u32[]{:S(2)}, u32[]{:S(2)}) collective-permute-start(f32[3,8,8,128]{3,2,1,0:T(8,128)S(1)} %get-tuple-element.72), channel_id=1, source_target_pairs={{1,2},{3,0},{2,1},{0,3},{5,6},{7,4},{6,5},{4,7},{9,10},{11,8},{10,... | collective-permute-start | bytes 294920 | tf_op jit(solution)/shard_map/ppermute | solution.py:573
  76.9 1.4 %collective-permute-start.13 = (f32[3,8,8,128]{3,2,1,0:T(8,128)S(1)}, f32[3,8,8,128]{3,2,1,0:T(8,128)S(1)}, u32[]{:S(2)}, u32[]{:S(2)}) collective-permute-start(f32[3,8,8,128]{3,2,1,0:T(8,128)S(1)} %get-tuple-element.75), channel_id=1, source_target_pairs={{0,1},{2,3},{1,0},{3,2},{4,5},{6,7},{5,4},{7,6},{8,9},{10,11},{9,8... | collective-permute-start | bytes 294920 | tf_op jit(solution)/shard_map/ppermute | solution.py:573
  77.3 4.8 %collective-permute-start.14 = (f32[3,8,8,128]{3,2,1,0:T(8,128)S(1)}, f32[3,8,8,128]{3,2,1,0:T(8,128)S(1)}, u32[]{:S(2)}, u32[]{:S(2)}) collective-permute-start(f32[3,8,8,128]{3,2,1,0:T(8,128)S(1)} %get-tuple-element.76), channel_id=1, source_target_pairs={{1,2},{3,0},{2,1},{0,3},{5,6},{7,4},{6,5},{4,7},{9,10},{11,8},{10,... | collective-permute-start | bytes 294920 | tf_op jit(solution)/shard_map/ppermute | solution.py:573
  82.1 12.2 %copy-start.1 = (f32[5,8,8,8,128]{4,3,2,1,0:T(8,128)S(1)}, f32[5,8,8,8,128]{4,3,2,1,0:T(8,128)}, u32[]{:S(2)}) copy-start(f32[5,8,8,8,128]{4,3,2,1,0:T(8,128)} %copy-done) | copy-start | bytes 3932164
  82.1 12.2 %copy-start.3 = (f32[5,8,8,8,128]{4,3,2,1,0:T(8,128)S(1)}, f32[5,8,8,8,128]{4,3,2,1,0:T(8,128)}, u32[]{:S(2)}) copy-start(f32[5,8,8,8,128]{4,3,2,1,0:T(8,128)} %copy-done.2) | copy-start | bytes 3932164
  82.1 12.2 %copy-start.5 = (f32[5,8,8,8,128]{4,3,2,1,0:T(8,128)S(1)}, f32[5,8,8,8,128]{4,3,2,1,0:T(8,128)}, u32[]{:S(2)}) copy-start(f32[5,8,8,8,128]{4,3,2,1,0:T(8,128)} %copy-done.4) | copy-start | bytes 3932164
  84.4 1.1 %copy-start.9 = (f32[5,8,8,8,128]{4,3,2,1,0:T(8,128)}, f32[5,8,8,8,128]{4,3,2,1,0:T(8,128)S(1)}, u32[]{:S(2)}) copy-start(f32[5,8,8,8,128]{4,3,2,1,0:T(8,128)S(1)} %get-tuple-element.83.v4) | copy-start | bytes 3932164

commit v3 on v2

--- a/solution.py
+++ b/solution.py
@@ -121,7 +121,7 @@
     return pltpu.VMEM(shape, dtype)
 
 
-def call(kernel, out_shape, *args, smem=0, scratch=(), limit=48, **kw):
+def call(kernel, out_shape, *args, smem=0, scratch=(), limit=12, **kw):
     specs = [pl.BlockSpec(memory_space=pltpu.SMEM)] * smem
     specs += [pl.BlockSpec(memory_space=pltpu.VMEM)] * (len(args) - smem)
     outs = [pl.BlockSpec(memory_space=pltpu.VMEM) for _ in out_shape]
@@ -175,22 +175,30 @@
     return a + b
 
 
-def source_kernel(na, par_ref, p_ref, q_ref, wt_ref, z_ref, a_ref, b_ref):
-    rows = weight_rows(wt_ref[...])
+def source_kernel(na, planes, par_ref, p_ref, q_ref, wr_ref, z_ref, a_ref, b_ref):
     step = 2 * na
-    for r in range(8):
+    for n in range(planes):
+        r = pl.program_id(0) * planes + n
+        wr = wr_ref[r]
+        ends = {}
         for s in range(8):
-            base = (r * 8 + s) * 8 * step
+            base = (n * 8 + s) * 8 * step
             for l in range(2):
                 for at in range(na):
                     pick = pl.ds(base + at * 2 + l, 8, stride=step)
-                    z_ref[l * na + at, r, s] = rows[r][s] * (coolant_throughput * p_ref[pick, :] + q_ref[pick, :])
-    for r in range(8):
+                    value = (wr * float(GLL_W[s])) * (coolant_throughput * p_ref[pick, :] + q_ref[pick, :])
+                    if (l, s) in ((0, 0), (0, 7), (1, 0), (1, 7)):
+                        ends[l, s, at] = value
+                    else:
+                        z_ref[l * na + at, r, s] = value
         for at in range(na):
-            shared = z_ref[at, r, 7] + z_ref[na + at, r, 0]
+            shared = ends[0, 7, at] + ends[1, 0, at]
             z_ref[at, r, 7] = shared
             z_ref[na + at, r, 0] = shared
-            send_faces(par_ref, (at, r), z_ref[at, r, 0], z_ref[na + at, r, 7], a_ref, b_ref)
+            lower, upper = ends[0, 0, at], ends[1, 7, at]
+            z_ref[at, r, 0] = lower
+            z_ref[na + at, r, 7] = upper
+            send_faces(par_ref, (at, r), lower, upper, a_ref, b_ref)
 
 
 def rim_kernel(na, par_ref, z_in, a_ref, b_ref, dc_ref, z_ref, behind_ref, ahead_ref):
@@ -360,7 +368,7 @@
 
 
 def unpack_kernel(
-    na, par_ref, own_ref, r1_ref, r2_ref, r3_ref, dc_ref, wt_ref, zb_ref, za_ref, wk_ref, behind_ref, ahead_ref
+    na, par_ref, own_ref, r1_ref, r2_ref, r3_ref, dc_ref, wt_ref, zb_ref, za_ref, wk_ref, a_ref, b_ref
 ):
     rows = weight_rows(wt_ref[...] * KRYLOV_SCALE)
     got = jnp.concatenate([r[0:512] for r in (r1_ref, r2_ref, r3_ref)], 1)
@@ -377,9 +385,11 @@
             for s in range(8):
                 wk_ref[j, r, s] = rows[r][s] * kappa[r, s]
     behind, ahead = send_rims(lambda j: wk_ref[j].reshape(512, LANES), na)
-    for ref, z_rim, rim, inside in ((behind_ref, zb_ref, behind, par_ref[3]), (ahead_ref, za_ref, ahead, par_ref[4])):
-        ref[:, 0:640] = jnp.where(inside > 0, z_rim[...], 0.0)
-        ref[:, 640:1152] = jnp.where(inside > 0, rim, 0.0)
+    behind = jnp.where(par_ref[3] > 0, jnp.concatenate([zb_ref[...], behind], 1), 0.0)
+    ahead = jnp.where(par_ref[4] > 0, jnp.concatenate([za_ref[...], ahead], 1), 0.0)
+    even = par_ref[5] == 0
+    a_ref[...] = jnp.where(even, ahead, behind)
+    b_ref[...] = jnp.where(even, behind, ahead)
 
 
 def lines_t(k_ref, x):
@@ -452,7 +462,7 @@
     take = lambda n: [refs.pop(0) for _ in range(n)]
     ghost = 2 * na
     if first:
-        par_ref, z_in, wk_ref, from_ahead, from_behind, dc_ref = take(6)
+        par_ref, z_in, wk_ref, a_in, b_in, dc_ref = take(6)
         prev = None
     else:
         par_ref, y_in, a_in, b_in, wk_ref, wkg_ref, cr_ref, prev = take(8)
@@ -462,7 +472,9 @@
     g, f, base = refs
     if first:
         v[0:ghost] = z_in[...]
-        rims = place_rims(from_ahead[...], from_behind[...])
+        even = par_ref[5] == 0
+        a, b = a_in[...], b_in[...]
+        rims = place_rims(jnp.where(even, a, b), jnp.where(even, b, a))
         v[ghost] = rims[0:512].reshape(8, 8, 8, LANES)
         wkg_ref[...] = rims[640:1152].reshape(8, 8, 8, LANES)
         for j in range(ghost):
@@ -521,7 +533,7 @@
     all_dots[...] = jnp.broadcast_to(out[None], all_dots.shape)
 
 
-def combine_kernel(na, m_ref, v0, v1, v2, v3, v4, out_ref):
+def solve_moments(m_ref, coef_ref):
     sums = jnp.sum(m_ref[:, 0, :], 0, keepdims=True)
     lane = lane_index(1)
     m = [jnp.sum(jnp.where(lane == k, sums, 0.0), 1, keepdims=True) for k in range(2 * ITERS)]
@@ -547,24 +559,38 @@
     for i in reversed(range(n)):
         for k in range(i + 1, n):
             c[i] = c[i] - low[k][i] * c[k]
-    c = [jnp.broadcast_to(x * KRYLOV_SCALE, (8, LANES)) for x in c]
+    for k, x in enumerate(c):
+        coef_ref[k] = jnp.broadcast_to(x * KRYLOV_SCALE, (8, LANES))
+
+
+def combine_kernel(na, planes, m_ref, v0, v1, v2, v3, v4, out_ref, coef_ref):
+    i = pl.program_id(0)
+
+    @pl.when(i == 0)
+    def _():
+        solve_moments(m_ref, coef_ref)
+
+    c = [coef_ref[k] for k in range(ITERS)]
     step = 2 * na
-    vs = (v0, v1, v2, v3, v4)
-    for r in range(8):
+    for n in range(planes):
+        r = i * planes + n
         for s in range(8):
-            base = (r * 8 + s) * 8 * step
+            base = (n * 8 + s) * 8 * step
             for l in range(2):
                 for at in range(na):
                     x = None
-                    for coef, v in zip(c, vs):
+                    for coef, v in zip(c, (v0, v1, v2, v3, v4)):
                         term = coef * v[l * na + at, r, s]
                         x = term if x is None else x + term
                     out_ref[pl.ds(base + at * 2 + l, 8, stride=step), :] = x
 
 
-def ring(x, axis, by):
-    n = lax.axis_size(axis)
-    return lax.ppermute(x, axis, [(i, (i + by) % n) for i in range(n)])
+def slab_swap(x, start):
+    n, m = lax.axis_size("slab"), lax.axis_size("chan")
+    pairs = [(i * m + c, (i + 1) * m + c) for i in range(start, n - 1, 2) for c in range(m)]
+    busy = {i for pair in pairs for i in pair}
+    pairs += [(i, i + 1) for i in range(0, n * m, 2) if i not in busy]
+    return lax.ppermute(x, ("slab", "chan"), pairs + [(j, i) for i, j in pairs])
 
 
 def swap(x, axis, start):
@@ -615,10 +641,12 @@
         chan_at < chan - 1,
         slab_at > 0,
         slab_at < lax.axis_size("slab") - 1,
+        slab_at % 2,
     ]
     position = jnp.stack([jnp.asarray(x, jnp.int32) for x in position])
 
     wt = jnp.asarray(np.broadcast_to(GLL_W[:, None], (8, LANES)), f32)
+    wr = jnp.asarray(np.broadcast_to((GLL_W[:, None] * GLL_W)[:, :, None], (8, 8, LANES)), f32)
     kf, kb = (jnp.asarray(k) for k in line_matrices())
     kfluid = jnp.asarray(fluid_matrix())
 
@@ -641,35 +669,41 @@
     split = elements // LANES
     width = LANES
     room = elements // 4
+    in_hbm = lambda x: pltpu.with_memory_space_constraint(x, pltpu.HBM)
+    here = lambda: pl.BlockSpec(memory_space=pltpu.VMEM)
+    scalars = pl.BlockSpec(memory_space=pltpu.SMEM)
+    steps = 4
+    rows = 512 * tiles // steps
+    z, a, b = pl.pallas_call(
+        functools.partial(source_kernel, na, 8 // steps),
+        grid=(steps,),
+        in_specs=[scalars]
+        + [pl.BlockSpec((rows, LANES), lambda i: (i, 0))] * 2
+        + [pl.BlockSpec((8, 8, LANES), lambda i: (0, 0, 0))],
+        out_specs=[here()] * 3,
+        out_shape=[kept(field), kept((na, 8, 8, LANES)), kept((na, 8, 8, LANES))],
+        compiler_params=pltpu.CompilerParams(vmem_limit_bytes=12 * 1024 * 1024),
+    )(position, in_hbm(as_rows(previous_panel_warmth)), in_hbm(as_rows(pointwise_energy_source)), in_hbm(wr))
+    a, b = swap(a, "chan", 0), swap(b, "chan", 1)
+
+    velocity, z = lax.optimization_barrier((stream_speed_field, z))
     out = pl.pallas_call(
         functools.partial(fluid_kernel, chan, total),
         grid=(split,),
         in_specs=[
-            pl.BlockSpec(memory_space=pltpu.SMEM),
+            scalars,
             pl.BlockSpec((3, 8, 8, 8, width), lambda i: (0, 0, 0, 0, i)),
-        ]
-        + [pl.BlockSpec(memory_space=pltpu.VMEM)] * 2,
-        out_specs=[pl.BlockSpec((3, 8, 8, 8, width), lambda i: (0, 0, 0, 0, i))]
-        + [pl.BlockSpec(memory_space=pltpu.VMEM)] * 4,
-        out_shape=[shape(stream_speed_field.shape, bf16), shape((512, elements), bf16)]
-        + [shape((528, room), bf16)] * 3,
+            pl.BlockSpec((1, elements), lambda i: (0, 0)),
+            pl.BlockSpec(kfluid.shape, lambda i: (0, 0)),
+        ],
+        out_specs=[pl.BlockSpec((3, 8, 8, 8, width), lambda i: (0, 0, 0, 0, i))] + [here()] * 4,
+        out_shape=[shape(stream_speed_field.shape, bf16), kept((512, elements), bf16)]
+        + [kept((528, room), bf16)] * 3,
         scratch_shapes=[pltpu.VMEM((split, 512, width), bf16), pltpu.VMEM((3, 8, 8, 8, width), f32)],
-        compiler_params=pltpu.CompilerParams(vmem_limit_bytes=48 * 1024 * 1024),
-    )(me, stream_speed_field, liquid_to_solid_element.reshape(1, elements), kfluid)
+        compiler_params=pltpu.CompilerParams(vmem_limit_bytes=24 * 1024 * 1024),
+    )(me, in_hbm(velocity), in_hbm(liquid_to_solid_element.reshape(1, elements)), in_hbm(kfluid))
     stepped, own, *outgoing = out
     received = [around(x, by) for x, by in zip(outgoing, (1, -1, chan))]
-
-    warmth, source, own = lax.optimization_barrier((previous_panel_warmth, pointwise_energy_source, own))
-    z, a, b = call(
-        functools.partial(source_kernel, na),
-        [kept(field), shape((na, 8, 8, LANES)), shape((na, 8, 8, LANES))],
-        position,
-        as_rows(warmth),
-        as_rows(source),
-        wt,
-        smem=1,
-    )
-    a, b = swap(a, "chan", 0), swap(b, "chan", 1)
     z, z_behind, z_ahead = call(
         functools.partial(rim_kernel, na),
         [kept(field), kept((2 * RIM, 640)), kept((2 * RIM, 640))],
@@ -680,9 +714,9 @@
         dc,
         smem=1,
     )
-    wk, behind, ahead = call(
+    wk, a, b = call(
         functools.partial(unpack_kernel, na),
-        [kept(field), shape((2 * RIM, 1152)), shape((2 * RIM, 1152))],
+        [kept(field), kept((2 * RIM, 1152)), kept((2 * RIM, 1152))],
         position,
         own,
         *received,
@@ -692,15 +726,14 @@
         z_ahead,
         smem=1,
     )
-    from_ahead = ring(behind, "slab", -1)
-    from_behind = ring(ahead, "slab", 1)
+    a, b = slab_swap(a, 0), slab_swap(b, 1)
 
     basis, products = [], []
     for number in range(ITERS - 1):
         first = number == 0
-        outs = [kept(whole), kept(whole), shape(face), shape(face), kept((2, 8, LANES))]
+        outs = [kept(whole), kept(whole), kept(face), kept(face), kept((2, 8, LANES))]
         if first:
-            args = (z, wk, from_ahead, from_behind, dc)
+            args = (z, wk, a, b, dc)
             outs += [kept((8, 8, 8, LANES)), kept((tiles + 1, 8, LANES))]
         else:
             args = (y, a, b, wk, wkg, cr, basis[-1])
@@ -724,7 +757,7 @@
         a, b = swap(a, "chan", 0), swap(b, "chan", 1)
     v, sums = call(
         functools.partial(last_kernel, na),
-        [kept(whole), shape((total, 1, LANES))],
+        [kept(whole), kept((total, 1, LANES))],
         position,
         y,
         a,
@@ -741,7 +774,15 @@
     )
     basis.append(v)
     sums = lax.all_to_all(sums, ("slab", "chan"), 0, 0)
-    (x,) = call(functools.partial(combine_kernel, na), [shape((512 * tiles, LANES))], sums, *basis)
+    x = pl.pallas_call(
+        functools.partial(combine_kernel, na, 8 // steps),
+        grid=(steps,),
+        in_specs=[here()] * 6,
+        out_specs=pl.BlockSpec((rows, LANES), lambda i: (i, 0)),
+        out_shape=shape((512 * tiles, LANES)),
+        scratch_shapes=[pltpu.VMEM((ITERS, 8, LANES), f32)],
+        compiler_params=pltpu.CompilerParams(vmem_limit_bytes=12 * 1024 * 1024),
+    )(sums, *basis)
     x = x.reshape(8, 8, 8, na, count_l, LANES).transpose(0, 1, 2, 4, 3, 5)
     return stepped, x.reshape(8, 8, 8, count_l, count_a)
 

time: 97.7 us -> 85.8 us (0.88)
  local copies, waits for them, and re-layouts: 8.93 us -> 0.36 us
  starting transfers between devices: 15.1 us -> 10.4 us
  Pallas kernels: 37.4 us -> 35.8 us
  waiting for transfers between devices: 26 us -> 27.6 us
  blocking collectives: 8.83 us -> 10.2 us
    unnamed x36 -> x12, local copies, waits for them, and re-layouts: 8.61 us -> 0.04 us
    pallas_call x9 -> x7, Pallas kernels: 30.5 us -> 23.9 us  [call(): pl.pallas_call(kernel, in_specs=specs, out_specs=outs, out_shape=out_shap...]
    ppermute x3, waiting for transfers between devices: 0.02 us -> 5.44 us  [around(): lax.ppermute(x, ('slab', 'chan'), [(i, (i + by) % n) for i in range(n)])]
    ppermute x2, starting transfers between devices: 4.75 us -> 0.11 us  [slab_swap(): return lax.ppermute(x, ('slab', 'chan'), pairs + [(j, i) for i, j in pairs])]
    pallas_call x0 -> x2, Pallas kernels: none -> 4.28 us  [the longest x1 2.43 us: on_device(): pl.pallas_call(functools.partial(source_kernel, na, 8 // steps), grid=(st...]
    ppermute x2, waiting for transfers between devices: 6.97 us -> 4.18 us  [slab_swap(): return lax.ppermute(x, ('slab', 'chan'), pairs + [(j, i) for i, j in pairs])]
    all_to_all x1, blocking collectives: 8.83 us -> 10.2 us  [on_device(): sums = lax.all_to_all(sums, ('slab', 'chan'), 0, 0)]
    ppermute x3, starting transfers between devices: 6.43 us -> 5.34 us  [around(): lax.ppermute(x, ('slab', 'chan'), [(i, (i + by) % n) for i in range(n)])]
  transfers between devices with their start and end apart: 15 -> 15, of which waited for: 12 -> 11; matrix products, arithmetic and copies ran while one was open for 1% -> 1% of each run, Pallas kernels for 3% -> 11%
where the time goes in v3:
time: 85.8 us; the launch traced here: 85.5 us
  Pallas kernels  35.8 us (42%)
  waiting for transfers between devices  27.6 us (32%)
  starting transfers between devices  10.4 us (12%)
  blocking collectives  10.2 us (12%)
  between operations  0.87 us (1%)
    pallas_call x7, Pallas kernels, call(): pl.pallas_call(kernel, in_specs=specs, out_specs=outs, out_shape=out_shap...  23.9 us
    ppermute x10, waiting for transfers between devices, swap(): return lax.ppermute(x, axis, pairs + [(j, i) for i, j in pairs])  18 us
    all_to_all x1, blocking collectives, on_device(): sums = lax.all_to_all(sums, ('slab', 'chan'), 0, 0)  10.2 us
    pallas_call x1, Pallas kernels, on_device(): pl.pallas_call(functools.partial(fluid_kernel, chan, total), grid=(split,...  7.68 us
    ppermute x3, waiting for transfers between devices, around(): lax.ppermute(x, ('slab', 'chan'), [(i, (i + by) % n) for i in range(n)])  5.44 us
    ppermute x3, starting transfers between devices, around(): lax.ppermute(x, ('slab', 'chan'), [(i, (i + by) % n) for i in range(n)])  5.34 us
    ppermute x10, starting transfers between devices, swap(): return lax.ppermute(x, axis, pairs + [(j, i) for i, j in pairs])  4.98 us
    ppermute x2, waiting for transfers between devices, slab_swap(): return lax.ppermute(x, ('slab', 'chan'), pairs + [(j, i) for i, j in pairs])  4.18 us
  transfers between devices with their start and end apart: 15, of which 11 were waited for; matrix products, arithmetic and copies ran while one was open for 1% of the time, Pallas kernels for 11%

profile of v3, /device:TPU:0, one launch (start us, length us, event | category | flops | bytes accessed | tf_op | source)
XLA Modules:
  0.0 85.5 jit_solution(9912262180246219037)
XLA Ops:
  0.7 0.1 stack.56.par_ref.refs_0_
  0.7 2.4 %shard_map.122 = (f32[4,8,8,8,128]{4,3,2,1,0:T(8,128)S(1)}, f32[2,8,8,128]{3,2,1,0:T(8,128)S(1)}, f32[2,8,8,128]{3,2,1,0:T(8,128)S(1)}) custom-call(s32[6]{0:T(128)S(1)} %stack.56.par_ref.refs_0_, f32[2048,128]{1,0:T(8,128)} %bitcast.35, f32[2048,128]{1,0:T(8,128)} %bitcast.36, f32[8,8,128]{2,1,0:T(8,128)} %constant.63.clone.wr_ref), custom_call_target="tpu_custom_call" | custom-call | tf_op jit(solution)/shard_map/pallas_call | solution.py:677
  3.2 0.0 copy-start.3
  3.2 0.0 copy-start.4
  3.2 0.5 collective-permute-start
  3.7 2.6 %collective-permute-start.1 = (f32[2,8,8,128]{3,2,1,0:T(8,128)S(1)}, f32[2,8,8,128]{3,2,1,0:T(8,128)S(1)}, u32[]{:S(2)}, u32[]{:S(2)}) collective-permute-start(f32[2,8,8,128]{3,2,1,0:T(8,128)S(1)} %get-tuple-element.47), channel_id=1, source_target_pairs={{1,2},{3,0},{2,1},{0,3},{5,6},{7,4},{6,5},{4,7},{9,10},{11,8},{10,... | collective-permute-start | bytes 196616 | tf_op jit(solution)/shard_map/ppermute | solution.py:599
  6.4 7.7 %shard_map.123 = (bf16[3,8,8,8,512]{4,3,2,1,0:T(8,128)(2,1)}, bf16[512,512]{1,0:T(8,128)(2,1)S(1)}, bf16[528,128]{1,0:T(8,128)(2,1)S(1)}, bf16[528,128]{1,0:T(8,128)(2,1)S(1)}, bf16[528,128]{1,0:T(8,128)(2,1)S(1)}) custom-call(s32[1]{0:T(128)} %bitcast.me_ref, bf16[3,8,8,8,512]{4,3,2,1,0:T(8,128)(2,1)} %u_ref, s32[1,512]{1,0:T(1,128)} %bitcast.40, ...), custom_call_target="tpu_custom_call" | custom-call | tf_op jit(solution)/shard_map/pallas_call | solution.py:690
  14.0 0.1 collective-permute-start.2
  14.1 5.3 %collective-permute-start.3 = (bf16[528,128]{1,0:T(8,128)(2,1)S(1)}, bf16[528,128]{1,0:T(8,128)(2,1)S(1)}, u32[]{:S(2)}, u32[]{:S(2)}) collective-permute-start(bf16[528,128]{1,0:T(8,128)(2,1)S(1)} %get-tuple-element.51), channel_id=1, source_target_pairs={{0,31},{1,0},{2,1},{3,2},{4,3},{5,4},{6,5},{7,6},{8,7},{9,8},{10,9... | collective-permute-start | bytes 405512 | tf_op jit(solution)/shard_map/ppermute | solution.py:604
  19.4 0.0 collective-permute-start.4
  19.5 0.0 copy-start
  19.5 0.0 copy-start.1
  19.5 0.1 pad_maximum_fusion.2
  19.6 0.1 mul.55
  19.7 0.1 copy.18
  19.9 0.0 collective-permute-done.1.b_ref
  19.9 1.9 %shard_map.124 = (f32[4,8,8,8,128]{4,3,2,1,0:T(8,128)S(1)}, f32[16,640]{1,0:T(8,128)S(1)}, f32[16,640]{1,0:T(8,128)S(1)}) custom-call(s32[6]{0:T(128)S(1)} %stack.56.par_ref.refs_0_, f32[4,8,8,8,128]{4,3,2,1,0:T(8,128)S(1)} %get-tuple-element.45.z_in, f32[2,8,8,128]{3,2,1,0:T(8,128)S(1)} %collective-permute-done.a_ref, ...), custom_call_target="tpu_custom_call" | custom-call | tf_op jit(solution)/shard_map/pallas_call | solution.py:128
  21.7 0.6 collective-permute-done.2.r1_ref
  22.3 0.0 collective-permute-done.3.r2_ref
  22.3 4.9 %collective-permute-done.4.r3_ref = bf16[528,128]{1,0:T(8,128)(2,1)S(1)} collective-permute-done((bf16[528,128]{1,0:T(8,128)(2,1)S(1)}, bf16[528,128]{1,0:T(8,128)(2,1)S(1)}, u32[]{:S(2)}, u32[]{:S(2)}) %collective-permute-start.4) | collective-permute-done | bytes 135200 | tf_op jit(solution)/shard_map/ppermute | solution.py:604
  27.2 2.0 %shard_map.125 = (f32[4,8,8,8,128]{4,3,2,1,0:T(8,128)S(1)}, f32[16,1152]{1,0:T(8,128)S(1)}, f32[16,1152]{1,0:T(8,128)S(1)}) custom-call(s32[6]{0:T(128)S(1)} %stack.56.par_ref.refs_0_, bf16[512,512]{1,0:T(8,128)(2,1)S(1)} %get-tuple-element.49.own_ref, bf16[528,128]{1,0:T(8,128)(2,1)S(1)} %collective-permute-done.2.r1_ref, ...), custom_call_target="tpu_custom_call" | custom-call | tf_op jit(solution)/shard_map/pallas_call | solution.py:128
  29.2 0.0 collective-permute-start.5
  29.2 0.1 collective-permute-start.6
  29.3 0.1 multiply_bitcast_fusion
  29.4 4.2 %collective-permute-done.5.refs_3_ = f32[16,1152]{1,0:T(8,128)S(1)} collective-permute-done((f32[16,1152]{1,0:T(8,128)S(1)}, f32[16,1152]{1,0:T(8,128)S(1)}, u32[]{:S(2)}, u32[]{:S(2)}) %collective-permute-start.5) | collective-permute-done | bytes 73760 | tf_op jit(solution)/shard_map/ppermute | solution.py:593
  33.6 5.5 %shard_map.126 = (f32[5,8,8,8,128]{4,3,2,1,0:T(8,128)S(1)}, f32[5,8,8,8,128]{4,3,2,1,0:T(8,128)S(1)}, f32[3,8,8,128]{3,2,1,0:T(8,128)S(1)}, f32[3,8,8,128]{3,2,1...) custom-call(s32[6]{0:T(128)S(1)} %stack.56.par_ref.refs_0_, ...), custom_call_target="tpu_custom_call" | custom-call | tf_op jit(solution)/shard_map/pallas_call | solution.py:128
  39.1 0.0 collective-permute-start.7
  39.1 0.1 collective-permute-start.8
  39.2 1.2 %collective-permute-done.7.refs_2_ = f32[3,8,8,128]{3,2,1,0:T(8,128)S(1)} collective-permute-done((f32[3,8,8,128]{3,2,1,0:T(8,128)S(1)}, f32[3,8,8,128]{3,2,1,0:T(8,128)S(1)}, u32[]{:S(2)}, u32[]{:S(2)}) %collective-permute-start.7) | collective-permute-done | bytes 98336 | tf_op jit(solution)/shard_map/ppermute | solution.py:599
  40.4 3.3 %collective-permute-done.8.refs_3_ = f32[3,8,8,128]{3,2,1,0:T(8,128)S(1)} collective-permute-done((f32[3,8,8,128]{3,2,1,0:T(8,128)S(1)}, f32[3,8,8,128]{3,2,1,0:T(8,128)S(1)}, u32[]{:S(2)}, u32[]{:S(2)}) %collective-permute-start.8) | collective-permute-done | bytes 98336 | tf_op jit(solution)/shard_map/ppermute | solution.py:599
  43.7 4.0 %shard_map.127 = (f32[5,8,8,8,128]{4,3,2,1,0:T(8,128)S(1)}, f32[5,8,8,8,128]{4,3,2,1,0:T(8,128)S(1)}, f32[3,8,8,128]{3,2,1,0:T(8,128)S(1)}, f32[3,8,8,128]{3,2,1,0:T(8,128)S(1)}, f32[2,8,128]{2,1,0:T(8,128)S(1)}) custom-call(s32[6]{0:T(128)S(1)} %stack.56.par_ref.refs_0_, f32[5,8,8,8,128]{4,3,2,1,0:T(8,128)S(1)} %get-tuple-element.58.refs_1_, ...), custom_call_target="tpu_custom_call" | custom-call | tf_op jit(solution)/shard_map/pallas_call | solution.py:128
  47.8 0.4 collective-permute-start.9
  48.2 0.4 collective-permute-start.10
  48.6 0.6 collective-permute-done.9.refs_2_
  49.1 3.8 %collective-permute-done.10.refs_3_ = f32[3,8,8,128]{3,2,1,0:T(8,128)S(1)} collective-permute-done((f32[3,8,8,128]{3,2,1,0:T(8,128)S(1)}, f32[3,8,8,128]{3,2,1,0:T(8,128)S(1)}, u32[]{:S(2)}, u32[]{:S(2)}) %collective-permute-start.10) | collective-permute-done | bytes 98336 | tf_op jit(solution)/shard_map/ppermute | solution.py:599
  53.0 4.2 %shard_map.128 = (f32[5,8,8,8,128]{4,3,2,1,0:T(8,128)S(1)}, f32[5,8,8,8,128]{4,3,2,1,0:T(8,128)S(1)}, f32[3,8,8,128]{3,2,1,0:T(8,128)S(1)}, f32[3,8,8,128]{3,2,1,0:T(8,128)S(1)}, f32[2,8,128]{2,1,0:T(8,128)S(1)}) custom-call(s32[6]{0:T(128)S(1)} %stack.56.par_ref.refs_0_, f32[5,8,8,8,128]{4,3,2,1,0:T(8,128)S(1)} %get-tuple-element.64.refs_1_, ...), custom_call_target="tpu_custom_call" | custom-call | tf_op jit(solution)/shard_map/pallas_call | solution.py:128
  57.2 0.2 collective-permute-start.11
  57.3 0.1 collective-permute-start.12
  57.4 1.1 %collective-permute-done.11.refs_2_ = f32[3,8,8,128]{3,2,1,0:T(8,128)S(1)} collective-permute-done((f32[3,8,8,128]{3,2,1,0:T(8,128)S(1)}, f32[3,8,8,128]{3,2,1,0:T(8,128)S(1)}, u32[]{:S(2)}, u32[]{:S(2)}) %collective-permute-start.11) | collective-permute-done | bytes 98336 | tf_op jit(solution)/shard_map/ppermute | solution.py:599
  58.5 3.5 %collective-permute-done.12.refs_3_ = f32[3,8,8,128]{3,2,1,0:T(8,128)S(1)} collective-permute-done((f32[3,8,8,128]{3,2,1,0:T(8,128)S(1)}, f32[3,8,8,128]{3,2,1,0:T(8,128)S(1)}, u32[]{:S(2)}, u32[]{:S(2)}) %collective-permute-start.12) | collective-permute-done | bytes 98336 | tf_op jit(solution)/shard_map/ppermute | solution.py:599
  62.0 4.0 %shard_map.129 = (f32[5,8,8,8,128]{4,3,2,1,0:T(8,128)S(1)}, f32[5,8,8,8,128]{4,3,2,1,0:T(8,128)S(1)}, f32[3,8,8,128]{3,2,1,0:T(8,128)S(1)}, f32[3,8,8,128]{3,2,1,0:T(8,128)S(1)}, f32[2,8,128]{2,1,0:T(8,128)S(1)}) custom-call(s32[6]{0:T(128)S(1)} %stack.56.par_ref.refs_0_, f32[5,8,8,8,128]{4,3,2,1,0:T(8,128)S(1)} %get-tuple-element.68.refs_1_, ...), custom_call_target="tpu_custom_call" | custom-call | tf_op jit(solution)/shard_map/pallas_call | solution.py:128
  66.0 0.3 collective-permute-start.13
  66.3 0.3 collective-permute-start.14
  66.6 0.7 collective-permute-done.13.a_in
  67.3 3.8 %collective-permute-done.14.b_in = f32[3,8,8,128]{3,2,1,0:T(8,128)S(1)} collective-permute-done((f32[3,8,8,128]{3,2,1,0:T(8,128)S(1)}, f32[3,8,8,128]{3,2,1,0:T(8,128)S(1)}, u32[]{:S(2)}, u32[]{:S(2)}) %collective-permute-start.14) | collective-permute-done | bytes 98336 | tf_op jit(solution)/shard_map/ppermute | solution.py:599
  71.1 2.3 %shard_map.130 = (f32[5,8,8,8,128]{4,3,2,1,0:T(8,128)S(1)}, f32[32,1,128]{2,1,0:T(1,128)S(1)}) custom-call(s32[6]{0:T(128)S(1)} %stack.56.par_ref.refs_0_, f32[5,8,8,8,128]{4,3,2,1,0:T(8,128)S(1)} %get-tuple-element.72.y_in, f32[3,8,8,128]{3,2,1,0:T(8,128)S(1)} %collective-permute-done.13.a_in, f32[3,8,8,128]{3,2,1,0:T(8,128)S(1)} %collective-permute-done.14.b_in, ...), custom_call_target="tpu_custom_call" | custom-call | tf_op jit(solution)/shard_map/pallas_call | solution.py:128
  73.4 10.2 %all_to_all.5.m_ref = f32[32,1,128]{2,1,0:T(1,128)S(1)} all-to-all(f32[32,1,128]{2,1,0:T(1,128)S(1)} %get-tuple-element.80), channel_id=1, replica_groups=mesh['slab'=8,'chan'=4] {'slab','chan'}, dimensions={0} | all-to-all | bytes 32768 | tf_op jit(solution)/shard_map/all_to_all | solution.py:776
  83.7 1.9 %shard_map.131 = f32[2048,128]{1,0:T(8,128)} custom-call(f32[32,1,128]{2,1,0:T(1,128)S(1)} %all_to_all.5.m_ref, f32[5,8,8,8,128]{4,3,2,1,0:T(8,128)S(1)} %get-tuple-element.63.refs_7_.v0, f32[5,8,8,8,128]{4,3,2,1,0:T(8,128)S(1)} %get-tuple-element.67.refs_7_.v1, f32[5,8,8,8,128]{4,3,2,1,0:T(8,128)S(1)} %get-tuple-element.71.refs_7_.v2, ...), custom_call_target="tpu_custom_call" | custom-call | tf_op jit(solution)/shard_map/pallas_call | solution.py:777
  (22 shorter events, 0.1 us)
Async XLA Ops:
  3.2 16.2 %copy-start.3 = (s32[2,256]{1,0:T(2,128)S(1)}, s32[2,256]{1,0:T(2,128)}, u32[]{:S(2)}) copy-start(s32[2,256]{1,0:T(2,128)} %param.16) | copy-start | bytes 6148
  3.2 16.2 %copy-start.4 = (s32[2,256]{1,0:T(2,128)S(1)}, s32[2,256]{1,0:T(2,128)}, u32[]{:S(2)}) copy-start(s32[2,256]{1,0:T(2,128)} %param.15) | copy-start | bytes 6148
  3.2 16.6 %collective-permute-start = (f32[2,8,8,128]{3,2,1,0:T(8,128)S(1)}, f32[2,8,8,128]{3,2,1,0:T(8,128)S(1)}, u32[]{:S(2)}, u32[]{:S(2)}) collective-permute-start(f32[2,8,8,128]{3,2,1,0:T(8,128)S(1)} %get-tuple-element.46), channel_id=1, source_target_pairs={{0,1},{2,3},{1,0},{3,2},{4,5},{6,7},{5,4},{7,6},{8,9},{10,11},{9,8... | collective-permute-start | bytes 196616 | tf_op jit(solution)/shard_map/ppermute | solution.py:599
  3.7 16.1 %collective-permute-start.1 = (f32[2,8,8,128]{3,2,1,0:T(8,128)S(1)}, f32[2,8,8,128]{3,2,1,0:T(8,128)S(1)}, u32[]{:S(2)}, u32[]{:S(2)}) collective-permute-start(f32[2,8,8,128]{3,2,1,0:T(8,128)S(1)} %get-tuple-element.47), channel_id=1, source_target_pairs={{1,2},{3,0},{2,1},{0,3},{5,6},{7,4},{6,5},{4,7},{9,10},{11,8},{10,... | collective-permute-start | bytes 196616 | tf_op jit(solution)/shard_map/ppermute | solution.py:599
  6.4 20.8 %copy-start.2 = (f32[8,128]{1,0:T(8,128)S(1)}, f32[8,128]{1,0:T(8,128)}, u32[]{:S(2)}) copy-start(f32[8,128]{1,0:T(8,128)} %constant.62.clone.wt_ref.refs_6_.refs_8_) | copy-start | bytes 12292
  14.0 8.3 %collective-permute-start.2 = (bf16[528,128]{1,0:T(8,128)(2,1)S(1)}, bf16[528,128]{1,0:T(8,128)(2,1)S(1)}, u32[]{:S(2)}, u32[]{:S(2)}) collective-permute-start(bf16[528,128]{1,0:T(8,128)(2,1)S(1)} %get-tuple-element.50), channel_id=1, source_target_pairs={{0,1},{1,2},{2,3},{3,4},{4,5},{5,6},{6,7},{7,8},{8,9},{9,10},{10,1... | collective-permute-start | bytes 405512 | tf_op jit(solution)/shard_map/ppermute | solution.py:604
  14.1 8.2 %collective-permute-start.3 = (bf16[528,128]{1,0:T(8,128)(2,1)S(1)}, bf16[528,128]{1,0:T(8,128)(2,1)S(1)}, u32[]{:S(2)}, u32[]{:S(2)}) collective-permute-start(bf16[528,128]{1,0:T(8,128)(2,1)S(1)} %get-tuple-element.51), channel_id=1, source_target_pairs={{0,31},{1,0},{2,1},{3,2},{4,3},{5,4},{6,5},{7,6},{8,7},{9,8},{10,9... | collective-permute-start | bytes 405512 | tf_op jit(solution)/shard_map/ppermute | solution.py:604
  19.4 7.8 %collective-permute-start.4 = (bf16[528,128]{1,0:T(8,128)(2,1)S(1)}, bf16[528,128]{1,0:T(8,128)(2,1)S(1)}, u32[]{:S(2)}, u32[]{:S(2)}) collective-permute-start(bf16[528,128]{1,0:T(8,128)(2,1)S(1)} %get-tuple-element.52), channel_id=1, source_target_pairs={{0,4},{1,5},{2,6},{3,7},{4,8},{5,9},{6,10},{7,11},{8,12},{9,13},{1... | collective-permute-start | bytes 405512 | tf_op jit(solution)/shard_map/ppermute | solution.py:604
  19.5 14.1 %copy-start = (bf16[256,256]{1,0:T(8,128)(2,1)S(1)}, bf16[256,256]{1,0:T(8,128)(2,1)}, u32[]{:S(2)}) copy-start(bf16[256,256]{1,0:T(8,128)(2,1)} %constant.64.clone.refs_8_.refs_10_.kf_ref) | copy-start | bytes 393220
  19.5 14.1 %copy-start.1 = (bf16[256,256]{1,0:T(8,128)(2,1)S(1)}, bf16[256,256]{1,0:T(8,128)(2,1)}, u32[]{:S(2)}) copy-start(bf16[256,256]{1,0:T(8,128)(2,1)} %constant.65.clone.refs_9_.refs_11_) | copy-start | bytes 393220
  29.2 4.4 %collective-permute-start.5 = (f32[16,1152]{1,0:T(8,128)S(1)}, f32[16,1152]{1,0:T(8,128)S(1)}, u32[]{:S(2)}, u32[]{:S(2)}) collective-permute-start(f32[16,1152]{1,0:T(8,128)S(1)} %get-tuple-element.56), channel_id=1, source_target_pairs={{0,4},{1,5},{2,6},{3,7},{8,12},{9,13},{10,14},{11,15},{16,20},{17,... | collective-permute-start | bytes 221192 | tf_op jit(solution)/shard_map/ppermute | solution.py:593
  29.2 4.3 %collective-permute-start.6 = (f32[16,1152]{1,0:T(8,128)S(1)}, f32[16,1152]{1,0:T(8,128)S(1)}, u32[]{:S(2)}, u32[]{:S(2)}) collective-permute-start(f32[16,1152]{1,0:T(8,128)S(1)} %get-tuple-element.57), channel_id=1, source_target_pairs={{4,8},{5,9},{6,10},{7,11},{12,16},{13,17},{14,18},{15,19},{20,24},... | collective-permute-start | bytes 221192 | tf_op jit(solution)/shard_map/ppermute | solution.py:593
  39.1 1.3 %collective-permute-start.7 = (f32[3,8,8,128]{3,2,1,0:T(8,128)S(1)}, f32[3,8,8,128]{3,2,1,0:T(8,128)S(1)}, u32[]{:S(2)}, u32[]{:S(2)}) collective-permute-start(f32[3,8,8,128]{3,2,1,0:T(8,128)S(1)} %get-tuple-element.59), channel_id=1, source_target_pairs={{0,1},{2,3},{1,0},{3,2},{4,5},{6,7},{5,4},{7,6},{8,9},{10,11},{9,8... | collective-permute-start | bytes 294920 | tf_op jit(solution)/shard_map/ppermute | solution.py:599
  39.1 4.6 %collective-permute-start.8 = (f32[3,8,8,128]{3,2,1,0:T(8,128)S(1)}, f32[3,8,8,128]{3,2,1,0:T(8,128)S(1)}, u32[]{:S(2)}, u32[]{:S(2)}) collective-permute-start(f32[3,8,8,128]{3,2,1,0:T(8,128)S(1)} %get-tuple-element.60), channel_id=1, source_target_pairs={{1,2},{3,0},{2,1},{0,3},{5,6},{7,4},{6,5},{4,7},{9,10},{11,8},{10,... | collective-permute-start | bytes 294920 | tf_op jit(solution)/shard_map/ppermute | solution.py:599
  47.8 1.4 %collective-permute-start.9 = (f32[3,8,8,128]{3,2,1,0:T(8,128)S(1)}, f32[3,8,8,128]{3,2,1,0:T(8,128)S(1)}, u32[]{:S(2)}, u32[]{:S(2)}) collective-permute-start(f32[3,8,8,128]{3,2,1,0:T(8,128)S(1)} %get-tuple-element.65), channel_id=1, source_target_pairs={{0,1},{2,3},{1,0},{3,2},{4,5},{6,7},{5,4},{7,6},{8,9},{10,11},{9,8... | collective-permute-start | bytes 294920 | tf_op jit(solution)/shard_map/ppermute | solution.py:599
  48.2 4.8 %collective-permute-start.10 = (f32[3,8,8,128]{3,2,1,0:T(8,128)S(1)}, f32[3,8,8,128]{3,2,1,0:T(8,128)S(1)}, u32[]{:S(2)}, u32[]{:S(2)}) collective-permute-start(f32[3,8,8,128]{3,2,1,0:T(8,128)S(1)} %get-tuple-element.66), channel_id=1, source_target_pairs={{1,2},{3,0},{2,1},{0,3},{5,6},{7,4},{6,5},{4,7},{9,10},{11,8},{10,... | collective-permute-start | bytes 294920 | tf_op jit(solution)/shard_map/ppermute | solution.py:599
  57.2 1.3 %collective-permute-start.11 = (f32[3,8,8,128]{3,2,1,0:T(8,128)S(1)}, f32[3,8,8,128]{3,2,1,0:T(8,128)S(1)}, u32[]{:S(2)}, u32[]{:S(2)}) collective-permute-start(f32[3,8,8,128]{3,2,1,0:T(8,128)S(1)} %get-tuple-element.69), channel_id=1, source_target_pairs={{0,1},{2,3},{1,0},{3,2},{4,5},{6,7},{5,4},{7,6},{8,9},{10,11},{9,8... | collective-permute-start | bytes 294920 | tf_op jit(solution)/shard_map/ppermute | solution.py:599
  57.3 4.6 %collective-permute-start.12 = (f32[3,8,8,128]{3,2,1,0:T(8,128)S(1)}, f32[3,8,8,128]{3,2,1,0:T(8,128)S(1)}, u32[]{:S(2)}, u32[]{:S(2)}) collective-permute-start(f32[3,8,8,128]{3,2,1,0:T(8,128)S(1)} %get-tuple-element.70), channel_id=1, source_target_pairs={{1,2},{3,0},{2,1},{0,3},{5,6},{7,4},{6,5},{4,7},{9,10},{11,8},{10,... | collective-permute-start | bytes 294920 | tf_op jit(solution)/shard_map/ppermute | solution.py:599
  66.0 1.3 %collective-permute-start.13 = (f32[3,8,8,128]{3,2,1,0:T(8,128)S(1)}, f32[3,8,8,128]{3,2,1,0:T(8,128)S(1)}, u32[]{:S(2)}, u32[]{:S(2)}) collective-permute-start(f32[3,8,8,128]{3,2,1,0:T(8,128)S(1)} %get-tuple-element.73), channel_id=1, source_target_pairs={{0,1},{2,3},{1,0},{3,2},{4,5},{6,7},{5,4},{7,6},{8,9},{10,11},{9,8... | collective-permute-start | bytes 294920 | tf_op jit(solution)/shard_map/ppermute | solution.py:599
  66.3 4.8 %collective-permute-start.14 = (f32[3,8,8,128]{3,2,1,0:T(8,128)S(1)}, f32[3,8,8,128]{3,2,1,0:T(8,128)S(1)}, u32[]{:S(2)}, u32[]{:S(2)}) collective-permute-start(f32[3,8,8,128]{3,2,1,0:T(8,128)S(1)} %get-tuple-element.74), channel_id=1, source_target_pairs={{1,2},{3,0},{2,1},{0,3},{5,6},{7,4},{6,5},{4,7},{9,10},{11,8},{10,... | collective-permute-start | bytes 294920 | tf_op jit(solution)/shard_map/ppermute | solution.py:599

commit v4 on v3

--- a/solution.py
+++ b/solution.py
@@ -230,40 +230,49 @@
     return jnp.where(even, b, a), jnp.where(even, a, b)
 
 
+def axial_row(l, far, near):
+    ghost = len(far) - 1
+    lane = lane_index()
+    half = LANES // 2
+    roll = pltpu.roll
+    right = [roll(x, 1, 1) for x in far]
+    left = [roll(x, LANES - 1, 1) for x in near]
+    new_far, new_near = [], []
+    for at in range(ghost):
+        if at > 0:
+            carry = right[at - 1]
+        else:
+            carry = roll(far[ghost], half + 1, 1) if l == 0 else right[ghost]
+        new_near.append(near[at] + jnp.where(lane == 0, carry, right[at]))
+        if at < ghost - 1:
+            carry = left[at + 1]
+        else:
+            carry = left[ghost] if l == 0 else roll(near[ghost], half - 1, 1)
+        new_far.append(far[at] + jnp.where(lane == LANES - 1, carry, left[at]))
+    carry = right[ghost - 1] if l == 0 else roll(far[ghost - 1], half + 1, 1)
+    new_near.append(near[ghost] + jnp.where(lane == half * l, carry, right[ghost]))
+    carry = roll(near[0], half - 1, 1) if l == 0 else left[0]
+    new_far.append(far[ghost] + jnp.where(lane == half * (l + 1) - 1, carry, left[ghost]))
+    return new_far, new_near
+
+
 def assemble_axial(na, y):
     ghost = 2 * na
-    lane = lane_index()
-    first = lane == 0
-    last = lane == LANES - 1
-    half = LANES // 2
-    roll = pltpu.roll
+    low = lane_index() < LANES // 2
     for s in range(8):
-        far = [y[j, 7, s] for j in range(ghost + 1)]
-        near = [y[j, 0, s] for j in range(ghost + 1)]
-        right = [roll(f, 1, 1) for f in far]
-        left = [roll(f, LANES - 1, 1) for f in near]
-        far_half = [roll(far[na * 2 - 1], half + 1, 1), roll(far[ghost], half + 1, 1)]
-        near_half = [roll(near[0], half - 1, 1), roll(near[ghost], half - 1, 1)]
+        rims = []
         for l in range(2):
-            for at in range(na):
-                j = l * na + at
-                if at > 0:
-                    carry = right[j - 1]
-                else:
-                    carry = far_half[1] if l == 0 else right[ghost]
-                y[j, 0, s] = near[j] + jnp.where(first, carry, right[j])
-                if at < na - 1:
-                    carry = left[j + 1]
-                else:
-                    carry = left[ghost] if l == 0 else near_half[1]
-                y[j, 7, s] = far[j] + jnp.where(last, carry, left[j])
-        from_left = jnp.where(first, right[na - 1], jnp.where(lane == half, far_half[0], right[ghost]))
-        y[ghost, 0, s] = near[ghost] + from_left
-        from_right = jnp.where(last, left[na], jnp.where(lane == half - 1, near_half[0], left[ghost]))
-        y[ghost, 7, s] = far[ghost] + from_right
-
-
-def assemble_lateral(na, par_ref, y, a_ref, b_ref):
+            tiles = list(range(l * na, l * na + na)) + [ghost]
+            far, near = axial_row(l, [y[j, 7, s] for j in tiles], [y[j, 0, s] for j in tiles])
+            for n, j in enumerate(tiles[:-1]):
+                y[j, 7, s] = far[n]
+                y[j, 0, s] = near[n]
+            rims.append((far[-1], near[-1]))
+        y[ghost, 7, s] = jnp.where(low, rims[0][0], rims[1][0])
+        y[ghost, 0, s] = jnp.where(low, rims[0][1], rims[1][1])
+
+
+def assemble_lateral(na, y):
     ghost = 2 * na
     half = LANES // 2
     low = lane_index() < half
@@ -272,29 +281,51 @@
             shared = y[at, r, 7] + y[na + at, r, 0]
             y[at, r, 7] = shared
             y[na + at, r, 0] = shared
-            send_faces(par_ref, (at, r), y[at, r, 0], y[na + at, r, 7], a_ref, b_ref)
         upper = y[ghost, r, 7]
         lower = y[ghost, r, 0]
-        new_upper = upper + jnp.where(low, pltpu.roll(lower, half, 1), 0.0)
-        new_lower = lower + jnp.where(low, 0.0, pltpu.roll(upper, half, 1))
-        y[ghost, r, 7] = new_upper
-        y[ghost, r, 0] = new_lower
-        to_lower = jnp.where(low, new_lower, 0.0)
-        to_upper = jnp.where(low, pltpu.roll(new_upper, half, 1), 0.0)
-        send_faces(par_ref, (na, r), to_lower, to_upper, a_ref, b_ref)
+        y[ghost, r, 7] = upper + jnp.where(low, pltpu.roll(lower, half, 1), 0.0)
+        y[ghost, r, 0] = lower + jnp.where(low, 0.0, pltpu.roll(upper, half, 1))
+
+
+def turn(x, by):
+    return x if by % LANES == 0 else pltpu.roll(x, by % LANES, 1)
+
+
+def pack_rim(planes, l):
+    lane = lane_index()
+    half = LANES // 2
+    out = None
+    for r, x in enumerate(planes):
+        at = 2 * RIM * r
+        near = turn(x, at - half * l)
+        far = turn(x, at + RIM - (half * (l + 1) - RIM))
+        near = jnp.where((lane >= at) & (lane < at + RIM), near, 0.0)
+        both = jnp.where((lane >= at + RIM) & (lane < at + 2 * RIM), far, near)
+        out = both if out is None else out + both
+    return out
+
+
+def unpack_rim(x, r, l):
+    lane = lane_index()
+    half = LANES // 2
+    at = 2 * RIM * r
+    near = turn(x, half * l - at)
+    far = turn(x, half * (l + 1) - RIM - (at + RIM))
+    near = jnp.where((lane >= half * l) & (lane < half * l + RIM), near, 0.0)
+    return jnp.where((lane >= half * (l + 1) - RIM) & (lane < half * (l + 1)), far, near)
 
 
 def add_faces(na, par_ref, v, a_ref, b_ref):
     ghost = 2 * na
+    for at in range(na):
+        for r in range(8):
+            lower, upper = got_faces(par_ref, at * 8 + r, a_ref, b_ref)
+            v[at, r, 0] = v[at, r, 0] + lower
+            v[na + at, r, 7] = v[na + at, r, 7] + upper
+    lower, upper = got_faces(par_ref, na * 8, a_ref, b_ref)
     for r in range(8):
-        for at in range(na + 1):
-            lower, upper = got_faces(par_ref, (at, r), a_ref, b_ref)
-            if at < na:
-                v[at, r, 0] = v[at, r, 0] + lower
-                v[na + at, r, 7] = v[na + at, r, 7] + upper
-            else:
-                v[ghost, r, 0] = v[ghost, r, 0] + lower
-                v[ghost, r, 7] = v[ghost, r, 7] + pltpu.roll(upper, LANES // 2, 1)
+        v[ghost, r, 0] = v[ghost, r, 0] + unpack_rim(lower, r, 0)
+        v[ghost, r, 7] = v[ghost, r, 7] + unpack_rim(upper, r, 1)
 
 
 def fluid_kernel(
@@ -362,8 +393,15 @@
         tagged = jnp.concatenate([cond, codes.astype(f32).astype(bf16)], 0)
         room = s1_ref.shape[-1]
         position = lax.broadcasted_iota(jnp.int32, (room, elements), 0)
-        for g, ref in ((1, s1_ref), (2, s2_ref), (3, s3_ref)):
-            take = ((position == rank[g : g + 1]) & (group == g)).astype(f32).astype(bf16)
+        even = me_ref[0] % 2 == 0
+        one, two = rank[1:2], rank[2:3]
+        sends = (
+            (jnp.where(even, 1, 2), jnp.where(even, one, two), s1_ref),
+            (jnp.where(even, 2, 1), jnp.where(even, two, one), s2_ref),
+            (3, rank[3:4], s3_ref),
+        )
+        for g, order, ref in sends:
+            take = ((position == order) & (group == g)).astype(f32).astype(bf16)
             ref[...] = lax.dot_general(tagged, take, NT, preferred_element_type=f32).astype(bf16)
 
 
@@ -392,17 +430,21 @@
     b_ref[...] = jnp.where(even, behind, ahead)
 
 
-def lines_t(k_ref, x):
-    x = x.reshape(4, 128, LANES)
+def lines_t(k_ref, blocks):
     out = []
-    for p in range(2):
-        pair = jnp.concatenate([x[2 * p], x[2 * p + 1]], 1)
+    for p in range(0, len(blocks), 2):
+        pair = jnp.concatenate(blocks[p : p + 2], 1)
         high = pair.astype(bf16)
         low = (pair - high.astype(f32)).astype(bf16)
         y = jnp.dot(k_ref[...], jnp.concatenate([high, low], 0), preferred_element_type=f32)
         y = y[:128] + y[128:]
-        out += [y[:, :LANES].reshape(2, 8, 8, LANES), y[:, LANES:].reshape(2, 8, 8, LANES)]
+        out += [y[:, n * LANES : (n + 1) * LANES].reshape(2, 8, 8, LANES) for n in range(len(blocks[p : p + 2]))]
     return out
+
+
+def blocks_of(x):
+    x = x.reshape(4, 128, LANES)
+    return [x[n] for n in range(4)]
 
 
 def squares(v, j, other, iw_ref):
@@ -428,28 +470,48 @@
             g[r, s] = value
 
 
-def apply_tile(v, j, wk, c, base, kf_ref, kb_ref, y, g, f):
-    for p, part in enumerate(lines_t(kf_ref, v[j])):
+def fluxes(v, j, wk, c, kf_ref, g, f1, f2, f3):
+    for p, part in enumerate(lines_t(kf_ref, blocks_of(v[j]))):
         for q in range(2):
-            f[2 * p + q] = wk(2 * p + q) * part[q]
+            f3[j, 2 * p + q] = wk(2 * p + q) * part[q]
     gradient_r(v, j, g)
     for r in range(8):
-        line = [v[j, r, s] for s in range(8)]
-        second = along(DERIV, line)
+        second = along(DERIV, [v[j, r, s] for s in range(8)])
         k = wk(r)
-        flux = []
         for s in range(8):
             first = g[r, s]
-            flux.append(k[s] * (second[s] + c * first))
-            g[r, s] = k[s] * (first + c * second[s])
-        for s, value in enumerate(along(DERIV.T, flux)):
-            y[j, r, s] = value + (base[r] * float(GLL_W[s])) * line[s]
-    parts = lines_t(kb_ref, f[...])
-    for s in range(8):
-        for r, value in enumerate(along(DERIV.T, [g[r, s] for r in range(8)])):
-            y[j, r, s] = y[j, r, s] + value
-    for p, part in enumerate(parts):
-        y[j, 2 * p : 2 * p + 2] = y[j, 2 * p : 2 * p + 2] + part
+            f2[j, r, s] = k[s] * (second[s] + c * first)
+            f1[j, r, s] = k[s] * (first + c * second[s])
+
+
+def lateral_faces(na, par_ref, v, f1, f2, f3, base, kb_ref, a_ref, b_ref):
+    rows = [[(l * na + at, 7 * l) for at in range(na)] + [(2 * na, 7 * l)] for l in range(2)]
+    flat = rows[0] + rows[1]
+    blocks = []
+    for n in range(0, len(flat), 2):
+        pair = [f3[j, :, s].reshape(64, LANES) for j, s in flat[n : n + 2]]
+        blocks.append(jnp.concatenate(pair, 0))
+    thirds = []
+    for part in lines_t(kb_ref, blocks):
+        part = part.reshape(2, 8, 8, LANES)
+        thirds += [part[0], part[1]]
+    faces = []
+    for (j, s), third in zip(flat, thirds):
+        first = along(DERIV.T, [f1[j, r, s] for r in range(8)])
+        face = []
+        for r in range(8):
+            second = sum(float(DERIV[i, s]) * f2[j, r, i] for i in range(8) if DERIV[i, s] != 0.0)
+            face.append(second + (base[r] * float(GLL_W[s])) * v[j, r, s] + first[r] + third[r])
+        faces.append(face)
+    for l in range(2):
+        row = faces[l * (na + 1) : (l + 1) * (na + 1)]
+        far, near = axial_row(l, [x[7] for x in row], [x[0] for x in row])
+        for x, last, start in zip(row, far, near):
+            x[7], x[0] = last, start
+    for at in range(na):
+        for r in range(8):
+            send_faces(par_ref, at * 8 + r, faces[at][r], faces[na + 1 + at][r], a_ref, b_ref)
+    send_faces(par_ref, na * 8, pack_rim(faces[na], 0), pack_rim(faces[2 * na + 1], 1), a_ref, b_ref)
 
 
 def mass_rows(wt, base):
@@ -457,19 +519,18 @@
         base[r] = wt * float(GLL_W[r] * coolant_throughput * KRYLOV_SCALE)
 
 
-def step_kernel(na, first, *refs):
+def flux_kernel(na, first, *refs):
     refs = list(refs)
     take = lambda n: [refs.pop(0) for _ in range(n)]
     ghost = 2 * na
     if first:
         par_ref, z_in, wk_ref, a_in, b_in, dc_ref = take(6)
-        prev = None
     else:
-        par_ref, y_in, a_in, b_in, wk_ref, wkg_ref, cr_ref, prev = take(8)
-    wt_ref, iw_ref, kf_ref, kb_ref, v, y, a_out, b_out, dots = take(9)
+        par_ref, _, a_in, b_in, wk_ref, wkg_ref, cr_ref = take(7)
+    wt_ref, kf_ref, kb_ref, v, f1, f2, f3, a_out, b_out = take(9)
     if first:
         wkg_ref, cr_ref = take(2)
-    g, f, base = refs
+    g, base = refs
     if first:
         v[0:ghost] = z_in[...]
         even = par_ref[5] == 0
@@ -482,33 +543,49 @@
         cr_ref[ghost] = rims[512:520]
         assemble_axial(na, v)
     else:
-        v[...] = y_in[...]
         add_faces(na, par_ref, v, a_in, b_in)
+    mass_rows(wt_ref[...], base)
+    for j in range(ghost + 1):
+        if j < ghost:
+            wk = lambda r: wk_ref[j, r]
+        else:
+            wk = lambda r: wkg_ref[r]
+        fluxes(v, j, wk, cr_ref[j], kf_ref, g.at[j % 2], f1, f2, f3)
+    lateral_faces(na, par_ref, v, f1, f2, f3, base, kb_ref, a_out, b_out)
+
+
+def rest_kernel(na, first, *refs):
+    refs = list(refs)
+    prev = None if first else refs.pop(0)
+    v, f1, f2, f3, wt_ref, iw_ref, kb_ref, y, dots, base = refs
+    ghost = 2 * na
     mass_rows(wt_ref[...], base)
     totals = None
     for j in range(ghost + 1):
         if j < ghost:
             sums = squares(v, j, prev, iw_ref)
             totals = sums if totals is None else [a + b for a, b in zip(totals, sums)]
-            wk = lambda r: wk_ref[j, r]
-        else:
-            wk = lambda r: wkg_ref[r]
-        apply_tile(v, j, wk, cr_ref[j], base, kf_ref, kb_ref, y, g.at[j % 2], f.at[j % 2])
+        parts = lines_t(kb_ref, blocks_of(f3[j]))
+        for r in range(8):
+            for s, value in enumerate(along(DERIV.T, [f2[j, r, s] for s in range(8)])):
+                y[j, r, s] = value + (base[r] * float(GLL_W[s])) * v[j, r, s]
+        for s in range(8):
+            for r, value in enumerate(along(DERIV.T, [f1[j, r, s] for r in range(8)])):
+                y[j, r, s] = y[j, r, s] + value + parts[r // 2][r % 2, s]
     for k, value in enumerate(totals):
         dots[k] = value
     assemble_axial(na, y)
-    assemble_lateral(na, par_ref, y, a_out, b_out)
-
-
-def last_kernel(na, par_ref, y_in, a_in, b_in, wk_ref, cr_ref, prev, wt_ref, iw_ref, kf_ref, d0, d1, d2, d3, v, all_dots, g, base):
+    assemble_lateral(na, y)
+
+
+def last_kernel(na, par_ref, _, a_in, b_in, wk_ref, cr_ref, prev, wt_ref, iw_ref, kf_ref, d0, d1, d2, d3, v, all_dots, g, base):
     ghost = 2 * na
-    v[...] = y_in[...]
     add_faces(na, par_ref, v, a_in, b_in)
     mass_rows(wt_ref[...], base)
     totals = None
     for j in range(ghost):
         gj = g.at[j % 2]
-        third = lines_t(kf_ref, v[j])
+        third = lines_t(kf_ref, blocks_of(v[j]))
         sums = list(squares(v, j, prev, iw_ref))
         gradient_r(v, j, gj)
         c = 2.0 * cr_ref[j]
@@ -604,6 +681,12 @@
     return lax.ppermute(x, ("slab", "chan"), [(i, (i + by) % n) for i in range(n)])
 
 
+def swap_around(x, start):
+    n = lax.axis_size("slab") * lax.axis_size("chan")
+    pairs = [((start + i) % n, (start + i + 1) % n) for i in range(0, n, 2)]
+    return lax.ppermute(x, ("slab", "chan"), pairs + [(j, i) for i, j in pairs])
+
+
 def product_weights(count_l, count_a):
     slab, chan = lax.axis_index("slab"), lax.axis_index("chan")
     axial = slab * count_a + jnp.arange(count_a)
@@ -663,7 +746,6 @@
 
     field = (tiles, 8, 8, 8, LANES)
     whole = (tiles + 1, 8, 8, 8, LANES)
-    face = (na + 1, 8, 8, LANES)
     shape = lambda s, d=f32: jax.ShapeDtypeStruct(s, d)
     kept = vmem
     split = elements // LANES
@@ -703,7 +785,7 @@
         compiler_params=pltpu.CompilerParams(vmem_limit_bytes=24 * 1024 * 1024),
     )(me, in_hbm(velocity), in_hbm(liquid_to_solid_element.reshape(1, elements)), in_hbm(kfluid))
     stepped, own, *outgoing = out
-    received = [around(x, by) for x, by in zip(outgoing, (1, -1, chan))]
+    received = [swap_around(outgoing[0], 0), swap_around(outgoing[1], 1), around(outgoing[2], chan)]
     z, z_behind, z_ahead = call(
         functools.partial(rim_kernel, na),
         [kept(field), kept((2 * RIM, 640)), kept((2 * RIM, 640))],
@@ -729,32 +811,46 @@
     a, b = slab_swap(a, 0), slab_swap(b, 1)
 
     basis, products = [], []
+    face = (8 * na + 1, 8, LANES)
     for number in range(ITERS - 1):
         first = number == 0
-        outs = [kept(whole), kept(whole), kept(face), kept(face), kept((2, 8, LANES))]
+        outs = [kept(whole)] * 4 + [kept(face)] * 2
         if first:
             args = (z, wk, a, b, dc)
             outs += [kept((8, 8, 8, LANES)), kept((tiles + 1, 8, LANES))]
         else:
-            args = (y, a, b, wk, wkg, cr, basis[-1])
+            args = (y, a, b, wk, wkg, cr)
         got = call(
-            functools.partial(step_kernel, na, first),
+            functools.partial(flux_kernel, na, first),
             outs,
             position,
             *args,
             wt,
-            iw,
             kf,
             kb,
             smem=1,
-            scratch=[pltpu.VMEM((2, 8, 8, 8, LANES), f32)] * 2 + [pltpu.VMEM((8, 8, LANES), f32)],
+            scratch=[pltpu.VMEM((2, 8, 8, 8, LANES), f32), pltpu.VMEM((8, 8, LANES), f32)],
+            input_output_aliases={} if first else {1: 0},
         )
         if first:
-            wkg, cr = got[5:]
-        v, y, a, b, dots = got[:5]
+            wkg, cr = got[6:]
+        v, f1, f2, f3, a, b = got[:6]
+        a, b = swap(a, "chan", 0), swap(b, "chan", 1)
+        y, dots = call(
+            functools.partial(rest_kernel, na, first),
+            [kept(whole), kept((2, 8, LANES))],
+            *basis[-1:],
+            v,
+            f1,
+            f2,
+            f3,
+            wt,
+            iw,
+            kb,
+            scratch=[pltpu.VMEM((8, 8, LANES), f32)],
+        )
         basis.append(v)
         products.append(dots)
-        a, b = swap(a, "chan", 0), swap(b, "chan", 1)
     v, sums = call(
         functools.partial(last_kernel, na),
         [kept(whole), kept((total, 1, LANES))],
@@ -770,6 +866,7 @@
         kf,
         *products,
         smem=1,
+        input_output_aliases={1: 0},
         scratch=[pltpu.VMEM((2, 8, 8, 8, LANES), f32), pltpu.VMEM((8, 8, LANES), f32)],
     )
     basis.append(v)

time: 85.8 us -> 76.8 us (0.90)
  waiting for transfers between devices: 27.6 us -> 18.3 us
    ppermute x10, waiting for transfers between devices: 18 us -> 8.45 us  [swap(): return lax.ppermute(x, axis, pairs + [(j, i) for i, j in pairs])]
    ppermute x3 -> x1, starting transfers between devices: 5.34 us -> 0.01 us  [around(): lax.ppermute(x, ('slab', 'chan'), [(i, (i + by) % n) for i in range(n)])]
    ppermute x0 -> x2, starting transfers between devices: none -> 4.65 us  [swap_around(): return lax.ppermute(x, ('slab', 'chan'), pairs + [(j, i) for i, j in pairs])]
    ppermute x0 -> x2, waiting for transfers between devices: none -> 1.7 us  [swap_around(): return lax.ppermute(x, ('slab', 'chan'), pairs + [(j, i) for i, j in pairs])]
    ppermute x3 -> x1, waiting for transfers between devices: 5.44 us -> 3.94 us  [around(): lax.ppermute(x, ('slab', 'chan'), [(i, (i + by) % n) for i in range(n)])]
    pallas_call x7 -> x11, Pallas kernels: 23.9 us -> 24.4 us  [call(): pl.pallas_call(kernel, in_specs=specs, out_specs=outs, out_shape=out_shap...]
  transfers between devices with their start and end apart: 15 -> 15, of which waited for: 11 -> 7; matrix products, arithmetic and copies ran while one was open for 1% -> 1% of each run, Pallas kernels for 11% -> 21%
where the time goes in v4:
time: 76.8 us; the launch traced here: 76.5 us
  Pallas kernels  36.5 us (48%)
  waiting for transfers between devices  18.3 us (24%)
  blocking collectives  10.3 us (13%)
  starting transfers between devices  10 us (13%)
  between operations  0.89 us (1%)
    pallas_call x11, Pallas kernels, call(): pl.pallas_call(kernel, in_specs=specs, out_specs=outs, out_shape=out_shap...  24.4 us
    all_to_all x1, blocking collectives, on_device(): sums = lax.all_to_all(sums, ('slab', 'chan'), 0, 0)  10.3 us
    ppermute x10, waiting for transfers between devices, swap(): return lax.ppermute(x, axis, pairs + [(j, i) for i, j in pairs])  8.45 us
    pallas_call x1, Pallas kernels, on_device(): pl.pallas_call(functools.partial(fluid_kernel, chan, total), grid=(split,...  7.82 us
    ppermute x10, starting transfers between devices, swap(): return lax.ppermute(x, axis, pairs + [(j, i) for i, j in pairs])  5.28 us
    ppermute x2, starting transfers between devices, swap_around(): return lax.ppermute(x, ('slab', 'chan'), pairs + [(j, i) for i, j in pairs])  4.65 us
    ppermute x2, waiting for transfers between devices, slab_swap(): return lax.ppermute(x, ('slab', 'chan'), pairs + [(j, i) for i, j in pairs])  4.19 us
    ppermute x1, waiting for transfers between devices, around(): lax.ppermute(x, ('slab', 'chan'), [(i, (i + by) % n) for i in range(n)])  3.94 us
  transfers between devices with their start and end apart: 15, of which 7 were waited for; matrix products, arithmetic and copies ran while one was open for 1% of the time, Pallas kernels for 21%

profile of v4, /device:TPU:0, one launch (start us, length us, event | category | flops | bytes accessed | tf_op | source)
XLA Modules:
  0.0 76.5 jit_solution(6518653262553958036)
XLA Ops:
  0.7 0.1 stack.56.par_ref.refs_0_
  0.7 2.4 %shard_map.122 = (f32[4,8,8,8,128]{4,3,2,1,0:T(8,128)S(1)}, f32[2,8,8,128]{3,2,1,0:T(8,128)S(1)}, f32[2,8,8,128]{3,2,1,0:T(8,128)S(1)}) custom-call(s32[6]{0:T(128)S(1)} %stack.56.par_ref.refs_0_, f32[2048,128]{1,0:T(8,128)} %bitcast.35, f32[2048,128]{1,0:T(8,128)} %bitcast.36, f32[8,8,128]{2,1,0:T(8,128)} %constant.63.clone.wr_ref), custom_call_target="tpu_custom_call" | custom-call | tf_op jit(solution)/shard_map/pallas_call | solution.py:759
  3.2 0.0 copy-start.3
  3.2 0.0 copy-start.4
  3.2 0.5 collective-permute-start
  3.7 2.6 %collective-permute-start.1 = (f32[2,8,8,128]{3,2,1,0:T(8,128)S(1)}, f32[2,8,8,128]{3,2,1,0:T(8,128)S(1)}, u32[]{:S(2)}, u32[]{:S(2)}) collective-permute-start(f32[2,8,8,128]{3,2,1,0:T(8,128)S(1)} %get-tuple-element.59), channel_id=1, source_target_pairs={{1,2},{3,0},{2,1},{0,3},{5,6},{7,4},{6,5},{4,7},{9,10},{11,8},{10,... | collective-permute-start | bytes 196616 | tf_op jit(solution)/shard_map/ppermute | solution.py:676
  6.4 7.8 %shard_map.123 = (bf16[3,8,8,8,512]{4,3,2,1,0:T(8,128)(2,1)}, bf16[512,512]{1,0:T(8,128)(2,1)S(1)}, bf16[528,128]{1,0:T(8,128)(2,1)}, bf16[528,128]{1,0:T(8,128)(2,1)}, bf16[528,128]{1,0:T(8,128)(2,1)}) custom-call(s32[1]{0:T(128)} %bitcast.me_ref, bf16[3,8,8,8,512]{4,3,2,1,0:T(8,128)(2,1)} %u_ref, s32[1,512]{1,0:T(1,128)} %bitcast.40, ...), custom_call_target="tpu_custom_call" | custom-call | tf_op jit(solution)/shard_map/pallas_call | solution.py:772
  14.2 0.1 collective-permute-start.2
  14.3 4.5 %collective-permute-start.3 = (bf16[528,128]{1,0:T(8,128)(2,1)}, bf16[528,128]{1,0:T(8,128)(2,1)S(1)}, u32[]{:S(2)}, u32[]{:S(2)}) collective-permute-start(bf16[528,128]{1,0:T(8,128)(2,1)} %get-tuple-element.63), channel_id=1, source_target_pairs={{1,2},{3,4},{5,6},{7,8},{9,10},{11,12},{13,14},{15,16},{17,18},{19... | collective-permute-start | bytes 405512 | tf_op jit(solution)/shard_map/ppermute | solution.py:687
  18.8 0.0 collective-permute-start.4
  18.9 0.1 pad_maximum_fusion.2
  19.0 0.1 mul.55
  19.1 0.1 copy.22
  19.2 0.0 collective-permute-done.a_ref
  19.2 0.0 collective-permute-done.1.b_ref
  19.2 1.9 %shard_map.124 = (f32[4,8,8,8,128]{4,3,2,1,0:T(8,128)S(1)}, f32[16,640]{1,0:T(8,128)S(1)}, f32[16,640]{1,0:T(8,128)S(1)}) custom-call(s32[6]{0:T(128)S(1)} %stack.56.par_ref.refs_0_, f32[4,8,8,8,128]{4,3,2,1,0:T(8,128)S(1)} %get-tuple-element.57.z_in, f32[2,8,8,128]{3,2,1,0:T(8,128)S(1)} %collective-permute-done.a_ref, ...), custom_call_target="tpu_custom_call" | custom-call | tf_op jit(solution)/shard_map/pallas_call | solution.py:128
  21.1 0.0 collective-permute-done.2.r1_ref
  21.1 1.7 %collective-permute-done.3.r2_ref = bf16[528,128]{1,0:T(8,128)(2,1)S(1)} collective-permute-done((bf16[528,128]{1,0:T(8,128)(2,1)}, bf16[528,128]{1,0:T(8,128)(2,1)S(1)}, u32[]{:S(2)}, u32[]{:S(2)}) %collective-permute-start.3) | collective-permute-done | bytes 135200 | tf_op jit(solution)/shard_map/ppermute | solution.py:687
  22.8 3.9 %collective-permute-done.4.r3_ref = bf16[528,128]{1,0:T(8,128)(2,1)S(1)} collective-permute-done((bf16[528,128]{1,0:T(8,128)(2,1)}, bf16[528,128]{1,0:T(8,128)(2,1)S(1)}, u32[]{:S(2)}, u32[]{:S(2)}) %collective-permute-start.4) | collective-permute-done | bytes 135200 | tf_op jit(solution)/shard_map/ppermute | solution.py:681
  26.8 2.0 %shard_map.125 = (f32[4,8,8,8,128]{4,3,2,1,0:T(8,128)S(1)}, f32[16,1152]{1,0:T(8,128)S(1)}, f32[16,1152]{1,0:T(8,128)S(1)}) custom-call(s32[6]{0:T(128)S(1)} %stack.56.par_ref.refs_0_, bf16[512,512]{1,0:T(8,128)(2,1)S(1)} %get-tuple-element.61.own_ref, bf16[528,128]{1,0:T(8,128)(2,1)S(1)} %collective-permute-done.2.r1_ref, ...), custom_call_target="tpu_custom_call" | custom-call | tf_op jit(solution)/shard_map/pallas_call | solution.py:128
  28.8 0.0 collective-permute-start.5
  28.8 0.1 collective-permute-start.6
  29.0 4.2 %collective-permute-done.5.refs_3_ = f32[16,1152]{1,0:T(8,128)S(1)} collective-permute-done((f32[16,1152]{1,0:T(8,128)S(1)}, f32[16,1152]{1,0:T(8,128)S(1)}, u32[]{:S(2)}, u32[]{:S(2)}) %collective-permute-start.5) | collective-permute-done | bytes 73760 | tf_op jit(solution)/shard_map/ppermute | solution.py:670
  33.2 0.0 collective-permute-done.6.refs_4_
  33.2 4.0 %shard_map.126 = (f32[5,8,8,8,128]{4,3,2,1,0:T(8,128)S(1)}, f32[5,8,8,8,128]{4,3,2,1,0:T(8,128)S(1)}, f32[5,8,8,8,128]{4,3,2,1,0:T(8,128)S(1)}, f32[5,8,8,8,128]...) custom-call(s32[6]{0:T(128)S(1)} %stack.56.par_ref.refs_0_, ...), custom_call_target="tpu_custom_call" | custom-call | tf_op jit(solution)/shard_map/pallas_call | solution.py:128
  37.2 0.1 collective-permute-start.7
  37.3 0.1 collective-permute-start.8
  37.4 0.1 multiply_bitcast_fusion
  37.5 1.6 %shard_map.127 = (f32[5,8,8,8,128]{4,3,2,1,0:T(8,128)S(1)}, f32[2,8,128]{2,1,0:T(8,128)S(1)}) custom-call(f32[5,8,8,8,128]{4,3,2,1,0:T(8,128)S(1)} %get-tuple-element.70.refs_0_.v0, f32[5,8,8,8,128]{4,3,2,1,0:T(8,128)S(1)} %get-tuple-element.71.refs_1_, f32[5,8,8,8,128]{4,3,2,1,0:T(8,128)S(1)} %get-tuple-element.72.refs_2_, ...), custom_call_target="tpu_custom_call" | custom-call | tf_op jit(solution)/shard_map/pallas_call | solution.py:128
  39.1 2.2 %collective-permute-done.8.refs_3_ = f32[17,8,128]{2,1,0:T(8,128)S(1)} collective-permute-done((f32[17,8,128]{2,1,0:T(8,128)S(1)}, f32[17,8,128]{2,1,0:T(8,128)S(1)}, u32[]{:S(2)}, u32[]{:S(2)}) %collective-permute-start.8) | collective-permute-done | bytes 69664 | tf_op jit(solution)/shard_map/ppermute | solution.py:676
  41.3 2.5 %shard_map.128 = (f32[5,8,8,8,128]{4,3,2,1,0:T(8,128)S(1)}, f32[5,8,8,8,128]{4,3,2,1,0:T(8,128)S(1)}, f32[5,8,8,8,128]{4,3,2,1,0:T(8,128)S(1)}, f32[5,8,8,8,128]...) custom-call(s32[6]{0:T(128)S(1)} %stack.56.par_ref.refs_0_, ...), custom_call_target="tpu_custom_call", output_to_operand_aliasing={{0}: (1, {})} | custom-call | tf_op jit(solution)/shard_map/pallas_call | solution.py:128
  43.7 0.5 collective-permute-start.9
  44.2 0.3 collective-permute-start.10
  44.5 1.7 %shard_map.129 = (f32[5,8,8,8,128]{4,3,2,1,0:T(8,128)S(1)}, f32[2,8,128]{2,1,0:T(8,128)S(1)}) custom-call(f32[5,8,8,8,128]{4,3,2,1,0:T(8,128)S(1)} %get-tuple-element.70.refs_0_.v0, f32[5,8,8,8,128]{4,3,2,1,0:T(8,128)S(1)} %get-tuple-element.79.refs_1_.refs_0_.v1, f32[5,8,8,8,128]{4,3,2,1,0:T(8,128)S(1)} %get-tuple-element.80.refs_2_, ...), custom_call_target="tpu_custom_call" | custom-call | tf_op jit(solution)/shard_map/pallas_call | solution.py:128
  46.2 2.1 %collective-permute-done.10.refs_3_ = f32[17,8,128]{2,1,0:T(8,128)S(1)} collective-permute-done((f32[17,8,128]{2,1,0:T(8,128)S(1)}, f32[17,8,128]{2,1,0:T(8,128)S(1)}, u32[]{:S(2)}, u32[]{:S(2)}) %collective-permute-start.10) | collective-permute-done | bytes 69664 | tf_op jit(solution)/shard_map/ppermute | solution.py:676
  48.4 2.7 %shard_map.130 = (f32[5,8,8,8,128]{4,3,2,1,0:T(8,128)S(1)}, f32[5,8,8,8,128]{4,3,2,1,0:T(8,128)S(1)}, f32[5,8,8,8,128]{4,3,2,1,0:T(8,128)S(1)}, f32[5,8,8,8,128]...) custom-call(s32[6]{0:T(128)S(1)} %stack.56.par_ref.refs_0_, ...), custom_call_target="tpu_custom_call", output_to_operand_aliasing={{0}: (1, {})} | custom-call | tf_op jit(solution)/shard_map/pallas_call | solution.py:128
  51.0 0.2 collective-permute-start.11
  51.2 0.2 collective-permute-start.12
  51.4 1.7 %shard_map.131 = (f32[5,8,8,8,128]{4,3,2,1,0:T(8,128)S(1)}, f32[2,8,128]{2,1,0:T(8,128)S(1)}) custom-call(f32[5,8,8,8,128]{4,3,2,1,0:T(8,128)S(1)} %get-tuple-element.79.refs_1_.refs_0_.v1, f32[5,8,8,8,128]{4,3,2,1,0:T(8,128)S(1)} %get-tuple-element.86.refs_1_.refs_0_.v2, f32[5,8,8,8,128]{4,3,2,1,0:T(8,128)S(1)} %get-tuple-element.87.refs_2_, ...), custom_call_target="tpu_custom_call" | custom-call | tf_op jit(solution)/shard_map/pallas_call | solution.py:128
  53.1 2.0 %collective-permute-done.12.refs_3_ = f32[17,8,128]{2,1,0:T(8,128)S(1)} collective-permute-done((f32[17,8,128]{2,1,0:T(8,128)S(1)}, f32[17,8,128]{2,1,0:T(8,128)S(1)}, u32[]{:S(2)}, u32[]{:S(2)}) %collective-permute-start.12) | collective-permute-done | bytes 69664 | tf_op jit(solution)/shard_map/ppermute | solution.py:676
  55.2 2.4 %shard_map.132 = (f32[5,8,8,8,128]{4,3,2,1,0:T(8,128)S(1)}, f32[5,8,8,8,128]{4,3,2,1,0:T(8,128)S(1)}, f32[5,8,8,8,128]{4,3,2,1,0:T(8,128)S(1)}, f32[5,8,8,8,128]...) custom-call(s32[6]{0:T(128)S(1)} %stack.56.par_ref.refs_0_, ...), custom_call_target="tpu_custom_call", output_to_operand_aliasing={{0}: (1, {})} | custom-call | tf_op jit(solution)/shard_map/pallas_call | solution.py:128
  57.6 0.4 collective-permute-start.13
  58.0 0.4 collective-permute-start.14
  58.4 1.7 %shard_map.133 = (f32[5,8,8,8,128]{4,3,2,1,0:T(8,128)S(1)}, f32[2,8,128]{2,1,0:T(8,128)S(1)}) custom-call(f32[5,8,8,8,128]{4,3,2,1,0:T(8,128)S(1)} %get-tuple-element.86.refs_1_.refs_0_.v2, f32[5,8,8,8,128]{4,3,2,1,0:T(8,128)S(1)} %get-tuple-element.93.refs_1_.prev.v3, f32[5,8,8,8,128]{4,3,2,1,0:T(8,128)S(1)} %get-tuple-element.94.refs_2_, ...), custom_call_target="tpu_custom_call" | custom-call | tf_op jit(solution)/shard_map/pallas_call | solution.py:128
  60.1 2.1 %collective-permute-done.14.b_in = f32[17,8,128]{2,1,0:T(8,128)S(1)} collective-permute-done((f32[17,8,128]{2,1,0:T(8,128)S(1)}, f32[17,8,128]{2,1,0:T(8,128)S(1)}, u32[]{:S(2)}, u32[]{:S(2)}) %collective-permute-start.14) | collective-permute-done | bytes 69664 | tf_op jit(solution)/shard_map/ppermute | solution.py:676
  62.2 2.2 %shard_map.134 = (f32[5,8,8,8,128]{4,3,2,1,0:T(8,128)S(1)}, f32[32,1,128]{2,1,0:T(1,128)S(1)}) custom-call(s32[6]{0:T(128)S(1)} %stack.56.par_ref.refs_0_, f32[5,8,8,8,128]{4,3,2,1,0:T(8,128)S(1)} %get-tuple-element.97._, f32[17,8,128]{2,1,0:T(8,128)S(1)} %collective-permute-done.13.a_in, ...), custom_call_target="tpu_custom_call", output_to_operand_aliasing={{0}: (1, {})} | custom-call | tf_op jit(solution)/shard_map/pallas_call | solution.py:128
  64.4 10.3 %all_to_all.5.m_ref = f32[32,1,128]{2,1,0:T(1,128)S(1)} all-to-all(f32[32,1,128]{2,1,0:T(1,128)S(1)} %get-tuple-element.104), channel_id=1, replica_groups=mesh['slab'=8,'chan'=4] {'slab','chan'}, dimensions={0} | all-to-all | bytes 32768 | tf_op jit(solution)/shard_map/all_to_all | solution.py:873
  74.7 1.8 %shard_map.135 = f32[2048,128]{1,0:T(8,128)} custom-call(f32[32,1,128]{2,1,0:T(1,128)S(1)} %all_to_all.5.m_ref, f32[5,8,8,8,128]{4,3,2,1,0:T(8,128)S(1)} %get-tuple-element.70.refs_0_.v0, f32[5,8,8,8,128]{4,3,2,1,0:T(8,128)S(1)} %get-tuple-element.79.refs_1_.refs_0_.v1, f32[5,8,8,8,128]{4,3,2,1,0:T(8,128)S(1)} %get-tuple-element.86.refs_1_.refs_0_.v2, ...), custom_call_target="tpu_custom_call" | custom-call | tf_op jit(solution)/shard_map/pallas_call | solution.py:874
  (26 shorter events, 0.1 us)
Async XLA Ops:
  3.2 15.7 %copy-start.3 = (s32[2,256]{1,0:T(2,128)S(1)}, s32[2,256]{1,0:T(2,128)}, u32[]{:S(2)}) copy-start(s32[2,256]{1,0:T(2,128)} %param.16) | copy-start | bytes 6148
  3.2 15.7 %copy-start.4 = (s32[2,256]{1,0:T(2,128)S(1)}, s32[2,256]{1,0:T(2,128)}, u32[]{:S(2)}) copy-start(s32[2,256]{1,0:T(2,128)} %param.15) | copy-start | bytes 6148
  3.2 16.0 %collective-permute-start = (f32[2,8,8,128]{3,2,1,0:T(8,128)S(1)}, f32[2,8,8,128]{3,2,1,0:T(8,128)S(1)}, u32[]{:S(2)}, u32[]{:S(2)}) collective-permute-start(f32[2,8,8,128]{3,2,1,0:T(8,128)S(1)} %get-tuple-element.58), channel_id=1, source_target_pairs={{0,1},{2,3},{1,0},{3,2},{4,5},{6,7},{5,4},{7,6},{8,9},{10,11},{9,8... | collective-permute-start | bytes 196616 | tf_op jit(solution)/shard_map/ppermute | solution.py:676
  3.7 15.5 %collective-permute-start.1 = (f32[2,8,8,128]{3,2,1,0:T(8,128)S(1)}, f32[2,8,8,128]{3,2,1,0:T(8,128)S(1)}, u32[]{:S(2)}, u32[]{:S(2)}) collective-permute-start(f32[2,8,8,128]{3,2,1,0:T(8,128)S(1)} %get-tuple-element.59), channel_id=1, source_target_pairs={{1,2},{3,0},{2,1},{0,3},{5,6},{7,4},{6,5},{4,7},{9,10},{11,8},{10,... | collective-permute-start | bytes 196616 | tf_op jit(solution)/shard_map/ppermute | solution.py:676
  6.4 20.4 %copy-start.2 = (f32[8,128]{1,0:T(8,128)S(1)}, f32[8,128]{1,0:T(8,128)}, u32[]{:S(2)}) copy-start(f32[8,128]{1,0:T(8,128)} %constant.62.clone.wt_ref.refs_6_.refs_4_.refs_7_.refs_5_) | copy-start | bytes 12292
  14.2 19.0 %copy-start = (bf16[256,256]{1,0:T(8,128)(2,1)S(1)}, bf16[256,256]{1,0:T(8,128)(2,1)}, u32[]{:S(2)}) copy-start(bf16[256,256]{1,0:T(8,128)(2,1)} %constant.65.clone.refs_8_.refs_6_.refs_9_.refs_7_) | copy-start | bytes 393220
  14.2 19.0 %copy-start.1 = (bf16[256,256]{1,0:T(8,128)(2,1)S(1)}, bf16[256,256]{1,0:T(8,128)(2,1)}, u32[]{:S(2)}) copy-start(bf16[256,256]{1,0:T(8,128)(2,1)} %constant.64.clone.refs_7_.refs_8_.kf_ref) | copy-start | bytes 393220
  14.2 6.9 %collective-permute-start.2 = (bf16[528,128]{1,0:T(8,128)(2,1)}, bf16[528,128]{1,0:T(8,128)(2,1)S(1)}, u32[]{:S(2)}, u32[]{:S(2)}) collective-permute-start(bf16[528,128]{1,0:T(8,128)(2,1)} %get-tuple-element.62), channel_id=1, source_target_pairs={{0,1},{2,3},{4,5},{6,7},{8,9},{10,11},{12,13},{14,15},{16,17},{18,... | collective-permute-start | bytes 405512 | tf_op jit(solution)/shard_map/ppermute | solution.py:687
  14.3 8.5 %collective-permute-start.3 = (bf16[528,128]{1,0:T(8,128)(2,1)}, bf16[528,128]{1,0:T(8,128)(2,1)S(1)}, u32[]{:S(2)}, u32[]{:S(2)}) collective-permute-start(bf16[528,128]{1,0:T(8,128)(2,1)} %get-tuple-element.63), channel_id=1, source_target_pairs={{1,2},{3,4},{5,6},{7,8},{9,10},{11,12},{13,14},{15,16},{17,18},{19... | collective-permute-start | bytes 405512 | tf_op jit(solution)/shard_map/ppermute | solution.py:687
  18.8 7.9 %collective-permute-start.4 = (bf16[528,128]{1,0:T(8,128)(2,1)}, bf16[528,128]{1,0:T(8,128)(2,1)S(1)}, u32[]{:S(2)}, u32[]{:S(2)}) collective-permute-start(bf16[528,128]{1,0:T(8,128)(2,1)} %get-tuple-element.64), channel_id=1, source_target_pairs={{0,4},{1,5},{2,6},{3,7},{4,8},{5,9},{6,10},{7,11},{8,12},{9,13},{1... | collective-permute-start | bytes 405512 | tf_op jit(solution)/shard_map/ppermute | solution.py:681
  28.8 4.4 %collective-permute-start.5 = (f32[16,1152]{1,0:T(8,128)S(1)}, f32[16,1152]{1,0:T(8,128)S(1)}, u32[]{:S(2)}, u32[]{:S(2)}) collective-permute-start(f32[16,1152]{1,0:T(8,128)S(1)} %get-tuple-element.68), channel_id=1, source_target_pairs={{0,4},{1,5},{2,6},{3,7},{8,12},{9,13},{10,14},{11,15},{16,20},{17,... | collective-permute-start | bytes 221192 | tf_op jit(solution)/shard_map/ppermute | solution.py:670
  28.8 4.3 %collective-permute-start.6 = (f32[16,1152]{1,0:T(8,128)S(1)}, f32[16,1152]{1,0:T(8,128)S(1)}, u32[]{:S(2)}, u32[]{:S(2)}) collective-permute-start(f32[16,1152]{1,0:T(8,128)S(1)} %get-tuple-element.69), channel_id=1, source_target_pairs={{4,8},{5,9},{6,10},{7,11},{12,16},{13,17},{14,18},{15,19},{20,24},... | collective-permute-start | bytes 221192 | tf_op jit(solution)/shard_map/ppermute | solution.py:670
  37.2 1.9 %collective-permute-start.7 = (f32[17,8,128]{2,1,0:T(8,128)S(1)}, f32[17,8,128]{2,1,0:T(8,128)S(1)}, u32[]{:S(2)}, u32[]{:S(2)}) collective-permute-start(f32[17,8,128]{2,1,0:T(8,128)S(1)} %get-tuple-element.75), channel_id=1, source_target_pairs={{0,1},{2,3},{1,0},{3,2},{4,5},{6,7},{5,4},{7,6},{8,9},{10,11},{9,8... | collective-permute-start | bytes 208904 | tf_op jit(solution)/shard_map/ppermute | solution.py:676
  37.3 4.0 %collective-permute-start.8 = (f32[17,8,128]{2,1,0:T(8,128)S(1)}, f32[17,8,128]{2,1,0:T(8,128)S(1)}, u32[]{:S(2)}, u32[]{:S(2)}) collective-permute-start(f32[17,8,128]{2,1,0:T(8,128)S(1)} %get-tuple-element.76), channel_id=1, source_target_pairs={{1,2},{3,0},{2,1},{0,3},{5,6},{7,4},{6,5},{4,7},{9,10},{11,8},{10,... | collective-permute-start | bytes 208904 | tf_op jit(solution)/shard_map/ppermute | solution.py:676
  43.7 2.5 %collective-permute-start.9 = (f32[17,8,128]{2,1,0:T(8,128)S(1)}, f32[17,8,128]{2,1,0:T(8,128)S(1)}, u32[]{:S(2)}, u32[]{:S(2)}) collective-permute-start(f32[17,8,128]{2,1,0:T(8,128)S(1)} %get-tuple-element.84), channel_id=1, source_target_pairs={{0,1},{2,3},{1,0},{3,2},{4,5},{6,7},{5,4},{7,6},{8,9},{10,11},{9,8... | collective-permute-start | bytes 208904 | tf_op jit(solution)/shard_map/ppermute | solution.py:676
  44.2 4.2 %collective-permute-start.10 = (f32[17,8,128]{2,1,0:T(8,128)S(1)}, f32[17,8,128]{2,1,0:T(8,128)S(1)}, u32[]{:S(2)}, u32[]{:S(2)}) collective-permute-start(f32[17,8,128]{2,1,0:T(8,128)S(1)} %get-tuple-element.85), channel_id=1, source_target_pairs={{1,2},{3,0},{2,1},{0,3},{5,6},{7,4},{6,5},{4,7},{9,10},{11,8},{10,... | collective-permute-start | bytes 208904 | tf_op jit(solution)/shard_map/ppermute | solution.py:676
  51.0 2.1 %collective-permute-start.11 = (f32[17,8,128]{2,1,0:T(8,128)S(1)}, f32[17,8,128]{2,1,0:T(8,128)S(1)}, u32[]{:S(2)}, u32[]{:S(2)}) collective-permute-start(f32[17,8,128]{2,1,0:T(8,128)S(1)} %get-tuple-element.91), channel_id=1, source_target_pairs={{0,1},{2,3},{1,0},{3,2},{4,5},{6,7},{5,4},{7,6},{8,9},{10,11},{9,8... | collective-permute-start | bytes 208904 | tf_op jit(solution)/shard_map/ppermute | solution.py:676
  51.2 3.9 %collective-permute-start.12 = (f32[17,8,128]{2,1,0:T(8,128)S(1)}, f32[17,8,128]{2,1,0:T(8,128)S(1)}, u32[]{:S(2)}, u32[]{:S(2)}) collective-permute-start(f32[17,8,128]{2,1,0:T(8,128)S(1)} %get-tuple-element.92), channel_id=1, source_target_pairs={{1,2},{3,0},{2,1},{0,3},{5,6},{7,4},{6,5},{4,7},{9,10},{11,8},{10,... | collective-permute-start | bytes 208904 | tf_op jit(solution)/shard_map/ppermute | solution.py:676
  57.6 2.5 %collective-permute-start.13 = (f32[17,8,128]{2,1,0:T(8,128)S(1)}, f32[17,8,128]{2,1,0:T(8,128)S(1)}, u32[]{:S(2)}, u32[]{:S(2)}) collective-permute-start(f32[17,8,128]{2,1,0:T(8,128)S(1)} %get-tuple-element.98), channel_id=1, source_target_pairs={{0,1},{2,3},{1,0},{3,2},{4,5},{6,7},{5,4},{7,6},{8,9},{10,11},{9,8... | collective-permute-start | bytes 208904 | tf_op jit(solution)/shard_map/ppermute | solution.py:676
  58.0 4.2 %collective-permute-start.14 = (f32[17,8,128]{2,1,0:T(8,128)S(1)}, f32[17,8,128]{2,1,0:T(8,128)S(1)}, u32[]{:S(2)}, u32[]{:S(2)}) collective-permute-start(f32[17,8,128]{2,1,0:T(8,128)S(1)} %get-tuple-element.99), channel_id=1, source_target_pairs={{1,2},{3,0},{2,1},{0,3},{5,6},{7,4},{6,5},{4,7},{9,10},{11,8},{10,... | collective-permute-start | bytes 208904 | tf_op jit(solution)/shard_map/ppermute | solution.py:676

commit v5 on v4

--- a/solution.py
+++ b/solution.py
@@ -88,9 +88,9 @@
 def fluid_matrix():
     eye8 = np.eye(8)
     square = DERIV @ DERIV
-    second = np.kron(DERIV, eye8)
-    third = np.kron(eye8, DERIV)
-    curve = np.kron(square, eye8) + np.kron(eye8, square)
+    second = time_step * np.kron(DERIV, eye8)
+    third = time_step * np.kron(eye8, DERIV)
+    curve = np.eye(64) + time_step * viscosity * (np.kron(square, eye8) + np.kron(eye8, square))
     return np.concatenate([np.concatenate(split_hi_lo(np.kron(np.eye(2), m)), 1) for m in (second, third, curve)], 0)
 
 
@@ -140,42 +140,47 @@
     return [[float(GLL_W[r] * GLL_W[s]) * wt for s in range(8)] for r in range(8)]
 
 
+def in_three(x):
+    high = x.astype(bf16)
+    rest = x - high.astype(f32)
+    middle = rest.astype(bf16)
+    return [high, middle, (rest - middle.astype(f32)).astype(bf16)]
+
+
 def sel_matrix(l, first_lane):
     row = lax.broadcasted_iota(jnp.int32, (2 * RIM, LANES), 0)
     lane = lax.broadcasted_iota(jnp.int32, (2 * RIM, LANES), 1)
-    return ((row - l * RIM + first_lane == lane) & (row >= l * RIM) & (row < (l + 1) * RIM)).astype(f32)
+    inside = (row >= l * RIM) & (row < (l + 1) * RIM)
+    return ((row - l * RIM + first_lane == lane) & inside).astype(f32).astype(bf16)
 
 
 def place_matrix(first_lane):
     row = lax.broadcasted_iota(jnp.int32, (2 * RIM, LANES), 0)
     lane = lax.broadcasted_iota(jnp.int32, (2 * RIM, LANES), 1)
     target = jnp.where(row < RIM, row + first_lane, row - RIM + first_lane + LANES // 2)
-    return (target == lane).astype(f32)
+    return (target == lane).astype(f32).astype(bf16)
 
 
 def send_rims(tile_rows, na):
-    behind = sum(
-        lax.dot_general(sel_matrix(l, 0), tile_rows(l * na), NT, precision=highest, preferred_element_type=f32)
-        for l in range(2)
-    )
-    ahead = sum(
-        lax.dot_general(
-            sel_matrix(l, LANES - RIM), tile_rows(l * na + na - 1), NT, precision=highest, preferred_element_type=f32
-        )
-        for l in range(2)
-    )
-    return behind, ahead
+    def pick(tiles, first_lane):
+        out = None
+        for l, j in enumerate(tiles):
+            terms = jnp.concatenate(in_three(tile_rows(j)), 1)
+            sel = jnp.concatenate([sel_matrix(l, first_lane)] * 3, 1)
+            part = lax.dot_general(sel, terms, NT, preferred_element_type=f32)
+            out = part if out is None else out + part
+        return out
+
+    return pick((0, na), 0), pick((na - 1, 2 * na - 1), LANES - RIM)
 
 
 def place_rims(from_ahead, from_behind):
-    a = lax.dot_general(from_ahead, place_matrix(0), TN, precision=highest, preferred_element_type=f32)
-    b = lax.dot_general(
-        from_behind, place_matrix(LANES // 2 - RIM), TN, precision=highest, preferred_element_type=f32
-    )
-    return a + b
-
-
-def source_kernel(na, planes, par_ref, p_ref, q_ref, wr_ref, z_ref, a_ref, b_ref):
+    terms = jnp.concatenate(in_three(from_ahead) + in_three(from_behind), 0)
+    places = jnp.concatenate([place_matrix(0)] * 3 + [place_matrix(LANES // 2 - RIM)] * 3, 0)
+    return lax.dot_general(terms, places, TN, preferred_element_type=f32)
+
+
+def source_planes(na, planes, par_ref, p_ref, q_ref, wr_ref, z_ref, a_ref, b_ref):
     step = 2 * na
     for n in range(planes):
         r = pl.program_id(0) * planes + n
@@ -201,7 +206,7 @@
             send_faces(par_ref, (at, r), lower, upper, a_ref, b_ref)
 
 
-def rim_kernel(na, par_ref, z_in, a_ref, b_ref, dc_ref, z_ref, behind_ref, ahead_ref):
+def rim_kernel(na, par_ref, z_in, b_ref, a_ref, dc_ref, z_ref, behind_ref, ahead_ref):
     z_ref[...] = z_in[...]
     for r in range(8):
         for at in range(na):
@@ -328,58 +333,65 @@
         v[ghost, r, 7] = v[ghost, r, 7] + unpack_rim(upper, r, 1)
 
 
+def owners(l2s, me, total, chan):
+    elements = l2s.shape[1]
+    if elements & (elements - 1) == 0:
+        owner = lax.shift_right_logical(l2s, elements.bit_length() - 1)
+        slot = l2s & (elements - 1)
+    else:
+        owner = l2s // elements
+        slot = l2s - owner * elements
+    ahead = owner - me
+    ahead = jnp.where(ahead < 0, ahead + total, ahead)
+    group = jnp.where(ahead == 1, 1, jnp.where(ahead == total - 1, 2, jnp.where(ahead == chan, 3, 0)))
+    return slot, group
+
+
 def fluid_kernel(
-    chan, total, me_ref, u_ref, l2s_ref, k_ref, out_ref, own_ref, s1_ref, s2_ref, s3_ref, c_ref, t_ref
+    na, planes, chan, total, me_ref, par_ref, u_ref, l2s_ref, k_ref, p_ref, q_ref, wr_ref,
+    out_ref, cond_ref, s1_ref, s2_ref, s3_ref, z_ref, fa_ref, fb_ref, t_ref, uf_ref
 ):
     i = pl.program_id(0)
     k = k_ref[...]
-    square = DERIV @ DERIV
+    curve_matrix = time_step * viscosity * (DERIV @ DERIV)
+    slope_matrix = time_step * DERIV
     for c in range(3):
         for s in range(8):
-            parts = halves_of([u_ref[c, r, s].astype(f32) for r in range(8)])
-            slope = combined(DERIV, parts, -1)
-            curve = combined(square, parts, 1)
+            line = [u_ref[c, r, s].astype(f32) for r in range(8)]
             for r in range(8):
-                t_ref[c, r, s] = viscosity * curve[r] - u_ref[0, r, s].astype(f32) * slope[r]
+                uf_ref[c, r, s] = line[r]
+            parts = halves_of(line)
+            slope = combined(slope_matrix, parts, -1)
+            curve = combined(curve_matrix, parts, 1)
+            for r in range(8):
+                t_ref[c, r, s] = curve[r] - uf_ref[0, r, s] * slope[r]
     for p in range(2):
-        speed = [None] * 4
+        speed = [None] * 32
         for c in range(3):
-            x = u_ref[c, 4 * p : 4 * p + 4].astype(f32).reshape(2, 128, LANES)
+            x = uf_ref[c, 4 * p : 4 * p + 4].reshape(2, 128, LANES)
             x = jnp.concatenate([x[0], x[1]], 1).astype(bf16)
             y = jnp.dot(k, jnp.concatenate([x, x], 0), preferred_element_type=f32)
             for h in range(2):
                 part = y[:, h * LANES : (h + 1) * LANES].reshape(3, 2, 8, 8, LANES)
                 for q in range(2):
                     r = 4 * p + 2 * h + q
-                    second, third, curve = part[0, q], part[1, q], part[2, q]
-                    u2, u3 = u_ref[1, r].astype(f32), u_ref[2, r].astype(f32)
-                    rate = t_ref[c, r] + viscosity * curve - u2 * second - u3 * third
-                    new = (u_ref[c, r].astype(f32) + time_step * rate).astype(bf16)
-                    out_ref[c, r] = new
-                    new = new.astype(f32)
-                    old = speed[2 * h + q]
-                    speed[2 * h + q] = new * new if old is None else old + new * new
+                    for s in range(8):
+                        change = t_ref[c, r, s] - uf_ref[1, r, s] * part[0, q, s] - uf_ref[2, r, s] * part[1, q, s]
+                        new = (part[2, q, s] + change).astype(bf16)
+                        out_ref[c, r, s] = new
+                        new = new.astype(f32)
+                        n = (2 * h + q) * 8 + s
+                        speed[n] = new * new if speed[n] is None else speed[n] + new * new
         for n, value in enumerate(speed):
-            r = 4 * p + n
-            c_ref[i, r * 64 : (r + 1) * 64] = (1.0 + 0.5 * value).astype(bf16).reshape(64, LANES)
+            t_ref[0, 4 * p + n // 8, n % 8] = 1.0 + 0.5 * value
+    cond_ref[i] = t_ref[0].reshape(512, LANES).astype(bf16)
+    source_planes(na, planes, par_ref, p_ref, q_ref, wr_ref, z_ref, fa_ref, fb_ref)
 
     @pl.when(i == pl.num_programs(0) - 1)
     def _():
         elements = l2s_ref.shape[-1]
-        cond = jnp.concatenate([c_ref[n] for n in range(c_ref.shape[0])], 1)
-        l2s = l2s_ref[...]
-        if elements & (elements - 1) == 0:
-            owner = lax.shift_right_logical(l2s, elements.bit_length() - 1)
-            slot = l2s & (elements - 1)
-        else:
-            owner = l2s // elements
-            slot = l2s - owner * elements
-        ahead = owner - me_ref[0]
-        ahead = jnp.where(ahead < 0, ahead + total, ahead)
-        group = jnp.where(ahead == 1, 1, jnp.where(ahead == total - 1, 2, jnp.where(ahead == chan, 3, 0)))
-        place = lax.broadcasted_iota(jnp.int32, (elements, elements), 0)
-        keep = ((place == slot) & (group == 0)).astype(f32).astype(bf16)
-        own_ref[...] = lax.dot_general(cond, keep, NT, preferred_element_type=f32).astype(bf16)
+        cond = jnp.concatenate([cond_ref[n] for n in range(cond_ref.shape[0])], 1)
+        slot, group = owners(l2s_ref[...], me_ref[0], total, chan)
         kinds = lax.broadcasted_iota(jnp.int32, (16, elements), 0)
         marks = (kinds == group).astype(f32).astype(bf16)
         before = lax.broadcasted_iota(jnp.int32, (elements, elements), 0) < lax.broadcasted_iota(
@@ -403,6 +415,15 @@
         for g, order, ref in sends:
             take = ((position == order) & (group == g)).astype(f32).astype(bf16)
             ref[...] = lax.dot_general(tagged, take, NT, preferred_element_type=f32).astype(bf16)
+
+
+def keep_kernel(chan, total, me_ref, cond_ref, l2s_ref, own_ref):
+    elements = l2s_ref.shape[-1]
+    cond = jnp.concatenate([cond_ref[n] for n in range(cond_ref.shape[0])], 1)
+    slot, group = owners(l2s_ref[...], me_ref[0], total, chan)
+    place = lax.broadcasted_iota(jnp.int32, (elements, elements), 0)
+    keep = ((place == slot) & (group == 0)).astype(f32).astype(bf16)
+    own_ref[...] = lax.dot_general(cond, keep, NT, preferred_element_type=f32).astype(bf16)
 
 
 def unpack_kernel(
@@ -524,9 +545,9 @@
     take = lambda n: [refs.pop(0) for _ in range(n)]
     ghost = 2 * na
     if first:
-        par_ref, z_in, wk_ref, a_in, b_in, dc_ref = take(6)
+        par_ref, z_in, wk_ref, b_in, a_in, dc_ref = take(6)
     else:
-        par_ref, _, a_in, b_in, wk_ref, wkg_ref, cr_ref = take(7)
+        par_ref, _, b_in, a_in, wk_ref, wkg_ref, cr_ref = take(7)
     wt_ref, kf_ref, kb_ref, v, f1, f2, f3, a_out, b_out = take(9)
     if first:
         wkg_ref, cr_ref = take(2)
@@ -578,7 +599,7 @@
     assemble_lateral(na, y)
 
 
-def last_kernel(na, par_ref, _, a_in, b_in, wk_ref, cr_ref, prev, wt_ref, iw_ref, kf_ref, d0, d1, d2, d3, v, all_dots, g, base):
+def last_kernel(na, par_ref, _, b_in, a_in, wk_ref, cr_ref, prev, wt_ref, iw_ref, kf_ref, d0, d1, d2, d3, v, all_dots, g, base):
     ghost = 2 * na
     add_faces(na, par_ref, v, a_in, b_in)
     mass_rows(wt_ref[...], base)
@@ -756,43 +777,49 @@
     scalars = pl.BlockSpec(memory_space=pltpu.SMEM)
     steps = 4
     rows = 512 * tiles // steps
-    z, a, b = pl.pallas_call(
-        functools.partial(source_kernel, na, 8 // steps),
-        grid=(steps,),
-        in_specs=[scalars]
-        + [pl.BlockSpec((rows, LANES), lambda i: (i, 0))] * 2
-        + [pl.BlockSpec((8, 8, LANES), lambda i: (0, 0, 0))],
-        out_specs=[here()] * 3,
-        out_shape=[kept(field), kept((na, 8, 8, LANES)), kept((na, 8, 8, LANES))],
-        compiler_params=pltpu.CompilerParams(vmem_limit_bytes=12 * 1024 * 1024),
-    )(position, in_hbm(as_rows(previous_panel_warmth)), in_hbm(as_rows(pointwise_energy_source)), in_hbm(wr))
-    a, b = swap(a, "chan", 0), swap(b, "chan", 1)
-
-    velocity, z = lax.optimization_barrier((stream_speed_field, z))
+    l2s = liquid_to_solid_element.reshape(1, elements)
     out = pl.pallas_call(
-        functools.partial(fluid_kernel, chan, total),
+        functools.partial(fluid_kernel, na, 8 // split, chan, total),
         grid=(split,),
         in_specs=[
+            scalars,
             scalars,
             pl.BlockSpec((3, 8, 8, 8, width), lambda i: (0, 0, 0, 0, i)),
             pl.BlockSpec((1, elements), lambda i: (0, 0)),
             pl.BlockSpec(kfluid.shape, lambda i: (0, 0)),
-        ],
-        out_specs=[pl.BlockSpec((3, 8, 8, 8, width), lambda i: (0, 0, 0, 0, i))] + [here()] * 4,
-        out_shape=[shape(stream_speed_field.shape, bf16), kept((512, elements), bf16)]
-        + [kept((528, room), bf16)] * 3,
-        scratch_shapes=[pltpu.VMEM((split, 512, width), bf16), pltpu.VMEM((3, 8, 8, 8, width), f32)],
+        ]
+        + [pl.BlockSpec((512 * tiles // split, LANES), lambda i: (i, 0))] * 2
+        + [pl.BlockSpec((8, 8, LANES), lambda i: (0, 0, 0))],
+        out_specs=[pl.BlockSpec((3, 8, 8, 8, width), lambda i: (0, 0, 0, 0, i))] + [here()] * 7,
+        out_shape=[shape(stream_speed_field.shape, bf16), kept((split, 512, width), bf16)]
+        + [kept((528, room), bf16)] * 3
+        + [kept(field), kept((na, 8, 8, LANES)), kept((na, 8, 8, LANES))],
+        scratch_shapes=[pltpu.VMEM((3, 8, 8, 8, width), f32)] * 2,
         compiler_params=pltpu.CompilerParams(vmem_limit_bytes=24 * 1024 * 1024),
-    )(me, in_hbm(velocity), in_hbm(liquid_to_solid_element.reshape(1, elements)), in_hbm(kfluid))
-    stepped, own, *outgoing = out
-    received = [swap_around(outgoing[0], 0), swap_around(outgoing[1], 1), around(outgoing[2], chan)]
+    )(
+        me,
+        position,
+        in_hbm(stream_speed_field),
+        in_hbm(l2s),
+        in_hbm(kfluid),
+        in_hbm(as_rows(previous_panel_warmth)),
+        in_hbm(as_rows(pointwise_energy_source)),
+        in_hbm(wr),
+    )
+    stepped, cond, out_even, out_odd, out_far, z, a, b = out
+    received = [around(out_far, chan), swap_around(out_odd, 1), swap_around(out_even, 0)]
+    (own,) = call(
+        functools.partial(keep_kernel, chan, total), [kept((512, elements), bf16)], me, cond, l2s, smem=1
+    )
+    a, b, own = lax.optimization_barrier((a, b, own))
+    b, a = swap(b, "chan", 1), swap(a, "chan", 0)
     z, z_behind, z_ahead = call(
         functools.partial(rim_kernel, na),
         [kept(field), kept((2 * RIM, 640)), kept((2 * RIM, 640))],
         position,
         z,
+        b,
         a,
-        b,
         dc,
         smem=1,
     )
@@ -808,7 +835,7 @@
         z_ahead,
         smem=1,
     )
-    a, b = slab_swap(a, 0), slab_swap(b, 1)
+    b, a = slab_swap(b, 1), slab_swap(a, 0)
 
     basis, products = [], []
     face = (8 * na + 1, 8, LANES)
@@ -816,10 +843,10 @@
         first = number == 0
         outs = [kept(whole)] * 4 + [kept(face)] * 2
         if first:
-            args = (z, wk, a, b, dc)
+            args = (z, wk, b, a, dc)
             outs += [kept((8, 8, 8, LANES)), kept((tiles + 1, 8, LANES))]
         else:
-            args = (y, a, b, wk, wkg, cr)
+            args = (y, b, a, wk, wkg, cr)
         got = call(
             functools.partial(flux_kernel, na, first),
             outs,
@@ -835,7 +862,7 @@
         if first:
             wkg, cr = got[6:]
         v, f1, f2, f3, a, b = got[:6]
-        a, b = swap(a, "chan", 0), swap(b, "chan", 1)
+        b, a = swap(b, "chan", 1), swap(a, "chan", 0)
         y, dots = call(
             functools.partial(rest_kernel, na, first),
             [kept(whole), kept((2, 8, LANES))],
@@ -856,8 +883,8 @@
         [kept(whole), kept((total, 1, LANES))],
         position,
         y,
+        b,
         a,
-        b,
         wk,
         cr,
         basis[-1],

time: 76.8 us -> 71.8 us (0.935)
  Pallas kernels: 36.5 us -> 31.8 us
  waiting for transfers between devices: 18.3 us -> 14.5 us
  starting transfers between devices: 10 us -> 12 us
  blocking collectives: 10.3 us -> 11.9 us
    ppermute x1, waiting for transfers between devices: 3.94 us -> 0.01 us  [around(): lax.ppermute(x, ('slab', 'chan'), [(i, (i + by) % n) for i in range(n)])]
    ppermute x1, starting transfers between devices: 0.01 us -> 2.99 us  [around(): lax.ppermute(x, ('slab', 'chan'), [(i, (i + by) % n) for i in range(n)])]
    pallas_call x2 -> x1, Pallas kernels: 10.2 us -> 7.48 us  [on_device(): pl.pallas_call(functools.partial(fluid_kernel, na, 8 // split, chan, tota...]
    ppermute x10, waiting for transfers between devices: 8.45 us -> 11.1 us  [swap(): return lax.ppermute(x, axis, pairs + [(j, i) for i, j in pairs])]
    pallas_call x11 -> x12, Pallas kernels: 24.4 us -> 22.5 us  [call(): pl.pallas_call(kernel, in_specs=specs, out_specs=outs, out_shape=out_shap...]
    ppermute x2, waiting for transfers between devices: 1.7 us -> 0.02 us  [swap_around(): return lax.ppermute(x, ('slab', 'chan'), pairs + [(j, i) for i, j in pairs])]
    all_to_all x1, blocking collectives: 10.3 us -> 11.9 us  [on_device(): sums = lax.all_to_all(sums, ('slab', 'chan'), 0, 0)]
    ppermute x2, starting transfers between devices: 4.65 us -> 3.51 us  [swap_around(): return lax.ppermute(x, ('slab', 'chan'), pairs + [(j, i) for i, j in pairs])]
  transfers between devices with their start and end apart: 15 -> 15, of which waited for: 7 -> 6; matrix products, arithmetic and copies ran while one was open for 1% -> 1% of each run, Pallas kernels for 21% -> 12%
where the time goes in v5:
time: 71.8 us; the launch traced here: 71.6 us
  Pallas kernels  31.8 us (44%)
  waiting for transfers between devices  14.5 us (20%)
  starting transfers between devices  12 us (17%)
  blocking collectives  11.9 us (17%)
  between operations  0.86 us (1%)
    pallas_call x12, Pallas kernels, call(): pl.pallas_call(kernel, in_specs=specs, out_specs=outs, out_shape=out_shap...  22.5 us
    all_to_all x1, blocking collectives, on_device(): sums = lax.all_to_all(sums, ('slab', 'chan'), 0, 0)  11.9 us
    ppermute x10, waiting for transfers between devices, swap(): return lax.ppermute(x, axis, pairs + [(j, i) for i, j in pairs])  11.1 us
    pallas_call x1, Pallas kernels, on_device(): pl.pallas_call(functools.partial(fluid_kernel, na, 8 // split, chan, tota...  7.48 us
    ppermute x10, starting transfers between devices, swap(): return lax.ppermute(x, axis, pairs + [(j, i) for i, j in pairs])  4.26 us
    ppermute x2, starting transfers between devices, swap_around(): return lax.ppermute(x, ('slab', 'chan'), pairs + [(j, i) for i, j in pairs])  3.51 us
    ppermute x2, waiting for transfers between devices, slab_swap(): return lax.ppermute(x, ('slab', 'chan'), pairs + [(j, i) for i, j in pairs])  3.39 us
    ppermute x1, starting transfers between devices, around(): lax.ppermute(x, ('slab', 'chan'), [(i, (i + by) % n) for i in range(n)])  2.99 us
  transfers between devices with their start and end apart: 15, of which 6 were waited for; matrix products, arithmetic and copies ran while one was open for 1% of the time, Pallas kernels for 12%

profile of v5, /device:TPU:0, one launch (start us, length us, event | category | flops | bytes accessed | tf_op | source)
XLA Modules:
  0.0 71.6 jit_solution(4315814329569681286)
XLA Ops:
  0.7 0.1 stack.56.par_ref.refs_0_
  0.8 7.5 %shard_map.122 = (bf16[3,8,8,8,512]{4,3,2,1,0:T(8,128)(2,1)}, bf16[4,512,128]{2,1,0:T(8,128)(2,1)S(1)}, bf16[528,128]{1,0:T(8,128)(2,1)}, bf16[528,128]{1,0:T(8,...) custom-call(s32[1]{0:T(128)} %bitcast.me_ref, ...), custom_call_target="tpu_custom_call" | custom-call | tf_op jit(solution)/shard_map/pallas_call | solution.py:781
  8.2 3.0 %collective-permute-start.2 = (bf16[528,128]{1,0:T(8,128)(2,1)}, bf16[528,128]{1,0:T(8,128)(2,1)S(1)}, u32[]{:S(2)}, u32[]{:S(2)}) collective-permute-start(bf16[528,128]{1,0:T(8,128)(2,1)} %get-tuple-element.64), channel_id=1, source_target_pairs={{0,4},{1,5},{2,6},{3,7},{4,8},{5,9},{6,10},{7,11},{8,12},{9,13},{1... | collective-permute-start | bytes 405512 | tf_op jit(solution)/shard_map/ppermute | solution.py:702
  11.2 3.5 %collective-permute-start.3 = (bf16[528,128]{1,0:T(8,128)(2,1)}, bf16[528,128]{1,0:T(8,128)(2,1)S(1)}, u32[]{:S(2)}, u32[]{:S(2)}) collective-permute-start(bf16[528,128]{1,0:T(8,128)(2,1)} %get-tuple-element.65), channel_id=1, source_target_pairs={{1,2},{3,4},{5,6},{7,8},{9,10},{11,12},{13,14},{15,16},{17,18},{19... | collective-permute-start | bytes 405512 | tf_op jit(solution)/shard_map/ppermute | solution.py:708
  14.7 0.0 collective-permute-start.4
  14.8 0.5 shard_map.123.own_ref
  15.2 0.0 copy-start
  15.3 0.0 copy-start.1
  15.3 0.1 collective-permute-start
  15.4 0.6 collective-permute-start.1
  16.0 0.1 pad_maximum_fusion.2
  16.1 0.1 mul.55
  16.2 0.1 copy.22
  16.3 4.4 %collective-permute-done.b_ref = f32[2,8,8,128]{3,2,1,0:T(8,128)S(1)} collective-permute-done((f32[2,8,8,128]{3,2,1,0:T(8,128)S(1)}, f32[2,8,8,128]{3,2,1,0:T(8,128)S(1)}, u32[]{:S(2)}, u32[]{:S(2)}) %collective-permute-start) | collective-permute-done | bytes 65568 | tf_op jit(solution)/shard_map/ppermute | solution.py:697
  20.7 0.0 collective-permute-done.1.a_ref
  20.7 1.2 %shard_map.124 = (f32[4,8,8,8,128]{4,3,2,1,0:T(8,128)S(1)}, f32[16,640]{1,0:T(8,128)S(1)}, f32[16,640]{1,0:T(8,128)S(1)}) custom-call(s32[6]{0:T(128)S(1)} %stack.56.par_ref.refs_0_, f32[4,8,8,8,128]{4,3,2,1,0:T(8,128)S(1)} %get-tuple-element.56.z_in, f32[2,8,8,128]{3,2,1,0:T(8,128)S(1)} %collective-permute-done.b_ref, ...), custom_call_target="tpu_custom_call" | custom-call | tf_op jit(solution)/shard_map/pallas_call | solution.py:128
  21.9 0.0 collective-permute-done.2.r1_ref
  21.9 0.0 collective-permute-done.3.r2_ref
  21.9 1.6 %shard_map.125 = (f32[4,8,8,8,128]{4,3,2,1,0:T(8,128)S(1)}, f32[16,1152]{1,0:T(8,128)S(1)}, f32[16,1152]{1,0:T(8,128)S(1)}) custom-call(s32[6]{0:T(128)S(1)} %stack.56.par_ref.refs_0_, bf16[512,512]{1,0:T(8,128)(2,1)S(1)} %shard_map.123.own_ref, bf16[528,128]{1,0:T(8,128)(2,1)S(1)} %collective-permute-done.2.r1_ref, ...), custom_call_target="tpu_custom_call" | custom-call | tf_op jit(solution)/shard_map/pallas_call | solution.py:128
  23.5 0.2 collective-permute-start.5
  23.7 1.1 %collective-permute-start.6 = (f32[16,1152]{1,0:T(8,128)S(1)}, f32[16,1152]{1,0:T(8,128)S(1)}, u32[]{:S(2)}, u32[]{:S(2)}) collective-permute-start(f32[16,1152]{1,0:T(8,128)S(1)} %get-tuple-element.71), channel_id=1, source_target_pairs={{0,4},{1,5},{2,6},{3,7},{8,12},{9,13},{10,14},{11,15},{16,20},{17,... | collective-permute-start | bytes 221192 | tf_op jit(solution)/shard_map/ppermute | solution.py:691
  24.8 0.0 collective-permute-done.5.refs_3_
  24.8 3.4 %collective-permute-done.6.refs_4_ = f32[16,1152]{1,0:T(8,128)S(1)} collective-permute-done((f32[16,1152]{1,0:T(8,128)S(1)}, f32[16,1152]{1,0:T(8,128)S(1)}, u32[]{:S(2)}, u32[]{:S(2)}) %collective-permute-start.6) | collective-permute-done | bytes 73760 | tf_op jit(solution)/shard_map/ppermute | solution.py:691
  28.2 2.8 %shard_map.126 = (f32[5,8,8,8,128]{4,3,2,1,0:T(8,128)S(1)}, f32[5,8,8,8,128]{4,3,2,1,0:T(8,128)S(1)}, f32[5,8,8,8,128]{4,3,2,1,0:T(8,128)S(1)}, f32[5,8,8,8,128]...) custom-call(s32[6]{0:T(128)S(1)} %stack.56.par_ref.refs_0_, ...), custom_call_target="tpu_custom_call" | custom-call | tf_op jit(solution)/shard_map/pallas_call | solution.py:128
  31.0 0.5 collective-permute-start.7
  31.5 0.5 collective-permute-start.8
  32.0 0.1 multiply_bitcast_fusion
  32.1 1.6 %shard_map.127 = (f32[5,8,8,8,128]{4,3,2,1,0:T(8,128)S(1)}, f32[2,8,128]{2,1,0:T(8,128)S(1)}) custom-call(f32[5,8,8,8,128]{4,3,2,1,0:T(8,128)S(1)} %get-tuple-element.72.refs_0_.v0, f32[5,8,8,8,128]{4,3,2,1,0:T(8,128)S(1)} %get-tuple-element.73.refs_1_, f32[5,8,8,8,128]{4,3,2,1,0:T(8,128)S(1)} %get-tuple-element.74.refs_2_, ...), custom_call_target="tpu_custom_call" | custom-call | tf_op jit(solution)/shard_map/pallas_call | solution.py:128
  33.7 1.6 %collective-permute-done.7.refs_2_ = f32[17,8,128]{2,1,0:T(8,128)S(1)} collective-permute-done((f32[17,8,128]{2,1,0:T(8,128)S(1)}, f32[17,8,128]{2,1,0:T(8,128)S(1)}, u32[]{:S(2)}, u32[]{:S(2)}) %collective-permute-start.7) | collective-permute-done | bytes 69664 | tf_op jit(solution)/shard_map/ppermute | solution.py:697
  35.3 2.5 %shard_map.128 = (f32[5,8,8,8,128]{4,3,2,1,0:T(8,128)S(1)}, f32[5,8,8,8,128]{4,3,2,1,0:T(8,128)S(1)}, f32[5,8,8,8,128]{4,3,2,1,0:T(8,128)S(1)}, f32[5,8,8,8,128]...) custom-call(s32[6]{0:T(128)S(1)} %stack.56.par_ref.refs_0_, ...), custom_call_target="tpu_custom_call", output_to_operand_aliasing={{0}: (1, {})} | custom-call | tf_op jit(solution)/shard_map/pallas_call | solution.py:128
  37.8 0.7 collective-permute-start.9
  38.4 0.4 collective-permute-start.10
  38.8 1.7 %shard_map.129 = (f32[5,8,8,8,128]{4,3,2,1,0:T(8,128)S(1)}, f32[2,8,128]{2,1,0:T(8,128)S(1)}) custom-call(f32[5,8,8,8,128]{4,3,2,1,0:T(8,128)S(1)} %get-tuple-element.72.refs_0_.v0, f32[5,8,8,8,128]{4,3,2,1,0:T(8,128)S(1)} %get-tuple-element.81.refs_1_.refs_0_.v1, f32[5,8,8,8,128]{4,3,2,1,0:T(8,128)S(1)} %get-tuple-element.82.refs_2_, ...), custom_call_target="tpu_custom_call" | custom-call | tf_op jit(solution)/shard_map/pallas_call | solution.py:128
  40.5 1.8 %collective-permute-done.9.refs_2_ = f32[17,8,128]{2,1,0:T(8,128)S(1)} collective-permute-done((f32[17,8,128]{2,1,0:T(8,128)S(1)}, f32[17,8,128]{2,1,0:T(8,128)S(1)}, u32[]{:S(2)}, u32[]{:S(2)}) %collective-permute-start.9) | collective-permute-done | bytes 69664 | tf_op jit(solution)/shard_map/ppermute | solution.py:697
  42.3 2.4 %shard_map.130 = (f32[5,8,8,8,128]{4,3,2,1,0:T(8,128)S(1)}, f32[5,8,8,8,128]{4,3,2,1,0:T(8,128)S(1)}, f32[5,8,8,8,128]{4,3,2,1,0:T(8,128)S(1)}, f32[5,8,8,8,128]...) custom-call(s32[6]{0:T(128)S(1)} %stack.56.par_ref.refs_0_, ...), custom_call_target="tpu_custom_call", output_to_operand_aliasing={{0}: (1, {})} | custom-call | tf_op jit(solution)/shard_map/pallas_call | solution.py:128
  44.8 0.4 collective-permute-start.11
  45.1 0.4 collective-permute-start.12
  45.5 1.9 %shard_map.131 = (f32[5,8,8,8,128]{4,3,2,1,0:T(8,128)S(1)}, f32[2,8,128]{2,1,0:T(8,128)S(1)}) custom-call(f32[5,8,8,8,128]{4,3,2,1,0:T(8,128)S(1)} %get-tuple-element.81.refs_1_.refs_0_.v1, f32[5,8,8,8,128]{4,3,2,1,0:T(8,128)S(1)} %get-tuple-element.88.refs_1_.refs_0_.v2, f32[5,8,8,8,128]{4,3,2,1,0:T(8,128)S(1)} %get-tuple-element.89.refs_2_, ...), custom_call_target="tpu_custom_call" | custom-call | tf_op jit(solution)/shard_map/pallas_call | solution.py:128
  47.4 1.6 %collective-permute-done.11.refs_2_ = f32[17,8,128]{2,1,0:T(8,128)S(1)} collective-permute-done((f32[17,8,128]{2,1,0:T(8,128)S(1)}, f32[17,8,128]{2,1,0:T(8,128)S(1)}, u32[]{:S(2)}, u32[]{:S(2)}) %collective-permute-start.11) | collective-permute-done | bytes 69664 | tf_op jit(solution)/shard_map/ppermute | solution.py:697
  49.0 0.0 collective-permute-done.12.refs_3_
  49.0 2.4 %shard_map.132 = (f32[5,8,8,8,128]{4,3,2,1,0:T(8,128)S(1)}, f32[5,8,8,8,128]{4,3,2,1,0:T(8,128)S(1)}, f32[5,8,8,8,128]{4,3,2,1,0:T(8,128)S(1)}, f32[5,8,8,8,128]...) custom-call(s32[6]{0:T(128)S(1)} %stack.56.par_ref.refs_0_, ...), custom_call_target="tpu_custom_call", output_to_operand_aliasing={{0}: (1, {})} | custom-call | tf_op jit(solution)/shard_map/pallas_call | solution.py:128
  51.4 0.4 collective-permute-start.13
  51.9 0.4 collective-permute-start.14
  52.3 1.7 %shard_map.133 = (f32[5,8,8,8,128]{4,3,2,1,0:T(8,128)S(1)}, f32[2,8,128]{2,1,0:T(8,128)S(1)}) custom-call(f32[5,8,8,8,128]{4,3,2,1,0:T(8,128)S(1)} %get-tuple-element.88.refs_1_.refs_0_.v2, f32[5,8,8,8,128]{4,3,2,1,0:T(8,128)S(1)} %get-tuple-element.95.refs_1_.prev.v3, f32[5,8,8,8,128]{4,3,2,1,0:T(8,128)S(1)} %get-tuple-element.96.refs_2_, ...), custom_call_target="tpu_custom_call" | custom-call | tf_op jit(solution)/shard_map/pallas_call | solution.py:128
  54.0 1.7 %collective-permute-done.13.b_in = f32[17,8,128]{2,1,0:T(8,128)S(1)} collective-permute-done((f32[17,8,128]{2,1,0:T(8,128)S(1)}, f32[17,8,128]{2,1,0:T(8,128)S(1)}, u32[]{:S(2)}, u32[]{:S(2)}) %collective-permute-start.13) | collective-permute-done | bytes 69664 | tf_op jit(solution)/shard_map/ppermute | solution.py:697
  55.7 2.2 %shard_map.134 = (f32[5,8,8,8,128]{4,3,2,1,0:T(8,128)S(1)}, f32[32,1,128]{2,1,0:T(1,128)S(1)}) custom-call(s32[6]{0:T(128)S(1)} %stack.56.par_ref.refs_0_, f32[5,8,8,8,128]{4,3,2,1,0:T(8,128)S(1)} %get-tuple-element.99._, f32[17,8,128]{2,1,0:T(8,128)S(1)} %collective-permute-done.13.b_in, ...), custom_call_target="tpu_custom_call", output_to_operand_aliasing={{0}: (1, {})} | custom-call | tf_op jit(solution)/shard_map/pallas_call | solution.py:128
  57.9 11.9 %all_to_all.5.m_ref = f32[32,1,128]{2,1,0:T(1,128)S(1)} all-to-all(f32[32,1,128]{2,1,0:T(1,128)S(1)} %get-tuple-element.106), channel_id=1, replica_groups=mesh['slab'=8,'chan'=4] {'slab','chan'}, dimensions={0} | all-to-all | bytes 32768 | tf_op jit(solution)/shard_map/all_to_all | solution.py:900
  69.8 1.8 %shard_map.135 = f32[2048,128]{1,0:T(8,128)} custom-call(f32[32,1,128]{2,1,0:T(1,128)S(1)} %all_to_all.5.m_ref, f32[5,8,8,8,128]{4,3,2,1,0:T(8,128)S(1)} %get-tuple-element.72.refs_0_.v0, f32[5,8,8,8,128]{4,3,2,1,0:T(8,128)S(1)} %get-tuple-element.81.refs_1_.refs_0_.v1, f32[5,8,8,8,128]{4,3,2,1,0:T(8,128)S(1)} %get-tuple-element.88.refs_1_.refs_0_.v2, ...), custom_call_target="tpu_custom_call" | custom-call | tf_op jit(solution)/shard_map/pallas_call | solution.py:901
  (28 shorter events, 0.1 us)
Async XLA Ops:
  0.7 14.0 %copy-start.3 = (s32[512]{0:T(512)S(1)}, s32[512]{0:T(512)}, u32[]{:S(2)}) copy-start(s32[512]{0:T(512)} %param.12) | copy-start | bytes 6148
  0.7 15.2 %copy-start.4 = (s32[2,256]{1,0:T(2,128)S(1)}, s32[2,256]{1,0:T(2,128)}, u32[]{:S(2)}) copy-start(s32[2,256]{1,0:T(2,128)} %param.16) | copy-start | bytes 6148
  0.7 15.2 %copy-start.5 = (s32[2,256]{1,0:T(2,128)S(1)}, s32[2,256]{1,0:T(2,128)}, u32[]{:S(2)}) copy-start(s32[2,256]{1,0:T(2,128)} %param.15) | copy-start | bytes 6148
  8.2 13.7 %copy-start.2 = (f32[8,128]{1,0:T(8,128)S(1)}, f32[8,128]{1,0:T(8,128)}, u32[]{:S(2)}) copy-start(f32[8,128]{1,0:T(8,128)} %constant.62.clone.wt_ref.refs_6_.refs_4_.refs_7_.refs_5_) | copy-start | bytes 12292
  8.2 13.6 %collective-permute-start.2 = (bf16[528,128]{1,0:T(8,128)(2,1)}, bf16[528,128]{1,0:T(8,128)(2,1)S(1)}, u32[]{:S(2)}, u32[]{:S(2)}) collective-permute-start(bf16[528,128]{1,0:T(8,128)(2,1)} %get-tuple-element.64), channel_id=1, source_target_pairs={{0,4},{1,5},{2,6},{3,7},{4,8},{5,9},{6,10},{7,11},{8,12},{9,13},{1... | collective-permute-start | bytes 405512 | tf_op jit(solution)/shard_map/ppermute | solution.py:702
  11.2 10.7 %collective-permute-start.3 = (bf16[528,128]{1,0:T(8,128)(2,1)}, bf16[528,128]{1,0:T(8,128)(2,1)S(1)}, u32[]{:S(2)}, u32[]{:S(2)}) collective-permute-start(bf16[528,128]{1,0:T(8,128)(2,1)} %get-tuple-element.65), channel_id=1, source_target_pairs={{1,2},{3,4},{5,6},{7,8},{9,10},{11,12},{13,14},{15,16},{17,18},{19... | collective-permute-start | bytes 405512 | tf_op jit(solution)/shard_map/ppermute | solution.py:708
  14.7 7.2 %collective-permute-start.4 = (bf16[528,128]{1,0:T(8,128)(2,1)}, bf16[528,128]{1,0:T(8,128)(2,1)S(1)}, u32[]{:S(2)}, u32[]{:S(2)}) collective-permute-start(bf16[528,128]{1,0:T(8,128)(2,1)} %get-tuple-element.66), channel_id=1, source_target_pairs={{0,1},{2,3},{4,5},{6,7},{8,9},{10,11},{12,13},{14,15},{16,17},{18,... | collective-permute-start | bytes 405512 | tf_op jit(solution)/shard_map/ppermute | solution.py:708
  15.2 12.9 %copy-start = (bf16[256,256]{1,0:T(8,128)(2,1)S(1)}, bf16[256,256]{1,0:T(8,128)(2,1)}, u32[]{:S(2)}) copy-start(bf16[256,256]{1,0:T(8,128)(2,1)} %constant.65.clone.refs_8_.refs_6_.refs_9_.refs_7_) | copy-start | bytes 393220
  15.3 12.9 %copy-start.1 = (bf16[256,256]{1,0:T(8,128)(2,1)S(1)}, bf16[256,256]{1,0:T(8,128)(2,1)}, u32[]{:S(2)}) copy-start(bf16[256,256]{1,0:T(8,128)(2,1)} %constant.64.clone.refs_7_.refs_8_.kf_ref) | copy-start | bytes 393220
  15.3 5.4 %collective-permute-start = (f32[2,8,8,128]{3,2,1,0:T(8,128)S(1)}, f32[2,8,8,128]{3,2,1,0:T(8,128)S(1)}, u32[]{:S(2)}, u32[]{:S(2)}) collective-permute-start(f32[2,8,8,128]{3,2,1,0:T(8,128)S(1)} %get-tuple-element.60), channel_id=1, source_target_pairs={{1,2},{3,0},{2,1},{0,3},{5,6},{7,4},{6,5},{4,7},{9,10},{11,8},{10,... | collective-permute-start | bytes 196616 | tf_op jit(solution)/shard_map/ppermute | solution.py:697
  15.4 5.3 %collective-permute-start.1 = (f32[2,8,8,128]{3,2,1,0:T(8,128)S(1)}, f32[2,8,8,128]{3,2,1,0:T(8,128)S(1)}, u32[]{:S(2)}, u32[]{:S(2)}) collective-permute-start(f32[2,8,8,128]{3,2,1,0:T(8,128)S(1)} %get-tuple-element.61), channel_id=1, source_target_pairs={{0,1},{2,3},{1,0},{3,2},{4,5},{6,7},{5,4},{7,6},{8,9},{10,11},{9,8... | collective-permute-start | bytes 196616 | tf_op jit(solution)/shard_map/ppermute | solution.py:697
  23.5 1.3 %collective-permute-start.5 = (f32[16,1152]{1,0:T(8,128)S(1)}, f32[16,1152]{1,0:T(8,128)S(1)}, u32[]{:S(2)}, u32[]{:S(2)}) collective-permute-start(f32[16,1152]{1,0:T(8,128)S(1)} %get-tuple-element.70), channel_id=1, source_target_pairs={{4,8},{5,9},{6,10},{7,11},{12,16},{13,17},{14,18},{15,19},{20,24},... | collective-permute-start | bytes 221192 | tf_op jit(solution)/shard_map/ppermute | solution.py:691
  23.7 4.5 %collective-permute-start.6 = (f32[16,1152]{1,0:T(8,128)S(1)}, f32[16,1152]{1,0:T(8,128)S(1)}, u32[]{:S(2)}, u32[]{:S(2)}) collective-permute-start(f32[16,1152]{1,0:T(8,128)S(1)} %get-tuple-element.71), channel_id=1, source_target_pairs={{0,4},{1,5},{2,6},{3,7},{8,12},{9,13},{10,14},{11,15},{16,20},{17,... | collective-permute-start | bytes 221192 | tf_op jit(solution)/shard_map/ppermute | solution.py:691
  31.0 4.3 %collective-permute-start.7 = (f32[17,8,128]{2,1,0:T(8,128)S(1)}, f32[17,8,128]{2,1,0:T(8,128)S(1)}, u32[]{:S(2)}, u32[]{:S(2)}) collective-permute-start(f32[17,8,128]{2,1,0:T(8,128)S(1)} %get-tuple-element.77), channel_id=1, source_target_pairs={{1,2},{3,0},{2,1},{0,3},{5,6},{7,4},{6,5},{4,7},{9,10},{11,8},{10,... | collective-permute-start | bytes 208904 | tf_op jit(solution)/shard_map/ppermute | solution.py:697
  31.5 3.8 %collective-permute-start.8 = (f32[17,8,128]{2,1,0:T(8,128)S(1)}, f32[17,8,128]{2,1,0:T(8,128)S(1)}, u32[]{:S(2)}, u32[]{:S(2)}) collective-permute-start(f32[17,8,128]{2,1,0:T(8,128)S(1)} %get-tuple-element.78), channel_id=1, source_target_pairs={{0,1},{2,3},{1,0},{3,2},{4,5},{6,7},{5,4},{7,6},{8,9},{10,11},{9,8... | collective-permute-start | bytes 208904 | tf_op jit(solution)/shard_map/ppermute | solution.py:697
  37.8 4.5 %collective-permute-start.9 = (f32[17,8,128]{2,1,0:T(8,128)S(1)}, f32[17,8,128]{2,1,0:T(8,128)S(1)}, u32[]{:S(2)}, u32[]{:S(2)}) collective-permute-start(f32[17,8,128]{2,1,0:T(8,128)S(1)} %get-tuple-element.86), channel_id=1, source_target_pairs={{1,2},{3,0},{2,1},{0,3},{5,6},{7,4},{6,5},{4,7},{9,10},{11,8},{10,... | collective-permute-start | bytes 208904 | tf_op jit(solution)/shard_map/ppermute | solution.py:697
  38.4 3.9 %collective-permute-start.10 = (f32[17,8,128]{2,1,0:T(8,128)S(1)}, f32[17,8,128]{2,1,0:T(8,128)S(1)}, u32[]{:S(2)}, u32[]{:S(2)}) collective-permute-start(f32[17,8,128]{2,1,0:T(8,128)S(1)} %get-tuple-element.87), channel_id=1, source_target_pairs={{0,1},{2,3},{1,0},{3,2},{4,5},{6,7},{5,4},{7,6},{8,9},{10,11},{9,8... | collective-permute-start | bytes 208904 | tf_op jit(solution)/shard_map/ppermute | solution.py:697
  44.8 4.2 %collective-permute-start.11 = (f32[17,8,128]{2,1,0:T(8,128)S(1)}, f32[17,8,128]{2,1,0:T(8,128)S(1)}, u32[]{:S(2)}, u32[]{:S(2)}) collective-permute-start(f32[17,8,128]{2,1,0:T(8,128)S(1)} %get-tuple-element.93), channel_id=1, source_target_pairs={{1,2},{3,0},{2,1},{0,3},{5,6},{7,4},{6,5},{4,7},{9,10},{11,8},{10,... | collective-permute-start | bytes 208904 | tf_op jit(solution)/shard_map/ppermute | solution.py:697
  45.1 3.9 %collective-permute-start.12 = (f32[17,8,128]{2,1,0:T(8,128)S(1)}, f32[17,8,128]{2,1,0:T(8,128)S(1)}, u32[]{:S(2)}, u32[]{:S(2)}) collective-permute-start(f32[17,8,128]{2,1,0:T(8,128)S(1)} %get-tuple-element.94), channel_id=1, source_target_pairs={{0,1},{2,3},{1,0},{3,2},{4,5},{6,7},{5,4},{7,6},{8,9},{10,11},{9,8... | collective-permute-start | bytes 208904 | tf_op jit(solution)/shard_map/ppermute | solution.py:697
  51.4 4.2 %collective-permute-start.13 = (f32[17,8,128]{2,1,0:T(8,128)S(1)}, f32[17,8,128]{2,1,0:T(8,128)S(1)}, u32[]{:S(2)}, u32[]{:S(2)}) collective-permute-start(f32[17,8,128]{2,1,0:T(8,128)S(1)} %get-tuple-element.100), channel_id=1, source_target_pairs={{1,2},{3,0},{2,1},{0,3},{5,6},{7,4},{6,5},{4,7},{9,10},{11,8},{10,... | collective-permute-start | bytes 208904 | tf_op jit(solution)/shard_map/ppermute | solution.py:697
  51.9 3.8 %collective-permute-start.14 = (f32[17,8,128]{2,1,0:T(8,128)S(1)}, f32[17,8,128]{2,1,0:T(8,128)S(1)}, u32[]{:S(2)}, u32[]{:S(2)}) collective-permute-start(f32[17,8,128]{2,1,0:T(8,128)S(1)} %get-tuple-element.101), channel_id=1, source_target_pairs={{0,1},{2,3},{1,0},{3,2},{4,5},{6,7},{5,4},{7,6},{8,9},{10,11},{9,8... | collective-permute-start | bytes 208904 | tf_op jit(solution)/shard_map/ppermute | solution.py:697

commit v6 on v5

--- a/solution.py
+++ b/solution.py
@@ -206,7 +206,7 @@
             send_faces(par_ref, (at, r), lower, upper, a_ref, b_ref)
 
 
-def rim_kernel(na, par_ref, z_in, b_ref, a_ref, dc_ref, z_ref, behind_ref, ahead_ref):
+def rim_kernel(na, par_ref, z_in, b_ref, a_ref, dc_ref, wkb_ref, wka_ref, z_ref, a_out, b_out):
     z_ref[...] = z_in[...]
     for r in range(8):
         for at in range(na):
@@ -218,7 +218,12 @@
         cross = jnp.broadcast_to(dc_ref[1:2, j * LANES : (j + 1) * LANES], (LANES, LANES))
         return jnp.concatenate([z_ref[j].reshape(512, LANES), cross], 0)
 
-    behind_ref[...], ahead_ref[...] = send_rims(tile_rows, na)
+    behind, ahead = send_rims(tile_rows, na)
+    behind = jnp.where(par_ref[3] > 0, jnp.concatenate([behind, wkb_ref[...]], 1), 0.0)
+    ahead = jnp.where(par_ref[4] > 0, jnp.concatenate([ahead, wka_ref[...]], 1), 0.0)
+    even = par_ref[5] == 0
+    a_out[...] = jnp.where(even, ahead, behind)
+    b_out[...] = jnp.where(even, behind, ahead)
 
 
 def send_faces(par_ref, at, lower, upper, a_ref, b_ref):
@@ -426,9 +431,7 @@
     own_ref[...] = lax.dot_general(cond, keep, NT, preferred_element_type=f32).astype(bf16)
 
 
-def unpack_kernel(
-    na, par_ref, own_ref, r1_ref, r2_ref, r3_ref, dc_ref, wt_ref, zb_ref, za_ref, wk_ref, a_ref, b_ref
-):
+def unpack_kernel(na, own_ref, r1_ref, r2_ref, r3_ref, dc_ref, wt_ref, wk_ref, behind_ref, ahead_ref):
     rows = weight_rows(wt_ref[...] * KRYLOV_SCALE)
     got = jnp.concatenate([r[0:512] for r in (r1_ref, r2_ref, r3_ref)], 1)
     tags = [r[512:528].astype(f32) for r in (r1_ref, r2_ref, r3_ref)]
@@ -443,12 +446,7 @@
         for r in range(8):
             for s in range(8):
                 wk_ref[j, r, s] = rows[r][s] * kappa[r, s]
-    behind, ahead = send_rims(lambda j: wk_ref[j].reshape(512, LANES), na)
-    behind = jnp.where(par_ref[3] > 0, jnp.concatenate([zb_ref[...], behind], 1), 0.0)
-    ahead = jnp.where(par_ref[4] > 0, jnp.concatenate([za_ref[...], ahead], 1), 0.0)
-    even = par_ref[5] == 0
-    a_ref[...] = jnp.where(even, ahead, behind)
-    b_ref[...] = jnp.where(even, behind, ahead)
+    behind_ref[...], ahead_ref[...] = send_rims(lambda j: wk_ref[j].reshape(512, LANES), na)
 
 
 def lines_t(k_ref, blocks):
@@ -491,10 +489,7 @@
             g[r, s] = value
 
 
-def fluxes(v, j, wk, c, kf_ref, g, f1, f2, f3):
-    for p, part in enumerate(lines_t(kf_ref, blocks_of(v[j]))):
-        for q in range(2):
-            f3[j, 2 * p + q] = wk(2 * p + q) * part[q]
+def fluxes(v, j, wk, c, g, f1, f2):
     gradient_r(v, j, g)
     for r in range(8):
         second = along(DERIV, [v[j, r, s] for s in range(8)])
@@ -505,17 +500,25 @@
             f1[j, r, s] = k[s] * (first + c * second[s])
 
 
-def lateral_faces(na, par_ref, v, f1, f2, f3, base, kb_ref, a_ref, b_ref):
+def lateral_faces(na, par_ref, v, wk, f1, f2, base, kf_ref, kb_ref, a_ref, b_ref):
     rows = [[(l * na + at, 7 * l) for at in range(na)] + [(2 * na, 7 * l)] for l in range(2)]
     flat = rows[0] + rows[1]
-    blocks = []
-    for n in range(0, len(flat), 2):
-        pair = [f3[j, :, s].reshape(64, LANES) for j, s in flat[n : n + 2]]
-        blocks.append(jnp.concatenate(pair, 0))
-    thirds = []
-    for part in lines_t(kb_ref, blocks):
-        part = part.reshape(2, 8, 8, LANES)
-        thirds += [part[0], part[1]]
+
+    def lines(k_ref, xs):
+        blocks = []
+        for n in range(0, len(xs), 2):
+            blocks.append(jnp.concatenate([x.reshape(64, LANES) for x in xs[n : n + 2]], 0))
+        out = []
+        for part in lines_t(k_ref, blocks):
+            part = part.reshape(2, 8, 8, LANES)
+            out += [part[0], part[1]]
+        return out
+
+    thirds = lines(kf_ref, [v[j, :, s] for j, s in flat])
+    scaled = []
+    for (j, s), third in zip(flat, thirds):
+        scaled.append(jnp.stack([wk(j, r, s) * third[r] for r in range(8)]))
+    thirds = lines(kb_ref, scaled)
     faces = []
     for (j, s), third in zip(flat, thirds):
         first = along(DERIV.T, [f1[j, r, s] for r in range(8)])
@@ -548,7 +551,7 @@
         par_ref, z_in, wk_ref, b_in, a_in, dc_ref = take(6)
     else:
         par_ref, _, b_in, a_in, wk_ref, wkg_ref, cr_ref = take(7)
-    wt_ref, kf_ref, kb_ref, v, f1, f2, f3, a_out, b_out = take(9)
+    wt_ref, kf_ref, kb_ref, v, f1, f2, a_out, b_out = take(8)
     if first:
         wkg_ref, cr_ref = take(2)
     g, base = refs
@@ -571,14 +574,15 @@
             wk = lambda r: wk_ref[j, r]
         else:
             wk = lambda r: wkg_ref[r]
-        fluxes(v, j, wk, cr_ref[j], kf_ref, g.at[j % 2], f1, f2, f3)
-    lateral_faces(na, par_ref, v, f1, f2, f3, base, kb_ref, a_out, b_out)
+        fluxes(v, j, wk, cr_ref[j], g.at[j % 2], f1, f2)
+    face_wk = lambda j, r, s: wk_ref[j, r, s] if j < ghost else wkg_ref[r, s]
+    lateral_faces(na, par_ref, v, face_wk, f1, f2, base, kf_ref, kb_ref, a_out, b_out)
 
 
 def rest_kernel(na, first, *refs):
     refs = list(refs)
     prev = None if first else refs.pop(0)
-    v, f1, f2, f3, wt_ref, iw_ref, kb_ref, y, dots, base = refs
+    v, f1, f2, wk_ref, wkg_ref, wt_ref, iw_ref, kf_ref, kb_ref, y, dots, base, f3 = refs
     ghost = 2 * na
     mass_rows(wt_ref[...], base)
     totals = None
@@ -586,7 +590,11 @@
         if j < ghost:
             sums = squares(v, j, prev, iw_ref)
             totals = sums if totals is None else [a + b for a, b in zip(totals, sums)]
-        parts = lines_t(kb_ref, blocks_of(f3[j]))
+        for p, part in enumerate(lines_t(kf_ref, blocks_of(v[j]))):
+            for q in range(2):
+                r = 2 * p + q
+                f3[j % 2, r] = (wk_ref[j, r] if j < ghost else wkg_ref[r]) * part[q]
+        parts = lines_t(kb_ref, blocks_of(f3[j % 2]))
         for r in range(8):
             for s, value in enumerate(along(DERIV.T, [f2[j, r, s] for s in range(8)])):
                 y[j, r, s] = value + (base[r] * float(GLL_W[s])) * v[j, r, s]
@@ -594,7 +602,7 @@
             for r, value in enumerate(along(DERIV.T, [f1[j, r, s] for r in range(8)])):
                 y[j, r, s] = y[j, r, s] + value + parts[r // 2][r % 2, s]
     for k, value in enumerate(totals):
-        dots[k] = value
+        dots[k] = jnp.broadcast_to(jnp.sum(jnp.sum(value, 0, keepdims=True), 1, keepdims=True), (8, LANES))
     assemble_axial(na, y)
     assemble_lateral(na, y)
 
@@ -627,7 +635,11 @@
     rows = [d0[0], d1[1], d1[0], d2[1], d2[0], d3[1], d3[0], totals[1], totals[0], totals[2]]
     out = jnp.zeros((1, LANES), f32)
     for k, row in enumerate(rows):
-        out = jnp.where(lane == k, jnp.sum(jnp.sum(row, 0, keepdims=True), 1, keepdims=True), out)
+        if k < 2 * ITERS - 3:
+            row = row[0:1]
+        else:
+            row = jnp.sum(jnp.sum(row, 0, keepdims=True), 1, keepdims=True)
+        out = jnp.where(lane == k, row, out)
     all_dots[...] = jnp.broadcast_to(out[None], all_dots.shape)
 
 
@@ -813,26 +825,24 @@
     )
     a, b, own = lax.optimization_barrier((a, b, own))
     b, a = swap(b, "chan", 1), swap(a, "chan", 0)
-    z, z_behind, z_ahead = call(
+    wk, wk_behind, wk_ahead = call(
+        functools.partial(unpack_kernel, na),
+        [kept(field), kept((2 * RIM, 512)), kept((2 * RIM, 512))],
+        own,
+        *received,
+        dc,
+        wt,
+    )
+    z, a, b = call(
         functools.partial(rim_kernel, na),
-        [kept(field), kept((2 * RIM, 640)), kept((2 * RIM, 640))],
+        [kept(field), kept((2 * RIM, 1152)), kept((2 * RIM, 1152))],
         position,
         z,
         b,
         a,
         dc,
-        smem=1,
-    )
-    wk, a, b = call(
-        functools.partial(unpack_kernel, na),
-        [kept(field), kept((2 * RIM, 1152)), kept((2 * RIM, 1152))],
-        position,
-        own,
-        *received,
-        dc,
-        wt,
-        z_behind,
-        z_ahead,
+        wk_behind,
+        wk_ahead,
         smem=1,
     )
     b, a = slab_swap(b, 1), slab_swap(a, 0)
@@ -841,7 +851,7 @@
     face = (8 * na + 1, 8, LANES)
     for number in range(ITERS - 1):
         first = number == 0
-        outs = [kept(whole)] * 4 + [kept(face)] * 2
+        outs = [kept(whole)] * 3 + [kept(face)] * 2
         if first:
             args = (z, wk, b, a, dc)
             outs += [kept((8, 8, 8, LANES)), kept((tiles + 1, 8, LANES))]
@@ -860,8 +870,8 @@
             input_output_aliases={} if first else {1: 0},
         )
         if first:
-            wkg, cr = got[6:]
-        v, f1, f2, f3, a, b = got[:6]
+            wkg, cr = got[5:]
+        v, f1, f2, a, b = got[:5]
         b, a = swap(b, "chan", 1), swap(a, "chan", 0)
         y, dots = call(
             functools.partial(rest_kernel, na, first),
@@ -870,11 +880,13 @@
             v,
             f1,
             f2,
-            f3,
+            wk,
+            wkg,
             wt,
             iw,
+            kf,
             kb,
-            scratch=[pltpu.VMEM((8, 8, LANES), f32)],
+            scratch=[pltpu.VMEM((8, 8, LANES), f32), pltpu.VMEM((2, 8, 8, 8, LANES), f32)],
         )
         basis.append(v)
         products.append(dots)

time: 71.8 us -> 71.1 us (level)
  local copies, waits for them, and re-layouts: 0.37 us -> 2.57 us
  starting transfers between devices: 12 us -> 9.82 us
  blocking collectives: 11.9 us -> 10.9 us
  Pallas kernels: 31.8 us -> 32.8 us
  waiting for transfers between devices: 14.5 us -> 13.7 us
    ppermute x10, waiting for transfers between devices: 11.1 us -> 6.09 us  [swap(): return lax.ppermute(x, axis, pairs + [(j, i) for i, j in pairs])]
    ppermute x2, waiting for transfers between devices: 0.02 us -> 2.39 us  [swap_around(): return lax.ppermute(x, ('slab', 'chan'), pairs + [(j, i) for i, j in pairs])]
    unnamed x14 -> x18, local copies, waits for them, and re-layouts: 0.04 us -> 2.24 us
    ppermute x10, starting transfers between devices: 4.26 us -> 2.23 us  [swap(): return lax.ppermute(x, axis, pairs + [(j, i) for i, j in pairs])]
    ppermute x1, waiting for transfers between devices: 0.01 us -> 1.7 us  [around(): lax.ppermute(x, ('slab', 'chan'), [(i, (i + by) % n) for i in range(n)])]
    pallas_call x12, Pallas kernels: 22.5 us -> 23.7 us  [call(): pl.pallas_call(kernel, in_specs=specs, out_specs=outs, out_shape=out_shap...]
    all_to_all x1, blocking collectives: 11.9 us -> 10.9 us  [on_device(): sums = lax.all_to_all(sums, ('slab', 'chan'), 0, 0)]
  transfers between devices with their start and end apart: 15 -> 15, of which waited for: 6 -> 8; matrix products, arithmetic and copies ran while one was open for 1% -> 1% of each run, Pallas kernels for 12% -> 16%
where the time goes in v6:
time: 71.1 us; the launch traced here: 70.9 us
  Pallas kernels  32.8 us (46%)
  waiting for transfers between devices  13.7 us (19%)
  blocking collectives  10.9 us (15%)
  starting transfers between devices  9.82 us (14%)
  local copies, waits for them, and re-layouts  2.57 us (4%)
  between operations  0.86 us (1%)
    pallas_call x12, Pallas kernels, call(): pl.pallas_call(kernel, in_specs=specs, out_specs=outs, out_shape=out_shap...  23.7 us
    all_to_all x1, blocking collectives, on_device(): sums = lax.all_to_all(sums, ('slab', 'chan'), 0, 0)  10.9 us
    pallas_call x1, Pallas kernels, on_device(): pl.pallas_call(functools.partial(fluid_kernel, na, 8 // split, chan, tota...  7.31 us
    ppermute x10, waiting for transfers between devices, swap(): return lax.ppermute(x, axis, pairs + [(j, i) for i, j in pairs])  6.09 us
    ppermute x2, starting transfers between devices, swap_around(): return lax.ppermute(x, ('slab', 'chan'), pairs + [(j, i) for i, j in pairs])  3.51 us
    ppermute x2, waiting for transfers between devices, slab_swap(): return lax.ppermute(x, ('slab', 'chan'), pairs + [(j, i) for i, j in pairs])  3.48 us
    ppermute x1, starting transfers between devices, around(): lax.ppermute(x, ('slab', 'chan'), [(i, (i + by) % n) for i in range(n)])  2.94 us
    ppermute x2, waiting for transfers between devices, swap_around(): return lax.ppermute(x, ('slab', 'chan'), pairs + [(j, i) for i, j in pairs])  2.39 us
  transfers between devices with their start and end apart: 15, of which 8 were waited for; matrix products, arithmetic and copies ran while one was open for 1% of the time, Pallas kernels for 16%

profile of v6, /device:TPU:0, one launch (start us, length us, event | category | flops | bytes accessed | tf_op | source)
XLA Modules:
  0.0 70.9 jit_solution(10587112142593087549)
XLA Ops:
  0.7 0.1 stack.56.par_ref.refs_0_
  0.8 0.0 copy-start.4
  0.8 7.3 %shard_map.122 = (bf16[3,8,8,8,512]{4,3,2,1,0:T(8,128)(2,1)}, bf16[4,512,128]{2,1,0:T(8,128)(2,1)S(1)}, bf16[528,128]{1,0:T(8,128)(2,1)S(1)}, bf16[528,128]{1,0:...) custom-call(s32[1]{0:T(128)} %bitcast.me_ref, ...), custom_call_target="tpu_custom_call" | custom-call | tf_op jit(solution)/shard_map/pallas_call | solution.py:793
  8.1 2.9 %collective-permute-start.2 = (bf16[528,128]{1,0:T(8,128)(2,1)S(1)}, bf16[528,128]{1,0:T(8,128)(2,1)S(1)}, u32[]{:S(2)}, u32[]{:S(2)}) collective-permute-start(bf16[528,128]{1,0:T(8,128)(2,1)S(1)} %get-tuple-element.59), channel_id=1, source_target_pairs={{0,4},{1,5},{2,6},{3,7},{4,8},{5,9},{6,10},{7,11},{8,12},{9,13},{1... | collective-permute-start | bytes 405512 | tf_op jit(solution)/shard_map/ppermute | solution.py:714
  11.0 3.5 %collective-permute-start.3 = (bf16[528,128]{1,0:T(8,128)(2,1)S(1)}, bf16[528,128]{1,0:T(8,128)(2,1)S(1)}, u32[]{:S(2)}, u32[]{:S(2)}) collective-permute-start(bf16[528,128]{1,0:T(8,128)(2,1)S(1)} %get-tuple-element.60), channel_id=1, source_target_pairs={{1,2},{3,4},{5,6},{7,8},{9,10},{11,12},{13,14},{15,16},{17,18},{19... | collective-permute-start | bytes 405512 | tf_op jit(solution)/shard_map/ppermute | solution.py:720
  14.5 0.0 collective-permute-start.4
  14.5 0.5 shard_map.123.own_ref
  15.0 0.0 copy-start
  15.0 0.0 copy-start.1
  15.0 0.1 collective-permute-start
  15.1 0.6 collective-permute-start.1
  15.8 0.1 pad_maximum_fusion.2
  15.9 0.1 mul.55
  15.9 0.1 copy.22
  16.1 1.7 %collective-permute-done.2.r1_ref = bf16[528,128]{1,0:T(8,128)(2,1)S(1)} collective-permute-done((bf16[528,128]{1,0:T(8,128)(2,1)S(1)}, bf16[528,128]{1,0:T(8,128)(2,1)S(1)}, u32[]{:S(2)}, u32[]{:S(2)}) %collective-permute-start.2) | collective-permute-done | bytes 135200 | tf_op jit(solution)/shard_map/ppermute | solution.py:714
  17.8 2.4 %collective-permute-done.3.r2_ref = bf16[528,128]{1,0:T(8,128)(2,1)S(1)} collective-permute-done((bf16[528,128]{1,0:T(8,128)(2,1)S(1)}, bf16[528,128]{1,0:T(8,128)(2,1)S(1)}, u32[]{:S(2)}, u32[]{:S(2)}) %collective-permute-start.3) | collective-permute-done | bytes 135200 | tf_op jit(solution)/shard_map/ppermute | solution.py:720
  20.1 0.0 collective-permute-done.4.r3_ref
  20.2 1.0 %shard_map.124 = (f32[4,8,8,8,128]{4,3,2,1,0:T(8,128)S(1)}, f32[16,512]{1,0:T(8,128)S(1)}, f32[16,512]{1,0:T(8,128)S(1)}) custom-call(bf16[512,512]{1,0:T(8,128)(2,1)S(1)} %shard_map.123.own_ref, bf16[528,128]{1,0:T(8,128)(2,1)S(1)} %collective-permute-done.2.r1_ref, bf16[528,128]{1,0:T(8,128)(2,1)S(1)} %collective-permute-done.3.r2_ref, ...), custom_call_target="tpu_custom_call" | custom-call | tf_op jit(solution)/shard_map/pallas_call | solution.py:128
  21.2 1.2 %shard_map.125 = (f32[4,8,8,8,128]{4,3,2,1,0:T(8,128)S(1)}, f32[16,1152]{1,0:T(8,128)S(1)}, f32[16,1152]{1,0:T(8,128)S(1)}) custom-call(s32[6]{0:T(128)S(1)} %stack.56.par_ref.refs_0_, f32[4,8,8,8,128]{4,3,2,1,0:T(8,128)S(1)} %get-tuple-element.52.z_in, f32[2,8,8,128]{3,2,1,0:T(8,128)S(1)} %collective-permute-done.b_ref, ...), custom_call_target="tpu_custom_call" | custom-call | tf_op jit(solution)/shard_map/pallas_call | solution.py:128
  22.4 1.0 %copy-done.2 = f32[4,8,8,8,128]{4,3,2,1,0:T(8,128)} copy-done((f32[4,8,8,8,128]{4,3,2,1,0:T(8,128)}, f32[4,8,8,8,128]{4,3,2,1,0:T(8,128)S(1)}, u32[]{:S(2)}) %copy-start.2) | copy-done | bytes 1048600
  23.4 1.1 %collective-permute-start.6 = (f32[16,1152]{1,0:T(8,128)S(1)}, f32[16,1152]{1,0:T(8,128)S(1)}, u32[]{:S(2)}, u32[]{:S(2)}) collective-permute-start(f32[16,1152]{1,0:T(8,128)S(1)} %get-tuple-element.67), channel_id=1, source_target_pairs={{0,4},{1,5},{2,6},{3,7},{8,12},{9,13},{10,14},{11,15},{16,20},{17,... | collective-permute-start | bytes 221192 | tf_op jit(solution)/shard_map/ppermute | solution.py:703
  24.6 0.1 collective-permute-done.5.refs_3_
  24.7 3.4 %collective-permute-done.6.refs_4_ = f32[16,1152]{1,0:T(8,128)S(1)} collective-permute-done((f32[16,1152]{1,0:T(8,128)S(1)}, f32[16,1152]{1,0:T(8,128)S(1)}, u32[]{:S(2)}, u32[]{:S(2)}) %collective-permute-start.6) | collective-permute-done | bytes 73760 | tf_op jit(solution)/shard_map/ppermute | solution.py:703
  28.1 1.2 %copy-done.3 = f32[4,8,8,8,128]{4,3,2,1,0:T(8,128)S(1)} copy-done((f32[4,8,8,8,128]{4,3,2,1,0:T(8,128)S(1)}, f32[4,8,8,8,128]{4,3,2,1,0:T(8,128)}, u32[]{:S(2)}) %copy-start.3) | copy-done | bytes 1048600
  29.3 2.6 %shard_map.126 = (f32[5,8,8,8,128]{4,3,2,1,0:T(8,128)S(1)}, f32[5,8,8,8,128]{4,3,2,1,0:T(8,128)S(1)}, f32[5,8,8,8,128]{4,3,2,1,0:T(8,128)S(1)}, f32[17,8,128]{2,...) custom-call(s32[6]{0:T(128)S(1)} %stack.56.par_ref.refs_0_, ...), custom_call_target="tpu_custom_call" | custom-call | tf_op jit(solution)/shard_map/pallas_call | solution.py:128
  31.9 0.1 collective-permute-start.7
  32.0 0.1 collective-permute-start.8
  32.1 0.1 multiply_bitcast_fusion
  32.2 2.3 %shard_map.127 = (f32[5,8,8,8,128]{4,3,2,1,0:T(8,128)S(1)}, f32[2,8,128]{2,1,0:T(8,128)S(1)}) custom-call(f32[5,8,8,8,128]{4,3,2,1,0:T(8,128)S(1)} %get-tuple-element.68.refs_0_.v0, f32[5,8,8,8,128]{4,3,2,1,0:T(8,128)S(1)} %get-tuple-element.69.refs_1_, f32[5,8,8,8,128]{4,3,2,1,0:T(8,128)S(1)} %get-tuple-element.70.refs_2_, ...), custom_call_target="tpu_custom_call" | custom-call | tf_op jit(solution)/shard_map/pallas_call | solution.py:128
  34.5 1.9 %collective-permute-done.7.refs_2_ = f32[17,8,128]{2,1,0:T(8,128)S(1)} collective-permute-done((f32[17,8,128]{2,1,0:T(8,128)S(1)}, f32[17,8,128]{2,1,0:T(8,128)S(1)}, u32[]{:S(2)}, u32[]{:S(2)}) %collective-permute-start.7) | collective-permute-done | bytes 69664 | tf_op jit(solution)/shard_map/ppermute | solution.py:709
  36.4 2.2 %shard_map.128 = (f32[5,8,8,8,128]{4,3,2,1,0:T(8,128)S(1)}, f32[5,8,8,8,128]{4,3,2,1,0:T(8,128)S(1)}, f32[5,8,8,8,128]{4,3,2,1,0:T(8,128)S(1)}, f32[17,8,128]{2,1,0:T(8,128)S(1)}, f32[17,8,128]{2,1,0:T(8,128)S(1)}) custom-call(s32[6]{0:T(128)S(1)} %stack.56.par_ref.refs_0_, ...), custom_call_target="tpu_custom_call", output_to_operand_aliasing={{0}: (1, {})} | custom-call | tf_op jit(solution)/shard_map/pallas_call | solution.py:128
  38.6 0.1 collective-permute-start.9
  38.7 0.3 collective-permute-start.10
  38.9 2.3 %shard_map.129 = (f32[5,8,8,8,128]{4,3,2,1,0:T(8,128)S(1)}, f32[2,8,128]{2,1,0:T(8,128)S(1)}) custom-call(f32[5,8,8,8,128]{4,3,2,1,0:T(8,128)S(1)} %get-tuple-element.68.refs_0_.v0, f32[5,8,8,8,128]{4,3,2,1,0:T(8,128)S(1)} %get-tuple-element.76.refs_1_.refs_0_.v1, f32[5,8,8,8,128]{4,3,2,1,0:T(8,128)S(1)} %get-tuple-element.77.refs_2_, ...), custom_call_target="tpu_custom_call" | custom-call | tf_op jit(solution)/shard_map/pallas_call | solution.py:128
  41.3 1.7 %collective-permute-done.9.refs_2_ = f32[17,8,128]{2,1,0:T(8,128)S(1)} collective-permute-done((f32[17,8,128]{2,1,0:T(8,128)S(1)}, f32[17,8,128]{2,1,0:T(8,128)S(1)}, u32[]{:S(2)}, u32[]{:S(2)}) %collective-permute-start.9) | collective-permute-done | bytes 69664 | tf_op jit(solution)/shard_map/ppermute | solution.py:709
  42.9 2.2 %shard_map.130 = (f32[5,8,8,8,128]{4,3,2,1,0:T(8,128)S(1)}, f32[5,8,8,8,128]{4,3,2,1,0:T(8,128)S(1)}, f32[5,8,8,8,128]{4,3,2,1,0:T(8,128)S(1)}, f32[17,8,128]{2,1,0:T(8,128)S(1)}, f32[17,8,128]{2,1,0:T(8,128)S(1)}) custom-call(s32[6]{0:T(128)S(1)} %stack.56.par_ref.refs_0_, ...), custom_call_target="tpu_custom_call", output_to_operand_aliasing={{0}: (1, {})} | custom-call | tf_op jit(solution)/shard_map/pallas_call | solution.py:128
  45.1 0.1 collective-permute-start.11
  45.2 0.3 collective-permute-start.12
  45.5 2.5 %shard_map.131 = (f32[5,8,8,8,128]{4,3,2,1,0:T(8,128)S(1)}, f32[2,8,128]{2,1,0:T(8,128)S(1)}) custom-call(f32[5,8,8,8,128]{4,3,2,1,0:T(8,128)S(1)} %get-tuple-element.76.refs_1_.refs_0_.v1, f32[5,8,8,8,128]{4,3,2,1,0:T(8,128)S(1)} %get-tuple-element.82.refs_1_.refs_0_.v2, f32[5,8,8,8,128]{4,3,2,1,0:T(8,128)S(1)} %get-tuple-element.83.refs_2_, ...), custom_call_target="tpu_custom_call" | custom-call | tf_op jit(solution)/shard_map/pallas_call | solution.py:128
  48.1 1.3 %collective-permute-done.11.refs_2_ = f32[17,8,128]{2,1,0:T(8,128)S(1)} collective-permute-done((f32[17,8,128]{2,1,0:T(8,128)S(1)}, f32[17,8,128]{2,1,0:T(8,128)S(1)}, u32[]{:S(2)}, u32[]{:S(2)}) %collective-permute-start.11) | collective-permute-done | bytes 69664 | tf_op jit(solution)/shard_map/ppermute | solution.py:709
  49.4 2.2 %shard_map.132 = (f32[5,8,8,8,128]{4,3,2,1,0:T(8,128)S(1)}, f32[5,8,8,8,128]{4,3,2,1,0:T(8,128)S(1)}, f32[5,8,8,8,128]{4,3,2,1,0:T(8,128)S(1)}, f32[17,8,128]{2,1,0:T(8,128)S(1)}, f32[17,8,128]{2,1,0:T(8,128)S(1)}) custom-call(s32[6]{0:T(128)S(1)} %stack.56.par_ref.refs_0_, ...), custom_call_target="tpu_custom_call", output_to_operand_aliasing={{0}: (1, {})} | custom-call | tf_op jit(solution)/shard_map/pallas_call | solution.py:128
  51.6 0.3 collective-permute-start.13
  51.9 0.4 collective-permute-start.14
  52.3 2.3 %shard_map.133 = (f32[5,8,8,8,128]{4,3,2,1,0:T(8,128)S(1)}, f32[2,8,128]{2,1,0:T(8,128)S(1)}) custom-call(f32[5,8,8,8,128]{4,3,2,1,0:T(8,128)S(1)} %get-tuple-element.82.refs_1_.refs_0_.v2, f32[5,8,8,8,128]{4,3,2,1,0:T(8,128)S(1)} %get-tuple-element.88.refs_1_.prev.v3, f32[5,8,8,8,128]{4,3,2,1,0:T(8,128)S(1)} %get-tuple-element.89.refs_2_, ...), custom_call_target="tpu_custom_call" | custom-call | tf_op jit(solution)/shard_map/pallas_call | solution.py:128
  54.6 1.2 %collective-permute-done.13.b_in = f32[17,8,128]{2,1,0:T(8,128)S(1)} collective-permute-done((f32[17,8,128]{2,1,0:T(8,128)S(1)}, f32[17,8,128]{2,1,0:T(8,128)S(1)}, u32[]{:S(2)}, u32[]{:S(2)}) %collective-permute-start.13) | collective-permute-done | bytes 69664 | tf_op jit(solution)/shard_map/ppermute | solution.py:709
  55.8 2.2 %shard_map.134 = (f32[5,8,8,8,128]{4,3,2,1,0:T(8,128)S(1)}, f32[32,1,128]{2,1,0:T(1,128)S(1)}) custom-call(s32[6]{0:T(128)S(1)} %stack.56.par_ref.refs_0_, f32[5,8,8,8,128]{4,3,2,1,0:T(8,128)S(1)} %get-tuple-element.91._, f32[17,8,128]{2,1,0:T(8,128)S(1)} %collective-permute-done.13.b_in, ...), custom_call_target="tpu_custom_call", output_to_operand_aliasing={{0}: (1, {})} | custom-call | tf_op jit(solution)/shard_map/pallas_call | solution.py:128
  58.1 10.9 %all_to_all.5.m_ref = f32[32,1,128]{2,1,0:T(1,128)S(1)} all-to-all(f32[32,1,128]{2,1,0:T(1,128)S(1)} %get-tuple-element.98), channel_id=1, replica_groups=mesh['slab'=8,'chan'=4] {'slab','chan'}, dimensions={0} | all-to-all | bytes 32768 | tf_op jit(solution)/shard_map/all_to_all | solution.py:912
  69.0 1.9 %shard_map.135 = f32[2048,128]{1,0:T(8,128)} custom-call(f32[32,1,128]{2,1,0:T(1,128)S(1)} %all_to_all.5.m_ref, f32[5,8,8,8,128]{4,3,2,1,0:T(8,128)S(1)} %get-tuple-element.68.refs_0_.v0, f32[5,8,8,8,128]{4,3,2,1,0:T(8,128)S(1)} %get-tuple-element.76.refs_1_.refs_0_.v1, f32[5,8,8,8,128]{4,3,2,1,0:T(8,128)S(1)} %get-tuple-element.82.refs_1_.refs_0_.v2, ...), custom_call_target="tpu_custom_call" | custom-call | tf_op jit(solution)/shard_map/pallas_call | solution.py:913
  (32 shorter events, 0.2 us)
Async XLA Ops:
  0.7 13.8 %copy-start.5 = (s32[512]{0:T(512)S(1)}, s32[512]{0:T(512)}, u32[]{:S(2)}) copy-start(s32[512]{0:T(512)} %param.12) | copy-start | bytes 6148
  0.7 15.0 %copy-start.6 = (s32[2,256]{1,0:T(2,128)S(1)}, s32[2,256]{1,0:T(2,128)}, u32[]{:S(2)}) copy-start(s32[2,256]{1,0:T(2,128)} %param.16) | copy-start | bytes 6148
  0.7 15.0 %copy-start.7 = (s32[2,256]{1,0:T(2,128)S(1)}, s32[2,256]{1,0:T(2,128)}, u32[]{:S(2)}) copy-start(s32[2,256]{1,0:T(2,128)} %param.15) | copy-start | bytes 6148
  0.8 19.4 %copy-start.4 = (f32[8,128]{1,0:T(8,128)S(1)}, f32[8,128]{1,0:T(8,128)}, u32[]{:S(2)}) copy-start(f32[8,128]{1,0:T(8,128)} %constant.62.clone.wt_ref.refs_6_.refs_5_.refs_7_) | copy-start | bytes 12292
  8.1 9.7 %collective-permute-start.2 = (bf16[528,128]{1,0:T(8,128)(2,1)S(1)}, bf16[528,128]{1,0:T(8,128)(2,1)S(1)}, u32[]{:S(2)}, u32[]{:S(2)}) collective-permute-start(bf16[528,128]{1,0:T(8,128)(2,1)S(1)} %get-tuple-element.59), channel_id=1, source_target_pairs={{0,4},{1,5},{2,6},{3,7},{4,8},{5,9},{6,10},{7,11},{8,12},{9,13},{1... | collective-permute-start | bytes 405512 | tf_op jit(solution)/shard_map/ppermute | solution.py:714
  11.0 9.1 %collective-permute-start.3 = (bf16[528,128]{1,0:T(8,128)(2,1)S(1)}, bf16[528,128]{1,0:T(8,128)(2,1)S(1)}, u32[]{:S(2)}, u32[]{:S(2)}) collective-permute-start(bf16[528,128]{1,0:T(8,128)(2,1)S(1)} %get-tuple-element.60), channel_id=1, source_target_pairs={{1,2},{3,4},{5,6},{7,8},{9,10},{11,12},{13,14},{15,16},{17,18},{19... | collective-permute-start | bytes 405512 | tf_op jit(solution)/shard_map/ppermute | solution.py:720
  14.5 5.6 %collective-permute-start.4 = (bf16[528,128]{1,0:T(8,128)(2,1)S(1)}, bf16[528,128]{1,0:T(8,128)(2,1)S(1)}, u32[]{:S(2)}, u32[]{:S(2)}) collective-permute-start(bf16[528,128]{1,0:T(8,128)(2,1)S(1)} %get-tuple-element.61), channel_id=1, source_target_pairs={{0,1},{2,3},{4,5},{6,7},{8,9},{10,11},{12,13},{14,15},{16,17},{18,... | collective-permute-start | bytes 405512 | tf_op jit(solution)/shard_map/ppermute | solution.py:720
  15.0 13.1 %copy-start = (bf16[256,256]{1,0:T(8,128)(2,1)S(1)}, bf16[256,256]{1,0:T(8,128)(2,1)}, u32[]{:S(2)}) copy-start(bf16[256,256]{1,0:T(8,128)(2,1)} %constant.64.clone.refs_7_.refs_8_.kf_ref) | copy-start | bytes 393220
  15.0 13.0 %copy-start.1 = (bf16[256,256]{1,0:T(8,128)(2,1)S(1)}, bf16[256,256]{1,0:T(8,128)(2,1)}, u32[]{:S(2)}) copy-start(bf16[256,256]{1,0:T(8,128)(2,1)} %constant.65.clone.refs_8_.refs_9_) | copy-start | bytes 393220
  15.0 6.1 %collective-permute-start = (f32[2,8,8,128]{3,2,1,0:T(8,128)}, f32[2,8,8,128]{3,2,1,0:T(8,128)S(1)}, u32[]{:S(2)}, u32[]{:S(2)}) collective-permute-start(f32[2,8,8,128]{3,2,1,0:T(8,128)} %get-tuple-element.56), channel_id=1, source_target_pairs={{1,2},{3,0},{2,1},{0,3},{5,6},{7,4},{6,5},{4,7},{9,10},{11,8},{10,... | collective-permute-start | bytes 196616 | tf_op jit(solution)/shard_map/ppermute | solution.py:709
  15.1 6.0 %collective-permute-start.1 = (f32[2,8,8,128]{3,2,1,0:T(8,128)S(1)}, f32[2,8,8,128]{3,2,1,0:T(8,128)S(1)}, u32[]{:S(2)}, u32[]{:S(2)}) collective-permute-start(f32[2,8,8,128]{3,2,1,0:T(8,128)S(1)} %get-tuple-element.57), channel_id=1, source_target_pairs={{0,1},{2,3},{1,0},{3,2},{4,5},{6,7},{5,4},{7,6},{8,9},{10,11},{9,8... | collective-permute-start | bytes 196616 | tf_op jit(solution)/shard_map/ppermute | solution.py:709
  22.4 1.0 %copy-start.2 = (f32[4,8,8,8,128]{4,3,2,1,0:T(8,128)}, f32[4,8,8,8,128]{4,3,2,1,0:T(8,128)S(1)}, u32[]{:S(2)}) copy-start(f32[4,8,8,8,128]{4,3,2,1,0:T(8,128)S(1)} %get-tuple-element.64.refs_1_) | copy-start | bytes 3145732
  23.4 1.3 %collective-permute-start.5 = (f32[16,1152]{1,0:T(8,128)S(1)}, f32[16,1152]{1,0:T(8,128)S(1)}, u32[]{:S(2)}, u32[]{:S(2)}) collective-permute-start(f32[16,1152]{1,0:T(8,128)S(1)} %get-tuple-element.66), channel_id=1, source_target_pairs={{4,8},{5,9},{6,10},{7,11},{12,16},{13,17},{14,18},{15,19},{20,24},... | collective-permute-start | bytes 221192 | tf_op jit(solution)/shard_map/ppermute | solution.py:703
  23.4 4.7 %collective-permute-start.6 = (f32[16,1152]{1,0:T(8,128)S(1)}, f32[16,1152]{1,0:T(8,128)S(1)}, u32[]{:S(2)}, u32[]{:S(2)}) collective-permute-start(f32[16,1152]{1,0:T(8,128)S(1)} %get-tuple-element.67), channel_id=1, source_target_pairs={{0,4},{1,5},{2,6},{3,7},{8,12},{9,13},{10,14},{11,15},{16,20},{17,... | collective-permute-start | bytes 221192 | tf_op jit(solution)/shard_map/ppermute | solution.py:703
  28.1 1.2 %copy-start.3 = (f32[4,8,8,8,128]{4,3,2,1,0:T(8,128)S(1)}, f32[4,8,8,8,128]{4,3,2,1,0:T(8,128)}, u32[]{:S(2)}) copy-start(f32[4,8,8,8,128]{4,3,2,1,0:T(8,128)} %copy-done.2) | copy-start | bytes 3145732
  31.9 4.5 %collective-permute-start.7 = (f32[17,8,128]{2,1,0:T(8,128)S(1)}, f32[17,8,128]{2,1,0:T(8,128)S(1)}, u32[]{:S(2)}, u32[]{:S(2)}) collective-permute-start(f32[17,8,128]{2,1,0:T(8,128)S(1)} %get-tuple-element.73), channel_id=1, source_target_pairs={{1,2},{3,0},{2,1},{0,3},{5,6},{7,4},{6,5},{4,7},{9,10},{11,8},{10,... | collective-permute-start | bytes 208904 | tf_op jit(solution)/shard_map/ppermute | solution.py:709
  32.0 4.4 %collective-permute-start.8 = (f32[17,8,128]{2,1,0:T(8,128)S(1)}, f32[17,8,128]{2,1,0:T(8,128)S(1)}, u32[]{:S(2)}, u32[]{:S(2)}) collective-permute-start(f32[17,8,128]{2,1,0:T(8,128)S(1)} %get-tuple-element.74), channel_id=1, source_target_pairs={{0,1},{2,3},{1,0},{3,2},{4,5},{6,7},{5,4},{7,6},{8,9},{10,11},{9,8... | collective-permute-start | bytes 208904 | tf_op jit(solution)/shard_map/ppermute | solution.py:709
  38.6 4.3 %collective-permute-start.9 = (f32[17,8,128]{2,1,0:T(8,128)S(1)}, f32[17,8,128]{2,1,0:T(8,128)S(1)}, u32[]{:S(2)}, u32[]{:S(2)}) collective-permute-start(f32[17,8,128]{2,1,0:T(8,128)S(1)} %get-tuple-element.80), channel_id=1, source_target_pairs={{1,2},{3,0},{2,1},{0,3},{5,6},{7,4},{6,5},{4,7},{9,10},{11,8},{10,... | collective-permute-start | bytes 208904 | tf_op jit(solution)/shard_map/ppermute | solution.py:709
  38.7 4.3 %collective-permute-start.10 = (f32[17,8,128]{2,1,0:T(8,128)S(1)}, f32[17,8,128]{2,1,0:T(8,128)S(1)}, u32[]{:S(2)}, u32[]{:S(2)}) collective-permute-start(f32[17,8,128]{2,1,0:T(8,128)S(1)} %get-tuple-element.81), channel_id=1, source_target_pairs={{0,1},{2,3},{1,0},{3,2},{4,5},{6,7},{5,4},{7,6},{8,9},{10,11},{9,8... | collective-permute-start | bytes 208904 | tf_op jit(solution)/shard_map/ppermute | solution.py:709
  45.1 4.2 %collective-permute-start.11 = (f32[17,8,128]{2,1,0:T(8,128)S(1)}, f32[17,8,128]{2,1,0:T(8,128)S(1)}, u32[]{:S(2)}, u32[]{:S(2)}) collective-permute-start(f32[17,8,128]{2,1,0:T(8,128)S(1)} %get-tuple-element.86), channel_id=1, source_target_pairs={{1,2},{3,0},{2,1},{0,3},{5,6},{7,4},{6,5},{4,7},{9,10},{11,8},{10,... | collective-permute-start | bytes 208904 | tf_op jit(solution)/shard_map/ppermute | solution.py:709
  45.2 4.2 %collective-permute-start.12 = (f32[17,8,128]{2,1,0:T(8,128)S(1)}, f32[17,8,128]{2,1,0:T(8,128)S(1)}, u32[]{:S(2)}, u32[]{:S(2)}) collective-permute-start(f32[17,8,128]{2,1,0:T(8,128)S(1)} %get-tuple-element.87), channel_id=1, source_target_pairs={{0,1},{2,3},{1,0},{3,2},{4,5},{6,7},{5,4},{7,6},{8,9},{10,11},{9,8... | collective-permute-start | bytes 208904 | tf_op jit(solution)/shard_map/ppermute | solution.py:709
  51.6 4.2 %collective-permute-start.13 = (f32[17,8,128]{2,1,0:T(8,128)S(1)}, f32[17,8,128]{2,1,0:T(8,128)S(1)}, u32[]{:S(2)}, u32[]{:S(2)}) collective-permute-start(f32[17,8,128]{2,1,0:T(8,128)S(1)} %get-tuple-element.92), channel_id=1, source_target_pairs={{1,2},{3,0},{2,1},{0,3},{5,6},{7,4},{6,5},{4,7},{9,10},{11,8},{10,... | collective-permute-start | bytes 208904 | tf_op jit(solution)/shard_map/ppermute | solution.py:709
  51.9 4.0 %collective-permute-start.14 = (f32[17,8,128]{2,1,0:T(8,128)S(1)}, f32[17,8,128]{2,1,0:T(8,128)S(1)}, u32[]{:S(2)}, u32[]{:S(2)}) collective-permute-start(f32[17,8,128]{2,1,0:T(8,128)S(1)} %get-tuple-element.93), channel_id=1, source_target_pairs={{0,1},{2,3},{1,0},{3,2},{4,5},{6,7},{5,4},{7,6},{8,9},{10,11},{9,8... | collective-permute-start | bytes 208904 | tf_op jit(solution)/shard_map/ppermute | solution.py:709

commit v7 on v6

--- a/solution.py
+++ b/solution.py
@@ -10,7 +10,7 @@
 
 ITERS = 5
 LANES = 128
-RIM = 8
+RIM = 4
 KRYLOV_SCALE = 1.0 / 256.0
 
 highest = lax.Precision.HIGHEST
@@ -151,32 +151,34 @@
     row = lax.broadcasted_iota(jnp.int32, (2 * RIM, LANES), 0)
     lane = lax.broadcasted_iota(jnp.int32, (2 * RIM, LANES), 1)
     inside = (row >= l * RIM) & (row < (l + 1) * RIM)
-    return ((row - l * RIM + first_lane == lane) & inside).astype(f32).astype(bf16)
+    return ((row - l * RIM + first_lane == lane) & inside).astype(f32)
 
 
 def place_matrix(first_lane):
     row = lax.broadcasted_iota(jnp.int32, (2 * RIM, LANES), 0)
     lane = lax.broadcasted_iota(jnp.int32, (2 * RIM, LANES), 1)
     target = jnp.where(row < RIM, row + first_lane, row - RIM + first_lane + LANES // 2)
-    return (target == lane).astype(f32).astype(bf16)
-
-
-def send_rims(tile_rows, na):
-    def pick(tiles, first_lane):
+    return (target == lane).astype(f32)
+
+
+def send_rims(near_rows, far_rows, na):
+    def pick(tile_rows, tiles, first_lane):
         out = None
         for l, j in enumerate(tiles):
             terms = jnp.concatenate(in_three(tile_rows(j)), 1)
-            sel = jnp.concatenate([sel_matrix(l, first_lane)] * 3, 1)
+            sel = jnp.concatenate([sel_matrix(l, first_lane)] * 3, 1).astype(bf16)
             part = lax.dot_general(sel, terms, NT, preferred_element_type=f32)
             out = part if out is None else out + part
         return out
 
-    return pick((0, na), 0), pick((na - 1, 2 * na - 1), LANES - RIM)
+    return pick(near_rows, (0, na), 0), pick(far_rows, (na - 1, 2 * na - 1), LANES - RIM)
 
 
 def place_rims(from_ahead, from_behind):
-    terms = jnp.concatenate(in_three(from_ahead) + in_three(from_behind), 0)
-    places = jnp.concatenate([place_matrix(0)] * 3 + [place_matrix(LANES // 2 - RIM)] * 3, 0)
+    terms = [x.astype(f32) for x in in_three(from_ahead) + in_three(from_behind)]
+    places = [place_matrix(0)] * 3 + [place_matrix(LANES // 2 - RIM)] * 3
+    terms = jnp.concatenate(terms, 0).astype(bf16)
+    places = jnp.concatenate(places, 0).astype(bf16)
     return lax.dot_general(terms, places, TN, preferred_element_type=f32)
 
 
@@ -206,19 +208,32 @@
             send_faces(par_ref, (at, r), lower, upper, a_ref, b_ref)
 
 
-def rim_kernel(na, par_ref, z_in, b_ref, a_ref, dc_ref, wkb_ref, wka_ref, z_ref, a_out, b_out):
-    z_ref[...] = z_in[...]
+def rim_kernel(na, par_ref, z_in, b_ref, a_ref, dc_ref, wkb_ref, wka_ref, v_ref, a_out, b_out):
+    v_ref[0 : 2 * na] = z_in[...]
     for r in range(8):
         for at in range(na):
             lower, upper = got_faces(par_ref, (at, r), a_ref, b_ref)
-            z_ref[at, r, 0] = z_ref[at, r, 0] + lower
-            z_ref[na + at, r, 7] = z_ref[na + at, r, 7] + upper
-
-    def tile_rows(j):
-        cross = jnp.broadcast_to(dc_ref[1:2, j * LANES : (j + 1) * LANES], (LANES, LANES))
-        return jnp.concatenate([z_ref[j].reshape(512, LANES), cross], 0)
-
-    behind, ahead = send_rims(tile_rows, na)
+            v_ref[at, r, 0] = v_ref[at, r, 0] + lower
+            v_ref[na + at, r, 7] = v_ref[na + at, r, 7] + upper
+
+    lane = lane_index()
+    cross = lambda j: jnp.broadcast_to(dc_ref[1:2, j * LANES : (j + 1) * LANES], (LANES, LANES))
+
+    def near_rows(j):
+        rows = []
+        for s in range(8):
+            inner = pltpu.roll(v_ref[j, 0, s], LANES - 1, 1)
+            rows.append(v_ref[j, 7, s] + jnp.where(lane == RIM - 1, inner, 0.0))
+        return jnp.concatenate([v_ref[j, 0:7].reshape(448, LANES)] + rows + [cross(j)], 0)
+
+    def far_rows(j):
+        rows = []
+        for s in range(8):
+            inner = pltpu.roll(v_ref[j, 7, s], 1, 1)
+            rows.append(v_ref[j, 0, s] + jnp.where(lane == LANES - RIM, inner, 0.0))
+        return jnp.concatenate(rows + [v_ref[j, 1:8].reshape(448, LANES), cross(j)], 0)
+
+    behind, ahead = send_rims(near_rows, far_rows, na)
     behind = jnp.where(par_ref[3] > 0, jnp.concatenate([behind, wkb_ref[...]], 1), 0.0)
     ahead = jnp.where(par_ref[4] > 0, jnp.concatenate([ahead, wka_ref[...]], 1), 0.0)
     even = par_ref[5] == 0
@@ -446,7 +461,8 @@
         for r in range(8):
             for s in range(8):
                 wk_ref[j, r, s] = rows[r][s] * kappa[r, s]
-    behind_ref[...], ahead_ref[...] = send_rims(lambda j: wk_ref[j].reshape(512, LANES), na)
+    rows = lambda j: wk_ref[j].reshape(512, LANES)
+    behind_ref[...], ahead_ref[...] = send_rims(rows, rows, na)
 
 
 def lines_t(k_ref, blocks):
@@ -548,7 +564,7 @@
     take = lambda n: [refs.pop(0) for _ in range(n)]
     ghost = 2 * na
     if first:
-        par_ref, z_in, wk_ref, b_in, a_in, dc_ref = take(6)
+        par_ref, _, wk_ref, b_in, a_in, dc_ref = take(6)
     else:
         par_ref, _, b_in, a_in, wk_ref, wkg_ref, cr_ref = take(7)
     wt_ref, kf_ref, kb_ref, v, f1, f2, a_out, b_out = take(8)
@@ -556,7 +572,6 @@
         wkg_ref, cr_ref = take(2)
     g, base = refs
     if first:
-        v[0:ghost] = z_in[...]
         even = par_ref[5] == 0
         a, b = a_in[...], b_in[...]
         rims = place_rims(jnp.where(even, a, b), jnp.where(even, b, a))
@@ -833,9 +848,9 @@
         dc,
         wt,
     )
-    z, a, b = call(
+    y, a, b = call(
         functools.partial(rim_kernel, na),
-        [kept(field), kept((2 * RIM, 1152)), kept((2 * RIM, 1152))],
+        [kept(whole), kept((2 * RIM, 1152)), kept((2 * RIM, 1152))],
         position,
         z,
         b,
@@ -853,7 +868,7 @@
         first = number == 0
         outs = [kept(whole)] * 3 + [kept(face)] * 2
         if first:
-            args = (z, wk, b, a, dc)
+            args = (y, wk, b, a, dc)
             outs += [kept((8, 8, 8, LANES)), kept((tiles + 1, 8, LANES))]
         else:
             args = (y, b, a, wk, wkg, cr)
@@ -867,7 +882,7 @@
             kb,
             smem=1,
             scratch=[pltpu.VMEM((2, 8, 8, 8, LANES), f32), pltpu.VMEM((8, 8, LANES), f32)],
-            input_output_aliases={} if first else {1: 0},
+            input_output_aliases={1: 0},
         )
         if first:
             wkg, cr = got[5:]

time: 71.1 us -> 69.9 us (0.983)
  waiting for transfers between devices: 13.7 us -> 12.2 us
    ppermute x2, waiting for transfers between devices: 3.48 us -> 2.53 us  [slab_swap(): return lax.ppermute(x, ('slab', 'chan'), pairs + [(j, i) for i, j in pairs])]
    ppermute x10, waiting for transfers between devices: 6.09 us -> 5.24 us  [swap(): return lax.ppermute(x, axis, pairs + [(j, i) for i, j in pairs])]
  transfers between devices with their start and end apart: 15 -> 15, of which waited for: 8 -> 7; matrix products, arithmetic and copies ran while one was open for 1% -> 1% of each run, Pallas kernels for 16% -> 16%
where the time goes in v7:
time: 69.9 us; the launch traced here: 69.6 us
  Pallas kernels  32.8 us (47%)
  waiting for transfers between devices  12.2 us (17%)
  blocking collectives  10.6 us (15%)
  starting transfers between devices  10.5 us (15%)
  local copies, waits for them, and re-layouts  2.59 us (4%)
  between operations  0.88 us (1%)
    pallas_call x12, Pallas kernels, call(): pl.pallas_call(kernel, in_specs=specs, out_specs=outs, out_shape=out_shap...  23.6 us
    all_to_all x1, blocking collectives, on_device(): sums = lax.all_to_all(sums, ('slab', 'chan'), 0, 0)  10.6 us
    pallas_call x1, Pallas kernels, on_device(): pl.pallas_call(functools.partial(fluid_kernel, na, 8 // split, chan, tota...  7.29 us
    ppermute x10, waiting for transfers between devices, swap(): return lax.ppermute(x, axis, pairs + [(j, i) for i, j in pairs])  5.24 us
    ppermute x2, starting transfers between devices, swap_around(): return lax.ppermute(x, ('slab', 'chan'), pairs + [(j, i) for i, j in pairs])  3.44 us
    ppermute x1, starting transfers between devices, around(): lax.ppermute(x, ('slab', 'chan'), [(i, (i + by) % n) for i in range(n)])  2.94 us
    ppermute x10, starting transfers between devices, swap(): return lax.ppermute(x, axis, pairs + [(j, i) for i, j in pairs])  2.89 us
    ppermute x2, waiting for transfers between devices, slab_swap(): return lax.ppermute(x, ('slab', 'chan'), pairs + [(j, i) for i, j in pairs])  2.53 us
  transfers between devices with their start and end apart: 15, of which 7 were waited for; matrix products, arithmetic and copies ran while one was open for 1% of the time, Pallas kernels for 16%

profile of v7, /device:TPU:0, one launch (start us, length us, event | category | flops | bytes accessed | tf_op | source)
XLA Modules:
  0.0 69.6 jit_solution(10518521762075057082)
XLA Ops:
  0.7 0.1 stack.56.par_ref.refs_0_
  0.8 0.0 copy-start.4
  0.8 7.3 %shard_map.122 = (bf16[3,8,8,8,512]{4,3,2,1,0:T(8,128)(2,1)}, bf16[4,512,128]{2,1,0:T(8,128)(2,1)S(1)}, bf16[528,128]{1,0:T(8,128)(2,1)S(1)}, bf16[528,128]{1,0:...) custom-call(s32[1]{0:T(128)} %bitcast.me_ref, ...), custom_call_target="tpu_custom_call" | custom-call | tf_op jit(solution)/shard_map/pallas_call | solution.py:808
  8.1 1.0 %copy-done.2 = f32[4,8,8,8,128]{4,3,2,1,0:T(8,128)} copy-done((f32[4,8,8,8,128]{4,3,2,1,0:T(8,128)}, f32[4,8,8,8,128]{4,3,2,1,0:T(8,128)S(1)}, u32[]{:S(2)}) %copy-start.2) | copy-done | bytes 1048600
  9.0 2.9 %collective-permute-start.2 = (bf16[528,128]{1,0:T(8,128)(2,1)S(1)}, bf16[528,128]{1,0:T(8,128)(2,1)S(1)}, u32[]{:S(2)}, u32[]{:S(2)}) collective-permute-start(bf16[528,128]{1,0:T(8,128)(2,1)S(1)} %get-tuple-element.59), channel_id=1, source_target_pairs={{0,4},{1,5},{2,6},{3,7},{4,8},{5,9},{6,10},{7,11},{8,12},{9,13},{1... | collective-permute-start | bytes 405512 | tf_op jit(solution)/shard_map/ppermute | solution.py:729
  12.0 3.4 %collective-permute-start.3 = (bf16[528,128]{1,0:T(8,128)(2,1)S(1)}, bf16[528,128]{1,0:T(8,128)(2,1)S(1)}, u32[]{:S(2)}, u32[]{:S(2)}) collective-permute-start(bf16[528,128]{1,0:T(8,128)(2,1)S(1)} %get-tuple-element.60), channel_id=1, source_target_pairs={{1,2},{3,4},{5,6},{7,8},{9,10},{11,12},{13,14},{15,16},{17,18},{19... | collective-permute-start | bytes 405512 | tf_op jit(solution)/shard_map/ppermute | solution.py:735
  15.4 0.0 collective-permute-start.4
  15.4 0.5 shard_map.123.own_ref
  15.9 0.0 copy-start
  15.9 0.0 copy-start.1
  15.9 0.1 collective-permute-start
  16.0 0.6 collective-permute-start.1
  16.7 2.0 %collective-permute-done.2.r1_ref = bf16[528,128]{1,0:T(8,128)(2,1)S(1)} collective-permute-done((bf16[528,128]{1,0:T(8,128)(2,1)S(1)}, bf16[528,128]{1,0:T(8,128)(2,1)S(1)}, u32[]{:S(2)}, u32[]{:S(2)}) %collective-permute-start.2) | collective-permute-done | bytes 135200 | tf_op jit(solution)/shard_map/ppermute | solution.py:729
  18.7 2.4 %collective-permute-done.3.r2_ref = bf16[528,128]{1,0:T(8,128)(2,1)S(1)} collective-permute-done((bf16[528,128]{1,0:T(8,128)(2,1)S(1)}, bf16[528,128]{1,0:T(8,128)(2,1)S(1)}, u32[]{:S(2)}, u32[]{:S(2)}) %collective-permute-start.3) | collective-permute-done | bytes 135200 | tf_op jit(solution)/shard_map/ppermute | solution.py:735
  21.1 0.0 collective-permute-done.4.r3_ref
  21.1 1.0 %shard_map.124 = (f32[4,8,8,8,128]{4,3,2,1,0:T(8,128)S(1)}, f32[8,512]{1,0:T(8,128)S(1)}, f32[8,512]{1,0:T(8,128)S(1)}) custom-call(bf16[512,512]{1,0:T(8,128)(2,1)S(1)} %shard_map.123.own_ref, bf16[528,128]{1,0:T(8,128)(2,1)S(1)} %collective-permute-done.2.r1_ref, bf16[528,128]{1,0:T(8,128)(2,1)S(1)} %collective-permute-done.3.r2_ref, ...), custom_call_target="tpu_custom_call" | custom-call | tf_op jit(solution)/shard_map/pallas_call | solution.py:128
  22.1 0.0 copy-start.3
  22.1 1.2 %copy-done.3 = f32[4,8,8,8,128]{4,3,2,1,0:T(8,128)S(1)} copy-done((f32[4,8,8,8,128]{4,3,2,1,0:T(8,128)S(1)}, f32[4,8,8,8,128]{4,3,2,1,0:T(8,128)}, u32[]{:S(2)}) %copy-start.3) | copy-done | bytes 1048600
  23.4 1.3 %shard_map.125 = (f32[5,8,8,8,128]{4,3,2,1,0:T(8,128)S(1)}, f32[8,1152]{1,0:T(8,128)S(1)}, f32[8,1152]{1,0:T(8,128)S(1)}) custom-call(s32[6]{0:T(128)S(1)} %stack.56.par_ref.refs_0_, f32[4,8,8,8,128]{4,3,2,1,0:T(8,128)S(1)} %copy-done.3, f32[2,8,8,128]{3,2,1,0:T(8,128)S(1)} %collective-permute-done.b_ref, f32[2,8,8,128]{3,2,1,0:T(8,128)S(1)} %collective-permute-done.1.a_ref, ...), custom_call_target="tpu_custom_call" | custom-call | tf_op jit(solution)/shard_map/pallas_call | solution.py:128
  24.6 1.2 %collective-permute-start.6 = (f32[8,1152]{1,0:T(8,128)S(1)}, f32[8,1152]{1,0:T(8,128)S(1)}, u32[]{:S(2)}, u32[]{:S(2)}) collective-permute-start(f32[8,1152]{1,0:T(8,128)S(1)} %get-tuple-element.67), channel_id=1, source_target_pairs={{0,4},{1,5},{2,6},{3,7},{8,12},{9,13},{10,14},{11,15},{16,20},{17,... | collective-permute-start | bytes 110600 | tf_op jit(solution)/shard_map/ppermute | solution.py:718
  25.8 0.1 pad_maximum_fusion.2
  25.9 0.1 mul.55
  26.0 0.1 copy.23
  26.1 2.5 %collective-permute-done.6.refs_4_ = f32[8,1152]{1,0:T(8,128)S(1)} collective-permute-done((f32[8,1152]{1,0:T(8,128)S(1)}, f32[8,1152]{1,0:T(8,128)S(1)}, u32[]{:S(2)}, u32[]{:S(2)}) %collective-permute-start.6) | collective-permute-done | bytes 36896 | tf_op jit(solution)/shard_map/ppermute | solution.py:718
  28.6 2.5 %shard_map.126 = (f32[5,8,8,8,128]{4,3,2,1,0:T(8,128)S(1)}, f32[5,8,8,8,128]{4,3,2,1,0:T(8,128)S(1)}, f32[5,8,8,8,128]{4,3,2,1,0:T(8,128)S(1)}, f32[17,8,128]{2,...) custom-call(s32[6]{0:T(128)S(1)} %stack.56.par_ref.refs_0_, ...), custom_call_target="tpu_custom_call", output_to_operand_aliasing={{0}: (1, {})} | custom-call | tf_op jit(solution)/shard_map/pallas_call | solution.py:128
  31.2 0.1 collective-permute-start.7
  31.2 0.3 collective-permute-start.8
  31.6 0.1 multiply_bitcast_fusion
  31.7 2.2 %shard_map.127 = (f32[5,8,8,8,128]{4,3,2,1,0:T(8,128)S(1)}, f32[2,8,128]{2,1,0:T(8,128)S(1)}) custom-call(f32[5,8,8,8,128]{4,3,2,1,0:T(8,128)S(1)} %get-tuple-element.68.refs_0_.v0, f32[5,8,8,8,128]{4,3,2,1,0:T(8,128)S(1)} %get-tuple-element.69.refs_1_, f32[5,8,8,8,128]{4,3,2,1,0:T(8,128)S(1)} %get-tuple-element.70.refs_2_, ...), custom_call_target="tpu_custom_call" | custom-call | tf_op jit(solution)/shard_map/pallas_call | solution.py:128
  33.9 1.3 %collective-permute-done.7.refs_2_ = f32[17,8,128]{2,1,0:T(8,128)S(1)} collective-permute-done((f32[17,8,128]{2,1,0:T(8,128)S(1)}, f32[17,8,128]{2,1,0:T(8,128)S(1)}, u32[]{:S(2)}, u32[]{:S(2)}) %collective-permute-start.7) | collective-permute-done | bytes 69664 | tf_op jit(solution)/shard_map/ppermute | solution.py:724
  35.2 2.2 %shard_map.128 = (f32[5,8,8,8,128]{4,3,2,1,0:T(8,128)S(1)}, f32[5,8,8,8,128]{4,3,2,1,0:T(8,128)S(1)}, f32[5,8,8,8,128]{4,3,2,1,0:T(8,128)S(1)}, f32[17,8,128]{2,1,0:T(8,128)S(1)}, f32[17,8,128]{2,1,0:T(8,128)S(1)}) custom-call(s32[6]{0:T(128)S(1)} %stack.56.par_ref.refs_0_, ...), custom_call_target="tpu_custom_call", output_to_operand_aliasing={{0}: (1, {})} | custom-call | tf_op jit(solution)/shard_map/pallas_call | solution.py:128
  37.4 0.2 collective-permute-start.9
  37.7 0.5 collective-permute-start.10
  38.1 2.4 %shard_map.129 = (f32[5,8,8,8,128]{4,3,2,1,0:T(8,128)S(1)}, f32[2,8,128]{2,1,0:T(8,128)S(1)}) custom-call(f32[5,8,8,8,128]{4,3,2,1,0:T(8,128)S(1)} %get-tuple-element.68.refs_0_.v0, f32[5,8,8,8,128]{4,3,2,1,0:T(8,128)S(1)} %get-tuple-element.76.refs_1_.refs_0_.v1, f32[5,8,8,8,128]{4,3,2,1,0:T(8,128)S(1)} %get-tuple-element.77.refs_2_, ...), custom_call_target="tpu_custom_call" | custom-call | tf_op jit(solution)/shard_map/pallas_call | solution.py:128
  40.5 1.3 %collective-permute-done.9.refs_2_ = f32[17,8,128]{2,1,0:T(8,128)S(1)} collective-permute-done((f32[17,8,128]{2,1,0:T(8,128)S(1)}, f32[17,8,128]{2,1,0:T(8,128)S(1)}, u32[]{:S(2)}, u32[]{:S(2)}) %collective-permute-start.9) | collective-permute-done | bytes 69664 | tf_op jit(solution)/shard_map/ppermute | solution.py:724
  41.9 2.2 %shard_map.130 = (f32[5,8,8,8,128]{4,3,2,1,0:T(8,128)S(1)}, f32[5,8,8,8,128]{4,3,2,1,0:T(8,128)S(1)}, f32[5,8,8,8,128]{4,3,2,1,0:T(8,128)S(1)}, f32[17,8,128]{2,1,0:T(8,128)S(1)}, f32[17,8,128]{2,1,0:T(8,128)S(1)}) custom-call(s32[6]{0:T(128)S(1)} %stack.56.par_ref.refs_0_, ...), custom_call_target="tpu_custom_call", output_to_operand_aliasing={{0}: (1, {})} | custom-call | tf_op jit(solution)/shard_map/pallas_call | solution.py:128
  44.1 0.2 collective-permute-start.11
  44.3 0.4 collective-permute-start.12
  44.7 2.5 %shard_map.131 = (f32[5,8,8,8,128]{4,3,2,1,0:T(8,128)S(1)}, f32[2,8,128]{2,1,0:T(8,128)S(1)}) custom-call(f32[5,8,8,8,128]{4,3,2,1,0:T(8,128)S(1)} %get-tuple-element.76.refs_1_.refs_0_.v1, f32[5,8,8,8,128]{4,3,2,1,0:T(8,128)S(1)} %get-tuple-element.82.refs_1_.refs_0_.v2, f32[5,8,8,8,128]{4,3,2,1,0:T(8,128)S(1)} %get-tuple-element.83.refs_2_, ...), custom_call_target="tpu_custom_call" | custom-call | tf_op jit(solution)/shard_map/pallas_call | solution.py:128
  47.2 1.3 %collective-permute-done.11.refs_2_ = f32[17,8,128]{2,1,0:T(8,128)S(1)} collective-permute-done((f32[17,8,128]{2,1,0:T(8,128)S(1)}, f32[17,8,128]{2,1,0:T(8,128)S(1)}, u32[]{:S(2)}, u32[]{:S(2)}) %collective-permute-start.11) | collective-permute-done | bytes 69664 | tf_op jit(solution)/shard_map/ppermute | solution.py:724
  48.5 2.2 %shard_map.132 = (f32[5,8,8,8,128]{4,3,2,1,0:T(8,128)S(1)}, f32[5,8,8,8,128]{4,3,2,1,0:T(8,128)S(1)}, f32[5,8,8,8,128]{4,3,2,1,0:T(8,128)S(1)}, f32[17,8,128]{2,1,0:T(8,128)S(1)}, f32[17,8,128]{2,1,0:T(8,128)S(1)}) custom-call(s32[6]{0:T(128)S(1)} %stack.56.par_ref.refs_0_, ...), custom_call_target="tpu_custom_call", output_to_operand_aliasing={{0}: (1, {})} | custom-call | tf_op jit(solution)/shard_map/pallas_call | solution.py:128
  50.7 0.1 collective-permute-start.13
  50.8 0.5 collective-permute-start.14
  51.2 2.4 %shard_map.133 = (f32[5,8,8,8,128]{4,3,2,1,0:T(8,128)S(1)}, f32[2,8,128]{2,1,0:T(8,128)S(1)}) custom-call(f32[5,8,8,8,128]{4,3,2,1,0:T(8,128)S(1)} %get-tuple-element.82.refs_1_.refs_0_.v2, f32[5,8,8,8,128]{4,3,2,1,0:T(8,128)S(1)} %get-tuple-element.88.refs_1_.prev.v3, f32[5,8,8,8,128]{4,3,2,1,0:T(8,128)S(1)} %get-tuple-element.89.refs_2_, ...), custom_call_target="tpu_custom_call" | custom-call | tf_op jit(solution)/shard_map/pallas_call | solution.py:128
  53.6 1.3 %collective-permute-done.13.b_in = f32[17,8,128]{2,1,0:T(8,128)S(1)} collective-permute-done((f32[17,8,128]{2,1,0:T(8,128)S(1)}, f32[17,8,128]{2,1,0:T(8,128)S(1)}, u32[]{:S(2)}, u32[]{:S(2)}) %collective-permute-start.13) | collective-permute-done | bytes 69664 | tf_op jit(solution)/shard_map/ppermute | solution.py:724
  55.0 2.2 %shard_map.134 = (f32[5,8,8,8,128]{4,3,2,1,0:T(8,128)S(1)}, f32[32,1,128]{2,1,0:T(1,128)S(1)}) custom-call(s32[6]{0:T(128)S(1)} %stack.56.par_ref.refs_0_, f32[5,8,8,8,128]{4,3,2,1,0:T(8,128)S(1)} %get-tuple-element.91._, f32[17,8,128]{2,1,0:T(8,128)S(1)} %collective-permute-done.13.b_in, ...), custom_call_target="tpu_custom_call", output_to_operand_aliasing={{0}: (1, {})} | custom-call | tf_op jit(solution)/shard_map/pallas_call | solution.py:128
  57.2 10.6 %all_to_all.5.m_ref = f32[32,1,128]{2,1,0:T(1,128)S(1)} all-to-all(f32[32,1,128]{2,1,0:T(1,128)S(1)} %get-tuple-element.98), channel_id=1, replica_groups=mesh['slab'=8,'chan'=4] {'slab','chan'}, dimensions={0} | all-to-all | bytes 32768 | tf_op jit(solution)/shard_map/all_to_all | solution.py:927
  67.7 1.9 %shard_map.135 = f32[2048,128]{1,0:T(8,128)} custom-call(f32[32,1,128]{2,1,0:T(1,128)S(1)} %all_to_all.5.m_ref, f32[5,8,8,8,128]{4,3,2,1,0:T(8,128)S(1)} %get-tuple-element.68.refs_0_.v0, f32[5,8,8,8,128]{4,3,2,1,0:T(8,128)S(1)} %get-tuple-element.76.refs_1_.refs_0_.v1, f32[5,8,8,8,128]{4,3,2,1,0:T(8,128)S(1)} %get-tuple-element.82.refs_1_.refs_0_.v2, ...), custom_call_target="tpu_custom_call" | custom-call | tf_op jit(solution)/shard_map/pallas_call | solution.py:928
  (32 shorter events, 0.1 us)
Async XLA Ops:
  0.7 14.7 %copy-start.5 = (s32[512]{0:T(512)S(1)}, s32[512]{0:T(512)}, u32[]{:S(2)}) copy-start(s32[512]{0:T(512)} %param.12) | copy-start | bytes 6148
  0.7 15.8 %copy-start.6 = (s32[2,256]{1,0:T(2,128)S(1)}, s32[2,256]{1,0:T(2,128)}, u32[]{:S(2)}) copy-start(s32[2,256]{1,0:T(2,128)} %param.16) | copy-start | bytes 6148
  0.7 15.8 %copy-start.7 = (s32[2,256]{1,0:T(2,128)S(1)}, s32[2,256]{1,0:T(2,128)}, u32[]{:S(2)}) copy-start(s32[2,256]{1,0:T(2,128)} %param.15) | copy-start | bytes 6148
  0.8 20.4 %copy-start.4 = (f32[8,128]{1,0:T(8,128)S(1)}, f32[8,128]{1,0:T(8,128)}, u32[]{:S(2)}) copy-start(f32[8,128]{1,0:T(8,128)} %constant.62.clone.wt_ref.refs_6_.refs_5_.refs_7_) | copy-start | bytes 12292
  8.1 1.0 %copy-start.2 = (f32[4,8,8,8,128]{4,3,2,1,0:T(8,128)}, f32[4,8,8,8,128]{4,3,2,1,0:T(8,128)S(1)}, u32[]{:S(2)}) copy-start(f32[4,8,8,8,128]{4,3,2,1,0:T(8,128)S(1)} %get-tuple-element.52.z_in) | copy-start | bytes 3145732
  9.0 9.7 %collective-permute-start.2 = (bf16[528,128]{1,0:T(8,128)(2,1)S(1)}, bf16[528,128]{1,0:T(8,128)(2,1)S(1)}, u32[]{:S(2)}, u32[]{:S(2)}) collective-permute-start(bf16[528,128]{1,0:T(8,128)(2,1)S(1)} %get-tuple-element.59), channel_id=1, source_target_pairs={{0,4},{1,5},{2,6},{3,7},{4,8},{5,9},{6,10},{7,11},{8,12},{9,13},{1... | collective-permute-start | bytes 405512 | tf_op jit(solution)/shard_map/ppermute | solution.py:729
  12.0 9.1 %collective-permute-start.3 = (bf16[528,128]{1,0:T(8,128)(2,1)S(1)}, bf16[528,128]{1,0:T(8,128)(2,1)S(1)}, u32[]{:S(2)}, u32[]{:S(2)}) collective-permute-start(bf16[528,128]{1,0:T(8,128)(2,1)S(1)} %get-tuple-element.60), channel_id=1, source_target_pairs={{1,2},{3,4},{5,6},{7,8},{9,10},{11,12},{13,14},{15,16},{17,18},{19... | collective-permute-start | bytes 405512 | tf_op jit(solution)/shard_map/ppermute | solution.py:735
  15.4 5.7 %collective-permute-start.4 = (bf16[528,128]{1,0:T(8,128)(2,1)S(1)}, bf16[528,128]{1,0:T(8,128)(2,1)S(1)}, u32[]{:S(2)}, u32[]{:S(2)}) collective-permute-start(bf16[528,128]{1,0:T(8,128)(2,1)S(1)} %get-tuple-element.61), channel_id=1, source_target_pairs={{0,1},{2,3},{4,5},{6,7},{8,9},{10,11},{12,13},{14,15},{16,17},{18,... | collective-permute-start | bytes 405512 | tf_op jit(solution)/shard_map/ppermute | solution.py:735
  15.9 12.7 %copy-start = (bf16[256,256]{1,0:T(8,128)(2,1)S(1)}, bf16[256,256]{1,0:T(8,128)(2,1)}, u32[]{:S(2)}) copy-start(bf16[256,256]{1,0:T(8,128)(2,1)} %constant.64.clone.refs_7_.refs_8_.kf_ref) | copy-start | bytes 393220
  15.9 12.7 %copy-start.1 = (bf16[256,256]{1,0:T(8,128)(2,1)S(1)}, bf16[256,256]{1,0:T(8,128)(2,1)}, u32[]{:S(2)}) copy-start(bf16[256,256]{1,0:T(8,128)(2,1)} %constant.65.clone.refs_8_.refs_9_) | copy-start | bytes 393220
  15.9 6.2 %collective-permute-start = (f32[2,8,8,128]{3,2,1,0:T(8,128)S(1)}, f32[2,8,8,128]{3,2,1,0:T(8,128)S(1)}, u32[]{:S(2)}, u32[]{:S(2)}) collective-permute-start(f32[2,8,8,128]{3,2,1,0:T(8,128)S(1)} %get-tuple-element.56), channel_id=1, source_target_pairs={{1,2},{3,0},{2,1},{0,3},{5,6},{7,4},{6,5},{4,7},{9,10},{11,8},{10,... | collective-permute-start | bytes 196616 | tf_op jit(solution)/shard_map/ppermute | solution.py:724
  16.0 6.1 %collective-permute-start.1 = (f32[2,8,8,128]{3,2,1,0:T(8,128)S(1)}, f32[2,8,8,128]{3,2,1,0:T(8,128)S(1)}, u32[]{:S(2)}, u32[]{:S(2)}) collective-permute-start(f32[2,8,8,128]{3,2,1,0:T(8,128)S(1)} %get-tuple-element.57), channel_id=1, source_target_pairs={{0,1},{2,3},{1,0},{3,2},{4,5},{6,7},{5,4},{7,6},{8,9},{10,11},{9,8... | collective-permute-start | bytes 196616 | tf_op jit(solution)/shard_map/ppermute | solution.py:724
  22.1 1.3 %copy-start.3 = (f32[4,8,8,8,128]{4,3,2,1,0:T(8,128)S(1)}, f32[4,8,8,8,128]{4,3,2,1,0:T(8,128)}, u32[]{:S(2)}) copy-start(f32[4,8,8,8,128]{4,3,2,1,0:T(8,128)} %copy-done.2) | copy-start | bytes 3145732
  24.6 1.5 %collective-permute-start.5 = (f32[8,1152]{1,0:T(8,128)S(1)}, f32[8,1152]{1,0:T(8,128)S(1)}, u32[]{:S(2)}, u32[]{:S(2)}) collective-permute-start(f32[8,1152]{1,0:T(8,128)S(1)} %get-tuple-element.66), channel_id=1, source_target_pairs={{4,8},{5,9},{6,10},{7,11},{12,16},{13,17},{14,18},{15,19},{20,24},... | collective-permute-start | bytes 110600 | tf_op jit(solution)/shard_map/ppermute | solution.py:718
  24.6 4.0 %collective-permute-start.6 = (f32[8,1152]{1,0:T(8,128)S(1)}, f32[8,1152]{1,0:T(8,128)S(1)}, u32[]{:S(2)}, u32[]{:S(2)}) collective-permute-start(f32[8,1152]{1,0:T(8,128)S(1)} %get-tuple-element.67), channel_id=1, source_target_pairs={{0,4},{1,5},{2,6},{3,7},{8,12},{9,13},{10,14},{11,15},{16,20},{17,... | collective-permute-start | bytes 110600 | tf_op jit(solution)/shard_map/ppermute | solution.py:718
  31.2 4.1 %collective-permute-start.7 = (f32[17,8,128]{2,1,0:T(8,128)S(1)}, f32[17,8,128]{2,1,0:T(8,128)S(1)}, u32[]{:S(2)}, u32[]{:S(2)}) collective-permute-start(f32[17,8,128]{2,1,0:T(8,128)S(1)} %get-tuple-element.73), channel_id=1, source_target_pairs={{1,2},{3,0},{2,1},{0,3},{5,6},{7,4},{6,5},{4,7},{9,10},{11,8},{10,... | collective-permute-start | bytes 208904 | tf_op jit(solution)/shard_map/ppermute | solution.py:724
  31.2 4.0 %collective-permute-start.8 = (f32[17,8,128]{2,1,0:T(8,128)S(1)}, f32[17,8,128]{2,1,0:T(8,128)S(1)}, u32[]{:S(2)}, u32[]{:S(2)}) collective-permute-start(f32[17,8,128]{2,1,0:T(8,128)S(1)} %get-tuple-element.74), channel_id=1, source_target_pairs={{0,1},{2,3},{1,0},{3,2},{4,5},{6,7},{5,4},{7,6},{8,9},{10,11},{9,8... | collective-permute-start | bytes 208904 | tf_op jit(solution)/shard_map/ppermute | solution.py:724
  37.4 4.4 %collective-permute-start.9 = (f32[17,8,128]{2,1,0:T(8,128)S(1)}, f32[17,8,128]{2,1,0:T(8,128)S(1)}, u32[]{:S(2)}, u32[]{:S(2)}) collective-permute-start(f32[17,8,128]{2,1,0:T(8,128)S(1)} %get-tuple-element.80), channel_id=1, source_target_pairs={{1,2},{3,0},{2,1},{0,3},{5,6},{7,4},{6,5},{4,7},{9,10},{11,8},{10,... | collective-permute-start | bytes 208904 | tf_op jit(solution)/shard_map/ppermute | solution.py:724
  37.7 4.2 %collective-permute-start.10 = (f32[17,8,128]{2,1,0:T(8,128)S(1)}, f32[17,8,128]{2,1,0:T(8,128)S(1)}, u32[]{:S(2)}, u32[]{:S(2)}) collective-permute-start(f32[17,8,128]{2,1,0:T(8,128)S(1)} %get-tuple-element.81), channel_id=1, source_target_pairs={{0,1},{2,3},{1,0},{3,2},{4,5},{6,7},{5,4},{7,6},{8,9},{10,11},{9,8... | collective-permute-start | bytes 208904 | tf_op jit(solution)/shard_map/ppermute | solution.py:724
  44.1 4.4 %collective-permute-start.11 = (f32[17,8,128]{2,1,0:T(8,128)S(1)}, f32[17,8,128]{2,1,0:T(8,128)S(1)}, u32[]{:S(2)}, u32[]{:S(2)}) collective-permute-start(f32[17,8,128]{2,1,0:T(8,128)S(1)} %get-tuple-element.86), channel_id=1, source_target_pairs={{1,2},{3,0},{2,1},{0,3},{5,6},{7,4},{6,5},{4,7},{9,10},{11,8},{10,... | collective-permute-start | bytes 208904 | tf_op jit(solution)/shard_map/ppermute | solution.py:724
  44.3 4.2 %collective-permute-start.12 = (f32[17,8,128]{2,1,0:T(8,128)S(1)}, f32[17,8,128]{2,1,0:T(8,128)S(1)}, u32[]{:S(2)}, u32[]{:S(2)}) collective-permute-start(f32[17,8,128]{2,1,0:T(8,128)S(1)} %get-tuple-element.87), channel_id=1, source_target_pairs={{0,1},{2,3},{1,0},{3,2},{4,5},{6,7},{5,4},{7,6},{8,9},{10,11},{9,8... | collective-permute-start | bytes 208904 | tf_op jit(solution)/shard_map/ppermute | solution.py:724
  50.7 4.2 %collective-permute-start.13 = (f32[17,8,128]{2,1,0:T(8,128)S(1)}, f32[17,8,128]{2,1,0:T(8,128)S(1)}, u32[]{:S(2)}, u32[]{:S(2)}) collective-permute-start(f32[17,8,128]{2,1,0:T(8,128)S(1)} %get-tuple-element.92), channel_id=1, source_target_pairs={{1,2},{3,0},{2,1},{0,3},{5,6},{7,4},{6,5},{4,7},{9,10},{11,8},{10,... | collective-permute-start | bytes 208904 | tf_op jit(solution)/shard_map/ppermute | solution.py:724
  50.8 4.2 %collective-permute-start.14 = (f32[17,8,128]{2,1,0:T(8,128)S(1)}, f32[17,8,128]{2,1,0:T(8,128)S(1)}, u32[]{:S(2)}, u32[]{:S(2)}) collective-permute-start(f32[17,8,128]{2,1,0:T(8,128)S(1)} %get-tuple-element.93), channel_id=1, source_target_pairs={{0,1},{2,3},{1,0},{3,2},{4,5},{6,7},{5,4},{7,6},{8,9},{10,11},{9,8... | collective-permute-start | bytes 208904 | tf_op jit(solution)/shard_map/ppermute | solution.py:724

commit v8 on v7

--- a/solution.py
+++ b/solution.py
@@ -121,9 +121,10 @@
     return pltpu.VMEM(shape, dtype)
 
 
-def call(kernel, out_shape, *args, smem=0, scratch=(), limit=12, **kw):
+def call(kernel, out_shape, *args, smem=0, hbm=0, scratch=(), limit=12, **kw):
     specs = [pl.BlockSpec(memory_space=pltpu.SMEM)] * smem
-    specs += [pl.BlockSpec(memory_space=pltpu.VMEM)] * (len(args) - smem)
+    specs += [pl.BlockSpec(memory_space=pltpu.HBM)] * hbm
+    specs += [pl.BlockSpec(memory_space=pltpu.VMEM)] * (len(args) - smem - hbm)
     outs = [pl.BlockSpec(memory_space=pltpu.VMEM) for _ in out_shape]
     return pl.pallas_call(
         kernel,
@@ -197,14 +198,14 @@
                     if (l, s) in ((0, 0), (0, 7), (1, 0), (1, 7)):
                         ends[l, s, at] = value
                     else:
-                        z_ref[l * na + at, r, s] = value
+                        z_ref[l * na + at, n, s] = value
         for at in range(na):
             shared = ends[0, 7, at] + ends[1, 0, at]
-            z_ref[at, r, 7] = shared
-            z_ref[na + at, r, 0] = shared
+            z_ref[at, n, 7] = shared
+            z_ref[na + at, n, 0] = shared
             lower, upper = ends[0, 0, at], ends[1, 7, at]
-            z_ref[at, r, 0] = lower
-            z_ref[na + at, r, 7] = upper
+            z_ref[at, n, 0] = lower
+            z_ref[na + at, n, 7] = upper
             send_faces(par_ref, (at, r), lower, upper, a_ref, b_ref)
 
 
@@ -446,7 +447,12 @@
     own_ref[...] = lax.dot_general(cond, keep, NT, preferred_element_type=f32).astype(bf16)
 
 
-def unpack_kernel(na, own_ref, r1_ref, r2_ref, r3_ref, dc_ref, wt_ref, wk_ref, behind_ref, ahead_ref):
+def unpack_kernel(
+    na, z_hbm, own_ref, r1_ref, r2_ref, r3_ref, dc_ref, wt_ref, wk_ref, behind_ref, ahead_ref, z_ref, sems
+):
+    copies = [pltpu.make_async_copy(z_hbm.at[j], z_ref.at[j], sems.at[j]) for j in range(2 * na)]
+    for copy in copies:
+        copy.start()
     rows = weight_rows(wt_ref[...] * KRYLOV_SCALE)
     got = jnp.concatenate([r[0:512] for r in (r1_ref, r2_ref, r3_ref)], 1)
     tags = [r[512:528].astype(f32) for r in (r1_ref, r2_ref, r3_ref)]
@@ -463,6 +469,8 @@
                 wk_ref[j, r, s] = rows[r][s] * kappa[r, s]
     rows = lambda j: wk_ref[j].reshape(512, LANES)
     behind_ref[...], ahead_ref[...] = send_rims(rows, rows, na)
+    for copy in copies:
+        copy.wait()
 
 
 def lines_t(k_ref, blocks):
@@ -817,10 +825,13 @@
         ]
         + [pl.BlockSpec((512 * tiles // split, LANES), lambda i: (i, 0))] * 2
         + [pl.BlockSpec((8, 8, LANES), lambda i: (0, 0, 0))],
-        out_specs=[pl.BlockSpec((3, 8, 8, 8, width), lambda i: (0, 0, 0, 0, i))] + [here()] * 7,
+        out_specs=[pl.BlockSpec((3, 8, 8, 8, width), lambda i: (0, 0, 0, 0, i))]
+        + [here()] * 4
+        + [pl.BlockSpec((tiles, 8 // split, 8, 8, LANES), lambda i: (0, i, 0, 0, 0))]
+        + [here()] * 2,
         out_shape=[shape(stream_speed_field.shape, bf16), kept((split, 512, width), bf16)]
         + [kept((528, room), bf16)] * 3
-        + [kept(field), kept((na, 8, 8, LANES)), kept((na, 8, 8, LANES))],
+        + [pltpu.HBM(field, f32), kept((na, 8, 8, LANES)), kept((na, 8, 8, LANES))],
         scratch_shapes=[pltpu.VMEM((3, 8, 8, 8, width), f32)] * 2,
         compiler_params=pltpu.CompilerParams(vmem_limit_bytes=24 * 1024 * 1024),
     )(
@@ -840,13 +851,16 @@
     )
     a, b, own = lax.optimization_barrier((a, b, own))
     b, a = swap(b, "chan", 1), swap(a, "chan", 0)
-    wk, wk_behind, wk_ahead = call(
+    wk, wk_behind, wk_ahead, z = call(
         functools.partial(unpack_kernel, na),
-        [kept(field), kept((2 * RIM, 512)), kept((2 * RIM, 512))],
+        [kept(field), kept((2 * RIM, 512)), kept((2 * RIM, 512)), kept(field)],
+        in_hbm(z),
         own,
         *received,
         dc,
         wt,
+        hbm=1,
+        scratch=[pltpu.SemaphoreType.DMA((tiles,))],
     )
     y, a, b = call(
         functools.partial(rim_kernel, na),

time: 69.9 us -> 68.3 us (0.977)
  local copies, waits for them, and re-layouts: 2.59 us -> 0.36 us
  Pallas kernels: 32.8 us -> 33.7 us
    unnamed x18 -> x14, local copies, waits for them, and re-layouts: 2.26 us -> 0.04 us
  transfers between devices with their start and end apart: 15 -> 15, of which waited for: 7 -> 7; matrix products, arithmetic and copies ran while one was open for 1% -> 1% of each run, Pallas kernels for 16% -> 17%
where the time goes in v8:
time: 68.3 us; the launch traced here: 68 us
  Pallas kernels  33.7 us (49%)
  waiting for transfers between devices  12.1 us (18%)
  starting transfers between devices  10.5 us (15%)
  blocking collectives  10.3 us (15%)
  between operations  0.88 us (1%)
    pallas_call x12, Pallas kernels, call(): pl.pallas_call(kernel, in_specs=specs, out_specs=outs, out_shape=out_shap...  24.3 us
    all_to_all x1, blocking collectives, on_device(): sums = lax.all_to_all(sums, ('slab', 'chan'), 0, 0)  10.3 us
    pallas_call x1, Pallas kernels, on_device(): pl.pallas_call(functools.partial(fluid_kernel, na, 8 // split, chan, tota...  7.49 us
    ppermute x10, waiting for transfers between devices, swap(): return lax.ppermute(x, axis, pairs + [(j, i) for i, j in pairs])  5.24 us
    ppermute x2, starting transfers between devices, swap_around(): return lax.ppermute(x, ('slab', 'chan'), pairs + [(j, i) for i, j in pairs])  3.5 us
    ppermute x1, starting transfers between devices, around(): lax.ppermute(x, ('slab', 'chan'), [(i, (i + by) % n) for i in range(n)])  2.95 us
    ppermute x10, starting transfers between devices, swap(): return lax.ppermute(x, axis, pairs + [(j, i) for i, j in pairs])  2.91 us
    ppermute x2, waiting for transfers between devices, slab_swap(): return lax.ppermute(x, ('slab', 'chan'), pairs + [(j, i) for i, j in pairs])  2.52 us
  transfers between devices with their start and end apart: 15, of which 7 were waited for; matrix products, arithmetic and copies ran while one was open for 1% of the time, Pallas kernels for 17%

profile of v8, /device:TPU:0, one launch (start us, length us, event | category | flops | bytes accessed | tf_op | source)
XLA Modules:
  0.0 68.0 jit_solution(12055647181116805045)
XLA Ops:
  0.7 0.1 stack.56.par_ref.refs_0_
  0.8 0.0 copy-start.2
  0.8 7.5 %shard_map.122 = (bf16[3,8,8,8,512]{4,3,2,1,0:T(8,128)(2,1)}, bf16[4,512,128]{2,1,0:T(8,128)(2,1)S(1)}, bf16[528,128]{1,0:T(8,128)(2,1)S(1)}, bf16[528,128]{1,0:...) custom-call(s32[1]{0:T(128)} %bitcast.me_ref, ...), custom_call_target="tpu_custom_call" | custom-call | tf_op jit(solution)/shard_map/pallas_call | solution.py:816
  8.3 2.9 %collective-permute-start = (bf16[528,128]{1,0:T(8,128)(2,1)S(1)}, bf16[528,128]{1,0:T(8,128)(2,1)S(1)}, u32[]{:S(2)}, u32[]{:S(2)}) collective-permute-start(bf16[528,128]{1,0:T(8,128)(2,1)S(1)} %get-tuple-element.58), channel_id=1, source_target_pairs={{0,4},{1,5},{2,6},{3,7},{4,8},{5,9},{6,10},{7,11},{8,12},{9,13},{1... | collective-permute-start | bytes 405512 | tf_op jit(solution)/shard_map/ppermute | solution.py:737
  11.2 3.5 %collective-permute-start.1 = (bf16[528,128]{1,0:T(8,128)(2,1)S(1)}, bf16[528,128]{1,0:T(8,128)(2,1)S(1)}, u32[]{:S(2)}, u32[]{:S(2)}) collective-permute-start(bf16[528,128]{1,0:T(8,128)(2,1)S(1)} %get-tuple-element.59), channel_id=1, source_target_pairs={{1,2},{3,4},{5,6},{7,8},{9,10},{11,12},{13,14},{15,16},{17,18},{19... | collective-permute-start | bytes 405512 | tf_op jit(solution)/shard_map/ppermute | solution.py:743
  14.7 0.5 shard_map.123.own_ref
  15.2 0.1 collective-permute-start.3
  15.3 0.6 collective-permute-start.4
  16.0 2.0 %collective-permute-done.r1_ref = bf16[528,128]{1,0:T(8,128)(2,1)S(1)} collective-permute-done((bf16[528,128]{1,0:T(8,128)(2,1)S(1)}, bf16[528,128]{1,0:T(8,128)(2,1)S(1)}, u32[]{:S(2)}, u32[]{:S(2)}) %collective-permute-start) | collective-permute-done | bytes 135200 | tf_op jit(solution)/shard_map/ppermute | solution.py:737
  17.9 2.4 %collective-permute-done.1.r2_ref = bf16[528,128]{1,0:T(8,128)(2,1)S(1)} collective-permute-done((bf16[528,128]{1,0:T(8,128)(2,1)S(1)}, bf16[528,128]{1,0:T(8,128)(2,1)S(1)}, u32[]{:S(2)}, u32[]{:S(2)}) %collective-permute-start.1) | collective-permute-done | bytes 135200 | tf_op jit(solution)/shard_map/ppermute | solution.py:743
  20.3 0.0 collective-permute-done.2.r3_ref
  20.3 0.0 copy-start.1
  20.4 1.7 %shard_map.124 = (f32[4,8,8,8,128]{4,3,2,1,0:T(8,128)S(1)}, f32[8,512]{1,0:T(8,128)S(1)}, f32[8,512]{1,0:T(8,128)S(1)}, f32[4,8,8,8,128]{4,3,2,1,0:T(8,128)S(1)}) custom-call(f32[4,8,8,8,128]{4,3,2,1,0:T(8,128)} %get-tuple-element.53.z_hbm, bf16[512,512]{1,0:T(8,128)(2,1)S(1)} %shard_map.123.own_ref, bf16[528,128]{1,0:T(8,128)(2,1)S(1)} %collective-permute-done.r1_ref, ...), custom_call_target="tpu_custom_call" | custom-call | tf_op jit(solution)/shard_map/pallas_call | solution.py:129
  22.1 0.0 collective-permute-done.4.a_ref
  22.1 1.2 %shard_map.125 = (f32[5,8,8,8,128]{4,3,2,1,0:T(8,128)S(1)}, f32[8,1152]{1,0:T(8,128)S(1)}, f32[8,1152]{1,0:T(8,128)S(1)}) custom-call(s32[6]{0:T(128)S(1)} %stack.56.par_ref.refs_0_, f32[4,8,8,8,128]{4,3,2,1,0:T(8,128)S(1)} %get-tuple-element.61.z_in, f32[2,8,8,128]{3,2,1,0:T(8,128)S(1)} %collective-permute-done.3.b_ref, ...), custom_call_target="tpu_custom_call" | custom-call | tf_op jit(solution)/shard_map/pallas_call | solution.py:129
  23.3 0.0 collective-permute-start.5
  23.3 1.2 %collective-permute-start.6 = (f32[8,1152]{1,0:T(8,128)S(1)}, f32[8,1152]{1,0:T(8,128)S(1)}, u32[]{:S(2)}, u32[]{:S(2)}) collective-permute-start(f32[8,1152]{1,0:T(8,128)S(1)} %get-tuple-element.69), channel_id=1, source_target_pairs={{0,4},{1,5},{2,6},{3,7},{8,12},{9,13},{10,14},{11,15},{16,20},{17,... | collective-permute-start | bytes 110600 | tf_op jit(solution)/shard_map/ppermute | solution.py:726
  24.5 0.1 pad_maximum_fusion.2
  24.6 0.1 mul.55
  24.7 0.1 copy.23
  24.8 0.0 collective-permute-done.5.refs_3_
  24.8 2.5 %collective-permute-done.6.refs_4_ = f32[8,1152]{1,0:T(8,128)S(1)} collective-permute-done((f32[8,1152]{1,0:T(8,128)S(1)}, f32[8,1152]{1,0:T(8,128)S(1)}, u32[]{:S(2)}, u32[]{:S(2)}) %collective-permute-start.6) | collective-permute-done | bytes 36896 | tf_op jit(solution)/shard_map/ppermute | solution.py:726
  27.4 2.5 %shard_map.126 = (f32[5,8,8,8,128]{4,3,2,1,0:T(8,128)S(1)}, f32[5,8,8,8,128]{4,3,2,1,0:T(8,128)S(1)}, f32[5,8,8,8,128]{4,3,2,1,0:T(8,128)S(1)}, f32[17,8,128]{2,...) custom-call(s32[6]{0:T(128)S(1)} %stack.56.par_ref.refs_0_, ...), custom_call_target="tpu_custom_call", output_to_operand_aliasing={{0}: (1, {})} | custom-call | tf_op jit(solution)/shard_map/pallas_call | solution.py:129
  29.9 0.1 collective-permute-start.7
  30.0 0.4 collective-permute-start.8
  30.3 0.1 multiply_bitcast_fusion
  30.4 2.2 %shard_map.127 = (f32[5,8,8,8,128]{4,3,2,1,0:T(8,128)S(1)}, f32[2,8,128]{2,1,0:T(8,128)S(1)}) custom-call(f32[5,8,8,8,128]{4,3,2,1,0:T(8,128)S(1)} %get-tuple-element.70.refs_0_.v0, f32[5,8,8,8,128]{4,3,2,1,0:T(8,128)S(1)} %get-tuple-element.71.refs_1_, f32[5,8,8,8,128]{4,3,2,1,0:T(8,128)S(1)} %get-tuple-element.72.refs_2_, ...), custom_call_target="tpu_custom_call" | custom-call | tf_op jit(solution)/shard_map/pallas_call | solution.py:129
  32.7 1.3 %collective-permute-done.7.refs_2_ = f32[17,8,128]{2,1,0:T(8,128)S(1)} collective-permute-done((f32[17,8,128]{2,1,0:T(8,128)S(1)}, f32[17,8,128]{2,1,0:T(8,128)S(1)}, u32[]{:S(2)}, u32[]{:S(2)}) %collective-permute-start.7) | collective-permute-done | bytes 69664 | tf_op jit(solution)/shard_map/ppermute | solution.py:732
  33.9 0.0 collective-permute-done.8.refs_3_
  33.9 2.2 %shard_map.128 = (f32[5,8,8,8,128]{4,3,2,1,0:T(8,128)S(1)}, f32[5,8,8,8,128]{4,3,2,1,0:T(8,128)S(1)}, f32[5,8,8,8,128]{4,3,2,1,0:T(8,128)S(1)}, f32[17,8,128]{2,1,0:T(8,128)S(1)}, f32[17,8,128]{2,1,0:T(8,128)S(1)}) custom-call(s32[6]{0:T(128)S(1)} %stack.56.par_ref.refs_0_, ...), custom_call_target="tpu_custom_call", output_to_operand_aliasing={{0}: (1, {})} | custom-call | tf_op jit(solution)/shard_map/pallas_call | solution.py:129
  36.2 0.2 collective-permute-start.9
  36.4 0.5 collective-permute-start.10
  36.9 2.4 %shard_map.129 = (f32[5,8,8,8,128]{4,3,2,1,0:T(8,128)S(1)}, f32[2,8,128]{2,1,0:T(8,128)S(1)}) custom-call(f32[5,8,8,8,128]{4,3,2,1,0:T(8,128)S(1)} %get-tuple-element.70.refs_0_.v0, f32[5,8,8,8,128]{4,3,2,1,0:T(8,128)S(1)} %get-tuple-element.78.refs_1_.refs_0_.v1, f32[5,8,8,8,128]{4,3,2,1,0:T(8,128)S(1)} %get-tuple-element.79.refs_2_, ...), custom_call_target="tpu_custom_call" | custom-call | tf_op jit(solution)/shard_map/pallas_call | solution.py:129
  39.2 1.3 %collective-permute-done.9.refs_2_ = f32[17,8,128]{2,1,0:T(8,128)S(1)} collective-permute-done((f32[17,8,128]{2,1,0:T(8,128)S(1)}, f32[17,8,128]{2,1,0:T(8,128)S(1)}, u32[]{:S(2)}, u32[]{:S(2)}) %collective-permute-start.9) | collective-permute-done | bytes 69664 | tf_op jit(solution)/shard_map/ppermute | solution.py:732
  40.6 0.0 collective-permute-done.10.refs_3_
  40.6 2.2 %shard_map.130 = (f32[5,8,8,8,128]{4,3,2,1,0:T(8,128)S(1)}, f32[5,8,8,8,128]{4,3,2,1,0:T(8,128)S(1)}, f32[5,8,8,8,128]{4,3,2,1,0:T(8,128)S(1)}, f32[17,8,128]{2,1,0:T(8,128)S(1)}, f32[17,8,128]{2,1,0:T(8,128)S(1)}) custom-call(s32[6]{0:T(128)S(1)} %stack.56.par_ref.refs_0_, ...), custom_call_target="tpu_custom_call", output_to_operand_aliasing={{0}: (1, {})} | custom-call | tf_op jit(solution)/shard_map/pallas_call | solution.py:129
  42.8 0.2 collective-permute-start.11
  43.0 0.4 collective-permute-start.12
  43.4 2.5 %shard_map.131 = (f32[5,8,8,8,128]{4,3,2,1,0:T(8,128)S(1)}, f32[2,8,128]{2,1,0:T(8,128)S(1)}) custom-call(f32[5,8,8,8,128]{4,3,2,1,0:T(8,128)S(1)} %get-tuple-element.78.refs_1_.refs_0_.v1, f32[5,8,8,8,128]{4,3,2,1,0:T(8,128)S(1)} %get-tuple-element.84.refs_1_.refs_0_.v2, f32[5,8,8,8,128]{4,3,2,1,0:T(8,128)S(1)} %get-tuple-element.85.refs_2_, ...), custom_call_target="tpu_custom_call" | custom-call | tf_op jit(solution)/shard_map/pallas_call | solution.py:129
  45.9 1.3 %collective-permute-done.11.refs_2_ = f32[17,8,128]{2,1,0:T(8,128)S(1)} collective-permute-done((f32[17,8,128]{2,1,0:T(8,128)S(1)}, f32[17,8,128]{2,1,0:T(8,128)S(1)}, u32[]{:S(2)}, u32[]{:S(2)}) %collective-permute-start.11) | collective-permute-done | bytes 69664 | tf_op jit(solution)/shard_map/ppermute | solution.py:732
  47.2 2.2 %shard_map.132 = (f32[5,8,8,8,128]{4,3,2,1,0:T(8,128)S(1)}, f32[5,8,8,8,128]{4,3,2,1,0:T(8,128)S(1)}, f32[5,8,8,8,128]{4,3,2,1,0:T(8,128)S(1)}, f32[17,8,128]{2,1,0:T(8,128)S(1)}, f32[17,8,128]{2,1,0:T(8,128)S(1)}) custom-call(s32[6]{0:T(128)S(1)} %stack.56.par_ref.refs_0_, ...), custom_call_target="tpu_custom_call", output_to_operand_aliasing={{0}: (1, {})} | custom-call | tf_op jit(solution)/shard_map/pallas_call | solution.py:129
  49.4 0.1 collective-permute-start.13
  49.5 0.5 collective-permute-start.14
  49.9 2.4 %shard_map.133 = (f32[5,8,8,8,128]{4,3,2,1,0:T(8,128)S(1)}, f32[2,8,128]{2,1,0:T(8,128)S(1)}) custom-call(f32[5,8,8,8,128]{4,3,2,1,0:T(8,128)S(1)} %get-tuple-element.84.refs_1_.refs_0_.v2, f32[5,8,8,8,128]{4,3,2,1,0:T(8,128)S(1)} %get-tuple-element.90.refs_1_.prev.v3, f32[5,8,8,8,128]{4,3,2,1,0:T(8,128)S(1)} %get-tuple-element.91.refs_2_, ...), custom_call_target="tpu_custom_call" | custom-call | tf_op jit(solution)/shard_map/pallas_call | solution.py:129
  52.3 1.4 %collective-permute-done.13.b_in = f32[17,8,128]{2,1,0:T(8,128)S(1)} collective-permute-done((f32[17,8,128]{2,1,0:T(8,128)S(1)}, f32[17,8,128]{2,1,0:T(8,128)S(1)}, u32[]{:S(2)}, u32[]{:S(2)}) %collective-permute-start.13) | collective-permute-done | bytes 69664 | tf_op jit(solution)/shard_map/ppermute | solution.py:732
  53.7 2.2 %shard_map.134 = (f32[5,8,8,8,128]{4,3,2,1,0:T(8,128)S(1)}, f32[32,1,128]{2,1,0:T(1,128)S(1)}) custom-call(s32[6]{0:T(128)S(1)} %stack.56.par_ref.refs_0_, f32[5,8,8,8,128]{4,3,2,1,0:T(8,128)S(1)} %get-tuple-element.93._, f32[17,8,128]{2,1,0:T(8,128)S(1)} %collective-permute-done.13.b_in, ...), custom_call_target="tpu_custom_call", output_to_operand_aliasing={{0}: (1, {})} | custom-call | tf_op jit(solution)/shard_map/pallas_call | solution.py:129
  55.9 10.3 %all_to_all.5.m_ref = f32[32,1,128]{2,1,0:T(1,128)S(1)} all-to-all(f32[32,1,128]{2,1,0:T(1,128)S(1)} %get-tuple-element.100), channel_id=1, replica_groups=mesh['slab'=8,'chan'=4] {'slab','chan'}, dimensions={0} | all-to-all | bytes 32768 | tf_op jit(solution)/shard_map/all_to_all | solution.py:941
  66.1 1.9 %shard_map.135 = f32[2048,128]{1,0:T(8,128)} custom-call(f32[32,1,128]{2,1,0:T(1,128)S(1)} %all_to_all.5.m_ref, f32[5,8,8,8,128]{4,3,2,1,0:T(8,128)S(1)} %get-tuple-element.70.refs_0_.v0, f32[5,8,8,8,128]{4,3,2,1,0:T(8,128)S(1)} %get-tuple-element.78.refs_1_.refs_0_.v1, f32[5,8,8,8,128]{4,3,2,1,0:T(8,128)S(1)} %get-tuple-element.84.refs_1_.refs_0_.v2, ...), custom_call_target="tpu_custom_call" | custom-call | tf_op jit(solution)/shard_map/pallas_call | solution.py:942
  (28 shorter events, 0.1 us)
Async XLA Ops:
  0.7 14.0 %copy-start.3 = (s32[512]{0:T(512)S(1)}, s32[512]{0:T(512)}, u32[]{:S(2)}) copy-start(s32[512]{0:T(512)} %param.12) | copy-start | bytes 6148
  0.7 15.1 %copy-start.4 = (s32[2,256]{1,0:T(2,128)S(1)}, s32[2,256]{1,0:T(2,128)}, u32[]{:S(2)}) copy-start(s32[2,256]{1,0:T(2,128)} %param.16) | copy-start | bytes 6148
  0.7 15.1 %copy-start.5 = (s32[2,256]{1,0:T(2,128)S(1)}, s32[2,256]{1,0:T(2,128)}, u32[]{:S(2)}) copy-start(s32[2,256]{1,0:T(2,128)} %param.15) | copy-start | bytes 6148
  0.8 19.6 %copy-start.2 = (f32[8,128]{1,0:T(8,128)S(1)}, f32[8,128]{1,0:T(8,128)}, u32[]{:S(2)}) copy-start(f32[8,128]{1,0:T(8,128)} %constant.62.clone.wt_ref.refs_6_.refs_5_.refs_7_) | copy-start | bytes 12292
  8.3 9.7 %collective-permute-start = (bf16[528,128]{1,0:T(8,128)(2,1)S(1)}, bf16[528,128]{1,0:T(8,128)(2,1)S(1)}, u32[]{:S(2)}, u32[]{:S(2)}) collective-permute-start(bf16[528,128]{1,0:T(8,128)(2,1)S(1)} %get-tuple-element.58), channel_id=1, source_target_pairs={{0,4},{1,5},{2,6},{3,7},{4,8},{5,9},{6,10},{7,11},{8,12},{9,13},{1... | collective-permute-start | bytes 405512 | tf_op jit(solution)/shard_map/ppermute | solution.py:737
  11.2 9.1 %collective-permute-start.1 = (bf16[528,128]{1,0:T(8,128)(2,1)S(1)}, bf16[528,128]{1,0:T(8,128)(2,1)S(1)}, u32[]{:S(2)}, u32[]{:S(2)}) collective-permute-start(bf16[528,128]{1,0:T(8,128)(2,1)S(1)} %get-tuple-element.59), channel_id=1, source_target_pairs={{1,2},{3,4},{5,6},{7,8},{9,10},{11,12},{13,14},{15,16},{17,18},{19... | collective-permute-start | bytes 405512 | tf_op jit(solution)/shard_map/ppermute | solution.py:743
  14.7 5.6 %collective-permute-start.2 = (bf16[528,128]{1,0:T(8,128)(2,1)S(1)}, bf16[528,128]{1,0:T(8,128)(2,1)S(1)}, u32[]{:S(2)}, u32[]{:S(2)}) collective-permute-start(bf16[528,128]{1,0:T(8,128)(2,1)S(1)} %get-tuple-element.60), channel_id=1, source_target_pairs={{0,1},{2,3},{4,5},{6,7},{8,9},{10,11},{12,13},{14,15},{16,17},{18,... | collective-permute-start | bytes 405512 | tf_op jit(solution)/shard_map/ppermute | solution.py:743
  15.2 6.9 %collective-permute-start.3 = (f32[2,8,8,128]{3,2,1,0:T(8,128)S(1)}, f32[2,8,8,128]{3,2,1,0:T(8,128)S(1)}, u32[]{:S(2)}, u32[]{:S(2)}) collective-permute-start(f32[2,8,8,128]{3,2,1,0:T(8,128)S(1)} %get-tuple-element.62), channel_id=1, source_target_pairs={{1,2},{3,0},{2,1},{0,3},{5,6},{7,4},{6,5},{4,7},{9,10},{11,8},{10,... | collective-permute-start | bytes 196616 | tf_op jit(solution)/shard_map/ppermute | solution.py:732
  15.3 6.8 %collective-permute-start.4 = (f32[2,8,8,128]{3,2,1,0:T(8,128)S(1)}, f32[2,8,8,128]{3,2,1,0:T(8,128)S(1)}, u32[]{:S(2)}, u32[]{:S(2)}) collective-permute-start(f32[2,8,8,128]{3,2,1,0:T(8,128)S(1)} %get-tuple-element.63), channel_id=1, source_target_pairs={{0,1},{2,3},{1,0},{3,2},{4,5},{6,7},{5,4},{7,6},{8,9},{10,11},{9,8... | collective-permute-start | bytes 196616 | tf_op jit(solution)/shard_map/ppermute | solution.py:732
  20.3 7.0 %copy-start = (bf16[256,256]{1,0:T(8,128)(2,1)S(1)}, bf16[256,256]{1,0:T(8,128)(2,1)}, u32[]{:S(2)}) copy-start(bf16[256,256]{1,0:T(8,128)(2,1)} %constant.64.clone.refs_7_.refs_8_.kf_ref) | copy-start | bytes 393220
  20.3 7.0 %copy-start.1 = (bf16[256,256]{1,0:T(8,128)(2,1)S(1)}, bf16[256,256]{1,0:T(8,128)(2,1)}, u32[]{:S(2)}) copy-start(bf16[256,256]{1,0:T(8,128)(2,1)} %constant.65.clone.refs_8_.refs_9_) | copy-start | bytes 393220
  23.3 1.5 %collective-permute-start.5 = (f32[8,1152]{1,0:T(8,128)S(1)}, f32[8,1152]{1,0:T(8,128)S(1)}, u32[]{:S(2)}, u32[]{:S(2)}) collective-permute-start(f32[8,1152]{1,0:T(8,128)S(1)} %get-tuple-element.68), channel_id=1, source_target_pairs={{4,8},{5,9},{6,10},{7,11},{12,16},{13,17},{14,18},{15,19},{20,24},... | collective-permute-start | bytes 110600 | tf_op jit(solution)/shard_map/ppermute | solution.py:726
  23.3 4.0 %collective-permute-start.6 = (f32[8,1152]{1,0:T(8,128)S(1)}, f32[8,1152]{1,0:T(8,128)S(1)}, u32[]{:S(2)}, u32[]{:S(2)}) collective-permute-start(f32[8,1152]{1,0:T(8,128)S(1)} %get-tuple-element.69), channel_id=1, source_target_pairs={{0,4},{1,5},{2,6},{3,7},{8,12},{9,13},{10,14},{11,15},{16,20},{17,... | collective-permute-start | bytes 110600 | tf_op jit(solution)/shard_map/ppermute | solution.py:726
  29.9 4.1 %collective-permute-start.7 = (f32[17,8,128]{2,1,0:T(8,128)S(1)}, f32[17,8,128]{2,1,0:T(8,128)S(1)}, u32[]{:S(2)}, u32[]{:S(2)}) collective-permute-start(f32[17,8,128]{2,1,0:T(8,128)S(1)} %get-tuple-element.75), channel_id=1, source_target_pairs={{1,2},{3,0},{2,1},{0,3},{5,6},{7,4},{6,5},{4,7},{9,10},{11,8},{10,... | collective-permute-start | bytes 208904 | tf_op jit(solution)/shard_map/ppermute | solution.py:732
  30.0 4.0 %collective-permute-start.8 = (f32[17,8,128]{2,1,0:T(8,128)S(1)}, f32[17,8,128]{2,1,0:T(8,128)S(1)}, u32[]{:S(2)}, u32[]{:S(2)}) collective-permute-start(f32[17,8,128]{2,1,0:T(8,128)S(1)} %get-tuple-element.76), channel_id=1, source_target_pairs={{0,1},{2,3},{1,0},{3,2},{4,5},{6,7},{5,4},{7,6},{8,9},{10,11},{9,8... | collective-permute-start | bytes 208904 | tf_op jit(solution)/shard_map/ppermute | solution.py:732
  36.2 4.4 %collective-permute-start.9 = (f32[17,8,128]{2,1,0:T(8,128)S(1)}, f32[17,8,128]{2,1,0:T(8,128)S(1)}, u32[]{:S(2)}, u32[]{:S(2)}) collective-permute-start(f32[17,8,128]{2,1,0:T(8,128)S(1)} %get-tuple-element.82), channel_id=1, source_target_pairs={{1,2},{3,0},{2,1},{0,3},{5,6},{7,4},{6,5},{4,7},{9,10},{11,8},{10,... | collective-permute-start | bytes 208904 | tf_op jit(solution)/shard_map/ppermute | solution.py:732
  36.4 4.2 %collective-permute-start.10 = (f32[17,8,128]{2,1,0:T(8,128)S(1)}, f32[17,8,128]{2,1,0:T(8,128)S(1)}, u32[]{:S(2)}, u32[]{:S(2)}) collective-permute-start(f32[17,8,128]{2,1,0:T(8,128)S(1)} %get-tuple-element.83), channel_id=1, source_target_pairs={{0,1},{2,3},{1,0},{3,2},{4,5},{6,7},{5,4},{7,6},{8,9},{10,11},{9,8... | collective-permute-start | bytes 208904 | tf_op jit(solution)/shard_map/ppermute | solution.py:732
  42.8 4.4 %collective-permute-start.11 = (f32[17,8,128]{2,1,0:T(8,128)S(1)}, f32[17,8,128]{2,1,0:T(8,128)S(1)}, u32[]{:S(2)}, u32[]{:S(2)}) collective-permute-start(f32[17,8,128]{2,1,0:T(8,128)S(1)} %get-tuple-element.88), channel_id=1, source_target_pairs={{1,2},{3,0},{2,1},{0,3},{5,6},{7,4},{6,5},{4,7},{9,10},{11,8},{10,... | collective-permute-start | bytes 208904 | tf_op jit(solution)/shard_map/ppermute | solution.py:732
  43.0 4.2 %collective-permute-start.12 = (f32[17,8,128]{2,1,0:T(8,128)S(1)}, f32[17,8,128]{2,1,0:T(8,128)S(1)}, u32[]{:S(2)}, u32[]{:S(2)}) collective-permute-start(f32[17,8,128]{2,1,0:T(8,128)S(1)} %get-tuple-element.89), channel_id=1, source_target_pairs={{0,1},{2,3},{1,0},{3,2},{4,5},{6,7},{5,4},{7,6},{8,9},{10,11},{9,8... | collective-permute-start | bytes 208904 | tf_op jit(solution)/shard_map/ppermute | solution.py:732
  49.4 4.2 %collective-permute-start.13 = (f32[17,8,128]{2,1,0:T(8,128)S(1)}, f32[17,8,128]{2,1,0:T(8,128)S(1)}, u32[]{:S(2)}, u32[]{:S(2)}) collective-permute-start(f32[17,8,128]{2,1,0:T(8,128)S(1)} %get-tuple-element.94), channel_id=1, source_target_pairs={{1,2},{3,0},{2,1},{0,3},{5,6},{7,4},{6,5},{4,7},{9,10},{11,8},{10,... | collective-permute-start | bytes 208904 | tf_op jit(solution)/shard_map/ppermute | solution.py:732
  49.5 4.2 %collective-permute-start.14 = (f32[17,8,128]{2,1,0:T(8,128)S(1)}, f32[17,8,128]{2,1,0:T(8,128)S(1)}, u32[]{:S(2)}, u32[]{:S(2)}) collective-permute-start(f32[17,8,128]{2,1,0:T(8,128)S(1)} %get-tuple-element.95), channel_id=1, source_target_pairs={{0,1},{2,3},{1,0},{3,2},{4,5},{6,7},{5,4},{7,6},{8,9},{10,11},{9,8... | collective-permute-start | bytes 208904 | tf_op jit(solution)/shard_map/ppermute | solution.py:732

commit v9 on v8

--- a/solution.py
+++ b/solution.py
@@ -940,10 +940,10 @@
     basis.append(v)
     sums = lax.all_to_all(sums, ("slab", "chan"), 0, 0)
     x = pl.pallas_call(
-        functools.partial(combine_kernel, na, 8 // steps),
-        grid=(steps,),
+        functools.partial(combine_kernel, na, 1),
+        grid=(8,),
         in_specs=[here()] * 6,
-        out_specs=pl.BlockSpec((rows, LANES), lambda i: (i, 0)),
+        out_specs=pl.BlockSpec((64 * tiles, LANES), lambda i: (i, 0)),
         out_shape=shape((512 * tiles, LANES)),
         scratch_shapes=[pltpu.VMEM((ITERS, 8, LANES), f32)],
         compiler_params=pltpu.CompilerParams(vmem_limit_bytes=12 * 1024 * 1024),

time: 68.3 us -> 69.5 us (1.018)
  Pallas kernels: 33.7 us -> 34.9 us
    pallas_call x1, Pallas kernels: 1.9 us -> 3.06 us  [on_device(): pl.pallas_call(functools.partial(combine_kernel, na, 1), grid=(8,), in_sp...]
where the time goes in v9:
time: 69.5 us; the launch traced here: 69.2 us
  Pallas kernels  34.9 us (50%)
  waiting for transfers between devices  12.1 us (17%)
  starting transfers between devices  10.5 us (15%)
  blocking collectives  10.3 us (15%)
  between operations  0.88 us (1%)
    pallas_call x12, Pallas kernels, call(): pl.pallas_call(kernel, in_specs=specs, out_specs=outs, out_shape=out_shap...  24.3 us
    all_to_all x1, blocking collectives, on_device(): sums = lax.all_to_all(sums, ('slab', 'chan'), 0, 0)  10.3 us
    pallas_call x1, Pallas kernels, on_device(): pl.pallas_call(functools.partial(fluid_kernel, na, 8 // split, chan, tota...  7.49 us
    ppermute x10, waiting for transfers between devices, swap(): return lax.ppermute(x, axis, pairs + [(j, i) for i, j in pairs])  5.24 us
    ppermute x2, starting transfers between devices, swap_around(): return lax.ppermute(x, ('slab', 'chan'), pairs + [(j, i) for i, j in pairs])  3.5 us
    pallas_call x1, Pallas kernels, on_device(): pl.pallas_call(functools.partial(combine_kernel, na, 1), grid=(8,), in_sp...  3.06 us
    ppermute x1, starting transfers between devices, around(): lax.ppermute(x, ('slab', 'chan'), [(i, (i + by) % n) for i in range(n)])  2.95 us
    ppermute x10, starting transfers between devices, swap(): return lax.ppermute(x, axis, pairs + [(j, i) for i, j in pairs])  2.91 us
  transfers between devices with their start and end apart: 15, of which 7 were waited for; matrix products, arithmetic and copies ran while one was open for 1% of the time, Pallas kernels for 17%

profile of v9, /device:TPU:0, one launch (start us, length us, event | category | flops | bytes accessed | tf_op | source)
XLA Modules:
  0.0 69.2 jit_solution(17141974076501964392)
XLA Ops:
  0.7 0.1 stack.56.par_ref.refs_0_
  0.8 0.0 copy-start.2
  0.8 7.5 %shard_map.122 = (bf16[3,8,8,8,512]{4,3,2,1,0:T(8,128)(2,1)}, bf16[4,512,128]{2,1,0:T(8,128)(2,1)S(1)}, bf16[528,128]{1,0:T(8,128)(2,1)S(1)}, bf16[528,128]{1,0:...) custom-call(s32[1]{0:T(128)} %bitcast.me_ref, ...), custom_call_target="tpu_custom_call" | custom-call | tf_op jit(solution)/shard_map/pallas_call | solution.py:816
  8.3 2.9 %collective-permute-start = (bf16[528,128]{1,0:T(8,128)(2,1)S(1)}, bf16[528,128]{1,0:T(8,128)(2,1)S(1)}, u32[]{:S(2)}, u32[]{:S(2)}) collective-permute-start(bf16[528,128]{1,0:T(8,128)(2,1)S(1)} %get-tuple-element.58), channel_id=1, source_target_pairs={{0,4},{1,5},{2,6},{3,7},{4,8},{5,9},{6,10},{7,11},{8,12},{9,13},{1... | collective-permute-start | bytes 405512 | tf_op jit(solution)/shard_map/ppermute | solution.py:737
  11.2 3.5 %collective-permute-start.1 = (bf16[528,128]{1,0:T(8,128)(2,1)S(1)}, bf16[528,128]{1,0:T(8,128)(2,1)S(1)}, u32[]{:S(2)}, u32[]{:S(2)}) collective-permute-start(bf16[528,128]{1,0:T(8,128)(2,1)S(1)} %get-tuple-element.59), channel_id=1, source_target_pairs={{1,2},{3,4},{5,6},{7,8},{9,10},{11,12},{13,14},{15,16},{17,18},{19... | collective-permute-start | bytes 405512 | tf_op jit(solution)/shard_map/ppermute | solution.py:743
  14.7 0.5 shard_map.123.own_ref
  15.2 0.1 collective-permute-start.3
  15.3 0.6 collective-permute-start.4
  16.0 2.0 %collective-permute-done.r1_ref = bf16[528,128]{1,0:T(8,128)(2,1)S(1)} collective-permute-done((bf16[528,128]{1,0:T(8,128)(2,1)S(1)}, bf16[528,128]{1,0:T(8,128)(2,1)S(1)}, u32[]{:S(2)}, u32[]{:S(2)}) %collective-permute-start) | collective-permute-done | bytes 135200 | tf_op jit(solution)/shard_map/ppermute | solution.py:737
  17.9 2.4 %collective-permute-done.1.r2_ref = bf16[528,128]{1,0:T(8,128)(2,1)S(1)} collective-permute-done((bf16[528,128]{1,0:T(8,128)(2,1)S(1)}, bf16[528,128]{1,0:T(8,128)(2,1)S(1)}, u32[]{:S(2)}, u32[]{:S(2)}) %collective-permute-start.1) | collective-permute-done | bytes 135200 | tf_op jit(solution)/shard_map/ppermute | solution.py:743
  20.3 0.0 collective-permute-done.2.r3_ref
  20.3 0.0 copy-start.1
  20.4 1.7 %shard_map.124 = (f32[4,8,8,8,128]{4,3,2,1,0:T(8,128)S(1)}, f32[8,512]{1,0:T(8,128)S(1)}, f32[8,512]{1,0:T(8,128)S(1)}, f32[4,8,8,8,128]{4,3,2,1,0:T(8,128)S(1)}) custom-call(f32[4,8,8,8,128]{4,3,2,1,0:T(8,128)} %get-tuple-element.53.z_hbm, bf16[512,512]{1,0:T(8,128)(2,1)S(1)} %shard_map.123.own_ref, bf16[528,128]{1,0:T(8,128)(2,1)S(1)} %collective-permute-done.r1_ref, ...), custom_call_target="tpu_custom_call" | custom-call | tf_op jit(solution)/shard_map/pallas_call | solution.py:129
  22.1 0.0 collective-permute-done.4.a_ref
  22.1 1.2 %shard_map.125 = (f32[5,8,8,8,128]{4,3,2,1,0:T(8,128)S(1)}, f32[8,1152]{1,0:T(8,128)S(1)}, f32[8,1152]{1,0:T(8,128)S(1)}) custom-call(s32[6]{0:T(128)S(1)} %stack.56.par_ref.refs_0_, f32[4,8,8,8,128]{4,3,2,1,0:T(8,128)S(1)} %get-tuple-element.61.z_in, f32[2,8,8,128]{3,2,1,0:T(8,128)S(1)} %collective-permute-done.3.b_ref, ...), custom_call_target="tpu_custom_call" | custom-call | tf_op jit(solution)/shard_map/pallas_call | solution.py:129
  23.3 0.0 collective-permute-start.5
  23.3 1.2 %collective-permute-start.6 = (f32[8,1152]{1,0:T(8,128)S(1)}, f32[8,1152]{1,0:T(8,128)S(1)}, u32[]{:S(2)}, u32[]{:S(2)}) collective-permute-start(f32[8,1152]{1,0:T(8,128)S(1)} %get-tuple-element.69), channel_id=1, source_target_pairs={{0,4},{1,5},{2,6},{3,7},{8,12},{9,13},{10,14},{11,15},{16,20},{17,... | collective-permute-start | bytes 110600 | tf_op jit(solution)/shard_map/ppermute | solution.py:726
  24.5 0.1 pad_maximum_fusion.2
  24.6 0.1 mul.55
  24.7 0.1 copy.23
  24.8 0.0 collective-permute-done.5.refs_3_
  24.8 2.5 %collective-permute-done.6.refs_4_ = f32[8,1152]{1,0:T(8,128)S(1)} collective-permute-done((f32[8,1152]{1,0:T(8,128)S(1)}, f32[8,1152]{1,0:T(8,128)S(1)}, u32[]{:S(2)}, u32[]{:S(2)}) %collective-permute-start.6) | collective-permute-done | bytes 36896 | tf_op jit(solution)/shard_map/ppermute | solution.py:726
  27.4 2.5 %shard_map.126 = (f32[5,8,8,8,128]{4,3,2,1,0:T(8,128)S(1)}, f32[5,8,8,8,128]{4,3,2,1,0:T(8,128)S(1)}, f32[5,8,8,8,128]{4,3,2,1,0:T(8,128)S(1)}, f32[17,8,128]{2,...) custom-call(s32[6]{0:T(128)S(1)} %stack.56.par_ref.refs_0_, ...), custom_call_target="tpu_custom_call", output_to_operand_aliasing={{0}: (1, {})} | custom-call | tf_op jit(solution)/shard_map/pallas_call | solution.py:129
  29.9 0.1 collective-permute-start.7
  30.0 0.4 collective-permute-start.8
  30.3 0.1 multiply_bitcast_fusion
  30.4 2.2 %shard_map.127 = (f32[5,8,8,8,128]{4,3,2,1,0:T(8,128)S(1)}, f32[2,8,128]{2,1,0:T(8,128)S(1)}) custom-call(f32[5,8,8,8,128]{4,3,2,1,0:T(8,128)S(1)} %get-tuple-element.70.refs_0_.v0, f32[5,8,8,8,128]{4,3,2,1,0:T(8,128)S(1)} %get-tuple-element.71.refs_1_, f32[5,8,8,8,128]{4,3,2,1,0:T(8,128)S(1)} %get-tuple-element.72.refs_2_, ...), custom_call_target="tpu_custom_call" | custom-call | tf_op jit(solution)/shard_map/pallas_call | solution.py:129
  32.7 1.3 %collective-permute-done.7.refs_2_ = f32[17,8,128]{2,1,0:T(8,128)S(1)} collective-permute-done((f32[17,8,128]{2,1,0:T(8,128)S(1)}, f32[17,8,128]{2,1,0:T(8,128)S(1)}, u32[]{:S(2)}, u32[]{:S(2)}) %collective-permute-start.7) | collective-permute-done | bytes 69664 | tf_op jit(solution)/shard_map/ppermute | solution.py:732
  33.9 0.0 collective-permute-done.8.refs_3_
  33.9 2.2 %shard_map.128 = (f32[5,8,8,8,128]{4,3,2,1,0:T(8,128)S(1)}, f32[5,8,8,8,128]{4,3,2,1,0:T(8,128)S(1)}, f32[5,8,8,8,128]{4,3,2,1,0:T(8,128)S(1)}, f32[17,8,128]{2,1,0:T(8,128)S(1)}, f32[17,8,128]{2,1,0:T(8,128)S(1)}) custom-call(s32[6]{0:T(128)S(1)} %stack.56.par_ref.refs_0_, ...), custom_call_target="tpu_custom_call", output_to_operand_aliasing={{0}: (1, {})} | custom-call | tf_op jit(solution)/shard_map/pallas_call | solution.py:129
  36.2 0.2 collective-permute-start.9
  36.4 0.5 collective-permute-start.10
  36.9 2.4 %shard_map.129 = (f32[5,8,8,8,128]{4,3,2,1,0:T(8,128)S(1)}, f32[2,8,128]{2,1,0:T(8,128)S(1)}) custom-call(f32[5,8,8,8,128]{4,3,2,1,0:T(8,128)S(1)} %get-tuple-element.70.refs_0_.v0, f32[5,8,8,8,128]{4,3,2,1,0:T(8,128)S(1)} %get-tuple-element.78.refs_1_.refs_0_.v1, f32[5,8,8,8,128]{4,3,2,1,0:T(8,128)S(1)} %get-tuple-element.79.refs_2_, ...), custom_call_target="tpu_custom_call" | custom-call | tf_op jit(solution)/shard_map/pallas_call | solution.py:129
  39.2 1.3 %collective-permute-done.9.refs_2_ = f32[17,8,128]{2,1,0:T(8,128)S(1)} collective-permute-done((f32[17,8,128]{2,1,0:T(8,128)S(1)}, f32[17,8,128]{2,1,0:T(8,128)S(1)}, u32[]{:S(2)}, u32[]{:S(2)}) %collective-permute-start.9) | collective-permute-done | bytes 69664 | tf_op jit(solution)/shard_map/ppermute | solution.py:732
  40.6 0.0 collective-permute-done.10.refs_3_
  40.6 2.2 %shard_map.130 = (f32[5,8,8,8,128]{4,3,2,1,0:T(8,128)S(1)}, f32[5,8,8,8,128]{4,3,2,1,0:T(8,128)S(1)}, f32[5,8,8,8,128]{4,3,2,1,0:T(8,128)S(1)}, f32[17,8,128]{2,1,0:T(8,128)S(1)}, f32[17,8,128]{2,1,0:T(8,128)S(1)}) custom-call(s32[6]{0:T(128)S(1)} %stack.56.par_ref.refs_0_, ...), custom_call_target="tpu_custom_call", output_to_operand_aliasing={{0}: (1, {})} | custom-call | tf_op jit(solution)/shard_map/pallas_call | solution.py:129
  42.8 0.2 collective-permute-start.11
  43.0 0.4 collective-permute-start.12
  43.4 2.5 %shard_map.131 = (f32[5,8,8,8,128]{4,3,2,1,0:T(8,128)S(1)}, f32[2,8,128]{2,1,0:T(8,128)S(1)}) custom-call(f32[5,8,8,8,128]{4,3,2,1,0:T(8,128)S(1)} %get-tuple-element.78.refs_1_.refs_0_.v1, f32[5,8,8,8,128]{4,3,2,1,0:T(8,128)S(1)} %get-tuple-element.84.refs_1_.refs_0_.v2, f32[5,8,8,8,128]{4,3,2,1,0:T(8,128)S(1)} %get-tuple-element.85.refs_2_, ...), custom_call_target="tpu_custom_call" | custom-call | tf_op jit(solution)/shard_map/pallas_call | solution.py:129
  45.9 1.3 %collective-permute-done.11.refs_2_ = f32[17,8,128]{2,1,0:T(8,128)S(1)} collective-permute-done((f32[17,8,128]{2,1,0:T(8,128)S(1)}, f32[17,8,128]{2,1,0:T(8,128)S(1)}, u32[]{:S(2)}, u32[]{:S(2)}) %collective-permute-start.11) | collective-permute-done | bytes 69664 | tf_op jit(solution)/shard_map/ppermute | solution.py:732
  47.2 2.2 %shard_map.132 = (f32[5,8,8,8,128]{4,3,2,1,0:T(8,128)S(1)}, f32[5,8,8,8,128]{4,3,2,1,0:T(8,128)S(1)}, f32[5,8,8,8,128]{4,3,2,1,0:T(8,128)S(1)}, f32[17,8,128]{2,1,0:T(8,128)S(1)}, f32[17,8,128]{2,1,0:T(8,128)S(1)}) custom-call(s32[6]{0:T(128)S(1)} %stack.56.par_ref.refs_0_, ...), custom_call_target="tpu_custom_call", output_to_operand_aliasing={{0}: (1, {})} | custom-call | tf_op jit(solution)/shard_map/pallas_call | solution.py:129
  49.4 0.1 collective-permute-start.13
  49.5 0.5 collective-permute-start.14
  49.9 2.4 %shard_map.133 = (f32[5,8,8,8,128]{4,3,2,1,0:T(8,128)S(1)}, f32[2,8,128]{2,1,0:T(8,128)S(1)}) custom-call(f32[5,8,8,8,128]{4,3,2,1,0:T(8,128)S(1)} %get-tuple-element.84.refs_1_.refs_0_.v2, f32[5,8,8,8,128]{4,3,2,1,0:T(8,128)S(1)} %get-tuple-element.90.refs_1_.prev.v3, f32[5,8,8,8,128]{4,3,2,1,0:T(8,128)S(1)} %get-tuple-element.91.refs_2_, ...), custom_call_target="tpu_custom_call" | custom-call | tf_op jit(solution)/shard_map/pallas_call | solution.py:129
  52.3 1.4 %collective-permute-done.13.b_in = f32[17,8,128]{2,1,0:T(8,128)S(1)} collective-permute-done((f32[17,8,128]{2,1,0:T(8,128)S(1)}, f32[17,8,128]{2,1,0:T(8,128)S(1)}, u32[]{:S(2)}, u32[]{:S(2)}) %collective-permute-start.13) | collective-permute-done | bytes 69664 | tf_op jit(solution)/shard_map/ppermute | solution.py:732
  53.7 2.2 %shard_map.134 = (f32[5,8,8,8,128]{4,3,2,1,0:T(8,128)S(1)}, f32[32,1,128]{2,1,0:T(1,128)S(1)}) custom-call(s32[6]{0:T(128)S(1)} %stack.56.par_ref.refs_0_, f32[5,8,8,8,128]{4,3,2,1,0:T(8,128)S(1)} %get-tuple-element.93._, f32[17,8,128]{2,1,0:T(8,128)S(1)} %collective-permute-done.13.b_in, ...), custom_call_target="tpu_custom_call", output_to_operand_aliasing={{0}: (1, {})} | custom-call | tf_op jit(solution)/shard_map/pallas_call | solution.py:129
  55.9 10.3 %all_to_all.5.m_ref = f32[32,1,128]{2,1,0:T(1,128)S(1)} all-to-all(f32[32,1,128]{2,1,0:T(1,128)S(1)} %get-tuple-element.100), channel_id=1, replica_groups=mesh['slab'=8,'chan'=4] {'slab','chan'}, dimensions={0} | all-to-all | bytes 32768 | tf_op jit(solution)/shard_map/all_to_all | solution.py:941
  66.1 3.1 %shard_map.135 = f32[2048,128]{1,0:T(8,128)} custom-call(f32[32,1,128]{2,1,0:T(1,128)S(1)} %all_to_all.5.m_ref, f32[5,8,8,8,128]{4,3,2,1,0:T(8,128)S(1)} %get-tuple-element.70.refs_0_.v0, f32[5,8,8,8,128]{4,3,2,1,0:T(8,128)S(1)} %get-tuple-element.78.refs_1_.refs_0_.v1, f32[5,8,8,8,128]{4,3,2,1,0:T(8,128)S(1)} %get-tuple-element.84.refs_1_.refs_0_.v2, ...), custom_call_target="tpu_custom_call" | custom-call | tf_op jit(solution)/shard_map/pallas_call | solution.py:942
  (28 shorter events, 0.1 us)
Async XLA Ops:
  0.7 14.0 %copy-start.3 = (s32[512]{0:T(512)S(1)}, s32[512]{0:T(512)}, u32[]{:S(2)}) copy-start(s32[512]{0:T(512)} %param.12) | copy-start | bytes 6148
  0.7 15.1 %copy-start.4 = (s32[2,256]{1,0:T(2,128)S(1)}, s32[2,256]{1,0:T(2,128)}, u32[]{:S(2)}) copy-start(s32[2,256]{1,0:T(2,128)} %param.16) | copy-start | bytes 6148
  0.7 15.1 %copy-start.5 = (s32[2,256]{1,0:T(2,128)S(1)}, s32[2,256]{1,0:T(2,128)}, u32[]{:S(2)}) copy-start(s32[2,256]{1,0:T(2,128)} %param.15) | copy-start | bytes 6148
  0.8 19.6 %copy-start.2 = (f32[8,128]{1,0:T(8,128)S(1)}, f32[8,128]{1,0:T(8,128)}, u32[]{:S(2)}) copy-start(f32[8,128]{1,0:T(8,128)} %constant.62.clone.wt_ref.refs_6_.refs_5_.refs_7_) | copy-start | bytes 12292
  8.3 9.7 %collective-permute-start = (bf16[528,128]{1,0:T(8,128)(2,1)S(1)}, bf16[528,128]{1,0:T(8,128)(2,1)S(1)}, u32[]{:S(2)}, u32[]{:S(2)}) collective-permute-start(bf16[528,128]{1,0:T(8,128)(2,1)S(1)} %get-tuple-element.58), channel_id=1, source_target_pairs={{0,4},{1,5},{2,6},{3,7},{4,8},{5,9},{6,10},{7,11},{8,12},{9,13},{1... | collective-permute-start | bytes 405512 | tf_op jit(solution)/shard_map/ppermute | solution.py:737
  11.2 9.1 %collective-permute-start.1 = (bf16[528,128]{1,0:T(8,128)(2,1)S(1)}, bf16[528,128]{1,0:T(8,128)(2,1)S(1)}, u32[]{:S(2)}, u32[]{:S(2)}) collective-permute-start(bf16[528,128]{1,0:T(8,128)(2,1)S(1)} %get-tuple-element.59), channel_id=1, source_target_pairs={{1,2},{3,4},{5,6},{7,8},{9,10},{11,12},{13,14},{15,16},{17,18},{19... | collective-permute-start | bytes 405512 | tf_op jit(solution)/shard_map/ppermute | solution.py:743
  14.7 5.6 %collective-permute-start.2 = (bf16[528,128]{1,0:T(8,128)(2,1)S(1)}, bf16[528,128]{1,0:T(8,128)(2,1)S(1)}, u32[]{:S(2)}, u32[]{:S(2)}) collective-permute-start(bf16[528,128]{1,0:T(8,128)(2,1)S(1)} %get-tuple-element.60), channel_id=1, source_target_pairs={{0,1},{2,3},{4,5},{6,7},{8,9},{10,11},{12,13},{14,15},{16,17},{18,... | collective-permute-start | bytes 405512 | tf_op jit(solution)/shard_map/ppermute | solution.py:743
  15.2 6.9 %collective-permute-start.3 = (f32[2,8,8,128]{3,2,1,0:T(8,128)S(1)}, f32[2,8,8,128]{3,2,1,0:T(8,128)S(1)}, u32[]{:S(2)}, u32[]{:S(2)}) collective-permute-start(f32[2,8,8,128]{3,2,1,0:T(8,128)S(1)} %get-tuple-element.62), channel_id=1, source_target_pairs={{1,2},{3,0},{2,1},{0,3},{5,6},{7,4},{6,5},{4,7},{9,10},{11,8},{10,... | collective-permute-start | bytes 196616 | tf_op jit(solution)/shard_map/ppermute | solution.py:732
  15.3 6.8 %collective-permute-start.4 = (f32[2,8,8,128]{3,2,1,0:T(8,128)S(1)}, f32[2,8,8,128]{3,2,1,0:T(8,128)S(1)}, u32[]{:S(2)}, u32[]{:S(2)}) collective-permute-start(f32[2,8,8,128]{3,2,1,0:T(8,128)S(1)} %get-tuple-element.63), channel_id=1, source_target_pairs={{0,1},{2,3},{1,0},{3,2},{4,5},{6,7},{5,4},{7,6},{8,9},{10,11},{9,8... | collective-permute-start | bytes 196616 | tf_op jit(solution)/shard_map/ppermute | solution.py:732
  20.3 7.0 %copy-start = (bf16[256,256]{1,0:T(8,128)(2,1)S(1)}, bf16[256,256]{1,0:T(8,128)(2,1)}, u32[]{:S(2)}) copy-start(bf16[256,256]{1,0:T(8,128)(2,1)} %constant.64.clone.refs_7_.refs_8_.kf_ref) | copy-start | bytes 393220
  20.3 7.0 %copy-start.1 = (bf16[256,256]{1,0:T(8,128)(2,1)S(1)}, bf16[256,256]{1,0:T(8,128)(2,1)}, u32[]{:S(2)}) copy-start(bf16[256,256]{1,0:T(8,128)(2,1)} %constant.65.clone.refs_8_.refs_9_) | copy-start | bytes 393220
  23.3 1.5 %collective-permute-start.5 = (f32[8,1152]{1,0:T(8,128)S(1)}, f32[8,1152]{1,0:T(8,128)S(1)}, u32[]{:S(2)}, u32[]{:S(2)}) collective-permute-start(f32[8,1152]{1,0:T(8,128)S(1)} %get-tuple-element.68), channel_id=1, source_target_pairs={{4,8},{5,9},{6,10},{7,11},{12,16},{13,17},{14,18},{15,19},{20,24},... | collective-permute-start | bytes 110600 | tf_op jit(solution)/shard_map/ppermute | solution.py:726
  23.3 4.0 %collective-permute-start.6 = (f32[8,1152]{1,0:T(8,128)S(1)}, f32[8,1152]{1,0:T(8,128)S(1)}, u32[]{:S(2)}, u32[]{:S(2)}) collective-permute-start(f32[8,1152]{1,0:T(8,128)S(1)} %get-tuple-element.69), channel_id=1, source_target_pairs={{0,4},{1,5},{2,6},{3,7},{8,12},{9,13},{10,14},{11,15},{16,20},{17,... | collective-permute-start | bytes 110600 | tf_op jit(solution)/shard_map/ppermute | solution.py:726
  29.9 4.1 %collective-permute-start.7 = (f32[17,8,128]{2,1,0:T(8,128)S(1)}, f32[17,8,128]{2,1,0:T(8,128)S(1)}, u32[]{:S(2)}, u32[]{:S(2)}) collective-permute-start(f32[17,8,128]{2,1,0:T(8,128)S(1)} %get-tuple-element.75), channel_id=1, source_target_pairs={{1,2},{3,0},{2,1},{0,3},{5,6},{7,4},{6,5},{4,7},{9,10},{11,8},{10,... | collective-permute-start | bytes 208904 | tf_op jit(solution)/shard_map/ppermute | solution.py:732
  30.0 4.0 %collective-permute-start.8 = (f32[17,8,128]{2,1,0:T(8,128)S(1)}, f32[17,8,128]{2,1,0:T(8,128)S(1)}, u32[]{:S(2)}, u32[]{:S(2)}) collective-permute-start(f32[17,8,128]{2,1,0:T(8,128)S(1)} %get-tuple-element.76), channel_id=1, source_target_pairs={{0,1},{2,3},{1,0},{3,2},{4,5},{6,7},{5,4},{7,6},{8,9},{10,11},{9,8... | collective-permute-start | bytes 208904 | tf_op jit(solution)/shard_map/ppermute | solution.py:732
  36.2 4.4 %collective-permute-start.9 = (f32[17,8,128]{2,1,0:T(8,128)S(1)}, f32[17,8,128]{2,1,0:T(8,128)S(1)}, u32[]{:S(2)}, u32[]{:S(2)}) collective-permute-start(f32[17,8,128]{2,1,0:T(8,128)S(1)} %get-tuple-element.82), channel_id=1, source_target_pairs={{1,2},{3,0},{2,1},{0,3},{5,6},{7,4},{6,5},{4,7},{9,10},{11,8},{10,... | collective-permute-start | bytes 208904 | tf_op jit(solution)/shard_map/ppermute | solution.py:732
  36.4 4.2 %collective-permute-start.10 = (f32[17,8,128]{2,1,0:T(8,128)S(1)}, f32[17,8,128]{2,1,0:T(8,128)S(1)}, u32[]{:S(2)}, u32[]{:S(2)}) collective-permute-start(f32[17,8,128]{2,1,0:T(8,128)S(1)} %get-tuple-element.83), channel_id=1, source_target_pairs={{0,1},{2,3},{1,0},{3,2},{4,5},{6,7},{5,4},{7,6},{8,9},{10,11},{9,8... | collective-permute-start | bytes 208904 | tf_op jit(solution)/shard_map/ppermute | solution.py:732
  42.8 4.4 %collective-permute-start.11 = (f32[17,8,128]{2,1,0:T(8,128)S(1)}, f32[17,8,128]{2,1,0:T(8,128)S(1)}, u32[]{:S(2)}, u32[]{:S(2)}) collective-permute-start(f32[17,8,128]{2,1,0:T(8,128)S(1)} %get-tuple-element.88), channel_id=1, source_target_pairs={{1,2},{3,0},{2,1},{0,3},{5,6},{7,4},{6,5},{4,7},{9,10},{11,8},{10,... | collective-permute-start | bytes 208904 | tf_op jit(solution)/shard_map/ppermute | solution.py:732
  43.0 4.2 %collective-permute-start.12 = (f32[17,8,128]{2,1,0:T(8,128)S(1)}, f32[17,8,128]{2,1,0:T(8,128)S(1)}, u32[]{:S(2)}, u32[]{:S(2)}) collective-permute-start(f32[17,8,128]{2,1,0:T(8,128)S(1)} %get-tuple-element.89), channel_id=1, source_target_pairs={{0,1},{2,3},{1,0},{3,2},{4,5},{6,7},{5,4},{7,6},{8,9},{10,11},{9,8... | collective-permute-start | bytes 208904 | tf_op jit(solution)/shard_map/ppermute | solution.py:732
  49.4 4.2 %collective-permute-start.13 = (f32[17,8,128]{2,1,0:T(8,128)S(1)}, f32[17,8,128]{2,1,0:T(8,128)S(1)}, u32[]{:S(2)}, u32[]{:S(2)}) collective-permute-start(f32[17,8,128]{2,1,0:T(8,128)S(1)} %get-tuple-element.94), channel_id=1, source_target_pairs={{1,2},{3,0},{2,1},{0,3},{5,6},{7,4},{6,5},{4,7},{9,10},{11,8},{10,... | collective-permute-start | bytes 208904 | tf_op jit(solution)/shard_map/ppermute | solution.py:732
  49.5 4.2 %collective-permute-start.14 = (f32[17,8,128]{2,1,0:T(8,128)S(1)}, f32[17,8,128]{2,1,0:T(8,128)S(1)}, u32[]{:S(2)}, u32[]{:S(2)}) collective-permute-start(f32[17,8,128]{2,1,0:T(8,128)S(1)} %get-tuple-element.95), channel_id=1, source_target_pairs={{0,1},{2,3},{1,0},{3,2},{4,5},{6,7},{5,4},{7,6},{8,9},{10,11},{9,8... | collective-permute-start | bytes 208904 | tf_op jit(solution)/shard_map/ppermute | solution.py:732
